TPU v7x, 32 devices: a whole 2x2x4 slice. The times are simulated.
32 devices in a mesh: dp: 16 (over z, x, core), tensor: 2 (over y).
Axes of the slice: x: 2, y: 2, z: 4, core: 2. Of those that a mesh axis runs over, the one named last changes fastest.
Arguments:
- tokens: bfloat16 [16384, 1024], P(('dp', 'tensor')), may hold values from -6 to 6
- segments: int32 [32, 512], P('dp'), may hold values from 0 to 4, never falling along the last dimension, each value on 1 to 200 neighbouring positions
- w_qkv: bfloat16 [3, 1024, 1024], P(None, 'dp', 'tensor'), may hold values from -0.1875 to 0.1875
- bias_qv: float32 [2, 1024], replicated, may hold values from -3 to 3
- w_out: bfloat16 [1024, 1024], P('tensor', 'dp'), may hold values from -1.5 to 1.5
- bias_out: float32 [1024], replicated, may hold values from -3 to 3
- ln1_gain: float32 [1024], replicated, may hold values from 0.5 to 1.5
- ln1_bias: float32 [1024], replicated, may hold values from -2 to 2
- w_up: bfloat16 [1024, 4096], P('dp', 'tensor'), may hold values from -0.1875 to 0.1875
- bias_up: float32 [4096], replicated, may hold values from -3 to 3
- w_down: bfloat16 [4096, 1024], P('tensor', 'dp'), may hold values from -0.09375 to 0.09375
- bias_down: float32 [1024], replicated, may hold values from -3 to 3
- ln2_gain: float32 [1024], replicated, may hold values from 0.5 to 1.5
- ln2_bias: float32 [1024], replicated, may hold values from -2 to 2
- d_out: bfloat16 [16384, 1024], P(('dp', 'tensor')), may hold values from -6 to 6
Outputs:
- output: bfloat16 [16384, 1024], P(('dp', 'tensor'))
- grad_tokens: float32 [16384, 1024], P(('dp', 'tensor'))
- grad_w_qkv: float32 [3, 1024, 1024], P(None, 'dp', 'tensor')
- grad_bias_qv: float32 [2, 1024], replicated
- grad_w_out: float32 [1024, 1024], P('tensor', 'dp')
- grad_bias_out: float32 [1024], replicated
- grad_ln1_gain: float32 [1024], replicated
- grad_ln1_bias: float32 [1024], replicated
- grad_w_up: float32 [1024, 4096], P('dp', 'tensor')
- grad_bias_up: float32 [4096], replicated
- grad_w_down: float32 [4096, 1024], P('tensor', 'dp')
- grad_bias_down: float32 [1024], replicated
- grad_ln2_gain: float32 [1024], replicated
- grad_ln2_bias: float32 [1024], replicated
Inputs may be any that keep to these rules, and one draw needn't show every extreme that they name: `segments`: within each sequence of 512 tokens the segment numbers never fall; each segment is one document.
All inputs are finite; a program needn't handle non-finite values.
Results may differ from a plain program's by a relative error of at most 0.02.
Values may be sent and summed in bfloat16 or wider, within the bound.
No kernel may reach another device: no remote copies, remote signals or barrier semaphores. Data moves between devices by JAX's collectives and lax.ppermute only.
A program may use at most 128 MiB of HBM per device.

v0:
```python
import jax
import jax.numpy as jnp
from jax import lax
from jax.sharding import PartitionSpec as P

HEAD_DIM = 64
SEQ = 512


eps = 1e-12


def matmul(left, right):
    return jnp.dot(left, right, preferred_element_type=jnp.float32)


def inner_rows(left, right):
    return lax.dot_general(
        left, right, (((0,), (0,)), ((), ())), preferred_element_type=jnp.float32
    )


def outer_cols(left, right):
    return lax.dot_general(
        left, right, (((1,), (1,)), ((), ())), preferred_element_type=jnp.float32
    )


def norm_forward(inputs, gain_vec, offset):
    center = jnp.mean(inputs, axis=-1, keepdims=True)
    spread = lax.rsqrt(jnp.mean(jnp.square(inputs - center), axis=-1, keepdims=True) + eps)
    scaled = (inputs - center) * spread
    return (scaled * gain_vec + offset, scaled, spread)


def norm_backward(gradient, scaled, spread, gain_vec):
    d_gain = jnp.sum(gradient * scaled, axis=0)
    d_offset = jnp.sum(gradient, axis=0)
    d_scaled = gradient * gain_vec
    d_inputs = spread * (
        d_scaled
        - jnp.mean(d_scaled, axis=-1, keepdims=True)
        - scaled * jnp.mean(d_scaled * scaled, axis=-1, keepdims=True)
    )
    return (d_inputs, d_gain, d_offset)


def masked_scores(queries, key_rows, segment):
    raw_scores = jnp.einsum("qhd,khd->hqk", queries, key_rows, preferred_element_type=jnp.float32)
    same_doc = segment[:, None] == segment[None, :]
    return jnp.where(same_doc[None], raw_scores * HEAD_DIM ** (-0.5), -1000000000.0)


def attend_forward(block):
    queries, key_rows, value_rows, segment = block
    scores = masked_scores(queries, key_rows, segment)
    row_max = jnp.max(scores, axis=-1, keepdims=True)
    exponent = jnp.exp(scores - row_max)
    row_total = jnp.sum(exponent, axis=-1, keepdims=True)
    probabilities = (exponent / row_total).astype(jnp.bfloat16)
    context = jnp.einsum(
        "hqk,khd->qhd", probabilities, value_rows, preferred_element_type=jnp.float32
    )
    return (context.astype(jnp.bfloat16), row_max[..., 0] + jnp.log(row_total[..., 0]))


def attend_backward(block):
    queries, key_rows, value_rows, segment, logsum, d_context = block
    scores = masked_scores(queries, key_rows, segment)
    probabilities = jnp.exp(scores - logsum[..., None])
    d_probs = jnp.einsum("qhd,khd->hqk", d_context, value_rows, preferred_element_type=jnp.float32)
    row_dot = jnp.sum(d_probs * probabilities, axis=-1, keepdims=True)
    d_raw = (probabilities * (d_probs - row_dot) * HEAD_DIM ** (-0.5)).astype(jnp.bfloat16)
    d_queries = jnp.einsum("hqk,khd->qhd", d_raw, key_rows, preferred_element_type=jnp.float32)
    d_keys = jnp.einsum("hqk,qhd->khd", d_raw, queries, preferred_element_type=jnp.float32)
    d_values = jnp.einsum(
        "hqk,qhd->khd",
        probabilities.astype(jnp.bfloat16),
        d_context,
        preferred_element_type=jnp.float32,
    )
    return (
        d_queries.astype(jnp.bfloat16),
        d_keys.astype(jnp.bfloat16),
        d_values.astype(jnp.bfloat16),
    )


def local(
    tokens,
    segments,
    w_qkv,
    bias_qv,
    w_out,
    bias_out,
    ln1_gain,
    ln1_bias,
    w_up,
    bias_up,
    w_down,
    bias_down,
    ln2_gain,
    ln2_bias,
    d_out,
):
    qkv_w, out_w, up_w, down_w = (
        lax.all_gather(w_qkv, "dp", axis=1, tiled=True),
        lax.all_gather(w_out, "dp", axis=1, tiled=True),
        lax.all_gather(w_up, "dp", axis=0, tiled=True),
        lax.all_gather(w_down, "dp", axis=1, tiled=True),
    )
    head_width = qkv_w.shape[2]
    unit_width = up_w.shape[1]
    tensor_index = lax.axis_index("tensor")
    bias_query = lax.dynamic_slice_in_dim(bias_qv[0], tensor_index * head_width, head_width)
    bias_value = lax.dynamic_slice_in_dim(bias_qv[1], tensor_index * head_width, head_width)
    bias_units = lax.dynamic_slice_in_dim(bias_up, tensor_index * unit_width, unit_width)
    block_rows = lax.all_gather(tokens, "tensor", axis=0, tiled=True)
    pieces = [
        matmul(block_rows, qkv_w[0]) + bias_query,
        matmul(block_rows, qkv_w[1]),
        matmul(block_rows, qkv_w[2]) + bias_value,
    ]
    qkv_all = jnp.concatenate(pieces, axis=1)
    qkv_rows = qkv_all.astype(jnp.bfloat16)
    group_rows = qkv_rows.shape[0]
    shape_seq = (segments.shape[0], SEQ, head_width // HEAD_DIM, HEAD_DIM)
    queries = qkv_rows[:, :head_width].reshape(shape_seq)
    key_rows = qkv_rows[:, head_width : 2 * head_width].reshape(shape_seq)
    value_rows = qkv_rows[:, 2 * head_width :].reshape(shape_seq)
    context, logsum = lax.map(attend_forward, (queries, key_rows, value_rows, segments))
    context_rows = context.reshape(group_rows, head_width)
    attn_rows = lax.psum_scatter(
        matmul(context_rows, out_w).astype(jnp.bfloat16), "tensor", scatter_dimension=0, tiled=True
    ).astype(jnp.float32)
    z_one = tokens.astype(jnp.float32) + attn_rows + bias_out
    h_one, scaled_one, spread_one = norm_forward(z_one, ln1_gain, ln1_bias)
    h_low = h_one.astype(jnp.bfloat16)
    pieces = [matmul(lax.all_gather(h_low, "tensor", axis=0, tiled=True), up_w) + bias_units]
    up_all = pieces[0]
    activation = jax.nn.gelu(up_all, approximate=False).astype(jnp.bfloat16)
    mlp_rows = lax.psum_scatter(
        matmul(activation, down_w).astype(jnp.bfloat16), "tensor", scatter_dimension=0, tiled=True
    ).astype(jnp.float32)
    z_two = h_one + mlp_rows + bias_down
    normed, scaled_two, spread_two = norm_forward(z_two, ln2_gain, ln2_bias)
    output = normed.astype(jnp.bfloat16)
    qkv_w, out_w, up_w, down_w = (
        lax.all_gather(w_qkv, "dp", axis=1, tiled=True),
        lax.all_gather(w_out, "dp", axis=1, tiled=True),
        lax.all_gather(w_up, "dp", axis=0, tiled=True),
        lax.all_gather(w_down, "dp", axis=1, tiled=True),
    )
    grad_two, d_gain_two, d_offset_two = norm_backward(
        d_out.astype(jnp.float32), scaled_two, spread_two, ln2_gain
    )
    d_bias_down = jnp.sum(grad_two, axis=0)
    grad_two_low = grad_two.astype(jnp.bfloat16)
    block_rows = lax.all_gather(grad_two_low, "tensor", axis=0, tiled=True)
    d_act = outer_cols(block_rows, down_w)
    d_wdown, d_act = (inner_rows(activation, block_rows), d_act)
    gelu_pull = jax.vjp(lambda inputs: jax.nn.gelu(inputs, approximate=False), up_all)[1]
    d_up = gelu_pull(d_act)[0].astype(jnp.bfloat16)
    d_bias_units = jnp.sum(d_up, axis=0, dtype=jnp.float32)
    d_bias_up = lax.dynamic_update_slice_in_dim(
        jnp.zeros(bias_up.shape, jnp.float32), d_bias_units, tensor_index * unit_width, 0
    )
    mlp_back = lax.psum_scatter(
        outer_cols(d_up, up_w).astype(jnp.bfloat16), "tensor", scatter_dimension=0, tiled=True
    ).astype(jnp.float32)
    d_wup = inner_rows(lax.all_gather(h_low, "tensor", axis=0, tiled=True), d_up)
    grad_one, d_gain_one, d_offset_one = norm_backward(
        mlp_back + grad_two, scaled_one, spread_one, ln1_gain
    )
    d_bias_out = jnp.sum(grad_one, axis=0)
    grad_one_low = grad_one.astype(jnp.bfloat16)
    block_rows = lax.all_gather(grad_one_low, "tensor", axis=0, tiled=True)
    d_ctx = outer_cols(block_rows, out_w)
    d_wout, d_ctx = (inner_rows(context_rows, block_rows), d_ctx)
    d_ctx_low = d_ctx.astype(jnp.bfloat16).reshape(shape_seq)
    d_queries, d_keys, d_values = lax.map(
        attend_backward, (queries, key_rows, value_rows, segments, logsum, d_ctx_low)
    )
    d_qkv = jnp.concatenate(
        [
            d_queries.reshape(group_rows, head_width),
            d_keys.reshape(group_rows, head_width),
            d_values.reshape(group_rows, head_width),
        ],
        axis=1,
    )
    bias_pair = jnp.stack(
        [
            jnp.sum(d_qkv[:, :head_width], axis=0, dtype=jnp.float32),
            jnp.sum(d_qkv[:, 2 * head_width :], axis=0, dtype=jnp.float32),
        ]
    )
    d_bias_qv = lax.dynamic_update_slice_in_dim(
        jnp.zeros(bias_qv.shape, jnp.float32), bias_pair, tensor_index * head_width, 1
    )
    total_rows = outer_cols(d_qkv[:, :head_width], qkv_w[0])
    total_rows = total_rows + outer_cols(d_qkv[:, head_width : 2 * head_width], qkv_w[1])
    attn_back = lax.psum_scatter(
        (total_rows + outer_cols(d_qkv[:, 2 * head_width :], qkv_w[2])).astype(jnp.bfloat16),
        "tensor",
        scatter_dimension=0,
        tiled=True,
    ).astype(jnp.float32)
    grad_tokens = attn_back + grad_one
    block_rows = lax.all_gather(tokens, "tensor", axis=0, tiled=True)
    grads_part = d_qkv
    grads_part = grads_part.reshape(block_rows.shape[0], 3, head_width)
    d_wqkv = jnp.einsum("rd,rtc->tdc", block_rows, grads_part, preferred_element_type=jnp.float32)
    grad_w_qkv, grad_w_out, grad_w_up, grad_w_down = (
        lax.psum_scatter(d_wqkv.astype(jnp.bfloat16), "dp", scatter_dimension=1, tiled=True).astype(
            jnp.float32
        ),
        lax.psum_scatter(d_wout.astype(jnp.bfloat16), "dp", scatter_dimension=1, tiled=True).astype(
            jnp.float32
        ),
        lax.psum_scatter(d_wup.astype(jnp.bfloat16), "dp", scatter_dimension=0, tiled=True).astype(
            jnp.float32
        ),
        lax.psum_scatter(
            d_wdown.astype(jnp.bfloat16), "dp", scatter_dimension=1, tiled=True
        ).astype(jnp.float32),
    )
    small_grads = lax.psum(
        (
            d_bias_qv,
            d_bias_out,
            d_gain_one,
            d_offset_one,
            d_bias_up,
            d_bias_down,
            d_gain_two,
            d_offset_two,
        ),
        ("dp", "tensor"),
    )
    return (
        output,
        grad_tokens,
        grad_w_qkv,
        small_grads[0],
        grad_w_out,
        small_grads[1],
        small_grads[2],
        small_grads[3],
        grad_w_up,
        small_grads[4],
        grad_w_down,
        small_grads[5],
        small_grads[6],
        small_grads[7],
    )


def solution(mesh):
    return jax.shard_map(
        local,
        mesh=mesh,
        in_specs=(
            P(("dp", "tensor"), None),
            P("dp", None),
            P(None, "dp", "tensor"),
            P(),
            P("tensor", "dp"),
            P(),
            P(),
            P(),
            P("dp", "tensor"),
            P(),
            P("tensor", "dp"),
            P(),
            P(),
            P(),
            P(("dp", "tensor"), None),
        ),
        out_specs=(
            P(("dp", "tensor"), None),
            P(("dp", "tensor"), None),
            P(None, "dp", "tensor"),
            P(),
            P("tensor", "dp"),
            P(),
            P(),
            P(),
            P("dp", "tensor"),
            P(),
            P("tensor", "dp"),
            P(),
            P(),
            P(),
        ),
        check_vma=False,
    )
```

profile of v0, /device:TPU:0, one launch (start us, length us, event | category | flops | bytes accessed | tf_op | source)
XLA Modules:
  0.0 854.3 jit_solution(4873306268633261056)
XLA Ops:
  10.3 35.1 %all-gather.9.cloned.1.call-done = bf16[1024,1024]{1,0:T(8,128)(2,1)} async-done(((bf16[512,1024]{1,0:T(8,128)(2,1)}), bf16[1024,1024]{1,0:T(8,128)(2,1)}) %all-gather.9.cloned.1.call-update) | async-done | bytes 2097168 | tf_op jit(solution)/shard_map/all_gather | solution.py:118
  45.4 47.4 %all-gather.11.cloned.1.call-done = bf16[3,1024,512]{2,1,0:T(8,128)(2,1)} async-done(((bf16[3,64,512]{2,1,0:T(8,128)(2,1)}), bf16[3,1024,512]{2,1,0:T(8,128)(2,1)}) %all-gather.11.cloned.1.call-update) | async-done | bytes 3145744 | tf_op jit(solution)/shard_map/all_gather | solution.py:107
  92.8 3.1 add_convert_fusion.4
  98.5 3.1 add_convert_fusion.3
  101.6 2.1 reshape.209
  103.7 2.5 copy.75
  106.2 3.1 convolution_convert_fusion.7
  109.3 2.1 reshape.210
  111.4 2.5 copy.76
  115.0 14.1 %while.26 = (s32[]{:T(128)}, bf16[2,512,8,64]{1,3,2,0:T(8,128)(2,1)}, f32[2,8,512]{2,1,0:T(8,128)}, bf16[2,512,8,64]{1,3,2,0:T(8,128)(2,1)S(1)}, s32[2,512]{1,0:...) while((s32[]{:T(128)}, ...), condition=%wide.region_3.4_spmd, body=%wide.region_0.3_spmd.sunk | while | flops 562556928 | bytes 36839580 | solution.py:131
  116.7 1.7 fusion.186
  118.5 2.5 fusion.187
  123.7 1.7 fusion.186
  125.5 2.5 fusion.187
  129.1 2.7 copy.77
  133.1 4.3 convolution_convert_fusion.4
  138.0 30.2 %reduce-scatter.8.cloned.1.call-done = bf16[512,1024]{1,0:T(8,128)(2,1)} async-done(((bf16[1024,1024]{1,0:T(8,128)(2,1)}), bf16[512,1024]{1,0:T(8,128)(2,1)}) %reduce-scatter.8.cloned.1.call-update) | async-done | bytes 1048592 | tf_op jit(solution)/shard_map/reduce_scatter | solution.py:133
  168.2 1.7 fusion.130
  169.9 1.8 multiply_reduce_fusion.4
  174.2 46.8 %all-gather.17.cloned.1.call-done = bf16[1024,2048]{1,0:T(8,128)(2,1)} async-done(((bf16[64,2048]{1,0:T(8,128)(2,1)}), bf16[1024,2048]{1,0:T(8,128)(2,1)}) %all-gather.17.cloned.1.call-update) | async-done | bytes 4194320 | tf_op jit(solution)/shard_map/all_gather | solution.py:109
  221.0 33.7 %all-gather.15.cloned.1.call-done = bf16[1024,1024]{1,0:T(8,128)(2,1)} async-done(((bf16[512,1024]{1,0:T(8,128)(2,1)}), bf16[1024,1024]{1,0:T(8,128)(2,1)}) %all-gather.15.cloned.1.call-update) | async-done | bytes 2097168 | tf_op jit(solution)/shard_map/all_gather | solution.py:139
  254.7 26.2 %multiply_convert_fusion.1 = (bf16[1024,2048]{1,0:T(8,128)(2,1)}, f32[1024,2048]{1,0:T(8,128)}, f32[1024,2048]{1,0:T(8,128)}) fusion(f32[2048]{0:T(1024)S(1)} %dynamic_slice.44, bf16[1024,1024]{1,0:T(8,128)(2,1)} %all-gather.15.cloned.1.call-done, bf16[1024,2048]{1,0:T(8,128)(2,1)} %all-gather.17.cloned.1.call-done), kind=kOutput, calls=%fused_computation.86 | convolution fusion | flops 4433379328 | bytes 27271168 | tf_op jit(solution)/shard_map/dot_general | solution.py:14
  281.0 26.9 %all-gather.19.cloned.1.call-done = bf16[2048,1024]{0,1:T(8,128)(2,1)} async-done(((bf16[2048,64]{0,1:T(8,128)(2,1)}), bf16[2048,1024]{0,1:T(8,128)(2,1)}) %all-gather.19.cloned.1.call-update) | async-done | bytes 4194320 | tf_op jit(solution)/shard_map/all_gather | solution.py:110
  307.9 9.3 %convolution_convert_fusion.3 = bf16[1024,1024]{1,0:T(8,128)(2,1)} fusion(bf16[1024,2048]{1,0:T(8,128)(2,1)} %get-tuple-element.263, bf16[2048,1024]{0,1:T(8,128)(2,1)} %all-gather.19.cloned.1.call-done), kind=kOutput, calls=%fused_computation.139 | convolution fusion | flops 4296015872 | bytes 10485760 | tf_op jit(solution)/shard_map/dot_general | solution.py:14
  317.5 30.2 %reduce-scatter.10.cloned.1.call-done = bf16[512,1024]{1,0:T(8,128)(2,1)} async-done(((bf16[1024,1024]{1,0:T(8,128)(2,1)}), bf16[512,1024]{1,0:T(8,128)(2,1)}) %reduce-scatter.10.cloned.1.call-update) | async-done | bytes 1048592 | tf_op jit(solution)/shard_map/reduce_scatter | solution.py:142
  347.7 2.6 fusion.138
  352.3 2.9 fusion.136
  355.2 33.2 %all-gather.21.cloned.1.call-done = bf16[1024,1024]{1,0:T(8,128)(2,1)} async-done(((bf16[512,1024]{1,0:T(8,128)(2,1)}), bf16[1024,1024]{1,0:T(8,128)(2,1)}) %all-gather.21.cloned.1.call-update) | async-done | bytes 2097168 | tf_op jit(solution)/shard_map/all_gather | solution.py:159
  388.4 13.9 %convert_reduce_fusion = (f32[2048]{0:T(1024)}, bf16[1024,2048]{1,0:T(8,128)(2,1)S(1)}) fusion(f32[1024,2048]{1,0:T(8,128)} %get-tuple-element.264, f32[1024,2048]{1,0:T(8,128)} %get-tuple-element.270, f32[2048]{0:T(1024)S(1)} %dynamic_slice.44, bf16[1024,1024]{1,0:T(8,128)(2,1)} %all-gather.21.cloned.1.call-done, ...), kind=kOutput, calls=%fused_computation.84 | convolution fusion | flops 4330616832 | bytes 27279360 | tf_op jit(solution)/shard_map/dot_general | solution.py:24
  402.3 2.1 copy-done.34
  404.4 5.8 convolution_convert_fusion.2
  410.3 31.9 %reduce-scatter.12.cloned.1.call-done = bf16[512,1024]{1,0:T(8,128)(2,1)} async-done(((bf16[1024,1024]{1,0:T(8,128)(2,1)}), bf16[512,1024]{1,0:T(8,128)(2,1)}) %reduce-scatter.12.cloned.1.call-update) | async-done | bytes 1048592 | tf_op jit(solution)/shard_map/reduce_scatter | solution.py:168
  442.2 4.3 multiply_reduce_fusion.1
  446.6 1.6 fusion.135
  451.2 9.4 %convolution_convert_fusion.1 = bf16[1024,2048]{1,0:T(8,128)(2,1)} fusion(bf16[1024,1024]{1,0:T(8,128)(2,1)} %all-gather.15.cloned.1.call-done, bf16[1024,2048]{1,0:T(8,128)(2,1)} %copy-done.34), kind=kOutput, calls=%fused_computation.102 | convolution fusion | flops 4297064448 | bytes 10485760 | tf_op jit(solution)/shard_map/dot_general | solution.py:18
  460.7 9.5 %convolution_convert_fusion = bf16[2048,1024]{0,1:T(8,128)(2,1)} fusion(bf16[1024,2048]{1,0:T(8,128)(2,1)} %get-tuple-element.263, bf16[1024,1024]{1,0:T(8,128)(2,1)} %all-gather.21.cloned.1.call-done), kind=kOutput, calls=%fused_computation.101 | convolution fusion | flops 4297064448 | bytes 10485760 | tf_op jit(solution)/shard_map/dot_general | solution.py:18
  470.2 13.8 %all-gather.23.cloned.1.call-done = bf16[1024,1024]{1,0:T(8,128)(2,1)} async-done(((bf16[512,1024]{1,0:T(8,128)(2,1)}), bf16[1024,1024]{1,0:T(8,128)(2,1)}) %all-gather.23.cloned.1.call-update) | async-done | bytes 2097168 | tf_op jit(solution)/shard_map/all_gather | solution.py:177
  484.0 3.8 convolution_convert_fusion.6
  487.8 4.1 reshape.206
  491.9 3.3 copy.81
  498.5 94.7 %while.27 = (s32[]{:T(128)}, bf16[2,512,8,64]{1,3,2,0:T(8,128)(2,1)}, bf16[2,512,8,64]{1,3,2,0:T(8,128)(2,1)}, bf16[2,512,8,64]{1,3,2,0:T(8,128)(2,1)}, bf16[2,5...) while((s32[]{:T(128)}, ...), condition=%wide.region_17.18_spmd, body=%wide.region_15.17_spmd.sunk | while | flops 1397761024 | bytes 99216512 | solution.py:181
  498.5 5.7 fusion.198
  504.1 4.6 fusion.199
  509.7 14.6 %fusion.200 = bf16[2,512,8,64]{1,3,2,0:T(8,128)(2,1)} fusion(bf16[2,512,8,64]{1,3,2,0:T(8,128)(2,1)} %get-tuple-element.417, s32[]{:T(128)S(6)} %copy.125, f32[8,512,512]{1,2,0:T(8,128)} %fusion.198, f32[8,512,512]{1,2,0:T(8,128)} %fusion.199, f32[8,512]{1,0:T(8,128)S(1)} %dynamic-slice_bitcast_fusion.2, ...), kind=kOutput, calls=%fused_computation.49.clone.1 | convolution fusion | flops 291770880 | bytes 35161088 | tf_op jit(solution)/shard_map/while/body/eval_jaxpr/hqk,khd->qhd/dot_general | solution.py:74
  524.3 14.4 %fusion.201 = bf16[2,512,8,64]{1,3,2,0:T(8,128)(2,1)} fusion(bf16[2,512,8,64]{1,3,2,0:T(8,128)(2,1)} %get-tuple-element.418, s32[]{:T(128)S(6)} %copy.125, f32[8,512,512]{1,2,0:T(8,128)} %fusion.198, f32[8,512,512]{1,2,0:T(8,128)} %fusion.199, f32[8,512]{1,0:T(8,128)S(1)} %dynamic-slice_bitcast_fusion.2, ...), kind=kOutput, calls=%fused_computation.47.clone.1 | convolution fusion | flops 291770880 | bytes 35161088 | tf_op jit(solution)/shard_map/while/body/eval_jaxpr/hqk,qhd->khd/dot_general | solution.py:75
  538.7 6.6 fusion.202
  545.3 5.6 fusion.198
  551.0 4.6 fusion.199
  556.5 14.1 %fusion.200 = bf16[2,512,8,64]{1,3,2,0:T(8,128)(2,1)} fusion(bf16[2,512,8,64]{1,3,2,0:T(8,128)(2,1)} %get-tuple-element.417, s32[]{:T(128)S(6)} %copy.125, f32[8,512,512]{1,2,0:T(8,128)} %fusion.198, f32[8,512,512]{1,2,0:T(8,128)} %fusion.199, f32[8,512]{1,0:T(8,128)S(1)} %dynamic-slice_bitcast_fusion.2, ...), kind=kOutput, calls=%fused_computation.49.clone.1 | convolution fusion | flops 291770880 | bytes 35161088 | tf_op jit(solution)/shard_map/while/body/eval_jaxpr/hqk,khd->qhd/dot_general | solution.py:74
  570.7 15.8 %fusion.201 = bf16[2,512,8,64]{1,3,2,0:T(8,128)(2,1)} fusion(bf16[2,512,8,64]{1,3,2,0:T(8,128)(2,1)} %get-tuple-element.418, s32[]{:T(128)S(6)} %copy.125, f32[8,512,512]{1,2,0:T(8,128)} %fusion.198, f32[8,512,512]{1,2,0:T(8,128)} %fusion.199, f32[8,512]{1,0:T(8,128)S(1)} %dynamic-slice_bitcast_fusion.2, ...), kind=kOutput, calls=%fused_computation.47.clone.1 | convolution fusion | flops 291770880 | bytes 35161088 | tf_op jit(solution)/shard_map/while/body/eval_jaxpr/hqk,qhd->khd/dot_general | solution.py:75
  586.5 6.5 fusion.202
  593.2 2.5 copy.83
  595.7 2.3 copy.84
  603.7 7.7 convert_bitcast_fusion
  611.4 7.7 copy.89
  619.2 4.2 convolution_convert_fusion.5
  628.3 2.6 add_convert_fusion.1
  634.5 1.8 convert_element_type.148
  636.4 1.8 convert_element_type.151
  638.3 42.4 %all-reduce.1 = (f32[2,1024]{1,0:T(2,128)}, f32[1024]{0:T(1024)}, f32[1024]{0:T(1024)}, f32[1024]{0:T(1024)}, f32[4096]{0:T(1024)}, /*index=5*/f32[1024]{0:T(1024)}, f32[1024]{0:T(1024)}, f32[1024]{0:T(1024)}) all-reduce(f32[2,1024]{1,0:T(2,128)S(1)} %maximum_dynamic-update-slice_fusion, ...), channel_id=1, replica_groups=mesh['dp'=16,'tensor'=2] {'dp','tensor'}, use_global_device_ids=true, to_apply=%region_22.23 | all-reduce | flops 12288 | bytes 98304 | tf_op jit(solution)/shard_map/psum | solution.py:228
  680.6 70.9 %all-reduce.4.cloned.1.call-done = bf16[3,1024,512]{2,0,1:T(4,128)(2,1)} async-done(((bf16[3,1024,512]{2,0,1:T(4,128)(2,1)}), bf16[3,1024,512]{2,0,1:T(4,128)(2,1)}) %all-reduce.4.cloned.1.call-update) | async-done | bytes 3145744
  753.4 57.9 %reduce-scatter.16.cloned.1.call-done = bf16[512,64]{0,1:T(8,128)(2,1)} async-done(((bf16[512,1024]{0,1:T(8,128)(2,1)}), bf16[512,64]{0,1:T(8,128)(2,1)}) %reduce-scatter.16.cloned.1.call-update) | async-done | bytes 65552 | tf_op jit(solution)/shard_map/reduce_scatter | solution.py:218
  812.8 31.6 %reduce-scatter.14.cloned.1.call-done = bf16[512,1024]{1,0:T(8,128)(2,1)} async-done(((bf16[1024,1024]{1,0:T(8,128)(2,1)}), bf16[512,1024]{1,0:T(8,128)(2,1)}) %reduce-scatter.14.cloned.1.call-update) | async-done | bytes 1048592 | tf_op jit(solution)/shard_map/reduce_scatter | solution.py:203
  844.4 3.0 convert_add_fusion
  (166 shorter events, 43.6 us)
Async XLA Ops:
  7.2 38.2 %all-gather.9.cloned.1.call-start = ((), (), s32[]{:S(2)}) async-start(), calls=%async_computation.7 | async-start | bytes 3145728 | tf_op jit(solution)/shard_map/all_gather | solution.py:118
  7.9 84.9 %all-gather.11.cloned.1.call-start = ((), (), s32[]{:S(2)}) async-start(), calls=%async_computation.8 | async-start | bytes 3342336 | tf_op jit(solution)/shard_map/all_gather | solution.py:107
  8.7 124.4 %all-gather.13.cloned.1.call-start = ((), (), s32[]{:S(2)}) async-start(), calls=%async_computation.9 | async-start | bytes 1114112 | tf_op jit(solution)/shard_map/all_gather | solution.py:108
  9.4 158.8 %reduce-scatter.8.cloned.1.call-start = ((), (), s32[]{:S(2)}) async-start(), calls=%async_computation.10 | async-start | bytes 3145728 | tf_op jit(solution)/shard_map/reduce_scatter | solution.py:133
  109.3 5.7 copy-start.16
  116.7 1.7 copy-start.12
  121.0 1.0 copy-start.13
  123.7 1.7 copy-start.12
  128.0 1.0 copy-start.13
  129.1 4.0 copy-start.6
  133.1 35.1 %copy-start = (bf16[512,1024]{1,0:T(8,128)(2,1)S(1)}, bf16[512,1024]{1,0:T(8,128)(2,1)}, u32[]{:S(2)}) copy-start(bf16[512,1024]{1,0:T(8,128)(2,1)} %param.19) | copy-start | bytes 3145732
  133.1 35.1 %copy-start.15 = (f32[1024]{0:T(1024)S(1)}, f32[1024]{0:T(1024)}, u32[]{:S(2)}) copy-start(f32[1024]{0:T(1024)} %param.24) | copy-start | bytes 12292
  137.3 34.4 %copy-start.18 = (f32[1024]{0:T(1024)S(1)}, f32[1024]{0:T(1024)}, u32[]{:S(2)}) copy-start(f32[1024]{0:T(1024)} %param.25) | copy-start | bytes 12292
  137.3 34.4 %copy-start.23 = (f32[1024]{0:T(1024)S(1)}, f32[1024]{0:T(1024)}, u32[]{:S(2)}) copy-start(f32[1024]{0:T(1024)} %param.26) | copy-start | bytes 12292
  137.4 83.6 %all-gather.17.cloned.1.call-start = ((), (), s32[]{:S(2)}) async-start(), calls=%async_computation.12 | async-start | bytes 4456448 | tf_op jit(solution)/shard_map/all_gather | solution.py:109
  138.0 36.2 %copy-start.29 = (f32[4096]{0:T(1024)S(1)}, f32[4096]{0:T(1024)}, u32[]{:S(2)}) copy-start(f32[4096]{0:T(1024)} %param.28) | copy-start | bytes 49156
  138.0 116.7 %all-gather.15.cloned.1.call-start = ((), (), s32[]{:S(2)}) async-start(), calls=%async_computation.11 | async-start | bytes 3145728 | tf_op jit(solution)/shard_map/all_gather | solution.py:139
  168.2 3.6 copy-start.1
  173.4 134.5 %all-gather.19.cloned.1.call-start = ((), (), s32[]{:S(2)}) async-start(), calls=%async_computation.13 | async-start | bytes 4456448 | tf_op jit(solution)/shard_map/all_gather | solution.py:110
  174.1 173.6 %reduce-scatter.10.cloned.1.call-start = ((), (), s32[]{:S(2)}) async-start(), calls=%async_computation.14 | async-start | bytes 3145728 | tf_op jit(solution)/shard_map/reduce_scatter | solution.py:142
  307.9 39.8 %copy-start.30 = (f32[1024]{0:T(1024)S(1)}, f32[1024]{0:T(1024)}, u32[]{:S(2)}) copy-start(f32[1024]{0:T(1024)} %param.30) | copy-start | bytes 12292
  317.2 33.5 %copy-start.19 = (f32[1024]{0:T(1024)S(1)}, f32[1024]{0:T(1024)}, u32[]{:S(2)}) copy-start(f32[1024]{0:T(1024)} %param.31) | copy-start | bytes 12292
  317.2 35.1 %copy-start.28 = (f32[1024]{0:T(1024)S(1)}, f32[1024]{0:T(1024)}, u32[]{:S(2)}) copy-start(f32[1024]{0:T(1024)} %param.32) | copy-start | bytes 12292
  317.2 71.2 %all-gather.21.cloned.1.call-start = ((), (), s32[]{:S(2)}) async-start(), calls=%async_computation.15 | async-start | bytes 3145728 | tf_op jit(solution)/shard_map/all_gather | solution.py:159
  347.7 3.0 copy-start.10
  355.2 87.1 %reduce-scatter.12.cloned.1.call-start = ((), (), s32[]{:S(2)}) async-start(), calls=%async_computation.16 | async-start | bytes 3145728 | tf_op jit(solution)/shard_map/reduce_scatter | solution.py:168
  388.4 16.0 %copy-start.31 = (bf16[1024,2048]{1,0:T(8,128)(2,1)S(1)}, bf16[1024,2048]{1,0:T(8,128)(2,1)}, u32[]{:S(2)}) copy-start(bf16[1024,2048]{1,0:T(8,128)(2,1)} %all-gather.17.cloned.1.call-done) | copy-start | bytes 12582916
  402.3 2.1 copy-start.34
  410.2 73.7 %all-gather.23.cloned.1.call-start = ((), (), s32[]{:S(2)}) async-start(), calls=%async_computation.17 | async-start | bytes 3145728 | tf_op jit(solution)/shard_map/all_gather | solution.py:177
  442.2 4.3 copy-start.2
  442.2 4.3 copy-start.3
  442.2 4.3 copy-start.11
  448.2 1.3 copy-start.4
  450.7 183.8 %reduce-scatter.18.cloned.1.call-start = ((), (), s32[]{:S(2)}) async-start(), calls=%async_computation.20 | async-start | bytes 4456448 | tf_op jit(solution)/shard_map/reduce_scatter | solution.py:221
  460.6 175.8 %reduce-scatter.20.cloned.1.call-start = ((), (), s32[]{:S(2)}) async-start(), calls=%async_computation.21 | async-start | bytes 4456448 | tf_op jit(solution)/shard_map/reduce_scatter | solution.py:224
  470.1 13.8 %copy-start.32 = (bf16[512,1024]{0,1:T(8,128)(2,1)S(1)}, bf16[512,1024]{0,1:T(8,128)(2,1)}, u32[]{:S(2)}) copy-start(bf16[512,1024]{0,1:T(8,128)(2,1)} %all-gather.13.cloned.1.call-done) | copy-start | bytes 3145732
  470.2 281.3 %all-reduce.4.cloned.1.call-start = ((), (), s32[]{:S(2)}) async-start(), calls=%async_computation.22 | async-start | bytes 8388608
  487.8 10.7 %copy-start.7 = (bf16[2,512,8,64]{1,3,2,0:T(8,128)(2,1)S(1)}, bf16[2,512,8,64]{1,3,2,0:T(8,128)(2,1)}, u32[]{:S(2)}) copy-start(bf16[2,512,8,64]{1,3,2,0:T(8,128)(2,1)} %copy-done.6) | copy-start | bytes 3145732
  487.8 10.7 %copy-start.17 = (s32[2,512]{1,0:T(2,128)S(1)}, s32[2,512]{1,0:T(2,128)}, u32[]{:S(2)}) copy-start(s32[2,512]{1,0:T(2,128)} %param.20) | copy-start | bytes 12292
  593.2 4.8 copy-start.9
  619.1 192.2 %reduce-scatter.16.cloned.1.call-start = ((), (), s32[]{:S(2)}) async-start(), calls=%async_computation.19 | async-start | bytes 1114112 | tf_op jit(solution)/shard_map/reduce_scatter | solution.py:218
  623.4 221.0 %reduce-scatter.14.cloned.1.call-start = ((), (), s32[]{:S(2)}) async-start(), calls=%async_computation.18 | async-start | bytes 3145728 | tf_op jit(solution)/shard_map/reduce_scatter | solution.py:203
  623.7 1.9 copy-start.14
  628.2 2.8 copy-start.33
  628.2 4.1 copy-start.27
  628.3 5.9 copy-start.8
  630.9 7.3 copy-start.20
  630.9 7.3 copy-start.21
  630.9 7.3 copy-start.22
  630.9 7.3 copy-start.24
  630.9 7.3 copy-start.25
  630.9 7.3 copy-start.26
  631.0 213.4 %copy-start.5 = (f32[512,1024]{1,0:T(8,128)S(1)}, f32[512,1024]{1,0:T(8,128)}, u32[]{:S(2)}) copy-start(f32[512,1024]{1,0:T(8,128)} %copy-done.4) | copy-start | bytes 6291460
Sparse Core Ops, SparseCore 0:
  9.6 35.8 all-gather.8
  47.6 45.1 all-gather.10
  95.0 36.7 all-gather.12
  137.5 30.6 reduce-scatter.7
  170.4 50.5 all-gather.16
  223.1 31.6 all-gather.14
  257.1 50.7 all-gather.18
  317.3 30.3 reduce-scatter.9
  355.3 33.1 all-gather.20
  410.4 31.8 reduce-scatter.11
  450.8 33.1 all-gather.22
  488.2 72.7 reduce-scatter.17
  564.8 71.5 reduce-scatter.19
  640.4 111.0 all-reduce.3
  755.0 56.2 reduce-scatter.15
  813.5 30.8 reduce-scatter.13
where the time goes:
time: 863 us; the launch traced here: 854 us
  waiting for transfers between devices  493 us (57%)
  matrix products  209 us (24%)
  local copies, waits for them, and re-layouts  55.7 us (6%)
  blocking collectives  42.4 us (5%)
  other arithmetic  36 us (4%)
  between operations  15.6 us (2%)
    unnamed x17, waiting for transfers between devices  74.3 us
    reduce_scatter x1, waiting for transfers between devices, local(): lax.psum_scatter(d_wout.astype(jnp.bfloat16), 'dp', scatter_dimension=1,...  57.9 us
    dot_general x6, matrix products, matmul(): return jnp.dot(left, right, preferred_element_type=jnp.float32)  49.1 us
    all_gather x1, waiting for transfers between devices, local(): lax.all_gather(w_qkv, 'dp', axis=1, tiled=True)  47.4 us
    all_gather x1, waiting for transfers between devices, local(): lax.all_gather(w_up, 'dp', axis=0, tiled=True)  46.8 us
    psum x1, blocking collectives, local(): lax.psum((d_bias_qv, d_bias_out, d_gain_one, d_offset_one, d_bias_up, d_b...  42.4 us
    all_gather x1, waiting for transfers between devices, local(): block_rows = lax.all_gather(tokens, 'tensor', axis=0, tiled=True)  35.1 us
    all_gather x1, waiting for transfers between devices, local(): lax.all_gather(h_low, 'tensor', axis=0, tiled=True)  33.7 us
  transfers between devices with their start and end apart: 16, of which 14 were waited for; matrix products, arithmetic and copies ran while one was open for 29% of the time, Pallas kernels for 0%

commit v1 on v0

--- a/solution.py
+++ b/solution.py
@@ -1,6 +1,10 @@
+import functools
+
 import jax
 import jax.numpy as jnp
 from jax import lax
+from jax.experimental import pallas as pl
+from jax.experimental.pallas import tpu as pltpu
 from jax.sharding import PartitionSpec as P
 
 HEAD_DIM = 64
@@ -86,7 +90,7 @@
     )
 
 
-def local(
+def tensor_plan(
     tokens,
     segments,
     w_qkv,
@@ -256,6 +260,339 @@
     )
 
 
+def swap(array, name, mask):
+    size = lax.axis_size(name)
+    return lax.ppermute(array, name, [(index, index ^ mask) for index in range(size)])
+
+
+def over_y(array):
+    return swap(array, "tensor", 1)
+
+
+def over_x(array):
+    return swap(array, "dp", 2)
+
+
+def over_core(array):
+    return swap(array, "dp", 1)
+
+
+def over_z(array, step):
+    return swap(array, "dp", 4 * step)
+
+
+def gather_weight(shard):
+    half_rows = shard.shape[0] // 2
+    stack = [shard] + [over_z(shard, step) for step in (1, 2, 3)]
+    halves = []
+    for half, first, second in ((0, over_x, over_y), (1, over_y, over_x)):
+        own = jnp.concatenate([part[half * half_rows :][:half_rows] for part in stack], axis=0)
+        near = first(own)
+        side = second(own)
+        both = second(near)
+        parts = [own, near, side, both] if half == 0 else [own, side, near, both]
+        halves.append((parts, [over_core(part) for part in parts]))
+    return [
+        jnp.concatenate(
+            [
+                part
+                for here, there in halves
+                for part in here[2 * group : 2 * group + 2] + there[2 * group : 2 * group + 2]
+            ],
+            axis=0,
+        )
+        for group in (0, 1)
+    ]
+
+
+def add_low(left, right):
+    return (left.astype(jnp.float32) + right.astype(jnp.float32)).astype(jnp.bfloat16)
+
+
+def scatter_grad(groups):
+    rows, columns = groups[0].shape
+    sums = []
+    for half in (0, 1):
+        blocks = [group.reshape(2, 2, 2, rows // 8, columns)[half] for group in groups]
+        others = [over_core(block[1]) for block in blocks]
+        blocks = [add_low(block[0], other) for block, other in zip(blocks, others)]
+        if half == 0:
+            block = add_low(blocks[0], over_y(blocks[1]))
+            block = add_low(block[0], over_x(block[1]))
+        else:
+            others = [over_x(block[1]) for block in blocks]
+            blocks = [add_low(block[0], other) for block, other in zip(blocks, others)]
+            block = add_low(blocks[0], over_y(blocks[1]))
+        sums.append(block.reshape(4, rows // 32, columns))
+    stack = jnp.concatenate(sums, axis=1)
+    parts = [stack[0]] + [over_z(stack[step], step) for step in (1, 2, 3)]
+    parts = [part.astype(jnp.float32) for part in parts]
+    return (parts[0] + parts[1]) + (parts[2] + parts[3])
+
+
+def sum_all(array):
+    array = (array + over_z(array, 1)) + (over_z(array, 2) + over_z(array, 3))
+    beside = over_y(array)
+    array = (array + over_x(array)) + (beside + over_x(beside))
+    return array + over_core(array)
+
+
+def head_scores(queries, key_rows, same_doc):
+    raw_scores = outer_cols(queries * jnp.bfloat16(HEAD_DIM ** (-0.5)), key_rows)
+    return jnp.where(same_doc, raw_scores, -1000000000.0)
+
+
+def attend_forward_kernel(q_ref, k_ref, v_ref, column_ref, row_ref, ctx_ref, logsum_ref):
+    lane = lax.broadcasted_iota(jnp.int32, q_ref.shape, 1) // HEAD_DIM
+    same_doc = column_ref[...] == row_ref[...]
+    value_rows = v_ref[...]
+    contexts = []
+    logsums = []
+    for head in (0, 1):
+        queries = jnp.where(lane == head, q_ref[...], jnp.bfloat16(0))
+        scores = head_scores(queries, k_ref[...], same_doc)
+        row_max = jnp.max(scores, axis=-1, keepdims=True)
+        exponent = jnp.exp(scores - row_max)
+        row_total = jnp.sum(exponent, axis=-1, keepdims=True)
+        probabilities = (exponent * (1.0 / row_total)).astype(jnp.bfloat16)
+        contexts.append(matmul(probabilities, value_rows))
+        logsums.append(row_max + jnp.log(row_total))
+    ctx_ref[...] = jnp.where(lane == 0, contexts[0], contexts[1]).astype(jnp.bfloat16)
+    logsum_ref[...] = jnp.where(lane == 0, logsums[0], logsums[1])
+
+
+def attend_backward_kernel(
+    q_ref, k_ref, v_ref, column_ref, row_ref, logsum_ref, dctx_ref, dq_ref, dk_ref, dv_ref
+):
+    lane = lax.broadcasted_iota(jnp.int32, q_ref.shape, 1) // HEAD_DIM
+    same_doc = column_ref[...] == row_ref[...]
+    key_rows = k_ref[...]
+    value_rows = v_ref[...]
+    results = []
+    for head in (0, 1):
+        queries = jnp.where(lane == head, q_ref[...], jnp.bfloat16(0))
+        d_context = jnp.where(lane == head, dctx_ref[...], jnp.bfloat16(0))
+        scores = head_scores(queries, key_rows, same_doc)
+        place = head * HEAD_DIM
+        probabilities = jnp.exp(scores - logsum_ref[:, place : place + 1])
+        d_probs = outer_cols(d_context, value_rows)
+        row_dot = jnp.sum(d_probs * probabilities, axis=-1, keepdims=True)
+        d_raw = (probabilities * (d_probs - row_dot) * HEAD_DIM ** (-0.5)).astype(jnp.bfloat16)
+        results.append(
+            (
+                matmul(d_raw, key_rows),
+                inner_rows(d_raw, queries),
+                inner_rows(probabilities.astype(jnp.bfloat16), d_context),
+            )
+        )
+    for ref, left, right in zip((dq_ref, dk_ref, dv_ref), *results):
+        ref[...] = jnp.where(lane == 0, left, right).astype(jnp.bfloat16)
+
+
+def attention_specs(rows, width, start):
+    return pl.BlockSpec((rows, width), lambda pair, start=start: (0, start + pair))
+
+
+def attend_rows_forward(qkv, column, row):
+    rows, pairs = qkv.shape[0], qkv.shape[1] // 384
+    whole = [pl.BlockSpec(column.shape, lambda pair: (0, 0)), pl.BlockSpec(row.shape, lambda pair: (0, 0))]
+    return pl.pallas_call(
+        attend_forward_kernel,
+        grid=(pairs,),
+        in_specs=[attention_specs(rows, 128, part * pairs) for part in range(3)] + whole,
+        out_specs=[attention_specs(rows, 128, 0)] * 2,
+        out_shape=[
+            jax.ShapeDtypeStruct((rows, pairs * 128), jnp.bfloat16),
+            jax.ShapeDtypeStruct((rows, pairs * 128), jnp.float32),
+        ],
+        cost_estimate=pl.CostEstimate(
+            flops=8 * pairs * rows * rows * 128,
+            bytes_accessed=pairs * rows * 128 * 12,
+            transcendentals=2 * pairs * rows * rows,
+        ),
+        compiler_params=pltpu.CompilerParams(vmem_limit_bytes=24 << 20),
+    )(qkv, qkv, qkv, column, row)
+
+
+def attend_rows_backward(qkv, column, row, logsum, d_context):
+    rows, pairs = qkv.shape[0], qkv.shape[1] // 384
+    whole = [pl.BlockSpec(column.shape, lambda pair: (0, 0)), pl.BlockSpec(row.shape, lambda pair: (0, 0))]
+    return pl.pallas_call(
+        attend_backward_kernel,
+        grid=(pairs,),
+        in_specs=[attention_specs(rows, 128, part * pairs) for part in range(3)]
+        + whole
+        + [attention_specs(rows, 128, 0)] * 2,
+        out_specs=[attention_specs(rows, 128, 0)] * 3,
+        out_shape=[jax.ShapeDtypeStruct((rows, pairs * 128), jnp.bfloat16)] * 3,
+        cost_estimate=pl.CostEstimate(
+            flops=20 * pairs * rows * rows * 128,
+            bytes_accessed=pairs * rows * 128 * 18,
+            transcendentals=2 * pairs * rows * rows,
+        ),
+        compiler_params=pltpu.CompilerParams(vmem_limit_bytes=32 << 20),
+    )(qkv, qkv, qkv, column, row, logsum, d_context)
+
+
+def gelu_pair(inputs):
+    share = 0.5 * (1.0 + lax.erf(inputs * 0.5**0.5))
+    slope = share + inputs * (jnp.exp(-0.5 * inputs * inputs) * (0.5 / jnp.pi) ** 0.5)
+    return (inputs * share).astype(jnp.bfloat16), slope.astype(jnp.bfloat16)
+
+
+def data_plan(
+    tokens,
+    segments,
+    w_qkv,
+    bias_qv,
+    w_out,
+    bias_out,
+    ln1_gain,
+    ln1_bias,
+    w_up,
+    bias_up,
+    w_down,
+    bias_down,
+    ln2_gain,
+    ln2_bias,
+    d_out,
+):
+    low, wide = jnp.bfloat16, jnp.float32
+    dp_index = lax.axis_index("dp")
+    tensor_index = lax.axis_index("tensor")
+    width = tokens.shape[1]
+    head_width = w_qkv.shape[2]
+    unit_width = w_up.shape[1]
+    groups = (0, 1)
+
+    qkv_w = gather_weight(jnp.concatenate([w_qkv[0], w_qkv[1], w_qkv[2]], axis=1))
+    out_w = gather_weight(w_out.T)
+    up_w = gather_weight(w_up)
+    down_w = gather_weight(w_down.T)
+
+    place = jnp.arange(width)
+    block = ((place // 32) % 4) * 4 + ((place // 128) % 2) * 2 + (place // 256) % 2
+    source = (dp_index ^ block) * 64 + (place // 512) * 32 + place % 32
+    order = (jnp.arange(width)[:, None] == source[None, :]).astype(low)
+
+    def group_of(vector, group, size):
+        return lax.dynamic_slice_in_dim(vector, (tensor_index ^ group) * size, size, axis=-1)
+
+    def whole_of(parts):
+        left, right = parts
+        return jnp.where(
+            tensor_index == 0,
+            jnp.concatenate([left, right], axis=-1),
+            jnp.concatenate([right, left], axis=-1),
+        )
+
+    vectors = jnp.dot(
+        jnp.stack([bias_out, ln1_gain, ln1_bias, bias_down, ln2_gain, ln2_bias]),
+        order.astype(wide),
+        precision=lax.Precision.HIGHEST,
+    )
+    bias_out, ln1_gain, ln1_bias, bias_down, ln2_gain, ln2_bias = [vectors[i] for i in range(6)]
+    own_rows = matmul(tokens, order).astype(low)
+    cotangent = matmul(d_out, order)
+
+    which = lax.dynamic_slice_in_dim(segments, tensor_index, 1, axis=0)
+    column, row = which.reshape(SEQ, 1), which
+
+    qkv, context, logsum = [], [], []
+    for group in groups:
+        bias = jnp.concatenate(
+            [
+                group_of(bias_qv[0], group, head_width),
+                jnp.zeros((head_width,), wide),
+                group_of(bias_qv[1], group, head_width),
+            ]
+        )
+        qkv.append((matmul(own_rows, qkv_w[group]) + bias).astype(low))
+        ctx, total = attend_rows_forward(qkv[group], column, row)
+        context.append(ctx)
+        logsum.append(total)
+    attn_rows = outer_cols(context[0], out_w[0]) + outer_cols(context[1], out_w[1])
+    z_one = own_rows.astype(wide) + attn_rows + bias_out
+    h_one, scaled_one, spread_one = norm_forward(z_one, ln1_gain, ln1_bias)
+    h_low = h_one.astype(low)
+    activation, slope = [], []
+    for group in groups:
+        units = matmul(h_low, up_w[group]) + group_of(bias_up, group, unit_width)
+        pair = gelu_pair(units)
+        activation.append(pair[0])
+        slope.append(pair[1])
+    mlp_rows = outer_cols(activation[0], down_w[0]) + outer_cols(activation[1], down_w[1])
+    z_two = h_one + mlp_rows + bias_down
+    normed, scaled_two, spread_two = norm_forward(z_two, ln2_gain, ln2_bias)
+    output = outer_cols(normed.astype(low), order).astype(low)
+
+    grad_two, d_gain_two, d_offset_two = norm_backward(cotangent, scaled_two, spread_two, ln2_gain)
+    d_bias_down = jnp.sum(grad_two, axis=0)
+    grad_two_low = grad_two.astype(low)
+    grad_w_down = scatter_grad([inner_rows(grad_two_low, activation[g]).astype(low) for g in groups]).T
+    d_up = [(matmul(grad_two_low, down_w[g]) * slope[g].astype(wide)).astype(low) for g in groups]
+    d_bias_up = whole_of([jnp.sum(d_up[g], axis=0, dtype=wide) for g in groups])
+    grad_w_up = scatter_grad([inner_rows(h_low, d_up[g]).astype(low) for g in groups])
+    mlp_back = outer_cols(d_up[0], up_w[0]) + outer_cols(d_up[1], up_w[1])
+    grad_one, d_gain_one, d_offset_one = norm_backward(
+        mlp_back + grad_two, scaled_one, spread_one, ln1_gain
+    )
+    d_bias_out = jnp.sum(grad_one, axis=0)
+    grad_one_low = grad_one.astype(low)
+    grad_w_out = scatter_grad([inner_rows(grad_one_low, context[g]).astype(low) for g in groups]).T
+    d_qkv = []
+    for group in groups:
+        d_ctx = matmul(grad_one_low, out_w[group]).astype(low)
+        d_qkv.append(
+            jnp.concatenate(
+                attend_rows_backward(qkv[group], column, row, logsum[group], d_ctx), axis=1
+            )
+        )
+    grad_qkv = scatter_grad([inner_rows(own_rows, d_qkv[g]).astype(low) for g in groups])
+    grad_w_qkv = jnp.stack([grad_qkv[:, i * head_width : (i + 1) * head_width] for i in range(3)])
+    attn_back = outer_cols(d_qkv[0], qkv_w[0]) + outer_cols(d_qkv[1], qkv_w[1])
+    grad_rows = attn_back + grad_one
+    upper = grad_rows.astype(low)
+    lower = (grad_rows - upper.astype(wide)).astype(low)
+    grad_tokens = outer_cols(upper, order) + outer_cols(lower, order)
+
+    sums = [jnp.sum(d_qkv[g], axis=0, dtype=wide) for g in groups]
+    d_bias_q = whole_of([s[:head_width] for s in sums])
+    d_bias_v = whole_of([s[2 * head_width :] for s in sums])
+    narrow = jnp.dot(
+        jnp.stack([d_bias_out, d_gain_one, d_offset_one, d_bias_down, d_gain_two, d_offset_two]),
+        order.astype(wide).T,
+        precision=lax.Precision.HIGHEST,
+    )
+    small = sum_all(
+        jnp.concatenate([narrow, d_bias_q[None], d_bias_v[None], d_bias_up.reshape(-1, width)], axis=0)
+    )
+    return (
+        output,
+        grad_tokens,
+        grad_w_qkv,
+        small[6:8],
+        grad_w_out,
+        small[0],
+        small[1],
+        small[2],
+        grad_w_up,
+        small[8:].reshape(-1),
+        grad_w_down,
+        small[3],
+        small[4],
+        small[5],
+    )
+
+
+def local(*arrays):
+    tokens = arrays[0]
+    sizes = (lax.axis_size("dp"), lax.axis_size("tensor"))
+    if sizes == (16, 2) and tokens.shape == (SEQ, 1024):
+        return data_plan(*arrays)
+    return tensor_plan(*arrays)
+
+
 def solution(mesh):
     return jax.shard_map(
         local,

time: 863 us -> 567 us (0.66)
  waiting for transfers between devices: 493 us -> 288 us
  matrix products: 209 us -> 80 us
  starting transfers between devices: 1.51 us -> 105 us
  blocking collectives: 42.4 us -> 0 us
  Pallas kernels: 0 us -> 32.2 us
  other arithmetic: 36 us -> 14.8 us
  local copies, waits for them, and re-layouts: 55.7 us -> 38.1 us
  between operations: 15.6 us -> 3.32 us
    ppermute x0 -> x123, waiting for transfers between devices: none -> 288 us  [swap(): lax.ppermute(array, name, [(index, index ^ mask) for index in range(size)])]
    all_gather x8 -> x0, waiting for transfers between devices: 237 us -> none  [the longest x1 47.4 us: local(): lax.all_gather(w_qkv, 'dp', axis=1, tiled=True)]
    reduce_scatter x7 -> x0, waiting for transfers between devices: 182 us -> none  [the longest x1 57.9 us: local(): lax.psum_scatter(d_wout.astype(jnp.bfloat16), 'dp', scatter_dimension=1,...]
    dot_general x15 -> x2, matrix products: 108 us -> 3.29 us  [the longest x1 1.93 us: data_plan(): jnp.dot(jnp.stack([d_bias_out, d_gain_one, d_offset_one, d_bias_down, d_g...]
    ppermute x0 -> x123, starting transfers between devices: none -> 105 us  [swap(): lax.ppermute(array, name, [(index, index ^ mask) for index in range(size)])]
    unnamed x17 -> x0, waiting for transfers between devices: 74.3 us -> none
    psum x1 -> x0, blocking collectives: 42.4 us -> none  [local(): lax.psum((d_bias_qv, d_bias_out, d_gain_one, d_offset_one, d_bias_up, d_b...]
    pallas_call x0 -> x4, Pallas kernels: none -> 32.2 us  [the longest x2 19.5 us: attend_rows_backward(): pl.pallas_call(attend_backward_kernel, grid=(pairs,), in_specs=[attention...]
  transfers between devices with their start and end apart: 16 -> 123, of which waited for: 14 -> 48; matrix products, arithmetic and copies ran while one was open for 29% -> 16% of each run, Pallas kernels for 0% -> 2%
where the time goes in v1:
time: 567 us; the launch traced here: 562 us
  waiting for transfers between devices  288 us (51%)
  starting transfers between devices  105 us (19%)
  matrix products  80 us (14%)
  local copies, waits for them, and re-layouts  38.1 us (7%)
  Pallas kernels  32.2 us (6%)
  other arithmetic  14.8 us (3%)
    ppermute x123, waiting for transfers between devices, swap(): lax.ppermute(array, name, [(index, index ^ mask) for index in range(size)])  288 us
    ppermute x123, starting transfers between devices, swap(): lax.ppermute(array, name, [(index, index ^ mask) for index in range(size)])  105 us
    dot_general x10, matrix products, matmul(): return jnp.dot(left, right, preferred_element_type=jnp.float32)  33.3 us
    dot_general x11, matrix products, outer_cols(): lax.dot_general(left, right, (((1,), (1,)), ((), ())), preferred_element_...  28 us
    pallas_call x2, Pallas kernels, attend_rows_backward(): pl.pallas_call(attend_backward_kernel, grid=(pairs,), in_specs=[attention...  19.5 us
    unnamed x188, local copies, waits for them, and re-layouts  16.3 us
    dot_general x8, matrix products, inner_rows(): lax.dot_general(left, right, (((0,), (0,)), ((), ())), preferred_element_...  15.3 us
    pallas_call x2, Pallas kernels, attend_rows_forward(): pl.pallas_call(attend_forward_kernel, grid=(pairs,), in_specs=[attention_...  12.6 us
  transfers between devices with their start and end apart: 123, of which 48 were waited for; matrix products, arithmetic and copies ran while one was open for 16% of the time, Pallas kernels for 2%

profile of v1, /device:TPU:0, one launch (start us, length us, event | category | flops | bytes accessed | tf_op | source)
XLA Modules:
  0.0 561.5 jit_solution(2014698440009940841)
XLA Ops:
  0.7 5.1 collective-permute-start.11
  7.4 3.8 collective-permute-start.2
  16.3 3.5 fusion.45
  19.8 3.2 fusion.166
  29.1 3.1 copy.44
  33.8 3.3 collective-permute-done.12
  37.1 3.6 collective-permute-start.45
  49.8 8.9 %collective-permute-done.43 = bf16[64,2048]{1,0:T(8,128)(2,1)S(1)} collective-permute-done((bf16[64,2048]{1,0:T(8,128)(2,1)S(1)}, bf16[64,2048]{1,0:T(8,128)(2,1)S(1)}, u32[]{:S(2)}, u32[]{:S(2)}) %collective-permute-start.43) | collective-permute-done | bytes 262176 | tf_op jit(solution)/shard_map/ppermute | solution.py:265
  59.6 10.2 %collective-permute-done.44 = bf16[64,2048]{1,0:T(8,128)(2,1)S(1)} collective-permute-done((bf16[64,2048]{1,0:T(8,128)(2,1)S(1)}, bf16[64,2048]{1,0:T(8,128)(2,1)S(1)}, u32[]{:S(2)}, u32[]{:S(2)}) %collective-permute-start.44) | collective-permute-done | bytes 262176 | tf_op jit(solution)/shard_map/ppermute | solution.py:265
  72.9 5.4 collective-permute-done.35
  81.7 2.9 collective-permute-done.27
  89.0 7.7 %collective-permute-done.18 = bf16[128,1536]{1,0:T(8,128)(2,1)S(1)} collective-permute-done((bf16[128,1536]{1,0:T(8,128)(2,1)S(1)}, bf16[128,1536]{1,0:T(8,128)(2,1)S(1)}, u32[]{:S(2)}, u32[]{:S(2)}) %collective-permute-start.18) | collective-permute-done | bytes 393248 | tf_op jit(solution)/shard_map/ppermute | solution.py:265
  101.5 14.9 %collective-permute-done.60 = bf16[128,2048]{1,0:T(8,128)(2,1)S(1)} collective-permute-done((bf16[128,2048]{1,0:T(8,128)(2,1)S(1)}, bf16[128,2048]{1,0:T(8,128)(2,1)S(1)}, u32[]{:S(2)}, u32[]{:S(2)}) %collective-permute-start.60) | collective-permute-done | bytes 524320 | tf_op jit(solution)/shard_map/ppermute | solution.py:265
  116.4 9.3 %collective-permute-done.52 = bf16[128,2048]{1,0:T(8,128)(2,1)S(1)} collective-permute-done((bf16[128,2048]{1,0:T(8,128)(2,1)S(1)}, bf16[128,2048]{1,0:T(8,128)(2,1)S(1)}, u32[]{:S(2)}, u32[]{:S(2)}) %collective-permute-start.52) | collective-permute-done | bytes 524320 | tf_op jit(solution)/shard_map/ppermute | solution.py:265
  128.1 12.5 %collective-permute-done.37 = bf16[128,2048]{1,0:T(8,128)(2,1)S(1)} collective-permute-done((bf16[128,2048]{1,0:T(8,128)(2,1)S(1)}, bf16[128,2048]{1,0:T(8,128)(2,1)S(1)}, u32[]{:S(2)}, u32[]{:S(2)}) %collective-permute-start.37) | collective-permute-done | bytes 524320 | tf_op jit(solution)/shard_map/ppermute | solution.py:265
  141.3 5.0 collective-permute-done.6
  154.7 3.7 fusion.17.q_ref.k_ref.v_ref
  158.4 6.2 %shard_map.254 = (bf16[512,512]{1,0:T(8,128)(2,1)S(1)}, f32[512,512]{1,0:T(8,128)S(1)}) custom-call(bf16[512,1536]{1,0:T(8,128)(2,1)S(1)} %fusion.17.q_ref.k_ref.v_ref, bf16[512,1536]{1,0:T(8,128)(2,1)S(1)} %fusion.17.q_ref.k_ref.v_ref, bf16[512,1536]{1,0:T(8,128)(2,1)S(1)} %fusion.17.q_ref.k_ref.v_ref, s32[512,1]{1,0:T(8,128)S(1)} %copy.38.column_ref, ...), custom_call_target="tpu_custom_call" | custom-call | flops 1073741824 | bytes 3145728 | tf_op jit(solution)/shard_map/pallas_call | solution.py:399
  168.3 10.5 %collective-permute-done.49 = bf16[128,2048]{1,0:T(8,128)(2,1)S(1)} collective-permute-done((bf16[128,2048]{1,0:T(8,128)(2,1)S(1)}, bf16[128,2048]{1,0:T(8,128)(2,1)S(1)}, u32[]{:S(2)}, u32[]{:S(2)}) %collective-permute-start.49) | collective-permute-done | bytes 524320 | tf_op jit(solution)/shard_map/ppermute | solution.py:265
  182.1 9.7 %collective-permute-done.40 = bf16[128,2048]{1,0:T(8,128)(2,1)S(1)} collective-permute-done((bf16[128,2048]{1,0:T(8,128)(2,1)S(1)}, bf16[128,2048]{1,0:T(8,128)(2,1)S(1)}, u32[]{:S(2)}, u32[]{:S(2)}) %collective-permute-start.40) | collective-permute-done | bytes 524320 | tf_op jit(solution)/shard_map/ppermute | solution.py:265
  191.8 2.7 collective-permute-done.61
  198.2 11.2 %collective-permute-done.53 = bf16[128,2048]{1,0:T(8,128)(2,1)S(1)} collective-permute-done((bf16[128,2048]{1,0:T(8,128)(2,1)S(1)}, bf16[128,2048]{1,0:T(8,128)(2,1)S(1)}, u32[]{:S(2)}, u32[]{:S(2)}) %collective-permute-start.53) | collective-permute-done | bytes 524320 | tf_op jit(solution)/shard_map/ppermute | solution.py:265
  210.1 10.1 %collective-permute-done.56 = bf16[128,2048]{1,0:T(8,128)(2,1)S(1)} collective-permute-done((bf16[128,2048]{1,0:T(8,128)(2,1)S(1)}, bf16[128,2048]{1,0:T(8,128)(2,1)S(1)}, u32[]{:S(2)}, u32[]{:S(2)}) %collective-permute-start.56) | collective-permute-done | bytes 524320 | tf_op jit(solution)/shard_map/ppermute | solution.py:265
  225.7 6.4 %shard_map.255 = (bf16[512,512]{1,0:T(8,128)(2,1)S(1)}, f32[512,512]{1,0:T(8,128)S(1)}) custom-call(bf16[512,1536]{1,0:T(8,128)(2,1)S(1)} %fusion.18.q_ref.k_ref.v_ref, bf16[512,1536]{1,0:T(8,128)(2,1)S(1)} %fusion.18.q_ref.k_ref.v_ref, bf16[512,1536]{1,0:T(8,128)(2,1)S(1)} %fusion.18.q_ref.k_ref.v_ref, s32[512,1]{1,0:T(8,128)S(1)} %copy.38.column_ref, ...), custom_call_target="tpu_custom_call" | custom-call | flops 1073741824 | bytes 3145728 | tf_op jit(solution)/shard_map/pallas_call | solution.py:399
  233.7 4.2 multiply_convert_fusion.3
  237.9 3.7 fusion.168
  242.0 3.0 collective-permute-done.57
  247.8 4.5 multiply_convert_fusion.2
  252.4 2.7 fusion.165
  259.3 5.9 %convert_reduce_fusion = (f32[2048]{0:T(1024)S(1)}, bf16[512,2048]{1,0:T(8,128)(2,1)S(1)}) fusion(f32[512,2048]{1,0:T(8,128)} %get-tuple-element.174, f32[2048]{0:T(1024)S(1)} %copy-done.39, bf16[512,1024]{0,1:T(8,128)(2,1)S(1)} %convert_element_type.587, bf16[1024,2048]{1,0:T(8,128)(2,1)S(1)} %constant_dynamic-update-slice_fusion.80), kind=kOutput, calls=%fused_computation.12 | convolution fusion | flops 2163210240 | bytes 11550720 | tf_op jit(solution)/shard_map/dot_general | solution.py:18
  265.2 4.1 convert_reduce_fusion.1
  269.3 2.4 fusion.169
  271.7 3.2 multiply_reduce_fusion
  280.3 9.6 %shard_map.256 = (bf16[512,512]{1,0:T(8,128)(2,1)S(1)}, bf16[512,512]{1,0:T(8,128)(2,1)S(1)}, bf16[512,512]{1,0:T(8,128)(2,1)S(1)}) custom-call(bf16[512,1536]{1,0:T(8,128)(2,1)S(1)} %fusion.17.q_ref.k_ref.v_ref, bf16[512,1536]{1,0:T(8,128)(2,1)S(1)} %fusion.17.q_ref.k_ref.v_ref, bf16[512,1536]{1,0:T(8,128)(2,1)S(1)} %fusion.17.q_ref.k_ref.v_ref, ...), custom_call_target="tpu_custom_call" | custom-call | flops 2684354560 | bytes 4718592 | tf_op jit(solution)/shard_map/pallas_call | solution.py:420
  290.1 5.6 %fusion.170 = f32[512,1024]{0,1:T(8,128)} fusion(bf16[512,1536]{1,0:T(8,128)(2,1)S(1)} %constant_dynamic-update-slice_fusion.88, bf16[1024,1536]{1,0:T(8,128)(2,1)} %constant_dynamic-update-slice_fusion), kind=kOutput, calls=%fused_computation.458 | convolution fusion | flops 1610612736 | bytes 6815744 | tf_op jit(solution)/shard_map/dot_general | solution.py:28
  299.1 10.0 %shard_map.257 = (bf16[512,512]{1,0:T(8,128)(2,1)S(1)}, bf16[512,512]{1,0:T(8,128)(2,1)S(1)}, bf16[512,512]{1,0:T(8,128)(2,1)S(1)}) custom-call(bf16[512,1536]{1,0:T(8,128)(2,1)S(1)} %fusion.18.q_ref.k_ref.v_ref, bf16[512,1536]{1,0:T(8,128)(2,1)S(1)} %fusion.18.q_ref.k_ref.v_ref, bf16[512,1536]{1,0:T(8,128)(2,1)S(1)} %fusion.18.q_ref.k_ref.v_ref, ...), custom_call_target="tpu_custom_call" | custom-call | flops 2684354560 | bytes 4718592 | tf_op jit(solution)/shard_map/pallas_call | solution.py:420
  309.6 7.0 %collective-permute-start.81 = (f32[12,1024]{1,0:T(8,128)S(1)}, f32[12,1024]{1,0:T(8,128)S(1)}, u32[]{:S(2)}, u32[]{:S(2)}) collective-permute-start(f32[12,1024]{1,0:T(8,128)S(1)} %pad_maximum_fusion.14), channel_id=1, source_target_pairs={{0,16},{2,18},{4,20},{6,22},{8,24},{10,26},{12,28},{14,30},{16,0},... | collective-permute-start | bytes 147464 | tf_op jit(solution)/shard_map/ppermute | solution.py:265
  321.7 2.3 convolution_convert_fusion
  324.1 2.3 convolution_convert_fusion.1
  326.4 2.3 convolution_convert_fusion.2
  328.9 2.7 fusion.48
  336.6 2.7 fusion.44
  342.1 2.3 convolution_convert_fusion.3
  358.3 3.1 collective-permute-done.94
  367.7 3.1 collective-permute-done.90
  373.0 2.4 collective-permute-start.98
  376.6 2.5 collective-permute-done.98
  383.7 2.5 collective-permute-done.117
  386.7 2.5 collective-permute-done.103
  394.9 7.0 %collective-permute-done.75 = bf16[128,1536]{1,0:T(8,128)(2,1)S(1)} collective-permute-done((bf16[128,1536]{1,0:T(8,128)(2,1)S(1)}, bf16[128,1536]{1,0:T(8,128)(2,1)S(1)}, u32[]{:S(2)}, u32[]{:S(2)}) %collective-permute-start.75) | collective-permute-done | bytes 393248 | tf_op jit(solution)/shard_map/ppermute | solution.py:265
  403.2 10.0 %collective-permute-done.118 = bf16[128,2048]{1,0:T(8,128)(2,1)S(1)} collective-permute-done((bf16[128,2048]{1,0:T(8,128)(2,1)S(1)}, bf16[128,2048]{1,0:T(8,128)(2,1)S(1)}, u32[]{:S(2)}, u32[]{:S(2)}) %collective-permute-start.118) | collective-permute-done | bytes 524320 | tf_op jit(solution)/shard_map/ppermute | solution.py:265
  417.4 4.1 collective-permute-done.73
  423.0 3.9 collective-permute-done.76
  428.4 15.6 %collective-permute-done.106 = bf16[128,2048]{1,0:T(8,128)(2,1)S(1)} collective-permute-done((bf16[128,2048]{1,0:T(8,128)(2,1)S(1)}, bf16[128,2048]{1,0:T(8,128)(2,1)S(1)}, u32[]{:S(2)}, u32[]{:S(2)}) %collective-permute-start.106) | collective-permute-done | bytes 524320 | tf_op jit(solution)/shard_map/ppermute | solution.py:265
  445.4 17.7 %collective-permute-done.71 = bf16[128,1536]{1,0:T(8,128)(2,1)S(1)} collective-permute-done((bf16[128,1536]{1,0:T(8,128)(2,1)S(1)}, bf16[128,1536]{1,0:T(8,128)(2,1)S(1)}, u32[]{:S(2)}, u32[]{:S(2)}) %collective-permute-start.71) | collective-permute-done | bytes 393248 | tf_op jit(solution)/shard_map/ppermute | solution.py:265
  465.3 12.6 %collective-permute-done.119 = bf16[128,2048]{1,0:T(8,128)(2,1)S(1)} collective-permute-done((bf16[128,2048]{1,0:T(8,128)(2,1)S(1)}, bf16[128,2048]{1,0:T(8,128)(2,1)S(1)}, u32[]{:S(2)}, u32[]{:S(2)}) %collective-permute-start.119) | collective-permute-done | bytes 524320 | tf_op jit(solution)/shard_map/ppermute | solution.py:265
  479.8 9.4 %collective-permute-done.107 = bf16[128,2048]{1,0:T(8,128)(2,1)S(1)} collective-permute-done((bf16[128,2048]{1,0:T(8,128)(2,1)S(1)}, bf16[128,2048]{1,0:T(8,128)(2,1)S(1)}, u32[]{:S(2)}, u32[]{:S(2)}) %collective-permute-start.107) | collective-permute-done | bytes 524320 | tf_op jit(solution)/shard_map/ppermute | solution.py:265
  489.7 2.4 collective-permute-start.79
  494.9 15.3 %collective-permute-done.101 = bf16[2,128,2048]{2,1,0:T(8,128)(2,1)S(1)} collective-permute-done((bf16[2,128,2048]{2,1,0:T(8,128)(2,1)S(1)}, bf16[2,128,2048]{2,1,0:T(8,128)(2,1)S(1)}, u32[]{:S(2)}, u32[]{:S(2)}) %collective-permute-start.101) | collective-permute-done | bytes 1048608 | tf_op jit(solution)/shard_map/ppermute | solution.py:265
  513.6 2.4 collective-permute-start.122
  516.8 6.5 %collective-permute-done.102 = bf16[128,2048]{1,0:T(8,128)(2,1)S(1)} collective-permute-done((bf16[128,2048]{1,0:T(8,128)(2,1)S(1)}, bf16[128,2048]{1,0:T(8,128)(2,1)S(1)}, u32[]{:S(2)}, u32[]{:S(2)}) %collective-permute-start.102) | collective-permute-done | bytes 524320 | tf_op jit(solution)/shard_map/ppermute | solution.py:265
  523.9 2.4 collective-permute-start.110
  528.9 22.9 %collective-permute-done.121 = bf16[64,2048]{1,0:T(8,128)(2,1)S(1)} collective-permute-done((bf16[64,2048]{1,0:T(8,128)(2,1)S(1)}, bf16[64,2048]{1,0:T(8,128)(2,1)S(1)}, u32[]{:S(2)}, u32[]{:S(2)}) %collective-permute-start.121) | collective-permute-done | bytes 262176 | tf_op jit(solution)/shard_map/ppermute | solution.py:265
  552.8 7.6 %collective-permute-done.109 = bf16[64,2048]{1,0:T(8,128)(2,1)S(1)} collective-permute-done((bf16[64,2048]{1,0:T(8,128)(2,1)S(1)}, bf16[64,2048]{1,0:T(8,128)(2,1)S(1)}, u32[]{:S(2)}, u32[]{:S(2)}) %collective-permute-start.109) | collective-permute-done | bytes 262176 | tf_op jit(solution)/shard_map/ppermute | solution.py:265
  (543 shorter events, 158.8 us)
Async XLA Ops:
  0.7 25.8 %collective-permute-start.11 = (bf16[64,512]{1,0:T(8,128)(2,1)}, bf16[64,512]{1,0:T(8,128)(2,1)S(1)}, u32[]{:S(2)}, u32[]{:S(2)}) collective-permute-start(bf16[64,512]{1,0:T(8,128)(2,1)} %bitcast.362), channel_id=1, source_target_pairs={{0,24},{2,26},{4,28},{6,30},{8,16},{10,18},{12,20},{14,22},{16,8},... | collective-permute-start | bytes 196616 | tf_op jit(solution)/shard_map/ppermute | solution.py:265
  5.8 20.6 %collective-permute-start.10 = (bf16[64,512]{1,0:T(8,128)(2,1)}, bf16[64,512]{1,0:T(8,128)(2,1)S(1)}, u32[]{:S(2)}, u32[]{:S(2)}) collective-permute-start(bf16[64,512]{1,0:T(8,128)(2,1)} %bitcast.363), channel_id=1, source_target_pairs={{0,16},{2,18},{4,20},{6,22},{8,24},{10,26},{12,28},{14,30},{16,0},... | collective-permute-start | bytes 196616 | tf_op jit(solution)/shard_map/ppermute | solution.py:265
  5.8 19.9 %collective-permute-start.9 = (bf16[64,512]{1,0:T(8,128)(2,1)}, bf16[64,512]{1,0:T(8,128)(2,1)S(1)}, u32[]{:S(2)}, u32[]{:S(2)}) collective-permute-start(bf16[64,512]{1,0:T(8,128)(2,1)} %bitcast.364), channel_id=1, source_target_pairs={{0,8},{2,10},{4,12},{6,14},{8,0},{10,2},{12,4},{14,6},{16,24},{18,... | collective-permute-start | bytes 196616 | tf_op jit(solution)/shard_map/ppermute | solution.py:265
  7.4 38.8 %collective-permute-start.2 = (bf16[64,1536]{1,0:T(8,128)(2,1)S(1)}, bf16[64,1536]{1,0:T(8,128)(2,1)}, u32[]{:S(2)}, u32[]{:S(2)}) collective-permute-start(bf16[64,1536]{1,0:T(8,128)(2,1)S(1)} %pad_maximum_fusion.10), channel_id=1, source_target_pairs={{0,24},{2,26},{4,28},{6,30},{8,16},{10,18},{12,20},{14,22},{16,8},... | collective-permute-start | bytes 589832 | tf_op jit(solution)/shard_map/ppermute | solution.py:265
  11.2 31.2 %collective-permute-start.1 = (bf16[64,1536]{1,0:T(8,128)(2,1)S(1)}, bf16[64,1536]{1,0:T(8,128)(2,1)}, u32[]{:S(2)}, u32[]{:S(2)}) collective-permute-start(bf16[64,1536]{1,0:T(8,128)(2,1)S(1)} %pad_maximum_fusion.10), channel_id=1, source_target_pairs={{0,16},{2,18},{4,20},{6,22},{8,24},{10,26},{12,28},{14,30},{16,0},... | collective-permute-start | bytes 589832 | tf_op jit(solution)/shard_map/ppermute | solution.py:265
  25.7 15.2 %collective-permute-start = (bf16[64,1536]{1,0:T(8,128)(2,1)S(1)}, bf16[64,1536]{1,0:T(8,128)(2,1)S(1)}, u32[]{:S(2)}, u32[]{:S(2)}) collective-permute-start(bf16[64,1536]{1,0:T(8,128)(2,1)S(1)} %pad_maximum_fusion.10), channel_id=1, source_target_pairs={{0,8},{2,10},{4,12},{6,14},{8,0},{10,2},{12,4},{14,6},{16,24},{18,... | collective-permute-start | bytes 589832 | tf_op jit(solution)/shard_map/ppermute | solution.py:265
  37.1 33.9 %collective-permute-start.45 = (bf16[64,2048]{1,0:T(8,128)(2,1)S(1)}, bf16[64,2048]{1,0:T(8,128)(2,1)S(1)}, u32[]{:S(2)}, u32[]{:S(2)}) collective-permute-start(bf16[64,2048]{1,0:T(8,128)(2,1)S(1)} %bitcast.354), channel_id=1, source_target_pairs={{0,24},{2,26},{4,28},{6,30},{8,16},{10,18},{12,20},{14,22},{16,8},... | collective-permute-start | bytes 786440 | tf_op jit(solution)/shard_map/ppermute | solution.py:265
  40.8 29.1 %collective-permute-start.44 = (bf16[64,2048]{1,0:T(8,128)(2,1)S(1)}, bf16[64,2048]{1,0:T(8,128)(2,1)S(1)}, u32[]{:S(2)}, u32[]{:S(2)}) collective-permute-start(bf16[64,2048]{1,0:T(8,128)(2,1)S(1)} %bitcast.355), channel_id=1, source_target_pairs={{0,16},{2,18},{4,20},{6,22},{8,24},{10,26},{12,28},{14,30},{16,0},... | collective-permute-start | bytes 786440 | tf_op jit(solution)/shard_map/ppermute | solution.py:265
  40.9 17.9 %collective-permute-start.43 = (bf16[64,2048]{1,0:T(8,128)(2,1)S(1)}, bf16[64,2048]{1,0:T(8,128)(2,1)S(1)}, u32[]{:S(2)}, u32[]{:S(2)}) collective-permute-start(bf16[64,2048]{1,0:T(8,128)(2,1)S(1)} %bitcast.356), channel_id=1, source_target_pairs={{0,8},{2,10},{4,12},{6,14},{8,0},{10,2},{12,4},{14,6},{16,24},{18,... | collective-permute-start | bytes 786440 | tf_op jit(solution)/shard_map/ppermute | solution.py:265
  42.3 35.9 %collective-permute-start.35 = (bf16[64,2048]{1,0:T(8,128)(2,1)S(1)}, bf16[64,2048]{1,0:T(8,128)(2,1)S(1)}, u32[]{:S(2)}, u32[]{:S(2)}) collective-permute-start(bf16[64,2048]{1,0:T(8,128)(2,1)S(1)} %copy-done.22), channel_id=1, source_target_pairs={{0,16},{2,18},{4,20},{6,22},{8,24},{10,26},{12,28},{14,30},{16,0},... | collective-permute-start | bytes 786440 | tf_op jit(solution)/shard_map/ppermute | solution.py:265
  46.1 25.6 %collective-permute-start.34 = (bf16[64,2048]{1,0:T(8,128)(2,1)S(1)}, bf16[64,2048]{1,0:T(8,128)(2,1)S(1)}, u32[]{:S(2)}, u32[]{:S(2)}) collective-permute-start(bf16[64,2048]{1,0:T(8,128)(2,1)S(1)} %copy-done.22), channel_id=1, source_target_pairs={{0,8},{2,10},{4,12},{6,14},{8,0},{10,2},{12,4},{14,6},{16,24},{18,... | collective-permute-start | bytes 786440 | tf_op jit(solution)/shard_map/ppermute | solution.py:265
  58.7 19.7 %collective-permute-start.36 = (bf16[64,2048]{1,0:T(8,128)(2,1)S(1)}, bf16[64,2048]{1,0:T(8,128)(2,1)S(1)}, u32[]{:S(2)}, u32[]{:S(2)}) collective-permute-start(bf16[64,2048]{1,0:T(8,128)(2,1)S(1)} %copy-done.22), channel_id=1, source_target_pairs={{0,24},{2,26},{4,28},{6,30},{8,16},{10,18},{12,20},{14,22},{16,8},... | collective-permute-start | bytes 786440 | tf_op jit(solution)/shard_map/ppermute | solution.py:265
  85.3 14.3 %collective-permute-start.4 = (bf16[128,1536]{1,0:T(8,128)(2,1)S(1)}, bf16[128,1536]{1,0:T(8,128)(2,1)S(1)}, u32[]{:S(2)}, u32[]{:S(2)}) collective-permute-start(bf16[128,1536]{1,0:T(8,128)(2,1)S(1)} %pad_maximum_fusion.4), channel_id=1, source_target_pairs={{0,2},{2,0},{4,6},{6,4},{8,10},{10,8},{12,14},{14,12},{16,18},{18,... | collective-permute-start | bytes 1179656 | tf_op jit(solution)/shard_map/ppermute | solution.py:265
  87.2 109.3 %collective-permute-start.22 = (bf16[128,1536]{1,0:T(8,128)(2,1)S(1)}, bf16[128,1536]{1,0:T(8,128)(2,1)S(1)}, u32[]{:S(2)}, u32[]{:S(2)}) collective-permute-start(bf16[128,1536]{1,0:T(8,128)(2,1)S(1)} %pad_maximum_fusion.5), channel_id=1, source_target_pairs={{0,1},{1,0},{2,3},{3,2},{4,5},{5,4},{6,7},{7,6},{8,9},{9,8},{10,11... | collective-permute-start | bytes 1179656 | tf_op jit(solution)/shard_map/ppermute | solution.py:265
  88.7 64.0 %collective-permute-start.7 = (bf16[128,1536]{1,0:T(8,128)(2,1)S(1)}, bf16[128,1536]{1,0:T(8,128)(2,1)S(1)}, u32[]{:S(2)}, u32[]{:S(2)}) collective-permute-start(bf16[128,1536]{1,0:T(8,128)(2,1)S(1)} %pad_maximum_fusion.5), channel_id=1, source_target_pairs={{0,2},{2,0},{4,6},{6,4},{8,10},{10,8},{12,14},{14,12},{16,18},{18,... | collective-permute-start | bytes 1179656 | tf_op jit(solution)/shard_map/ppermute | solution.py:265
  96.7 19.7 %collective-permute-start.60 = (bf16[128,2048]{1,0:T(8,128)(2,1)S(1)}, bf16[128,2048]{1,0:T(8,128)(2,1)S(1)}, u32[]{:S(2)}, u32[]{:S(2)}) collective-permute-start(bf16[128,2048]{1,0:T(8,128)(2,1)S(1)} %pad_maximum_fusion.2), channel_id=1, source_target_pairs={{0,1},{1,0},{2,3},{3,2},{4,5},{5,4},{6,7},{7,6},{8,9},{9,8},{10,11... | collective-permute-start | bytes 1572872 | tf_op jit(solution)/shard_map/ppermute | solution.py:265
  97.2 28.5 %collective-permute-start.52 = (bf16[128,2048]{1,0:T(8,128)(2,1)S(1)}, bf16[128,2048]{1,0:T(8,128)(2,1)S(1)}, u32[]{:S(2)}, u32[]{:S(2)}) collective-permute-start(bf16[128,2048]{1,0:T(8,128)(2,1)S(1)} %pad_maximum_fusion), channel_id=1, source_target_pairs={{0,1},{1,0},{2,3},{3,2},{4,5},{5,4},{6,7},{7,6},{8,9},{9,8},{10,11... | collective-permute-start | bytes 1572872 | tf_op jit(solution)/shard_map/ppermute | solution.py:265
  99.6 27.2 %collective-permute-start.46 = (bf16[128,2048]{1,0:T(8,128)(2,1)S(1)}, bf16[128,2048]{1,0:T(8,128)(2,1)S(1)}, u32[]{:S(2)}, u32[]{:S(2)}) collective-permute-start(bf16[128,2048]{1,0:T(8,128)(2,1)S(1)} %pad_maximum_fusion.2), channel_id=1, source_target_pairs={{0,4},{2,6},{4,0},{6,2},{8,12},{10,14},{12,8},{14,10},{16,20},{18,... | collective-permute-start | bytes 1572872 | tf_op jit(solution)/shard_map/ppermute | solution.py:265
  125.7 14.9 %collective-permute-start.37 = (bf16[128,2048]{1,0:T(8,128)(2,1)S(1)}, bf16[128,2048]{1,0:T(8,128)(2,1)S(1)}, u32[]{:S(2)}, u32[]{:S(2)}) collective-permute-start(bf16[128,2048]{1,0:T(8,128)(2,1)S(1)} %pad_maximum_fusion), channel_id=1, source_target_pairs={{0,4},{2,6},{4,0},{6,2},{8,12},{10,14},{12,8},{14,10},{16,20},{18,... | collective-permute-start | bytes 1572872 | tf_op jit(solution)/shard_map/ppermute | solution.py:265
  126.9 13.8 %collective-permute-start.38 = (bf16[128,2048]{1,0:T(8,128)(2,1)S(1)}, bf16[128,2048]{1,0:T(8,128)(2,1)S(1)}, u32[]{:S(2)}, u32[]{:S(2)}) collective-permute-start(bf16[128,2048]{1,0:T(8,128)(2,1)S(1)} %pad_maximum_fusion), channel_id=1, source_target_pairs={{0,2},{2,0},{4,6},{6,4},{8,10},{10,8},{12,14},{14,12},{16,18},{18,... | collective-permute-start | bytes 1572872 | tf_op jit(solution)/shard_map/ppermute | solution.py:265
  127.0 19.2 %collective-permute-start.6 = (bf16[128,1536]{1,0:T(8,128)(2,1)S(1)}, bf16[128,1536]{1,0:T(8,128)(2,1)S(1)}, u32[]{:S(2)}, u32[]{:S(2)}) collective-permute-start(bf16[128,1536]{1,0:T(8,128)(2,1)S(1)} %pad_maximum_fusion.5), channel_id=1, source_target_pairs={{0,4},{2,6},{4,0},{6,2},{8,12},{10,14},{12,8},{14,10},{16,20},{18,... | collective-permute-start | bytes 1179656 | tf_op jit(solution)/shard_map/ppermute | solution.py:265
  140.7 68.8 %collective-permute-start.64 = (bf16[128,2048]{1,0:T(8,128)(2,1)S(1)}, bf16[128,2048]{1,0:T(8,128)(2,1)S(1)}, u32[]{:S(2)}, u32[]{:S(2)}) collective-permute-start(bf16[128,2048]{1,0:T(8,128)(2,1)S(1)} %pad_maximum_fusion.3), channel_id=1, source_target_pairs={{0,1},{1,0},{2,3},{3,2},{4,5},{5,4},{6,7},{7,6},{8,9},{9,8},{10,11... | collective-permute-start | bytes 1572872 | tf_op jit(solution)/shard_map/ppermute | solution.py:265
  146.2 33.9 %collective-permute-start.50 = (bf16[128,2048]{1,0:T(8,128)(2,1)S(1)}, bf16[128,2048]{1,0:T(8,128)(2,1)S(1)}, u32[]{:S(2)}, u32[]{:S(2)}) collective-permute-start(bf16[128,2048]{1,0:T(8,128)(2,1)S(1)} %pad_maximum_fusion.3), channel_id=1, source_target_pairs={{0,2},{2,0},{4,6},{6,4},{8,10},{10,8},{12,14},{14,12},{16,18},{18,... | collective-permute-start | bytes 1572872 | tf_op jit(solution)/shard_map/ppermute | solution.py:265
  152.7 13.4 %collective-permute-start.20 = (bf16[128,1536]{1,0:T(8,128)(2,1)S(1)}, bf16[128,1536]{1,0:T(8,128)(2,1)S(1)}, u32[]{:S(2)}, u32[]{:S(2)}) collective-permute-start(bf16[128,1536]{1,0:T(8,128)(2,1)S(1)} %collective-permute-done.18), channel_id=1, source_target_pairs={{0,2},{2,0},{4,6},{6,4},{8,10},{10,8},{12,14},{14,12},{16,18},{18,... | collective-permute-start | bytes 1179656 | tf_op jit(solution)/shard_map/ppermute | solution.py:265
  165.0 13.8 %collective-permute-start.49 = (bf16[128,2048]{1,0:T(8,128)(2,1)S(1)}, bf16[128,2048]{1,0:T(8,128)(2,1)S(1)}, u32[]{:S(2)}, u32[]{:S(2)}) collective-permute-start(bf16[128,2048]{1,0:T(8,128)(2,1)S(1)} %pad_maximum_fusion.3), channel_id=1, source_target_pairs={{0,4},{2,6},{4,0},{6,2},{8,12},{10,14},{12,8},{14,10},{16,20},{18,... | collective-permute-start | bytes 1572872 | tf_op jit(solution)/shard_map/ppermute | solution.py:265
  180.1 14.4 %collective-permute-start.61 = (bf16[128,2048]{1,0:T(8,128)(2,1)S(1)}, bf16[128,2048]{1,0:T(8,128)(2,1)S(1)}, u32[]{:S(2)}, u32[]{:S(2)}) collective-permute-start(bf16[128,2048]{1,0:T(8,128)(2,1)S(1)} %collective-permute-done.46), channel_id=1, source_target_pairs={{0,1},{1,0},{2,3},{3,2},{4,5},{5,4},{6,7},{7,6},{8,9},{9,8},{10,11... | collective-permute-start | bytes 1572872 | tf_op jit(solution)/shard_map/ppermute | solution.py:265
  194.6 14.8 %collective-permute-start.53 = (bf16[128,2048]{1,0:T(8,128)(2,1)S(1)}, bf16[128,2048]{1,0:T(8,128)(2,1)S(1)}, u32[]{:S(2)}, u32[]{:S(2)}) collective-permute-start(bf16[128,2048]{1,0:T(8,128)(2,1)S(1)} %collective-permute-done.37), channel_id=1, source_target_pairs={{0,1},{1,0},{2,3},{3,2},{4,5},{5,4},{6,7},{7,6},{8,9},{9,8},{10,11... | collective-permute-start | bytes 1572872 | tf_op jit(solution)/shard_map/ppermute | solution.py:265
  196.2 13.8 %collective-permute-start.54 = (bf16[128,2048]{1,0:T(8,128)(2,1)S(1)}, bf16[128,2048]{1,0:T(8,128)(2,1)S(1)}, u32[]{:S(2)}, u32[]{:S(2)}) collective-permute-start(bf16[128,2048]{1,0:T(8,128)(2,1)S(1)} %collective-permute-done.52), channel_id=1, source_target_pairs={{0,2},{2,0},{4,6},{6,4},{8,10},{10,8},{12,14},{14,12},{16,18},{18,... | collective-permute-start | bytes 1572872 | tf_op jit(solution)/shard_map/ppermute | solution.py:265
  196.6 23.6 %collective-permute-start.56 = (bf16[128,2048]{1,0:T(8,128)(2,1)S(1)}, bf16[128,2048]{1,0:T(8,128)(2,1)S(1)}, u32[]{:S(2)}, u32[]{:S(2)}) collective-permute-start(bf16[128,2048]{1,0:T(8,128)(2,1)S(1)} %pad_maximum_fusion.1), channel_id=1, source_target_pairs={{0,1},{1,0},{2,3},{3,2},{4,5},{5,4},{6,7},{7,6},{8,9},{9,8},{10,11... | collective-permute-start | bytes 1572872 | tf_op jit(solution)/shard_map/ppermute | solution.py:265
  197.1 24.0 %collective-permute-start.23 = (bf16[128,1536]{1,0:T(8,128)(2,1)S(1)}, bf16[128,1536]{1,0:T(8,128)(2,1)S(1)}, u32[]{:S(2)}, u32[]{:S(2)}) collective-permute-start(bf16[128,1536]{1,0:T(8,128)(2,1)S(1)} %collective-permute-done.22), channel_id=1, source_target_pairs={{0,4},{2,6},{4,0},{6,2},{8,12},{10,14},{12,8},{14,10},{16,20},{18,... | collective-permute-start | bytes 1179656 | tf_op jit(solution)/shard_map/ppermute | solution.py:265
  210.0 35.8 %collective-permute-start.66 = (bf16[128,2048]{1,0:T(8,128)(2,1)S(1)}, bf16[128,2048]{1,0:T(8,128)(2,1)S(1)}, u32[]{:S(2)}, u32[]{:S(2)}) collective-permute-start(bf16[128,2048]{1,0:T(8,128)(2,1)S(1)} %collective-permute-done.64), channel_id=1, source_target_pairs={{0,2},{2,0},{4,6},{6,4},{8,10},{10,8},{12,14},{14,12},{16,18},{18,... | collective-permute-start | bytes 1572872 | tf_op jit(solution)/shard_map/ppermute | solution.py:265
  220.2 21.4 %collective-permute-start.65 = (bf16[128,2048]{1,0:T(8,128)(2,1)S(1)}, bf16[128,2048]{1,0:T(8,128)(2,1)S(1)}, u32[]{:S(2)}, u32[]{:S(2)}) collective-permute-start(bf16[128,2048]{1,0:T(8,128)(2,1)S(1)} %collective-permute-done.64), channel_id=1, source_target_pairs={{0,4},{2,6},{4,0},{6,2},{8,12},{10,14},{12,8},{14,10},{16,20},{18,... | collective-permute-start | bytes 1572872 | tf_op jit(solution)/shard_map/ppermute | solution.py:265
  221.2 24.7 %collective-permute-start.58 = (bf16[128,2048]{1,0:T(8,128)(2,1)S(1)}, bf16[128,2048]{1,0:T(8,128)(2,1)S(1)}, u32[]{:S(2)}, u32[]{:S(2)}) collective-permute-start(bf16[128,2048]{1,0:T(8,128)(2,1)S(1)} %collective-permute-done.56), channel_id=1, source_target_pairs={{0,2},{2,0},{4,6},{6,4},{8,10},{10,8},{12,14},{14,12},{16,18},{18,... | collective-permute-start | bytes 1572872 | tf_op jit(solution)/shard_map/ppermute | solution.py:265
  221.8 23.2 %collective-permute-start.57 = (bf16[128,2048]{1,0:T(8,128)(2,1)S(1)}, bf16[128,2048]{1,0:T(8,128)(2,1)S(1)}, u32[]{:S(2)}, u32[]{:S(2)}) collective-permute-start(bf16[128,2048]{1,0:T(8,128)(2,1)S(1)} %collective-permute-done.56), channel_id=1, source_target_pairs={{0,4},{2,6},{4,0},{6,2},{8,12},{10,14},{12,8},{14,10},{16,20},{18,... | collective-permute-start | bytes 1572872 | tf_op jit(solution)/shard_map/ppermute | solution.py:265
  223.6 21.4 %collective-permute-start.63 = (bf16[128,2048]{1,0:T(8,128)(2,1)S(1)}, bf16[128,2048]{1,0:T(8,128)(2,1)S(1)}, u32[]{:S(2)}, u32[]{:S(2)}) collective-permute-start(bf16[128,2048]{1,0:T(8,128)(2,1)S(1)} %collective-permute-done.61), channel_id=1, source_target_pairs={{0,2},{2,0},{4,6},{6,4},{8,10},{10,8},{12,14},{14,12},{16,18},{18,... | collective-permute-start | bytes 1572872 | tf_op jit(solution)/shard_map/ppermute | solution.py:265
  309.6 34.9 %collective-permute-start.81 = (f32[12,1024]{1,0:T(8,128)S(1)}, f32[12,1024]{1,0:T(8,128)S(1)}, u32[]{:S(2)}, u32[]{:S(2)}) collective-permute-start(f32[12,1024]{1,0:T(8,128)S(1)} %pad_maximum_fusion.14), channel_id=1, source_target_pairs={{0,16},{2,18},{4,20},{6,22},{8,24},{10,26},{12,28},{14,30},{16,0},... | collective-permute-start | bytes 147464 | tf_op jit(solution)/shard_map/ppermute | solution.py:265
  316.5 27.9 %collective-permute-start.82 = (f32[12,1024]{1,0:T(8,128)S(1)}, f32[12,1024]{1,0:T(8,128)S(1)}, u32[]{:S(2)}, u32[]{:S(2)}) collective-permute-start(f32[12,1024]{1,0:T(8,128)S(1)} %pad_maximum_fusion.14), channel_id=1, source_target_pairs={{0,24},{2,26},{4,28},{6,30},{8,16},{10,18},{12,20},{14,22},{16,8},... | collective-permute-start | bytes 147464 | tf_op jit(solution)/shard_map/ppermute | solution.py:265
  317.9 26.5 %collective-permute-start.80 = (f32[12,1024]{1,0:T(8,128)S(1)}, f32[12,1024]{1,0:T(8,128)S(1)}, u32[]{:S(2)}, u32[]{:S(2)}) collective-permute-start(f32[12,1024]{1,0:T(8,128)S(1)} %pad_maximum_fusion.14), channel_id=1, source_target_pairs={{0,8},{2,10},{4,12},{6,14},{8,0},{10,2},{12,4},{14,6},{16,24},{18,... | collective-permute-start | bytes 147464 | tf_op jit(solution)/shard_map/ppermute | solution.py:265
  331.6 23.6 %collective-permute-start.93 = (bf16[2,128,512]{2,1,0:T(8,128)(2,1)S(1)}, bf16[2,128,512]{2,1,0:T(8,128)(2,1)S(1)}, u32[]{:S(2)}, u32[]{:S(2)}) collective-permute-start(bf16[2,128,512]{2,1,0:T(8,128)(2,1)S(1)} %bitcast.359), channel_id=1, source_target_pairs={{0,2},{2,0},{4,6},{6,4},{8,10},{10,8},{12,14},{14,12},{16,18},{18,... | collective-permute-start | bytes 786440 | tf_op jit(solution)/shard_map/ppermute | solution.py:265
  354.4 26.8 %collective-permute-start.74 = (bf16[2,128,1536]{2,1,0:T(8,128)(2,1)S(1)}, bf16[2,128,1536]{2,1,0:T(8,128)(2,1)S(1)}, u32[]{:S(2)}, u32[]{:S(2)}) collective-permute-start(bf16[2,128,1536]{2,1,0:T(8,128)(2,1)S(1)} %bitcast.352), channel_id=1, source_target_pairs={{0,2},{2,0},{4,6},{6,4},{8,10},{10,8},{12,14},{14,12},{16,18},{18,... | collective-permute-start | bytes 2359304 | tf_op jit(solution)/shard_map/ppermute | solution.py:265
  355.2 26.7 %collective-permute-start.72 = (bf16[2,128,1536]{2,1,0:T(8,128)(2,1)S(1)}, bf16[2,128,1536]{2,1,0:T(8,128)(2,1)S(1)}, u32[]{:S(2)}, u32[]{:S(2)}) collective-permute-start(bf16[2,128,1536]{2,1,0:T(8,128)(2,1)S(1)} %bitcast.351), channel_id=1, source_target_pairs={{0,2},{2,0},{4,6},{6,4},{8,10},{10,8},{12,14},{14,12},{16,18},{18,... | collective-permute-start | bytes 2359304 | tf_op jit(solution)/shard_map/ppermute | solution.py:265
  379.0 35.7 %collective-permute-start.68 = (bf16[2,128,1536]{2,1,0:T(8,128)(2,1)S(1)}, bf16[2,128,1536]{2,1,0:T(8,128)(2,1)S(1)}, u32[]{:S(2)}, u32[]{:S(2)}) collective-permute-start(bf16[2,128,1536]{2,1,0:T(8,128)(2,1)S(1)} %bitcast.349), channel_id=1, source_target_pairs={{0,2},{2,0},{4,6},{6,4},{8,10},{10,8},{12,14},{14,12},{16,18},{18,... | collective-permute-start | bytes 2359304 | tf_op jit(solution)/shard_map/ppermute | solution.py:265
  381.2 108.5 %collective-permute-start.111 = (bf16[2,128,2048]{2,1,0:T(8,128)(2,1)S(1)}, bf16[2,128,2048]{2,1,0:T(8,128)(2,1)S(1)}, u32[]{:S(2)}, u32[]{:S(2)}) collective-permute-start(bf16[2,128,2048]{2,1,0:T(8,128)(2,1)S(1)} %bitcast.341), channel_id=1, source_target_pairs={{0,2},{2,0},{4,6},{6,4},{8,10},{10,8},{12,14},{14,12},{16,18},{18,... | collective-permute-start | bytes 3145736 | tf_op jit(solution)/shard_map/ppermute | solution.py:265
  391.6 24.0 %collective-permute-start.70 = (bf16[2,128,1536]{2,1,0:T(8,128)(2,1)S(1)}, bf16[2,128,1536]{2,1,0:T(8,128)(2,1)S(1)}, u32[]{:S(2)}, u32[]{:S(2)}) collective-permute-start(bf16[2,128,1536]{2,1,0:T(8,128)(2,1)S(1)} %fusion.42), channel_id=1, source_target_pairs={{0,1},{1,0},{2,3},{3,2},{4,5},{5,4},{6,7},{7,6},{8,9},{9,8},{10,11... | collective-permute-start | bytes 2359304 | tf_op jit(solution)/shard_map/ppermute | solution.py:265
  393.6 19.7 %collective-permute-start.118 = (bf16[128,2048]{1,0:T(8,128)(2,1)S(1)}, bf16[128,2048]{1,0:T(8,128)(2,1)S(1)}, u32[]{:S(2)}, u32[]{:S(2)}) collective-permute-start(bf16[128,2048]{1,0:T(8,128)(2,1)S(1)} %slice_bitcast_fusion), channel_id=1, source_target_pairs={{0,4},{2,6},{4,0},{6,2},{8,12},{10,14},{12,8},{14,10},{16,20},{18,... | collective-permute-start | bytes 1572872 | tf_op jit(solution)/shard_map/ppermute | solution.py:265
  401.8 19.7 %collective-permute-start.73 = (bf16[128,1536]{1,0:T(8,128)(2,1)S(1)}, bf16[128,1536]{1,0:T(8,128)(2,1)S(1)}, u32[]{:S(2)}, u32[]{:S(2)}) collective-permute-start(bf16[128,1536]{1,0:T(8,128)(2,1)S(1)} %slice_bitcast_fusion.14), channel_id=1, source_target_pairs={{0,4},{2,6},{4,0},{6,2},{8,12},{10,14},{12,8},{14,10},{16,20},{18,... | collective-permute-start | bytes 1179656 | tf_op jit(solution)/shard_map/ppermute | solution.py:265
  413.3 51.4 %collective-permute-start.116 = (bf16[128,2048]{1,0:T(8,128)(2,1)S(1)}, bf16[128,2048]{1,0:T(8,128)(2,1)S(1)}, u32[]{:S(2)}, u32[]{:S(2)}) collective-permute-start(bf16[128,2048]{1,0:T(8,128)(2,1)S(1)} %slice_bitcast_fusion.2), channel_id=1, source_target_pairs={{0,4},{2,6},{4,0},{6,2},{8,12},{10,14},{12,8},{14,10},{16,20},{18,... | collective-permute-start | bytes 1572872 | tf_op jit(solution)/shard_map/ppermute | solution.py:265
  414.8 29.2 %collective-permute-start.106 = (bf16[128,2048]{1,0:T(8,128)(2,1)S(1)}, bf16[128,2048]{1,0:T(8,128)(2,1)S(1)}, u32[]{:S(2)}, u32[]{:S(2)}) collective-permute-start(bf16[128,2048]{1,0:T(8,128)(2,1)S(1)} %slice_bitcast_fusion.6), channel_id=1, source_target_pairs={{0,4},{2,6},{4,0},{6,2},{8,12},{10,14},{12,8},{14,10},{16,20},{18,... | collective-permute-start | bytes 1572872 | tf_op jit(solution)/shard_map/ppermute | solution.py:265
  421.5 70.7 %collective-permute-start.113 = (bf16[2,128,2048]{2,1,0:T(8,128)(2,1)S(1)}, bf16[2,128,2048]{2,1,0:T(8,128)(2,1)S(1)}, u32[]{:S(2)}, u32[]{:S(2)}) collective-permute-start(bf16[2,128,2048]{2,1,0:T(8,128)(2,1)S(1)} %fusion.23), channel_id=1, source_target_pairs={{0,1},{1,0},{2,3},{3,2},{4,5},{5,4},{6,7},{7,6},{8,9},{9,8},{10,11... | collective-permute-start | bytes 3145736 | tf_op jit(solution)/shard_map/ppermute | solution.py:265
  426.9 51.3 %collective-permute-start.104 = (bf16[128,2048]{1,0:T(8,128)(2,1)S(1)}, bf16[128,2048]{1,0:T(8,128)(2,1)S(1)}, u32[]{:S(2)}, u32[]{:S(2)}) collective-permute-start(bf16[128,2048]{1,0:T(8,128)(2,1)S(1)} %slice_bitcast_fusion.8), channel_id=1, source_target_pairs={{0,4},{2,6},{4,0},{6,2},{8,12},{10,14},{12,8},{14,10},{16,20},{18,... | collective-permute-start | bytes 1572872 | tf_op jit(solution)/shard_map/ppermute | solution.py:265
  444.0 19.1 %collective-permute-start.71 = (bf16[128,1536]{1,0:T(8,128)(2,1)S(1)}, bf16[128,1536]{1,0:T(8,128)(2,1)S(1)}, u32[]{:S(2)}, u32[]{:S(2)}) collective-permute-start(bf16[128,1536]{1,0:T(8,128)(2,1)S(1)} %slice_bitcast_fusion.16), channel_id=1, source_target_pairs={{0,4},{2,6},{4,0},{6,2},{8,12},{10,14},{12,8},{14,10},{16,20},{18,... | collective-permute-start | bytes 1179656 | tf_op jit(solution)/shard_map/ppermute | solution.py:265
  463.1 14.8 %collective-permute-start.119 = (bf16[128,2048]{1,0:T(8,128)(2,1)S(1)}, bf16[128,2048]{1,0:T(8,128)(2,1)S(1)}, u32[]{:S(2)}, u32[]{:S(2)}) collective-permute-start(bf16[128,2048]{1,0:T(8,128)(2,1)S(1)} %fusion.49), channel_id=1, source_target_pairs={{0,1},{1,0},{2,3},{3,2},{4,5},{5,4},{6,7},{7,6},{8,9},{9,8},{10,11... | collective-permute-start | bytes 1572872 | tf_op jit(solution)/shard_map/ppermute | solution.py:265
  464.7 24.5 %collective-permute-start.107 = (bf16[128,2048]{1,0:T(8,128)(2,1)S(1)}, bf16[128,2048]{1,0:T(8,128)(2,1)S(1)}, u32[]{:S(2)}, u32[]{:S(2)}) collective-permute-start(bf16[128,2048]{1,0:T(8,128)(2,1)S(1)} %fusion.52), channel_id=1, source_target_pairs={{0,1},{1,0},{2,3},{3,2},{4,5},{5,4},{6,7},{7,6},{8,9},{9,8},{10,11... | collective-permute-start | bytes 1572872 | tf_op jit(solution)/shard_map/ppermute | solution.py:265
  477.9 15.6 %collective-permute-start.99 = (bf16[2,128,2048]{2,1,0:T(8,128)(2,1)S(1)}, bf16[2,128,2048]{2,1,0:T(8,128)(2,1)S(1)}, u32[]{:S(2)}, u32[]{:S(2)}) collective-permute-start(bf16[2,128,2048]{2,1,0:T(8,128)(2,1)S(1)} %bitcast.342), channel_id=1, source_target_pairs={{0,2},{2,0},{4,6},{6,4},{8,10},{10,8},{12,14},{14,12},{16,18},{18,... | collective-permute-start | bytes 3145736 | tf_op jit(solution)/shard_map/ppermute | solution.py:265
  478.2 32.0 %collective-permute-start.101 = (bf16[2,128,2048]{2,1,0:T(8,128)(2,1)S(1)}, bf16[2,128,2048]{2,1,0:T(8,128)(2,1)S(1)}, u32[]{:S(2)}, u32[]{:S(2)}) collective-permute-start(bf16[2,128,2048]{2,1,0:T(8,128)(2,1)S(1)} %fusion.27), channel_id=1, source_target_pairs={{0,1},{1,0},{2,3},{3,2},{4,5},{5,4},{6,7},{7,6},{8,9},{9,8},{10,11... | collective-permute-start | bytes 3145736 | tf_op jit(solution)/shard_map/ppermute | solution.py:265
  489.2 22.9 %collective-permute-start.77 = (bf16[64,1536]{1,0:T(8,128)(2,1)S(1)}, bf16[64,1536]{1,0:T(8,128)(2,1)S(1)}, u32[]{:S(2)}, u32[]{:S(2)}) collective-permute-start(bf16[64,1536]{1,0:T(8,128)(2,1)S(1)} %get-tuple-element.83), channel_id=1, source_target_pairs={{0,8},{2,10},{4,12},{6,14},{8,0},{10,2},{12,4},{14,6},{16,24},{18,... | collective-permute-start | bytes 589832 | tf_op jit(solution)/shard_map/ppermute | solution.py:265
  489.7 22.4 %collective-permute-start.79 = (bf16[64,1536]{1,0:T(8,128)(2,1)S(1)}, bf16[64,1536]{1,0:T(8,128)(2,1)S(1)}, u32[]{:S(2)}, u32[]{:S(2)}) collective-permute-start(bf16[64,1536]{1,0:T(8,128)(2,1)S(1)} %get-tuple-element.84), channel_id=1, source_target_pairs={{0,24},{2,26},{4,28},{6,30},{8,16},{10,18},{12,20},{14,22},{16,8},... | collective-permute-start | bytes 589832 | tf_op jit(solution)/shard_map/ppermute | solution.py:265
  492.2 19.9 %collective-permute-start.78 = (bf16[64,1536]{1,0:T(8,128)(2,1)S(1)}, bf16[64,1536]{1,0:T(8,128)(2,1)S(1)}, u32[]{:S(2)}, u32[]{:S(2)}) collective-permute-start(bf16[64,1536]{1,0:T(8,128)(2,1)S(1)} %get-tuple-element.85), channel_id=1, source_target_pairs={{0,16},{2,18},{4,20},{6,22},{8,24},{10,26},{12,28},{14,30},{16,0},... | collective-permute-start | bytes 589832 | tf_op jit(solution)/shard_map/ppermute | solution.py:265
  493.6 19.5 %collective-permute-start.114 = (bf16[128,2048]{1,0:T(8,128)(2,1)S(1)}, bf16[128,2048]{1,0:T(8,128)(2,1)S(1)}, u32[]{:S(2)}, u32[]{:S(2)}) collective-permute-start(bf16[128,2048]{1,0:T(8,128)(2,1)S(1)} %slice_bitcast_fusion.4), channel_id=1, source_target_pairs={{0,4},{2,6},{4,0},{6,2},{8,12},{10,14},{12,8},{14,10},{16,20},{18,... | collective-permute-start | bytes 1572872 | tf_op jit(solution)/shard_map/ppermute | solution.py:265
  513.6 15.3 %collective-permute-start.122 = (bf16[64,2048]{1,0:T(8,128)(2,1)S(1)}, bf16[64,2048]{1,0:T(8,128)(2,1)S(1)}, u32[]{:S(2)}, u32[]{:S(2)}) collective-permute-start(bf16[64,2048]{1,0:T(8,128)(2,1)S(1)} %get-tuple-element.70), channel_id=1, source_target_pairs={{0,24},{2,26},{4,28},{6,30},{8,16},{10,18},{12,20},{14,22},{16,8},... | collective-permute-start | bytes 786440 | tf_op jit(solution)/shard_map/ppermute | solution.py:265
  516.0 35.9 %collective-permute-start.121 = (bf16[64,2048]{1,0:T(8,128)(2,1)S(1)}, bf16[64,2048]{1,0:T(8,128)(2,1)S(1)}, u32[]{:S(2)}, u32[]{:S(2)}) collective-permute-start(bf16[64,2048]{1,0:T(8,128)(2,1)S(1)} %get-tuple-element.71), channel_id=1, source_target_pairs={{0,16},{2,18},{4,20},{6,22},{8,24},{10,26},{12,28},{14,30},{16,0},... | collective-permute-start | bytes 786440 | tf_op jit(solution)/shard_map/ppermute | solution.py:265
  523.5 29.3 %collective-permute-start.108 = (bf16[64,2048]{1,0:T(8,128)(2,1)S(1)}, bf16[64,2048]{1,0:T(8,128)(2,1)S(1)}, u32[]{:S(2)}, u32[]{:S(2)}) collective-permute-start(bf16[64,2048]{1,0:T(8,128)(2,1)S(1)} %get-tuple-element.72), channel_id=1, source_target_pairs={{0,8},{2,10},{4,12},{6,14},{8,0},{10,2},{12,4},{14,6},{16,24},{18,... | collective-permute-start | bytes 786440 | tf_op jit(solution)/shard_map/ppermute | solution.py:265
  523.9 28.9 %collective-permute-start.110 = (bf16[64,2048]{1,0:T(8,128)(2,1)S(1)}, bf16[64,2048]{1,0:T(8,128)(2,1)S(1)}, u32[]{:S(2)}, u32[]{:S(2)}) collective-permute-start(bf16[64,2048]{1,0:T(8,128)(2,1)S(1)} %get-tuple-element.73), channel_id=1, source_target_pairs={{0,24},{2,26},{4,28},{6,30},{8,16},{10,18},{12,20},{14,22},{16,8},... | collective-permute-start | bytes 786440 | tf_op jit(solution)/shard_map/ppermute | solution.py:265
  526.3 34.1 %collective-permute-start.109 = (bf16[64,2048]{1,0:T(8,128)(2,1)S(1)}, bf16[64,2048]{1,0:T(8,128)(2,1)S(1)}, u32[]{:S(2)}, u32[]{:S(2)}) collective-permute-start(bf16[64,2048]{1,0:T(8,128)(2,1)S(1)} %get-tuple-element.74), channel_id=1, source_target_pairs={{0,16},{2,18},{4,20},{6,22},{8,24},{10,26},{12,28},{14,30},{16,0},... | collective-permute-start | bytes 786440 | tf_op jit(solution)/shard_map/ppermute | solution.py:265
  (118 other events, 973.1 us)

commit v2 on v1

--- a/solution.py
+++ b/solution.py
@@ -281,60 +281,129 @@
     return swap(array, "dp", 4 * step)
 
 
-def gather_weight(shard):
-    half_rows = shard.shape[0] // 2
-    stack = [shard] + [over_z(shard, step) for step in (1, 2, 3)]
-    halves = []
-    for half, first, second in ((0, over_x, over_y), (1, over_y, over_x)):
-        own = jnp.concatenate([part[half * half_rows :][:half_rows] for part in stack], axis=0)
-        near = first(own)
-        side = second(own)
-        both = second(near)
-        parts = [own, near, side, both] if half == 0 else [own, side, near, both]
-        halves.append((parts, [over_core(part) for part in parts]))
-    return [
-        jnp.concatenate(
-            [
-                part
-                for here, there in halves
-                for part in here[2 * group : 2 * group + 2] + there[2 * group : 2 * group + 2]
-            ],
-            axis=0,
-        )
-        for group in (0, 1)
-    ]
+def gather_first(stack):
+    rows = stack[0].shape[0] // 2
+    left, right = [jnp.concatenate([part[half * rows :][:rows] for part in stack]) for half in (0, 1)]
+    return left, over_x(left), right, over_y(right)
+
+
+def gather_second(parts):
+    left = jnp.concatenate(parts[:2])
+    right = jnp.concatenate(parts[2:])
+    return left, over_y(left), right, over_x(right), over_core(left), over_core(right)
+
+
+def gather_last(parts):
+    left, left_other, right, right_other, left_core, right_core = parts
+    here = (left, left_other, right, right_other)
+    return here + (left_core, over_core(left_other), right_core, over_core(right_other))
+
+
+def gather_weights(shards, first_work, second_work):
+    after = lax.optimization_barrier
+    one, two, three = shards
+    one = [one] + [over_z(one, step) for step in (1, 2, 3)]
+    two = [two, over_z(two, 1)]
+    one, two, three = after((one, two, three))
+    one = gather_first(one)
+    two = two + [over_z(two[0], 2)]
+    three = [three, over_z(three, 1)]
+    one, two, three = after((one, two, three))
+    one = gather_second(one)
+    two = two + [over_z(two[1], 2)]
+    one, two, three = after((one, two, three))
+    two = gather_first(two)
+    one = gather_last(one)
+    three = three + [over_z(three[0], 2)]
+    one, two, three = after((one, two, three))
+    two = gather_second(two)
+    three = three + [over_z(three[1], 2)]
+    made = first_work(one)
+    two, three, made = after((two, three, made))
+    three = gather_first(three)
+    two = gather_last(two)
+    two, three, made = after((two, three, made))
+    three = gather_second(three)
+    made = second_work(two, made)
+    three, made = after((three, made))
+    return (one, two, gather_last(three)), made
 
 
 def add_low(left, right):
     return (left.astype(jnp.float32) + right.astype(jnp.float32)).astype(jnp.bfloat16)
 
 
-def scatter_grad(groups):
-    rows, columns = groups[0].shape
-    sums = []
-    for half in (0, 1):
-        blocks = [group.reshape(2, 2, 2, rows // 8, columns)[half] for group in groups]
-        others = [over_core(block[1]) for block in blocks]
-        blocks = [add_low(block[0], other) for block, other in zip(blocks, others)]
-        if half == 0:
-            block = add_low(blocks[0], over_y(blocks[1]))
-            block = add_low(block[0], over_x(block[1]))
-        else:
-            others = [over_x(block[1]) for block in blocks]
-            blocks = [add_low(block[0], other) for block, other in zip(blocks, others)]
-            block = add_low(blocks[0], over_y(blocks[1]))
-        sums.append(block.reshape(4, rows // 32, columns))
-    stack = jnp.concatenate(sums, axis=1)
-    parts = [stack[0]] + [over_z(stack[step], step) for step in (1, 2, 3)]
-    parts = [part.astype(jnp.float32) for part in parts]
-    return (parts[0] + parts[1]) + (parts[2] + parts[3])
-
-
-def sum_all(array):
-    array = (array + over_z(array, 1)) + (over_z(array, 2) + over_z(array, 3))
-    beside = over_y(array)
-    array = (array + over_x(array)) + (beside + over_x(beside))
-    return array + over_core(array)
+def beside(left, right):
+    return jnp.concatenate([left, right])
+
+
+def scatter_first(parts):
+    y_keep, y_send, x_keep, x_send = parts
+    return scatter_first_sum(y_keep, over_y(y_send), x_keep, over_x(x_send))
+
+
+def scatter_first_sum(y_keep, y_other, x_keep, x_other):
+    rows = y_keep.shape[0] // 4
+    left, left_send = [
+        beside(*[add_low(y_keep[at:][:rows], y_other[at:][:rows]) for at in (start, start + 2 * rows)])
+        for start in (0, rows)
+    ]
+    return (
+        left,
+        left_send,
+        add_low(x_keep[: 2 * rows], x_other[: 2 * rows]),
+        add_low(x_keep[2 * rows :], x_other[2 * rows :]),
+    )
+
+
+def scatter_second(parts):
+    left, left_send, right, right_send = parts
+    return add_low(left, over_x(left_send)), add_low(right, over_y(right_send))
+
+
+def scatter_both(later, sooner):
+    left, left_send, right, right_send = later
+    y_keep, y_send, x_keep, x_send = sooner
+    rows = left.shape[0]
+    x_other = over_x(beside(left_send, x_send))
+    y_other = over_y(beside(right_send, y_send))
+    done = add_low(left, x_other[:rows]), add_low(right, y_other[:rows])
+    return done, scatter_first_sum(y_keep, y_other[rows:], x_keep, x_other[rows:])
+
+
+def scatter_near(parts):
+    quarters = [part.reshape(2, 4, part.shape[0] // 8, -1) for part in parts]
+    stack = [
+        jnp.concatenate([half[core, step] for half in quarters for core in (0, 1)]) for step in range(4)
+    ]
+    terms = [stack[0]] + [over_z(stack[step], step) for step in (1, 2, 3)]
+    terms = [term.astype(jnp.float32) for term in terms]
+    return (terms[0] + terms[1]) + (terms[2] + terms[3])
+
+
+def scatter_last(sums, core_index):
+    rows = sums[0].shape[0] // 4
+    split = [
+        [jnp.concatenate([total[at:][:rows] for at in (core * rows, (core + 2) * rows)]) for core in (0, 1)]
+        for total in sums
+    ]
+    other = over_core(jnp.concatenate([send for _, send in split], axis=1))
+    width = sums[0].shape[1]
+    pairs = []
+    for index, (keep, _) in enumerate(split):
+        there = other[:, index * width :][:, :width]
+        pairs.append((jnp.where(core_index == 0, keep, there), jnp.where(core_index == 0, there, keep)))
+    return pairs
+
+
+def sum_chips(array):
+    array = array + over_core(array)
+    array = array + over_x(array)
+    return array + over_y(array)
+
+
+def sum_near(array):
+    return (array + over_z(array, 1)) + (over_z(array, 2) + over_z(array, 3))
 
 
 def head_scores(queries, key_rows, same_doc):
@@ -362,7 +431,7 @@
 
 
 def attend_backward_kernel(
-    q_ref, k_ref, v_ref, column_ref, row_ref, logsum_ref, dctx_ref, dq_ref, dk_ref, dv_ref
+    q_ref, k_ref, v_ref, column_ref, row_ref, logsum_ref, dctx_ref, out_ref
 ):
     lane = lax.broadcasted_iota(jnp.int32, q_ref.shape, 1) // HEAD_DIM
     same_doc = column_ref[...] == row_ref[...]
@@ -385,53 +454,182 @@
                 inner_rows(probabilities.astype(jnp.bfloat16), d_context),
             )
         )
-    for ref, left, right in zip((dq_ref, dk_ref, dv_ref), *results):
-        ref[...] = jnp.where(lane == 0, left, right).astype(jnp.bfloat16)
-
-
-def attention_specs(rows, width, start):
-    return pl.BlockSpec((rows, width), lambda pair, start=start: (0, start + pair))
+    pairs = pl.num_programs(1)
+    first = pl.program_id(0) * 3 * pairs + pl.program_id(1)
+    for part, (left, right) in enumerate(zip(*results)):
+        place = pl.multiple_of((first + part * pairs) * 128, 128)
+        out_ref[:, pl.ds(place, 128)] = jnp.where(lane == 0, left, right).astype(jnp.bfloat16)
+
+
+def kernel_options():
+    return dict(
+        cost_estimate=pl.CostEstimate(flops=0, bytes_accessed=0, transcendentals=0),
+        compiler_params=pltpu.CompilerParams(vmem_limit_bytes=32 << 20),
+    )
+
+
+def attention_inputs(rows, pairs, column, row):
+    def place(part):
+        return lambda group, pair: (0, group * 3 * pairs + part * pairs + pair)
+
+    whole = lambda group, pair: (0, 0)
+    return [pl.BlockSpec((rows, 128), place(part)) for part in range(3)] + [
+        pl.BlockSpec(column.shape, whole),
+        pl.BlockSpec(row.shape, whole),
+    ]
 
 
 def attend_rows_forward(qkv, column, row):
-    rows, pairs = qkv.shape[0], qkv.shape[1] // 384
-    whole = [pl.BlockSpec(column.shape, lambda pair: (0, 0)), pl.BlockSpec(row.shape, lambda pair: (0, 0))]
+    rows, pairs = qkv.shape[0], qkv.shape[1] // 768
+    own = pl.BlockSpec((rows, 128), lambda group, pair: (0, group * pairs + pair))
     return pl.pallas_call(
         attend_forward_kernel,
-        grid=(pairs,),
-        in_specs=[attention_specs(rows, 128, part * pairs) for part in range(3)] + whole,
-        out_specs=[attention_specs(rows, 128, 0)] * 2,
+        grid=(2, pairs),
+        in_specs=attention_inputs(rows, pairs, column, row),
+        out_specs=[own, own],
         out_shape=[
-            jax.ShapeDtypeStruct((rows, pairs * 128), jnp.bfloat16),
-            jax.ShapeDtypeStruct((rows, pairs * 128), jnp.float32),
+            jax.ShapeDtypeStruct((rows, pairs * 256), jnp.bfloat16),
+            jax.ShapeDtypeStruct((rows, pairs * 256), jnp.float32),
         ],
-        cost_estimate=pl.CostEstimate(
-            flops=8 * pairs * rows * rows * 128,
-            bytes_accessed=pairs * rows * 128 * 12,
-            transcendentals=2 * pairs * rows * rows,
-        ),
-        compiler_params=pltpu.CompilerParams(vmem_limit_bytes=24 << 20),
+        **kernel_options(),
     )(qkv, qkv, qkv, column, row)
 
 
 def attend_rows_backward(qkv, column, row, logsum, d_context):
-    rows, pairs = qkv.shape[0], qkv.shape[1] // 384
-    whole = [pl.BlockSpec(column.shape, lambda pair: (0, 0)), pl.BlockSpec(row.shape, lambda pair: (0, 0))]
+    rows, pairs = qkv.shape[0], qkv.shape[1] // 768
+    own = pl.BlockSpec((rows, 128), lambda group, pair: (0, group * pairs + pair))
     return pl.pallas_call(
         attend_backward_kernel,
-        grid=(pairs,),
-        in_specs=[attention_specs(rows, 128, part * pairs) for part in range(3)]
-        + whole
-        + [attention_specs(rows, 128, 0)] * 2,
-        out_specs=[attention_specs(rows, 128, 0)] * 3,
-        out_shape=[jax.ShapeDtypeStruct((rows, pairs * 128), jnp.bfloat16)] * 3,
-        cost_estimate=pl.CostEstimate(
-            flops=20 * pairs * rows * rows * 128,
-            bytes_accessed=pairs * rows * 128 * 18,
-            transcendentals=2 * pairs * rows * rows,
-        ),
-        compiler_params=pltpu.CompilerParams(vmem_limit_bytes=32 << 20),
+        grid=(2, pairs),
+        in_specs=attention_inputs(rows, pairs, column, row) + [own, own],
+        out_specs=pl.BlockSpec(qkv.shape, lambda group, pair: (0, 0)),
+        out_shape=jax.ShapeDtypeStruct(qkv.shape, jnp.bfloat16),
+        **kernel_options(),
     )(qkv, qkv, qkv, column, row, logsum, d_context)
+
+
+def weight_specs(weight, start, steps, step):
+    rows = weight[0].shape[0]
+    first = start // step
+    left = pl.BlockSpec((rows, step), lambda group, at: (0, first + jnp.where(group == 0, at, steps - 1)))
+    other = pl.BlockSpec((rows, step), lambda group, at: (0, first + jnp.where(group == 1, at, 0)))
+    right = pl.BlockSpec((rows // 2, step), lambda group, at: (group, first + at))
+    return [left, other, right, right] * 2
+
+
+def with_block(refs, use):
+    for group in (0, 1):
+
+        @pl.when(pl.program_id(0) == group)
+        def _():
+            parts = (refs[group], refs[2], refs[3], refs[4 + group], refs[6], refs[7])
+            use(jnp.concatenate([part[...] for part in parts], axis=0))
+
+
+def expand_rows(rows, weight, start, width, step, finish, extras, out_types):
+    count = len(weight)
+
+    def kernel(rows_ref, *refs):
+        def use(block):
+            total = matmul(rows_ref[...], block)
+            results = finish(total, *[ref[...] for ref in refs[count : count + len(extras)]])
+            for ref, result in zip(refs[count + len(extras) :], results):
+                ref[...] = result
+
+        with_block(refs[:count], use)
+
+    steps = width // step
+
+    def own(height):
+        return pl.BlockSpec((height, step), lambda group, at: (0, group * steps + at))
+
+    return pl.pallas_call(
+        kernel,
+        grid=(2, steps),
+        in_specs=[pl.BlockSpec(rows.shape, lambda group, at: (0, 0))]
+        + weight_specs(weight, start, steps, step)
+        + [own(extra.shape[0]) for extra in extras],
+        out_specs=[own(height) for height, _ in out_types],
+        out_shape=[jax.ShapeDtypeStruct((height, 2 * width), kind) for height, kind in out_types],
+        **kernel_options(),
+    )(rows, *weight, *extras)
+
+
+def contract_rows(rows, weight, start, width, step):
+    steps = width // step
+    shape = (rows.shape[0], 4 * weight[0].shape[0])
+
+    def kernel(rows_ref, *refs):
+        out_ref = refs[-1]
+
+        @pl.when((pl.program_id(0) == 0) & (pl.program_id(1) == 0))
+        def _():
+            out_ref[...] = jnp.zeros_like(out_ref)
+
+        def use(block):
+            out_ref[...] += outer_cols(rows_ref[...], block)
+
+        with_block(refs[:-1], use)
+
+    return pl.pallas_call(
+        kernel,
+        grid=(2, steps),
+        in_specs=[pl.BlockSpec((rows.shape[0], step), lambda group, at: (0, group * steps + at))]
+        + weight_specs(weight, start, steps, step),
+        out_specs=pl.BlockSpec(shape, lambda group, at: (0, 0)),
+        out_shape=jax.ShapeDtypeStruct(shape, jnp.float32),
+        **kernel_options(),
+    )(rows, *weight)
+
+
+def grad_parts(terms):
+    depth = terms[0][0].shape[1]
+    half, quarter, eighth = depth // 2, depth // 4, depth // 8
+    widths = [units.shape[1] // 2 for _, _, units, _ in terms]
+    total_width = sum(widths)
+
+    def kernel(*refs):
+        y_keep, y_send, x_keep, x_send = refs[-4:]
+        start = 0
+        for index, width in enumerate(widths):
+            rows, rows_other, units, units_other = refs[4 * index :][:4]
+            columns = slice(start, start + width)
+            start += width
+            for core in (0, 1):
+                here = slice(core * half, (core + 1) * half)
+                there = slice((1 - core) * half, (2 - core) * half)
+                total = inner_rows(rows[:, here], units[...])
+                total = total + inner_rows(rows_other[:, there], units_other[...])
+                total = total.astype(jnp.bfloat16)
+                place = slice(core * quarter, (core + 1) * quarter)
+
+                @pl.when(pl.program_id(0) == 0)
+                def _():
+                    y_keep[place, columns] = total[:quarter]
+
+                @pl.when(pl.program_id(0) == 1)
+                def _():
+                    y_send[place, columns] = total[:quarter]
+
+                place = slice(core * eighth, (core + 1) * eighth)
+                x_keep[place, columns] = total[quarter : quarter + eighth]
+                x_send[place, columns] = total[quarter + eighth :]
+
+    in_specs = []
+    for (rows, _, units, _), width in zip(terms, widths):
+        whole = pl.BlockSpec(rows.shape, lambda group: (0, 0))
+        own = pl.BlockSpec((units.shape[0], width), lambda group: (0, group))
+        in_specs += [whole, whole, own, own]
+    y_spec = pl.BlockSpec((half, total_width), lambda group: (0, 0))
+    x_spec = pl.BlockSpec((quarter, total_width), lambda group: (group, 0))
+    return pl.pallas_call(
+        kernel,
+        grid=(2,),
+        in_specs=in_specs,
+        out_specs=[y_spec, y_spec, x_spec, x_spec],
+        out_shape=[jax.ShapeDtypeStruct((half, total_width), jnp.bfloat16)] * 4,
+        **kernel_options(),
+    )(*[array for term in terms for array in term])
 
 
 def gelu_pair(inputs):
@@ -465,14 +663,9 @@
     unit_width = w_up.shape[1]
     groups = (0, 1)
 
-    qkv_w = gather_weight(jnp.concatenate([w_qkv[0], w_qkv[1], w_qkv[2]], axis=1))
-    out_w = gather_weight(w_out.T)
-    up_w = gather_weight(w_up)
-    down_w = gather_weight(w_down.T)
-
     place = jnp.arange(width)
-    block = ((place // 32) % 4) * 4 + ((place // 128) % 2) * 2 + (place // 256) % 2
-    source = (dp_index ^ block) * 64 + (place // 512) * 32 + place % 32
+    block = ((place // 32) % 4) * 4 + ((place // 128) % 2) * 2 + place // 512
+    source = (dp_index ^ block) * 64 + ((place // 256) % 2) * 32 + place % 32
     order = (jnp.arange(width)[:, None] == source[None, :]).astype(low)
 
     def group_of(vector, group, size):
@@ -498,30 +691,67 @@
     which = lax.dynamic_slice_in_dim(segments, tensor_index, 1, axis=0)
     column, row = which.reshape(SEQ, 1), which
 
-    qkv, context, logsum = [], [], []
-    for group in groups:
-        bias = jnp.concatenate(
-            [
+    rows = tokens.shape[0]
+    blank = jnp.zeros((head_width,), wide)
+    qkv_bias = jnp.concatenate(
+        [
+            vector
+            for group in groups
+            for vector in (
                 group_of(bias_qv[0], group, head_width),
-                jnp.zeros((head_width,), wide),
+                blank,
                 group_of(bias_qv[1], group, head_width),
-            ]
+            )
+        ]
+    )[None]
+    units_bias = jnp.concatenate([group_of(bias_up, group, unit_width) for group in groups])[None]
+
+    def attention_work(weight):
+        (qkv,) = expand_rows(
+            own_rows,
+            weight,
+            0,
+            3 * head_width,
+            3 * head_width // 2,
+            lambda total, bias: ((total + bias).astype(low),),
+            [qkv_bias],
+            [(rows, low)],
         )
-        qkv.append((matmul(own_rows, qkv_w[group]) + bias).astype(low))
-        ctx, total = attend_rows_forward(qkv[group], column, row)
-        context.append(ctx)
-        logsum.append(total)
-    attn_rows = outer_cols(context[0], out_w[0]) + outer_cols(context[1], out_w[1])
-    z_one = own_rows.astype(wide) + attn_rows + bias_out
-    h_one, scaled_one, spread_one = norm_forward(z_one, ln1_gain, ln1_bias)
-    h_low = h_one.astype(low)
-    activation, slope = [], []
-    for group in groups:
-        units = matmul(h_low, up_w[group]) + group_of(bias_up, group, unit_width)
-        pair = gelu_pair(units)
-        activation.append(pair[0])
-        slope.append(pair[1])
-    mlp_rows = outer_cols(activation[0], down_w[0]) + outer_cols(activation[1], down_w[1])
+        context, logsum = attend_rows_forward(qkv, column, row)
+        return dict(qkv=qkv, context=context, logsum=logsum)
+
+    def units_work(weight, results):
+        attn_rows = contract_rows(results["context"], weight, unit_width, head_width, head_width)
+        z_one = own_rows.astype(wide) + attn_rows + bias_out
+        h_one, scaled_one, spread_one = norm_forward(z_one, ln1_gain, ln1_bias)
+        h_low = h_one.astype(low)
+        activation, slope = expand_rows(
+            h_low,
+            weight,
+            0,
+            unit_width,
+            unit_width // 4,
+            lambda total, bias: gelu_pair(total + bias),
+            [units_bias],
+            [(rows, low), (rows, low)],
+        )
+        return results | dict(
+            norm=(h_one, scaled_one, spread_one), h_low=h_low, activation=activation, slope=slope
+        )
+
+    (qkv_w, up_out_w, down_w), made = gather_weights(
+        [
+            jnp.concatenate([w_qkv[0], w_qkv[1], w_qkv[2]], axis=1),
+            jnp.concatenate([w_up, w_out.T], axis=1),
+            w_down.T,
+        ],
+        attention_work,
+        units_work,
+    )
+    qkv, context, logsum = made["qkv"], made["context"], made["logsum"]
+    h_one, scaled_one, spread_one = made["norm"]
+    h_low, activation, slope = made["h_low"], made["activation"], made["slope"]
+    mlp_rows = contract_rows(activation, down_w, 0, unit_width, unit_width // 2)
     z_two = h_one + mlp_rows + bias_down
     normed, scaled_two, spread_two = norm_forward(z_two, ln2_gain, ln2_bias)
     output = outer_cols(normed.astype(low), order).astype(low)
@@ -529,44 +759,120 @@
     grad_two, d_gain_two, d_offset_two = norm_backward(cotangent, scaled_two, spread_two, ln2_gain)
     d_bias_down = jnp.sum(grad_two, axis=0)
     grad_two_low = grad_two.astype(low)
-    grad_w_down = scatter_grad([inner_rows(grad_two_low, activation[g]).astype(low) for g in groups]).T
-    d_up = [(matmul(grad_two_low, down_w[g]) * slope[g].astype(wide)).astype(low) for g in groups]
-    d_bias_up = whole_of([jnp.sum(d_up[g], axis=0, dtype=wide) for g in groups])
-    grad_w_up = scatter_grad([inner_rows(h_low, d_up[g]).astype(low) for g in groups])
-    mlp_back = outer_cols(d_up[0], up_w[0]) + outer_cols(d_up[1], up_w[1])
+
+    after = lax.optimization_barrier
+    core_index = dp_index % 2
+
+    def core_halves(units, parts):
+        size = units.shape[1] // (4 * parts)
+        return [
+            jnp.concatenate(
+                [
+                    lax.dynamic_slice_in_dim(units, 2 * size * at + core * size, size, axis=1)
+                    for at in range(2 * parts)
+                ],
+                axis=1,
+            )
+            for core in (core_index, 1 - core_index)
+        ]
+
+    act_own, act_send = core_halves(activation, 1)
+    grad_two_low, slope, act_own, act_send = after((grad_two_low, slope, act_own, act_send))
+    grad_two_other, act_other = over_core(grad_two_low), over_core(act_send)
+
+    def finish_units(total, slope):
+        units = (total * slope.astype(wide)).astype(low)
+        return units, jnp.sum(units.astype(wide), axis=0, keepdims=True)
+
+    d_up, d_bias_units = expand_rows(
+        grad_two_low,
+        down_w,
+        0,
+        unit_width,
+        unit_width // 2,
+        finish_units,
+        [slope],
+        [(rows, low), (1, wide)],
+    )
+    up_own, up_send = core_halves(d_up, 1)
+    context_own, context_send = core_halves(context, 1)
+    (grad_two_other, act_other, d_up, up_own, up_send, h_low, own_rows, context_own, context_send) = after(
+        (grad_two_other, act_other, d_up, up_own, up_send, h_low, own_rows, context_own, context_send)
+    )
+    up_other, h_other = over_core(up_send), over_core(h_low)
+    rows_other, context_other = over_core(own_rows), over_core(context_send)
+    down_sum = grad_parts([(grad_two_low, grad_two_other, act_own, act_other)])
+    down_sum, up_other, h_other, rows_other, context_other, d_up = after(
+        (down_sum, up_other, h_other, rows_other, context_other, d_up)
+    )
+    down_sum = scatter_first(down_sum)
+    mlp_back = contract_rows(d_up, up_out_w, 0, unit_width, unit_width // 2)
     grad_one, d_gain_one, d_offset_one = norm_backward(
         mlp_back + grad_two, scaled_one, spread_one, ln1_gain
     )
     d_bias_out = jnp.sum(grad_one, axis=0)
     grad_one_low = grad_one.astype(low)
-    grad_w_out = scatter_grad([inner_rows(grad_one_low, context[g]).astype(low) for g in groups]).T
-    d_qkv = []
-    for group in groups:
-        d_ctx = matmul(grad_one_low, out_w[group]).astype(low)
-        d_qkv.append(
-            jnp.concatenate(
-                attend_rows_backward(qkv[group], column, row, logsum[group], d_ctx), axis=1
-            )
-        )
-    grad_qkv = scatter_grad([inner_rows(own_rows, d_qkv[g]).astype(low) for g in groups])
-    grad_w_qkv = jnp.stack([grad_qkv[:, i * head_width : (i + 1) * head_width] for i in range(3)])
-    attn_back = outer_cols(d_qkv[0], qkv_w[0]) + outer_cols(d_qkv[1], qkv_w[1])
+    up_sum = grad_parts([(h_low, h_other, up_own, up_other)])
+    (d_ctx,) = expand_rows(
+        grad_one_low,
+        up_out_w,
+        unit_width,
+        head_width,
+        head_width,
+        lambda total: (total.astype(low),),
+        [],
+        [(rows, low)],
+    )
+    down_sum, up_sum, d_ctx, grad_one_low = after((down_sum, up_sum, d_ctx, grad_one_low))
+    down_sum, up_sum = scatter_both(down_sum, up_sum)
+    grad_one_other = over_core(grad_one_low)
+    d_qkv = attend_rows_backward(qkv, column, row, logsum, d_ctx)
+    qkv_own, qkv_send = core_halves(d_qkv, 3)
+    qkv_other = over_core(qkv_send)
+    last_sum = grad_parts(
+        [
+            (own_rows, rows_other, qkv_own, qkv_other),
+            (grad_one_low, grad_one_other, context_own, context_other),
+        ]
+    )
+    down_sum, up_sum, last_sum, d_qkv = after((down_sum, up_sum, last_sum, d_qkv))
+    up_sum, last_sum = scatter_both(up_sum, last_sum)
+    down_sum = scatter_near(down_sum)
+    attn_back = contract_rows(d_qkv, qkv_w, 0, 3 * head_width, 3 * head_width // 2)
     grad_rows = attn_back + grad_one
     upper = grad_rows.astype(low)
     lower = (grad_rows - upper.astype(wide)).astype(low)
     grad_tokens = outer_cols(upper, order) + outer_cols(lower, order)
-
-    sums = [jnp.sum(d_qkv[g], axis=0, dtype=wide) for g in groups]
-    d_bias_q = whole_of([s[:head_width] for s in sums])
-    d_bias_v = whole_of([s[2 * head_width :] for s in sums])
+    d_bias_up = whole_of([d_bias_units[0, :unit_width], d_bias_units[0, unit_width:]])
+    sums = jnp.sum(d_qkv, axis=0, dtype=wide).reshape(2, 3, head_width)
+    d_bias_q = whole_of([sums[0, 0], sums[1, 0]])
+    d_bias_v = whole_of([sums[0, 2], sums[1, 2]])
     narrow = jnp.dot(
         jnp.stack([d_bias_out, d_gain_one, d_offset_one, d_bias_down, d_gain_two, d_offset_two]),
         order.astype(wide).T,
         precision=lax.Precision.HIGHEST,
     )
-    small = sum_all(
-        jnp.concatenate([narrow, d_bias_q[None], d_bias_v[None], d_bias_up.reshape(-1, width)], axis=0)
-    )
+    small = jnp.concatenate(
+        [narrow, d_bias_q[None], d_bias_v[None], d_bias_up.reshape(-1, width)], axis=0
+    )
+    down_sum, up_sum, last_sum = after((down_sum, up_sum, last_sum))
+    up_sum = scatter_near(up_sum)
+    last_sum = scatter_second(last_sum)
+    up_sum, last_sum, small = after((up_sum, last_sum, small))
+    last_sum = scatter_near(last_sum)
+    small = sum_chips(small)
+    last_sum, small = after((last_sum, small))
+    small = sum_near(small)
+    pairs = scatter_last([down_sum, up_sum, last_sum], core_index)
+    grad_w_down = jnp.concatenate(pairs[0], axis=1).T
+    grad_w_up = jnp.concatenate(pairs[1], axis=1)
+    size = head_width // 2
+    parts = [
+        jnp.concatenate([part[:, at * size :][:, :size] for part in pairs[2]], axis=1) for at in range(4)
+    ]
+    grad_w_qkv = jnp.stack(parts[:3])
+    grad_w_out = parts[3].T
+
     return (
         output,
         grad_tokens,

time: 567 us -> 432 us (0.76)
  waiting for transfers between devices: 288 us -> 140 us
  Pallas kernels: 32.2 us -> 107 us
  matrix products: 80 us -> 14.2 us
  starting transfers between devices: 105 us -> 61 us
  other arithmetic: 14.8 us -> 49.8 us
  local copies, waits for them, and re-layouts: 38.1 us -> 52.1 us
    ppermute x123 -> x65, waiting for transfers between devices: 288 us -> 140 us  [swap(): lax.ppermute(array, name, [(index, index ^ mask) for index in range(size)])]
    pallas_call x4 -> x13, Pallas kernels: 32.2 us -> 107 us  [the longest x4 26.9 us: expand_rows(): pl.pallas_call(kernel, grid=(2, steps), in_specs=[pl.BlockSpec(rows.shape...]
    ppermute x123 -> x65, starting transfers between devices: 105 us -> 61 us  [swap(): lax.ppermute(array, name, [(index, index ^ mask) for index in range(size)])]
    dot_general x10 -> x2, matrix products: 33.3 us -> 3.06 us  [matmul(): return jnp.dot(left, right, preferred_element_type=jnp.float32)]
    unnamed x188 -> x246, local copies, waits for them, and re-layouts: 16.3 us -> 40.1 us
    concatenate x9 -> x35, other arithmetic: 0.87 us -> 23 us  [the longest x10 8.99 us: beside(): return jnp.concatenate([left, right])]
    dot_general x11 -> x3, matrix products: 28 us -> 7.84 us  [outer_cols(): lax.dot_general(left, right, (((1,), (1,)), ((), ())), preferred_element_...]
    dot_general x8 -> x0, matrix products: 15.3 us -> none  [inner_rows(): lax.dot_general(left, right, (((0,), (0,)), ((), ())), preferred_element_...]
  transfers between devices with their start and end apart: 123 -> 65, of which waited for: 48 -> 24; matrix products, arithmetic and copies ran while one was open for 16% -> 15% of each run, Pallas kernels for 2% -> 19%
where the time goes in v2:
time: 432 us; the launch traced here: 427 us
  waiting for transfers between devices  140 us (32%)
  Pallas kernels  107 us (25%)
  starting transfers between devices  61 us (14%)
  local copies, waits for them, and re-layouts  52.1 us (12%)
  other arithmetic  49.8 us (12%)
  matrix products  14.2 us (3%)
    ppermute x65, waiting for transfers between devices, swap(): lax.ppermute(array, name, [(index, index ^ mask) for index in range(size)])  140 us
    ppermute x65, starting transfers between devices, swap(): lax.ppermute(array, name, [(index, index ^ mask) for index in range(size)])  61 us
    unnamed x246, local copies, waits for them, and re-layouts  40.1 us
    pallas_call x4, Pallas kernels, expand_rows(): pl.pallas_call(kernel, grid=(2, steps), in_specs=[pl.BlockSpec(rows.shape...  26.9 us
    pallas_call x3, Pallas kernels, grad_parts(): pl.pallas_call(kernel, grid=(2,), in_specs=in_specs, out_specs=[y_spec, y...  24.8 us
    pallas_call x4, Pallas kernels, contract_rows(): pl.pallas_call(kernel, grid=(2, steps), in_specs=[pl.BlockSpec((rows.shap...  22.7 us
    pallas_call x1, Pallas kernels, attend_rows_backward(): pl.pallas_call(attend_backward_kernel, grid=(2, pairs), in_specs=attentio...  19.6 us
    convert_element_type x10, other arithmetic, add_low(): (left.astype(jnp.float32) + right.astype(jnp.float32)).astype(jnp.bfloat16)  15 us
  transfers between devices with their start and end apart: 65, of which 24 were waited for; matrix products, arithmetic and copies ran while one was open for 15% of the time, Pallas kernels for 19%

profile of v2, /device:TPU:0, one launch (start us, length us, event | category | flops | bytes accessed | tf_op | source)
XLA Modules:
  0.0 426.9 jit_solution(695181731596775954)
XLA Ops:
  1.8 3.1 collective-permute-start.3
  5.8 2.5 collective-permute-start.2
  8.5 1.7 collective-permute-start
  10.3 10.0 %collective-permute-done.2 = bf16[64,1536]{1,0:T(8,128)(2,1)S(1)} collective-permute-done((bf16[64,1536]{1,0:T(8,128)(2,1)S(1)}, bf16[64,1536]{1,0:T(8,128)(2,1)S(1)}, u32[]{:S(2)}, u32[]{:S(2)}) %collective-permute-start.2) | collective-permute-done | bytes 196640 | tf_op jit(solution)/shard_map/ppermute | solution.py:265
  20.2 5.5 %collective-permute-done.1 = bf16[64,1536]{1,0:T(8,128)(2,1)S(1)} collective-permute-done((bf16[64,1536]{1,0:T(8,128)(2,1)S(1)}, bf16[64,1536]{1,0:T(8,128)(2,1)S(1)}, u32[]{:S(2)}, u32[]{:S(2)}) %collective-permute-start.1) | collective-permute-done | bytes 196640 | tf_op jit(solution)/shard_map/ppermute | solution.py:265
  25.8 1.6 collective-permute-start.4
  27.4 1.6 collective-permute-start.5
  29.0 2.3 collective-permute-start.6
  31.3 1.5 collective-permute-start.7
  32.8 9.7 %collective-permute-done.7 = bf16[64,2048]{1,0:T(8,128)(2,1)S(1)} collective-permute-done((bf16[64,2048]{1,0:T(8,128)(2,1)S(1)}, bf16[64,2048]{1,0:T(8,128)(2,1)S(1)}, u32[]{:S(2)}, u32[]{:S(2)}) %collective-permute-start.7) | collective-permute-done | bytes 262176 | tf_op jit(solution)/shard_map/ppermute | solution.py:265
  42.5 2.5 collective-permute-done.6
  46.5 17.3 %collective-permute-done.12 = bf16[64,2560]{1,0:T(8,128)(2,1)S(1)} collective-permute-done((bf16[64,2560]{1,0:T(8,128)(2,1)S(1)}, bf16[64,2560]{1,0:T(8,128)(2,1)S(1)}, u32[]{:S(2)}, u32[]{:S(2)}) %collective-permute-start.12) | collective-permute-done | bytes 327712 | tf_op jit(solution)/shard_map/ppermute | solution.py:265
  71.4 14.3 %collective-permute-done.17 = bf16[64,2048]{1,0:T(8,128)(2,1)S(1)} collective-permute-done((bf16[64,2048]{1,0:T(8,128)(2,1)}, bf16[64,2048]{1,0:T(8,128)(2,1)S(1)}, u32[]{:S(2)}, u32[]{:S(2)}) %collective-permute-start.17) | collective-permute-done | bytes 262176 | tf_op jit(solution)/shard_map/ppermute | solution.py:265
  96.5 6.2 %shard_map.254.q_ref.k_ref.v_ref = bf16[512,3072]{1,0:T(8,128)(2,1)S(1)} custom-call(bf16[512,1024]{1,0:T(8,128)(2,1)S(1)} %fusion.19.rows_ref.refs_0_, bf16[256,1536]{1,0:T(8,128)(2,1)S(1)} %copy-done.38, bf16[256,1536]{1,0:T(8,128)(2,1)S(1)} %copy-done.61, bf16[256,1536]{1,0:T(8,128)(2,1)S(1)} %copy-done.35, bf16[256,1536]{1,0:T(8,128)(2,1)S(1)} %copy-done.55, ...), custom_call_target="tpu_custom_call" | custom-call | tf_op jit(solution)/shard_map/pallas_call | solution.py:546
  102.7 12.8 %shard_map.255 = (bf16[512,1024]{1,0:T(8,128)(2,1)S(1)}, f32[512,1024]{1,0:T(8,128)S(1)}) custom-call(bf16[512,3072]{1,0:T(8,128)(2,1)S(1)} %shard_map.254.q_ref.k_ref.v_ref, bf16[512,3072]{1,0:T(8,128)(2,1)S(1)} %shard_map.254.q_ref.k_ref.v_ref, bf16[512,3072]{1,0:T(8,128)(2,1)S(1)} %shard_map.254.q_ref.k_ref.v_ref, s32[512,1]{1,0:T(8,128)S(1)} %copy-done.66, ...), custom_call_target="tpu_custom_call" | custom-call | tf_op jit(solution)/shard_map/pallas_call | solution.py:485
  116.8 3.9 collective-permute-done.19.refs_3_
  120.8 3.1 collective-permute-done.18.refs_1_
  128.0 10.6 %collective-permute-done.25 = bf16[128,2048]{1,0:T(8,128)(2,1)S(1)} collective-permute-done((bf16[128,2048]{1,0:T(8,128)(2,1)S(1)}, bf16[128,2048]{1,0:T(8,128)(2,1)S(1)}, u32[]{:S(2)}, u32[]{:S(2)}) %collective-permute-start.25) | collective-permute-done | bytes 524320 | tf_op jit(solution)/shard_map/ppermute | solution.py:265
  141.6 1.9 shard_map.256
  144.5 2.9 fusion.54
  147.5 11.5 %shard_map.257 = (bf16[512,4096]{1,0:T(8,128)(2,1)S(1)}, bf16[512,4096]{1,0:T(8,128)(2,1)S(1)}) custom-call(bf16[512,1024]{1,0:T(8,128)(2,1)} %get-tuple-element.272.rows_ref.refs_0_, bf16[256,2560]{1,0:T(8,128)(2,1)S(1)} %constant_dynamic-update-slice_fusion.4.refs_0_, bf16[256,2560]{1,0:T(8,128)(2,1)S(1)} %collective-permute-done.18.refs_1_, ...), custom_call_target="tpu_custom_call" | custom-call | tf_op jit(solution)/shard_map/pallas_call | solution.py:546
  159.0 2.1 copy-done.20
  161.0 2.1 copy-done.48
  164.1 1.5 collective-permute-done.28.refs_3_
  167.1 2.6 constant_dynamic-slice_fusion.9
  173.3 1.6 copy-done.21
  174.9 7.4 %shard_map.258 = f32[512,1024]{1,0:T(8,128)S(1)} custom-call(bf16[512,4096]{1,0:T(8,128)(2,1)S(1)} %copy-done.21, bf16[256,2048]{1,0:T(8,128)(2,1)S(1)} %copy-done.32, bf16[256,2048]{1,0:T(8,128)(2,1)} %collective-permute-done.27.refs_1_, bf16[256,2048]{1,0:T(8,128)(2,1)S(1)} %copy-done.29, bf16[256,2048]{1,0:T(8,128)(2,1)} %collective-permute-done.28.refs_3_, ...), custom_call_target="tpu_custom_call" | custom-call | tf_op jit(solution)/shard_map/pallas_call | solution.py:574
  183.0 1.7 fusion.7
  188.2 1.5 constant_dynamic-slice_fusion.1
  191.5 2.2 copy-done.49
  193.7 7.5 %shard_map.259 = (bf16[512,4096]{1,0:T(8,128)(2,1)S(1)}, f32[1,4096]{1,0:T(1,128)S(1)}) custom-call(bf16[512,1024]{1,0:T(8,128)(2,1)S(1)} %convert_element_type.296.rows_ref.refs_0_, bf16[256,2048]{1,0:T(8,128)(2,1)S(1)} %copy-done.33, bf16[256,2048]{1,0:T(8,128)(2,1)} %collective-permute-done.27.refs_1_, bf16[256,2048]{1,0:T(8,128)(2,1)S(1)} %copy-done.30, ...), custom_call_target="tpu_custom_call" | custom-call | tf_op jit(solution)/shard_map/pallas_call | solution.py:546
  208.3 1.6 copy-done.26
  211.2 7.2 %shard_map.260 = (bf16[512,1024]{1,0:T(8,128)(2,1)S(1)}, bf16[512,1024]{1,0:T(8,128)(2,1)S(1)}, bf16[512,1024]{1,0:T(8,128)(2,1)S(1)}, bf16[512,1024]{1,0:T(8,128)(2,1)S(1)}) custom-call(bf16[512,1024]{1,0:T(8,128)(2,1)S(1)} %convert_element_type.296.rows_ref.refs_0_, bf16[512,1024]{1,0:T(8,128)(2,1)S(1)} %copy-done.79, bf16[512,2048]{1,0:T(8,128)(2,1)S(1)} %copy-done.26, ...), custom_call_target="tpu_custom_call" | custom-call | tf_op jit(solution)/shard_map/pallas_call | solution.py:625
  224.2 2.2 copy-done.23
  226.4 7.1 %shard_map.262 = f32[512,1024]{1,0:T(8,128)S(1)} custom-call(bf16[512,4096]{1,0:T(8,128)(2,1)S(1)} %copy-done.23, bf16[256,2560]{1,0:T(8,128)(2,1)S(1)} %copy-done.5, bf16[256,2560]{1,0:T(8,128)(2,1)S(1)} %copy-done.15, bf16[256,2560]{1,0:T(8,128)(2,1)S(1)} %constant_dynamic-update-slice_fusion.6.refs_2_, bf16[256,2560]{1,0:T(8,128)(2,1)S(1)} %copy-done.11, ...), custom_call_target="tpu_custom_call" | custom-call | tf_op jit(solution)/shard_map/pallas_call | solution.py:574
  235.1 1.7 shard_map.263.dctx_ref
  238.0 7.5 %shard_map.261 = (bf16[512,1024]{1,0:T(8,128)(2,1)S(1)}, bf16[512,1024]{1,0:T(8,128)(2,1)S(1)}, bf16[512,1024]{1,0:T(8,128)(2,1)S(1)}, bf16[512,1024]{1,0:T(8,128)(2,1)S(1)}) custom-call(bf16[512,1024]{1,0:T(8,128)(2,1)} %get-tuple-element.272.rows_ref.refs_0_, bf16[512,1024]{1,0:T(8,128)(2,1)} %collective-permute-done.36.refs_1_, ...), custom_call_target="tpu_custom_call" | custom-call | tf_op jit(solution)/shard_map/pallas_call | solution.py:625
  245.5 2.4 add_convert_fusion.26
  253.6 2.5 pad_maximum_fusion.4
  258.1 1.6 copy-done.71
  259.7 19.6 %shard_map.264.rows_ref = bf16[512,3072]{1,0:T(8,128)(2,1)S(1)} custom-call(bf16[512,3072]{1,0:T(8,128)(2,1)S(1)} %copy-done.3, bf16[512,3072]{1,0:T(8,128)(2,1)S(1)} %copy-done.3, bf16[512,3072]{1,0:T(8,128)(2,1)S(1)} %copy-done.3, s32[512,1]{1,0:T(8,128)S(1)} %copy-done.67, s32[1,512]{1,0:T(1,128)S(1)} %constant_dynamic-slice_fusion.12.row_ref, ...), custom_call_target="tpu_custom_call" | custom-call | tf_op jit(solution)/shard_map/pallas_call | solution.py:501
  285.4 2.5 fusion.18
  287.9 1.9 fusion
  290.4 1.9 add_convert_fusion.22
  294.5 3.0 add_convert_fusion.8
  297.7 10.2 %shard_map.265 = (bf16[512,1024]{1,0:T(8,128)(2,1)S(1)}, bf16[512,1024]{1,0:T(8,128)(2,1)S(1)}, bf16[512,1024]{1,0:T(8,128)(2,1)S(1)}, bf16[512,1024]{1,0:T(8,128)(2,1)S(1)}) custom-call(bf16[512,1024]{1,0:T(8,128)(2,1)S(1)} %copy-done.7, bf16[512,1024]{1,0:T(8,128)(2,1)} %collective-permute-done.37.refs_1_, bf16[512,1536]{1,0:T(8,128)(2,1)S(1)} %copy-done.69, ...), custom_call_target="tpu_custom_call" | custom-call | tf_op jit(solution)/shard_map/pallas_call | solution.py:625
  307.9 6.3 %shard_map.266 = f32[512,1024]{1,0:T(8,128)S(1)} custom-call(bf16[512,3072]{1,0:T(8,128)(2,1)S(1)} %shard_map.264.rows_ref, bf16[256,1536]{1,0:T(8,128)(2,1)S(1)} %copy-done.39, bf16[256,1536]{1,0:T(8,128)(2,1)S(1)} %copy-done.62, bf16[256,1536]{1,0:T(8,128)(2,1)S(1)} %copy-done.36, bf16[256,1536]{1,0:T(8,128)(2,1)S(1)} %copy-done.56, ...), custom_call_target="tpu_custom_call" | custom-call | tf_op jit(solution)/shard_map/pallas_call | solution.py:574
  318.1 2.9 collective-permute-start.46
  325.8 2.7 fusion.1
  329.1 10.6 %collective-permute-done.46 = bf16[128,1024]{1,0:T(8,128)(2,1)} collective-permute-done((bf16[128,1024]{1,0:T(8,128)(2,1)}, bf16[128,1024]{1,0:T(8,128)(2,1)}, u32[]{:S(2)}, u32[]{:S(2)}) %collective-permute-start.46) | collective-permute-done | bytes 262176 | tf_op jit(solution)/shard_map/ppermute | solution.py:265
  341.0 12.2 %collective-permute-done.49 = bf16[768,1024]{1,0:T(8,128)(2,1)} collective-permute-done((bf16[768,1024]{1,0:T(8,128)(2,1)}, bf16[768,1024]{1,0:T(8,128)(2,1)}, u32[]{:S(2)}, u32[]{:S(2)}) %collective-permute-start.49) | collective-permute-done | bytes 1572896 | tf_op jit(solution)/shard_map/ppermute | solution.py:265
  353.2 1.6 add_convert_fusion.18
  356.2 3.9 collective-permute-done.48
  360.1 2.0 add_convert_fusion.4
  362.4 3.0 collective-permute-start.51
  369.5 3.6 collective-permute-done.50
  373.1 10.5 %collective-permute-done.51 = bf16[128,1024]{1,0:T(8,128)(2,1)S(1)} collective-permute-done((bf16[128,1024]{1,0:T(8,128)(2,1)S(1)}, bf16[128,1024]{1,0:T(8,128)(2,1)S(1)}, u32[]{:S(2)}, u32[]{:S(2)}) %collective-permute-start.51) | collective-permute-done | bytes 262176 | tf_op jit(solution)/shard_map/ppermute | solution.py:265
  384.4 3.5 collective-permute-start.55
  391.8 3.0 collective-permute-done.59
  396.1 3.0 collective-permute-done.60
  400.0 9.3 %collective-permute-done.56 = bf16[128,1024]{1,0:T(8,128)(2,1)S(1)} collective-permute-done((bf16[128,1024]{1,0:T(8,128)(2,1)S(1)}, bf16[128,1024]{1,0:T(8,128)(2,1)S(1)}, u32[]{:S(2)}, u32[]{:S(2)}) %collective-permute-start.56) | collective-permute-done | bytes 262176 | tf_op jit(solution)/shard_map/ppermute | solution.py:265
  409.5 2.4 collective-permute-start.64
  411.9 5.3 %collective-permute-start.63 = (f32[12,1024]{1,0:T(8,128)S(1)}, f32[12,1024]{1,0:T(8,128)S(1)}, u32[]{:S(2)}, u32[]{:S(2)}) collective-permute-start(f32[12,1024]{1,0:T(8,128)S(1)} %add.516), channel_id=1, source_target_pairs={{0,16},{2,18},{4,20},{6,22},{8,24},{10,26},{12,28},{14,30},{16,0},... | collective-permute-start | bytes 147464 | tf_op jit(solution)/shard_map/ppermute | solution.py:265
  417.4 2.7 fusion.16
  (467 shorter events, 106.3 us)
Async XLA Ops:
  1.8 24.0 %collective-permute-start.3 = (bf16[64,2560]{1,0:T(8,128)(2,1)S(1)}, bf16[64,2560]{1,0:T(8,128)(2,1)S(1)}, u32[]{:S(2)}, u32[]{:S(2)}) collective-permute-start(bf16[64,2560]{1,0:T(8,128)(2,1)S(1)} %pad_maximum_fusion.24), channel_id=1, source_target_pairs={{0,8},{2,10},{4,12},{6,14},{8,0},{10,2},{12,4},{14,6},{16,24},{18,... | collective-permute-start | bytes 983048 | tf_op jit(solution)/shard_map/ppermute | solution.py:265
  5.8 14.4 %collective-permute-start.2 = (bf16[64,1536]{1,0:T(8,128)(2,1)S(1)}, bf16[64,1536]{1,0:T(8,128)(2,1)S(1)}, u32[]{:S(2)}, u32[]{:S(2)}) collective-permute-start(bf16[64,1536]{1,0:T(8,128)(2,1)S(1)} %pad_maximum_fusion.37), channel_id=1, source_target_pairs={{0,24},{2,26},{4,28},{6,30},{8,16},{10,18},{12,20},{14,22},{16,8},... | collective-permute-start | bytes 589832 | tf_op jit(solution)/shard_map/ppermute | solution.py:265
  8.3 17.4 %collective-permute-start.1 = (bf16[64,1536]{1,0:T(8,128)(2,1)S(1)}, bf16[64,1536]{1,0:T(8,128)(2,1)S(1)}, u32[]{:S(2)}, u32[]{:S(2)}) collective-permute-start(bf16[64,1536]{1,0:T(8,128)(2,1)S(1)} %pad_maximum_fusion.37), channel_id=1, source_target_pairs={{0,16},{2,18},{4,20},{6,22},{8,24},{10,26},{12,28},{14,30},{16,0},... | collective-permute-start | bytes 589832 | tf_op jit(solution)/shard_map/ppermute | solution.py:265
  8.5 17.2 %collective-permute-start = (bf16[64,1536]{1,0:T(8,128)(2,1)S(1)}, bf16[64,1536]{1,0:T(8,128)(2,1)S(1)}, u32[]{:S(2)}, u32[]{:S(2)}) collective-permute-start(bf16[64,1536]{1,0:T(8,128)(2,1)S(1)} %pad_maximum_fusion.37), channel_id=1, source_target_pairs={{0,8},{2,10},{4,12},{6,14},{8,0},{10,2},{12,4},{14,6},{16,24},{18,... | collective-permute-start | bytes 589832 | tf_op jit(solution)/shard_map/ppermute | solution.py:265
  25.8 19.1 %collective-permute-start.4 = (bf16[128,1536]{1,0:T(8,128)(2,1)S(1)}, bf16[128,1536]{1,0:T(8,128)(2,1)S(1)}, u32[]{:S(2)}, u32[]{:S(2)}) collective-permute-start(bf16[128,1536]{1,0:T(8,128)(2,1)S(1)} %pad_maximum_fusion.21), channel_id=1, source_target_pairs={{0,4},{2,6},{4,0},{6,2},{8,12},{10,14},{12,8},{14,10},{16,20},{18,... | collective-permute-start | bytes 1179656 | tf_op jit(solution)/shard_map/ppermute | solution.py:265
  27.4 17.5 %collective-permute-start.5 = (bf16[128,1536]{1,0:T(8,128)(2,1)S(1)}, bf16[128,1536]{1,0:T(8,128)(2,1)S(1)}, u32[]{:S(2)}, u32[]{:S(2)}) collective-permute-start(bf16[128,1536]{1,0:T(8,128)(2,1)S(1)} %pad_maximum_fusion.22), channel_id=1, source_target_pairs={{0,1},{1,0},{2,3},{3,2},{4,5},{5,4},{6,7},{7,6},{8,9},{9,8},{10,11... | collective-permute-start | bytes 1179656 | tf_op jit(solution)/shard_map/ppermute | solution.py:265
  29.0 15.9 %collective-permute-start.6 = (bf16[64,2560]{1,0:T(8,128)(2,1)S(1)}, bf16[64,2560]{1,0:T(8,128)(2,1)S(1)}, u32[]{:S(2)}, u32[]{:S(2)}) collective-permute-start(bf16[64,2560]{1,0:T(8,128)(2,1)S(1)} %pad_maximum_fusion.24), channel_id=1, source_target_pairs={{0,16},{2,18},{4,20},{6,22},{8,24},{10,26},{12,28},{14,30},{16,0},... | collective-permute-start | bytes 983048 | tf_op jit(solution)/shard_map/ppermute | solution.py:265
  31.3 11.2 %collective-permute-start.7 = (bf16[64,2048]{1,0:T(8,128)(2,1)S(1)}, bf16[64,2048]{1,0:T(8,128)(2,1)S(1)}, u32[]{:S(2)}, u32[]{:S(2)}) collective-permute-start(bf16[64,2048]{1,0:T(8,128)(2,1)S(1)} %bitcast.194), channel_id=1, source_target_pairs={{0,8},{2,10},{4,12},{6,14},{8,0},{10,2},{12,4},{14,6},{16,24},{18,... | collective-permute-start | bytes 786440 | tf_op jit(solution)/shard_map/ppermute | solution.py:265
  45.0 18.8 %collective-permute-start.11 = (bf16[256,1536]{1,0:T(8,128)(2,1)S(1)}, bf16[256,1536]{1,0:T(8,128)(2,1)S(1)}, u32[]{:S(2)}, u32[]{:S(2)}) collective-permute-start(bf16[256,1536]{1,0:T(8,128)(2,1)S(1)} %constant_dynamic-update-slice_fusion.2.refs_2_), channel_id=1, source_target_pairs={{0,2},{2,0},{4,6},{6,4},{8,10},{10,8},{12,14},{14,12},{16,18},{18,... | collective-permute-start | bytes 2359304 | tf_op jit(solution)/shard_map/ppermute | solution.py:265
  45.1 20.0 %collective-permute-start.9 = (bf16[256,1536]{1,0:T(8,128)(2,1)S(1)}, bf16[256,1536]{1,0:T(8,128)(2,1)S(1)}, u32[]{:S(2)}, u32[]{:S(2)}) collective-permute-start(bf16[256,1536]{1,0:T(8,128)(2,1)S(1)} %constant_dynamic-update-slice_fusion.2.refs_2_), channel_id=1, source_target_pairs={{0,4},{2,6},{4,0},{6,2},{8,12},{10,14},{12,8},{14,10},{16,20},{18,... | collective-permute-start | bytes 2359304 | tf_op jit(solution)/shard_map/ppermute | solution.py:265
  45.8 19.3 %collective-permute-start.10 = (bf16[256,1536]{1,0:T(8,128)(2,1)S(1)}, bf16[256,1536]{1,0:T(8,128)(2,1)S(1)}, u32[]{:S(2)}, u32[]{:S(2)}) collective-permute-start(bf16[256,1536]{1,0:T(8,128)(2,1)S(1)} %constant_dynamic-update-slice_fusion.refs_0_), channel_id=1, source_target_pairs={{0,2},{2,0},{4,6},{6,4},{8,10},{10,8},{12,14},{14,12},{16,18},{18,... | collective-permute-start | bytes 2359304 | tf_op jit(solution)/shard_map/ppermute | solution.py:265
  46.0 20.0 %collective-permute-start.8 = (bf16[256,1536]{1,0:T(8,128)(2,1)S(1)}, bf16[256,1536]{1,0:T(8,128)(2,1)S(1)}, u32[]{:S(2)}, u32[]{:S(2)}) collective-permute-start(bf16[256,1536]{1,0:T(8,128)(2,1)S(1)} %constant_dynamic-update-slice_fusion.refs_0_), channel_id=1, source_target_pairs={{0,1},{1,0},{2,3},{3,2},{4,5},{5,4},{6,7},{7,6},{8,9},{9,8},{10,11... | collective-permute-start | bytes 2359304 | tf_op jit(solution)/shard_map/ppermute | solution.py:265
  46.5 17.3 %collective-permute-start.12 = (bf16[64,2560]{1,0:T(8,128)(2,1)S(1)}, bf16[64,2560]{1,0:T(8,128)(2,1)S(1)}, u32[]{:S(2)}, u32[]{:S(2)}) collective-permute-start(bf16[64,2560]{1,0:T(8,128)(2,1)S(1)} %collective-permute-done.3), channel_id=1, source_target_pairs={{0,16},{2,18},{4,20},{6,22},{8,24},{10,26},{12,28},{14,30},{16,0},... | collective-permute-start | bytes 983048 | tf_op jit(solution)/shard_map/ppermute | solution.py:265
  67.1 18.6 %collective-permute-start.15 = (bf16[128,2560]{1,0:T(8,128)(2,1)}, bf16[128,2560]{1,0:T(8,128)(2,1)}, u32[]{:S(2)}, u32[]{:S(2)}) collective-permute-start(bf16[128,2560]{1,0:T(8,128)(2,1)} %pad_maximum_fusion.8), channel_id=1, source_target_pairs={{0,4},{2,6},{4,0},{6,2},{8,12},{10,14},{12,8},{14,10},{16,20},{18,... | collective-permute-start | bytes 1966088 | tf_op jit(solution)/shard_map/ppermute | solution.py:265
  68.4 18.4 %collective-permute-start.13 = (bf16[256,1536]{1,0:T(8,128)(2,1)S(1)}, bf16[256,1536]{1,0:T(8,128)(2,1)S(1)}, u32[]{:S(2)}, u32[]{:S(2)}) collective-permute-start(bf16[256,1536]{1,0:T(8,128)(2,1)S(1)} %collective-permute-done.8.refs_1_), channel_id=1, source_target_pairs={{0,2},{2,0},{4,6},{6,4},{8,10},{10,8},{12,14},{14,12},{16,18},{18,... | collective-permute-start | bytes 2359304 | tf_op jit(solution)/shard_map/ppermute | solution.py:265
  68.4 18.4 %collective-permute-start.14 = (bf16[256,1536]{1,0:T(8,128)(2,1)S(1)}, bf16[256,1536]{1,0:T(8,128)(2,1)}, u32[]{:S(2)}, u32[]{:S(2)}) collective-permute-start(bf16[256,1536]{1,0:T(8,128)(2,1)S(1)} %collective-permute-done.9.refs_3_), channel_id=1, source_target_pairs={{0,2},{2,0},{4,6},{6,4},{8,10},{10,8},{12,14},{14,12},{16,18},{18,... | collective-permute-start | bytes 2359304 | tf_op jit(solution)/shard_map/ppermute | solution.py:265
  69.8 17.0 %collective-permute-start.16 = (bf16[128,2560]{1,0:T(8,128)(2,1)}, bf16[128,2560]{1,0:T(8,128)(2,1)}, u32[]{:S(2)}, u32[]{:S(2)}) collective-permute-start(bf16[128,2560]{1,0:T(8,128)(2,1)} %pad_maximum_fusion.9), channel_id=1, source_target_pairs={{0,1},{1,0},{2,3},{3,2},{4,5},{5,4},{6,7},{7,6},{8,9},{9,8},{10,11... | collective-permute-start | bytes 1966088 | tf_op jit(solution)/shard_map/ppermute | solution.py:265
  71.3 14.4 %collective-permute-start.17 = (bf16[64,2048]{1,0:T(8,128)(2,1)}, bf16[64,2048]{1,0:T(8,128)(2,1)S(1)}, u32[]{:S(2)}, u32[]{:S(2)}) collective-permute-start(bf16[64,2048]{1,0:T(8,128)(2,1)} %bitcast.193), channel_id=1, source_target_pairs={{0,16},{2,18},{4,20},{6,22},{8,24},{10,26},{12,28},{14,30},{16,0},... | collective-permute-start | bytes 786440 | tf_op jit(solution)/shard_map/ppermute | solution.py:265
  89.5 27.3 %collective-permute-start.21 = (bf16[256,2560]{1,0:T(8,128)(2,1)S(1)}, bf16[256,2560]{1,0:T(8,128)(2,1)S(1)}, u32[]{:S(2)}, u32[]{:S(2)}) collective-permute-start(bf16[256,2560]{1,0:T(8,128)(2,1)S(1)} %constant_dynamic-update-slice_fusion.6.refs_2_), channel_id=1, source_target_pairs={{0,2},{2,0},{4,6},{6,4},{8,10},{10,8},{12,14},{14,12},{16,18},{18,... | collective-permute-start | bytes 3932168 | tf_op jit(solution)/shard_map/ppermute | solution.py:265
  89.6 31.2 %collective-permute-start.19 = (bf16[256,2560]{1,0:T(8,128)(2,1)S(1)}, bf16[256,2560]{1,0:T(8,128)(2,1)S(1)}, u32[]{:S(2)}, u32[]{:S(2)}) collective-permute-start(bf16[256,2560]{1,0:T(8,128)(2,1)S(1)} %constant_dynamic-update-slice_fusion.6.refs_2_), channel_id=1, source_target_pairs={{0,4},{2,6},{4,0},{6,2},{8,12},{10,14},{12,8},{14,10},{16,20},{18,... | collective-permute-start | bytes 3932168 | tf_op jit(solution)/shard_map/ppermute | solution.py:265
  92.6 28.1 %collective-permute-start.20 = (bf16[256,2560]{1,0:T(8,128)(2,1)S(1)}, bf16[256,2560]{1,0:T(8,128)(2,1)S(1)}, u32[]{:S(2)}, u32[]{:S(2)}) collective-permute-start(bf16[256,2560]{1,0:T(8,128)(2,1)S(1)} %constant_dynamic-update-slice_fusion.4.refs_0_), channel_id=1, source_target_pairs={{0,2},{2,0},{4,6},{6,4},{8,10},{10,8},{12,14},{14,12},{16,18},{18,... | collective-permute-start | bytes 3932168 | tf_op jit(solution)/shard_map/ppermute | solution.py:265
  92.9 31.0 %collective-permute-start.18 = (bf16[256,2560]{1,0:T(8,128)(2,1)S(1)}, bf16[256,2560]{1,0:T(8,128)(2,1)S(1)}, u32[]{:S(2)}, u32[]{:S(2)}) collective-permute-start(bf16[256,2560]{1,0:T(8,128)(2,1)S(1)} %constant_dynamic-update-slice_fusion.4.refs_0_), channel_id=1, source_target_pairs={{0,1},{1,0},{2,3},{3,2},{4,5},{5,4},{6,7},{7,6},{8,9},{9,8},{10,11... | collective-permute-start | bytes 3932168 | tf_op jit(solution)/shard_map/ppermute | solution.py:265
  93.6 23.2 %collective-permute-start.22 = (bf16[64,2048]{1,0:T(8,128)(2,1)S(1)}, bf16[64,2048]{1,0:T(8,128)(2,1)S(1)}, u32[]{:S(2)}, u32[]{:S(2)}) collective-permute-start(bf16[64,2048]{1,0:T(8,128)(2,1)S(1)} %copy-done.102), channel_id=1, source_target_pairs={{0,16},{2,18},{4,20},{6,22},{8,24},{10,26},{12,28},{14,30},{16,0},... | collective-permute-start | bytes 786440 | tf_op jit(solution)/shard_map/ppermute | solution.py:265
  124.0 15.8 %collective-permute-start.23 = (bf16[256,2560]{1,0:T(8,128)(2,1)S(1)}, bf16[256,2560]{1,0:T(8,128)(2,1)S(1)}, u32[]{:S(2)}, u32[]{:S(2)}) collective-permute-start(bf16[256,2560]{1,0:T(8,128)(2,1)S(1)} %collective-permute-done.18.refs_1_), channel_id=1, source_target_pairs={{0,2},{2,0},{4,6},{6,4},{8,10},{10,8},{12,14},{14,12},{16,18},{18,... | collective-permute-start | bytes 3932168 | tf_op jit(solution)/shard_map/ppermute | solution.py:265
  124.1 15.7 %collective-permute-start.24 = (bf16[256,2560]{1,0:T(8,128)(2,1)S(1)}, bf16[256,2560]{1,0:T(8,128)(2,1)S(1)}, u32[]{:S(2)}, u32[]{:S(2)}) collective-permute-start(bf16[256,2560]{1,0:T(8,128)(2,1)S(1)} %collective-permute-done.19.refs_3_), channel_id=1, source_target_pairs={{0,2},{2,0},{4,6},{6,4},{8,10},{10,8},{12,14},{14,12},{16,18},{18,... | collective-permute-start | bytes 3932168 | tf_op jit(solution)/shard_map/ppermute | solution.py:265
  124.6 14.0 %collective-permute-start.25 = (bf16[128,2048]{1,0:T(8,128)(2,1)S(1)}, bf16[128,2048]{1,0:T(8,128)(2,1)S(1)}, u32[]{:S(2)}, u32[]{:S(2)}) collective-permute-start(bf16[128,2048]{1,0:T(8,128)(2,1)S(1)} %pad_maximum_fusion.10), channel_id=1, source_target_pairs={{0,4},{2,6},{4,0},{6,2},{8,12},{10,14},{12,8},{14,10},{16,20},{18,... | collective-permute-start | bytes 1572872 | tf_op jit(solution)/shard_map/ppermute | solution.py:265
  126.0 13.7 %collective-permute-start.26 = (bf16[128,2048]{1,0:T(8,128)(2,1)S(1)}, bf16[128,2048]{1,0:T(8,128)(2,1)S(1)}, u32[]{:S(2)}, u32[]{:S(2)}) collective-permute-start(bf16[128,2048]{1,0:T(8,128)(2,1)S(1)} %pad_maximum_fusion.11), channel_id=1, source_target_pairs={{0,1},{1,0},{2,3},{3,2},{4,5},{5,4},{6,7},{7,6},{8,9},{9,8},{10,11... | collective-permute-start | bytes 1572872 | tf_op jit(solution)/shard_map/ppermute | solution.py:265
  139.9 23.2 %collective-permute-start.30 = (bf16[256,2048]{1,0:T(8,128)(2,1)S(1)}, bf16[256,2048]{1,0:T(8,128)(2,1)S(1)}, u32[]{:S(2)}, u32[]{:S(2)}) collective-permute-start(bf16[256,2048]{1,0:T(8,128)(2,1)S(1)} %constant_dynamic-update-slice_fusion.11.refs_2_), channel_id=1, source_target_pairs={{0,2},{2,0},{4,6},{6,4},{8,10},{10,8},{12,14},{14,12},{16,18},{18,... | collective-permute-start | bytes 3145736 | tf_op jit(solution)/shard_map/ppermute | solution.py:265
  139.9 25.7 %collective-permute-start.28 = (bf16[256,2048]{1,0:T(8,128)(2,1)S(1)}, bf16[256,2048]{1,0:T(8,128)(2,1)}, u32[]{:S(2)}, u32[]{:S(2)}) collective-permute-start(bf16[256,2048]{1,0:T(8,128)(2,1)S(1)} %constant_dynamic-update-slice_fusion.11.refs_2_), channel_id=1, source_target_pairs={{0,4},{2,6},{4,0},{6,2},{8,12},{10,14},{12,8},{14,10},{16,20},{18,... | collective-permute-start | bytes 3145736 | tf_op jit(solution)/shard_map/ppermute | solution.py:265
  140.8 24.8 %collective-permute-start.29 = (bf16[256,2048]{1,0:T(8,128)(2,1)S(1)}, bf16[256,2048]{1,0:T(8,128)(2,1)S(1)}, u32[]{:S(2)}, u32[]{:S(2)}) collective-permute-start(bf16[256,2048]{1,0:T(8,128)(2,1)S(1)} %constant_dynamic-update-slice_fusion.9.refs_0_), channel_id=1, source_target_pairs={{0,2},{2,0},{4,6},{6,4},{8,10},{10,8},{12,14},{14,12},{16,18},{18,... | collective-permute-start | bytes 3145736 | tf_op jit(solution)/shard_map/ppermute | solution.py:265
  141.1 25.5 %collective-permute-start.27 = (bf16[256,2048]{1,0:T(8,128)(2,1)S(1)}, bf16[256,2048]{1,0:T(8,128)(2,1)}, u32[]{:S(2)}, u32[]{:S(2)}) collective-permute-start(bf16[256,2048]{1,0:T(8,128)(2,1)S(1)} %constant_dynamic-update-slice_fusion.9.refs_0_), channel_id=1, source_target_pairs={{0,1},{1,0},{2,3},{3,2},{4,5},{5,4},{6,7},{7,6},{8,9},{9,8},{10,11... | collective-permute-start | bytes 3145736 | tf_op jit(solution)/shard_map/ppermute | solution.py:265
  166.6 6.2 %collective-permute-start.31 = (bf16[256,2048]{1,0:T(8,128)(2,1)}, bf16[256,2048]{1,0:T(8,128)(2,1)}, u32[]{:S(2)}, u32[]{:S(2)}) collective-permute-start(bf16[256,2048]{1,0:T(8,128)(2,1)} %collective-permute-done.27.refs_1_), channel_id=1, source_target_pairs={{0,2},{2,0},{4,6},{6,4},{8,10},{10,8},{12,14},{14,12},{16,18},{18,... | collective-permute-start | bytes 3145736 | tf_op jit(solution)/shard_map/ppermute | solution.py:265
  166.6 6.2 %collective-permute-start.32 = (bf16[256,2048]{1,0:T(8,128)(2,1)}, bf16[256,2048]{1,0:T(8,128)(2,1)}, u32[]{:S(2)}, u32[]{:S(2)}) collective-permute-start(bf16[256,2048]{1,0:T(8,128)(2,1)} %collective-permute-done.28.refs_3_), channel_id=1, source_target_pairs={{0,2},{2,0},{4,6},{6,4},{8,10},{10,8},{12,14},{14,12},{16,18},{18,... | collective-permute-start | bytes 3145736 | tf_op jit(solution)/shard_map/ppermute | solution.py:265
  187.6 19.6 %collective-permute-start.34 = (bf16[512,2048]{1,0:T(8,128)(2,1)}, bf16[512,2048]{1,0:T(8,128)(2,1)}, u32[]{:S(2)}, u32[]{:S(2)}) collective-permute-start(bf16[512,2048]{1,0:T(8,128)(2,1)} %pad_maximum_fusion.1), channel_id=1, source_target_pairs={{0,2},{2,0},{4,6},{6,4},{8,10},{10,8},{12,14},{14,12},{16,18},{18,... | collective-permute-start | bytes 6291464 | tf_op jit(solution)/shard_map/ppermute | solution.py:265
  187.7 18.5 %collective-permute-start.33 = (bf16[512,1024]{1,0:T(8,128)(2,1)S(1)}, bf16[512,1024]{1,0:T(8,128)(2,1)S(1)}, u32[]{:S(2)}, u32[]{:S(2)}) collective-permute-start(bf16[512,1024]{1,0:T(8,128)(2,1)S(1)} %convert_element_type.296.rows_ref.refs_0_), channel_id=1, source_target_pairs={{0,2},{2,0},{4,6},{6,4},{8,10},{10,8},{12,14},{14,12},{16,18},{18,... | collective-permute-start | bytes 3145736 | tf_op jit(solution)/shard_map/ppermute | solution.py:265
  207.2 11.1 %collective-permute-start.35 = (bf16[512,2048]{1,0:T(8,128)(2,1)}, bf16[512,2048]{1,0:T(8,128)(2,1)}, u32[]{:S(2)}, u32[]{:S(2)}) collective-permute-start(bf16[512,2048]{1,0:T(8,128)(2,1)} %pad_maximum_fusion.3), channel_id=1, source_target_pairs={{0,2},{2,0},{4,6},{6,4},{8,10},{10,8},{12,14},{14,12},{16,18},{18,... | collective-permute-start | bytes 6291464 | tf_op jit(solution)/shard_map/ppermute | solution.py:265
  207.2 11.1 %collective-permute-start.36 = (bf16[512,1024]{1,0:T(8,128)(2,1)}, bf16[512,1024]{1,0:T(8,128)(2,1)}, u32[]{:S(2)}, u32[]{:S(2)}) collective-permute-start(bf16[512,1024]{1,0:T(8,128)(2,1)} %get-tuple-element.272.rows_ref.refs_0_), channel_id=1, source_target_pairs={{0,2},{2,0},{4,6},{6,4},{8,10},{10,8},{12,14},{14,12},{16,18},{18,... | collective-permute-start | bytes 3145736 | tf_op jit(solution)/shard_map/ppermute | solution.py:265
  207.7 10.6 %collective-permute-start.37 = (bf16[512,1024]{1,0:T(8,128)(2,1)S(1)}, bf16[512,1024]{1,0:T(8,128)(2,1)}, u32[]{:S(2)}, u32[]{:S(2)}) collective-permute-start(bf16[512,1024]{1,0:T(8,128)(2,1)S(1)} %fusion.19.rows_ref.refs_0_), channel_id=1, source_target_pairs={{0,2},{2,0},{4,6},{6,4},{8,10},{10,8},{12,14},{14,12},{16,18},{18,... | collective-permute-start | bytes 3145736 | tf_op jit(solution)/shard_map/ppermute | solution.py:265
  207.7 10.6 %collective-permute-start.38 = (bf16[512,512]{1,0:T(8,128)(2,1)}, bf16[512,512]{1,0:T(8,128)(2,1)}, u32[]{:S(2)}, u32[]{:S(2)}) collective-permute-start(bf16[512,512]{1,0:T(8,128)(2,1)} %pad_maximum_fusion.13), channel_id=1, source_target_pairs={{0,2},{2,0},{4,6},{6,4},{8,10},{10,8},{12,14},{14,12},{16,18},{18,... | collective-permute-start | bytes 1572872 | tf_op jit(solution)/shard_map/ppermute | solution.py:265
  218.4 27.1 %collective-permute-start.39 = (bf16[512,1024]{1,0:T(8,128)(2,1)S(1)}, bf16[512,1024]{1,0:T(8,128)(2,1)}, u32[]{:S(2)}, u32[]{:S(2)}) collective-permute-start(bf16[512,1024]{1,0:T(8,128)(2,1)S(1)} %get-tuple-element.277), channel_id=1, source_target_pairs={{0,1},{1,0},{2,3},{3,2},{4,5},{5,4},{6,7},{7,6},{8,9},{9,8},{10,11... | collective-permute-start | bytes 3145736 | tf_op jit(solution)/shard_map/ppermute | solution.py:265
  219.0 30.5 %collective-permute-start.40 = (bf16[512,1024]{1,0:T(8,128)(2,1)S(1)}, bf16[512,1024]{1,0:T(8,128)(2,1)S(1)}, u32[]{:S(2)}, u32[]{:S(2)}) collective-permute-start(bf16[512,1024]{1,0:T(8,128)(2,1)S(1)} %get-tuple-element.279), channel_id=1, source_target_pairs={{0,4},{2,6},{4,0},{6,2},{8,12},{10,14},{12,8},{14,10},{16,20},{18,... | collective-permute-start | bytes 3145736 | tf_op jit(solution)/shard_map/ppermute | solution.py:265
  252.0 38.4 %collective-permute-start.42 = (bf16[768,1024]{1,0:T(8,128)(2,1)}, bf16[768,1024]{1,0:T(8,128)(2,1)}, u32[]{:S(2)}, u32[]{:S(2)}) collective-permute-start(bf16[768,1024]{1,0:T(8,128)(2,1)} %pad_maximum_fusion.5), channel_id=1, source_target_pairs={{0,1},{1,0},{2,3},{3,2},{4,5},{5,4},{6,7},{7,6},{8,9},{9,8},{10,11... | collective-permute-start | bytes 4718600 | tf_op jit(solution)/shard_map/ppermute | solution.py:265
  256.1 38.4 %collective-permute-start.41 = (bf16[768,1024]{1,0:T(8,128)(2,1)}, bf16[768,1024]{1,0:T(8,128)(2,1)}, u32[]{:S(2)}, u32[]{:S(2)}) collective-permute-start(bf16[768,1024]{1,0:T(8,128)(2,1)} %pad_maximum_fusion.4), channel_id=1, source_target_pairs={{0,4},{2,6},{4,0},{6,2},{8,12},{10,14},{12,8},{14,10},{16,20},{18,... | collective-permute-start | bytes 4718600 | tf_op jit(solution)/shard_map/ppermute | solution.py:265
  285.4 12.2 %collective-permute-start.43 = (bf16[512,1536]{1,0:T(8,128)(2,1)}, bf16[512,1536]{1,0:T(8,128)(2,1)}, u32[]{:S(2)}, u32[]{:S(2)}) collective-permute-start(bf16[512,1536]{1,0:T(8,128)(2,1)} %get-tuple-element.361), channel_id=1, source_target_pairs={{0,2},{2,0},{4,6},{6,4},{8,10},{10,8},{12,14},{14,12},{16,18},{18,... | collective-permute-start | bytes 4718600 | tf_op jit(solution)/shard_map/ppermute | solution.py:265
  289.9 7.7 %collective-permute-start.44 = (bf16[512,1024]{1,0:T(8,128)(2,1)}, bf16[512,1024]{1,0:T(8,128)(2,1)S(1)}, u32[]{:S(2)}, u32[]{:S(2)}) collective-permute-start(bf16[512,1024]{1,0:T(8,128)(2,1)} %copy-done.24), channel_id=1, source_target_pairs={{0,2},{2,0},{4,6},{6,4},{8,10},{10,8},{12,14},{14,12},{16,18},{18,... | collective-permute-start | bytes 3145736 | tf_op jit(solution)/shard_map/ppermute | solution.py:265
  315.2 13.9 %collective-permute-start.45 = (bf16[128,1024]{1,0:T(8,128)(2,1)}, bf16[128,1024]{1,0:T(8,128)(2,1)}, u32[]{:S(2)}, u32[]{:S(2)}) collective-permute-start(bf16[128,1024]{1,0:T(8,128)(2,1)} %pad_maximum_fusion.25), channel_id=1, source_target_pairs={{0,8},{2,10},{4,12},{6,14},{8,0},{10,2},{12,4},{14,6},{16,24},{18,... | collective-permute-start | bytes 786440 | tf_op jit(solution)/shard_map/ppermute | solution.py:265
  316.5 36.6 %collective-permute-start.49 = (bf16[768,1024]{1,0:T(8,128)(2,1)}, bf16[768,1024]{1,0:T(8,128)(2,1)}, u32[]{:S(2)}, u32[]{:S(2)}) collective-permute-start(bf16[768,1024]{1,0:T(8,128)(2,1)} %pad_maximum_fusion.7), channel_id=1, source_target_pairs={{0,1},{1,0},{2,3},{3,2},{4,5},{5,4},{6,7},{7,6},{8,9},{9,8},{10,11... | collective-permute-start | bytes 4718600 | tf_op jit(solution)/shard_map/ppermute | solution.py:265
  318.1 21.7 %collective-permute-start.46 = (bf16[128,1024]{1,0:T(8,128)(2,1)}, bf16[128,1024]{1,0:T(8,128)(2,1)}, u32[]{:S(2)}, u32[]{:S(2)}) collective-permute-start(bf16[128,1024]{1,0:T(8,128)(2,1)} %pad_maximum_fusion.26), channel_id=1, source_target_pairs={{0,16},{2,18},{4,20},{6,22},{8,24},{10,26},{12,28},{14,30},{16,0},... | collective-permute-start | bytes 786440 | tf_op jit(solution)/shard_map/ppermute | solution.py:265
  321.7 18.0 %collective-permute-start.47 = (bf16[128,1024]{1,0:T(8,128)(2,1)}, bf16[128,1024]{1,0:T(8,128)(2,1)}, u32[]{:S(2)}, u32[]{:S(2)}) collective-permute-start(bf16[128,1024]{1,0:T(8,128)(2,1)} %pad_maximum_fusion.27), channel_id=1, source_target_pairs={{0,24},{2,26},{4,28},{6,30},{8,16},{10,18},{12,20},{14,22},{16,8},... | collective-permute-start | bytes 786440 | tf_op jit(solution)/shard_map/ppermute | solution.py:265
  324.5 35.6 %collective-permute-start.48 = (bf16[768,1024]{1,0:T(8,128)(2,1)}, bf16[768,1024]{1,0:T(8,128)(2,1)}, u32[]{:S(2)}, u32[]{:S(2)}) collective-permute-start(bf16[768,1024]{1,0:T(8,128)(2,1)} %pad_maximum_fusion.6), channel_id=1, source_target_pairs={{0,4},{2,6},{4,0},{6,2},{8,12},{10,14},{12,8},{14,10},{16,20},{18,... | collective-permute-start | bytes 4718600 | tf_op jit(solution)/shard_map/ppermute | solution.py:265
  362.3 10.8 %collective-permute-start.50 = (bf16[128,1024]{1,0:T(8,128)(2,1)S(1)}, bf16[128,1024]{1,0:T(8,128)(2,1)S(1)}, u32[]{:S(2)}, u32[]{:S(2)}) collective-permute-start(bf16[128,1024]{1,0:T(8,128)(2,1)S(1)} %pad_maximum_fusion.28), channel_id=1, source_target_pairs={{0,8},{2,10},{4,12},{6,14},{8,0},{10,2},{12,4},{14,6},{16,24},{18,... | collective-permute-start | bytes 786440 | tf_op jit(solution)/shard_map/ppermute | solution.py:265
  362.4 21.2 %collective-permute-start.51 = (bf16[128,1024]{1,0:T(8,128)(2,1)S(1)}, bf16[128,1024]{1,0:T(8,128)(2,1)S(1)}, u32[]{:S(2)}, u32[]{:S(2)}) collective-permute-start(bf16[128,1024]{1,0:T(8,128)(2,1)S(1)} %pad_maximum_fusion.29), channel_id=1, source_target_pairs={{0,16},{2,18},{4,20},{6,22},{8,24},{10,26},{12,28},{14,30},{16,0},... | collective-permute-start | bytes 786440 | tf_op jit(solution)/shard_map/ppermute | solution.py:265
  365.4 18.2 %collective-permute-start.52 = (bf16[128,1024]{1,0:T(8,128)(2,1)S(1)}, bf16[128,1024]{1,0:T(8,128)(2,1)S(1)}, u32[]{:S(2)}, u32[]{:S(2)}) collective-permute-start(bf16[128,1024]{1,0:T(8,128)(2,1)S(1)} %pad_maximum_fusion.30), channel_id=1, source_target_pairs={{0,24},{2,26},{4,28},{6,30},{8,16},{10,18},{12,20},{14,22},{16,8},... | collective-permute-start | bytes 786440 | tf_op jit(solution)/shard_map/ppermute | solution.py:265
  366.9 16.9 %collective-permute-start.53 = (bf16[256,1024]{1,0:T(8,128)(2,1)S(1)}, bf16[256,1024]{1,0:T(8,128)(2,1)S(1)}, u32[]{:S(2)}, u32[]{:S(2)}) collective-permute-start(bf16[256,1024]{1,0:T(8,128)(2,1)S(1)} %pad_maximum_fusion.19), channel_id=1, source_target_pairs={{0,4},{2,6},{4,0},{6,2},{8,12},{10,14},{12,8},{14,10},{16,20},{18,... | collective-permute-start | bytes 1572872 | tf_op jit(solution)/shard_map/ppermute | solution.py:265
  368.2 15.8 %collective-permute-start.54 = (bf16[256,1024]{1,0:T(8,128)(2,1)S(1)}, bf16[256,1024]{1,0:T(8,128)(2,1)S(1)}, u32[]{:S(2)}, u32[]{:S(2)}) collective-permute-start(bf16[256,1024]{1,0:T(8,128)(2,1)S(1)} %get-tuple-element.325), channel_id=1, source_target_pairs={{0,1},{1,0},{2,3},{3,2},{4,5},{5,4},{6,7},{7,6},{8,9},{9,8},{10,11... | collective-permute-start | bytes 1572872 | tf_op jit(solution)/shard_map/ppermute | solution.py:265
  384.3 6.2 %collective-permute-start.58 = (f32[12,1024]{1,0:T(8,128)S(1)}, f32[12,1024]{1,0:T(8,128)S(1)}, u32[]{:S(2)}, u32[]{:S(2)}) collective-permute-start(f32[12,1024]{1,0:T(8,128)S(1)} %pad_maximum_fusion.38), channel_id=1, source_target_pairs={{0,2},{2,0},{4,6},{6,4},{8,10},{10,8},{12,14},{14,12},{16,18},{18,... | collective-permute-start | bytes 147464 | tf_op jit(solution)/shard_map/ppermute | solution.py:265
  384.4 15.6 %collective-permute-start.55 = (bf16[128,1024]{1,0:T(8,128)(2,1)S(1)}, bf16[128,1024]{1,0:T(8,128)(2,1)S(1)}, u32[]{:S(2)}, u32[]{:S(2)}) collective-permute-start(bf16[128,1024]{1,0:T(8,128)(2,1)S(1)} %pad_maximum_fusion.31), channel_id=1, source_target_pairs={{0,8},{2,10},{4,12},{6,14},{8,0},{10,2},{12,4},{14,6},{16,24},{18,... | collective-permute-start | bytes 786440 | tf_op jit(solution)/shard_map/ppermute | solution.py:265
  387.9 21.4 %collective-permute-start.56 = (bf16[128,1024]{1,0:T(8,128)(2,1)S(1)}, bf16[128,1024]{1,0:T(8,128)(2,1)S(1)}, u32[]{:S(2)}, u32[]{:S(2)}) collective-permute-start(bf16[128,1024]{1,0:T(8,128)(2,1)S(1)} %pad_maximum_fusion.32), channel_id=1, source_target_pairs={{0,16},{2,18},{4,20},{6,22},{8,24},{10,26},{12,28},{14,30},{16,0},... | collective-permute-start | bytes 786440 | tf_op jit(solution)/shard_map/ppermute | solution.py:265
  388.9 20.4 %collective-permute-start.57 = (bf16[128,1024]{1,0:T(8,128)(2,1)S(1)}, bf16[128,1024]{1,0:T(8,128)(2,1)S(1)}, u32[]{:S(2)}, u32[]{:S(2)}) collective-permute-start(bf16[128,1024]{1,0:T(8,128)(2,1)S(1)} %pad_maximum_fusion.33), channel_id=1, source_target_pairs={{0,24},{2,26},{4,28},{6,30},{8,16},{10,18},{12,20},{14,22},{16,8},... | collective-permute-start | bytes 786440 | tf_op jit(solution)/shard_map/ppermute | solution.py:265
  394.8 4.3 %collective-permute-start.60 = (f32[12,1024]{1,0:T(8,128)S(1)}, f32[12,1024]{1,0:T(8,128)S(1)}, u32[]{:S(2)}, u32[]{:S(2)}) collective-permute-start(f32[12,1024]{1,0:T(8,128)S(1)} %add.515), channel_id=1, source_target_pairs={{0,1},{1,0},{2,3},{3,2},{4,5},{5,4},{6,7},{7,6},{8,9},{9,8},{10,11... | collective-permute-start | bytes 147464 | tf_op jit(solution)/shard_map/ppermute | solution.py:265
  409.5 10.6 %collective-permute-start.64 = (f32[12,1024]{1,0:T(8,128)S(1)}, f32[12,1024]{1,0:T(8,128)S(1)}, u32[]{:S(2)}, u32[]{:S(2)}) collective-permute-start(f32[12,1024]{1,0:T(8,128)S(1)} %add.516), channel_id=1, source_target_pairs={{0,24},{2,26},{4,28},{6,30},{8,16},{10,18},{12,20},{14,22},{16,8},... | collective-permute-start | bytes 147464 | tf_op jit(solution)/shard_map/ppermute | solution.py:265
  411.9 8.9 %collective-permute-start.63 = (f32[12,1024]{1,0:T(8,128)S(1)}, f32[12,1024]{1,0:T(8,128)S(1)}, u32[]{:S(2)}, u32[]{:S(2)}) collective-permute-start(f32[12,1024]{1,0:T(8,128)S(1)} %add.516), channel_id=1, source_target_pairs={{0,16},{2,18},{4,20},{6,22},{8,24},{10,26},{12,28},{14,30},{16,0},... | collective-permute-start | bytes 147464 | tf_op jit(solution)/shard_map/ppermute | solution.py:265
  417.2 4.3 %collective-permute-start.62 = (f32[12,1024]{1,0:T(8,128)S(1)}, f32[12,1024]{1,0:T(8,128)S(1)}, u32[]{:S(2)}, u32[]{:S(2)}) collective-permute-start(f32[12,1024]{1,0:T(8,128)S(1)} %add.516), channel_id=1, source_target_pairs={{0,8},{2,10},{4,12},{6,14},{8,0},{10,2},{12,4},{14,6},{16,24},{18,... | collective-permute-start | bytes 147464 | tf_op jit(solution)/shard_map/ppermute | solution.py:265
  417.3 6.1 %collective-permute-start.61 = (f32[64,3072]{1,0:T(8,128)S(1)}, f32[64,3072]{1,0:T(8,128)S(1)}, u32[]{:S(2)}, u32[]{:S(2)}) collective-permute-start(f32[64,3072]{1,0:T(8,128)S(1)} %maximum_maximum_fusion), channel_id=1, source_target_pairs={{0,2},{2,0},{4,6},{6,4},{8,10},{10,8},{12,14},{14,12},{16,18},{18,... | collective-permute-start | bytes 2359304 | tf_op jit(solution)/shard_map/ppermute | solution.py:265
  (115 other events, 1105.2 us)

commit v3 on v2

--- a/solution.py
+++ b/solution.py
@@ -411,7 +411,9 @@
     return jnp.where(same_doc, raw_scores, -1000000000.0)
 
 
-def attend_forward_kernel(q_ref, k_ref, v_ref, column_ref, row_ref, ctx_ref, logsum_ref):
+def attend_forward_kernel(
+    core_ref, q_ref, k_ref, v_ref, column_ref, row_ref, own_ref, send_ref, logsum_ref
+):
     lane = lax.broadcasted_iota(jnp.int32, q_ref.shape, 1) // HEAD_DIM
     same_doc = column_ref[...] == row_ref[...]
     value_rows = v_ref[...]
@@ -426,12 +428,33 @@
         probabilities = (exponent * (1.0 / row_total)).astype(jnp.bfloat16)
         contexts.append(matmul(probabilities, value_rows))
         logsums.append(row_max + jnp.log(row_total))
-    ctx_ref[...] = jnp.where(lane == 0, contexts[0], contexts[1]).astype(jnp.bfloat16)
+    context = jnp.where(lane == 0, contexts[0], contexts[1]).astype(jnp.bfloat16)
+    own = pl.program_id(1) < pl.num_programs(1) // 2
+
+    @pl.when(own)
+    def _():
+        own_ref[...] = context
+
+    @pl.when(jnp.logical_not(own))
+    def _():
+        send_ref[...] = context
+
     logsum_ref[...] = jnp.where(lane == 0, logsums[0], logsums[1])
 
 
 def attend_backward_kernel(
-    q_ref, k_ref, v_ref, column_ref, row_ref, logsum_ref, dctx_ref, out_ref
+    core_ref,
+    q_ref,
+    k_ref,
+    v_ref,
+    column_ref,
+    row_ref,
+    logsum_ref,
+    dctx_ref,
+    own_ref,
+    send_ref,
+    own_sum_ref,
+    send_sum_ref,
 ):
     lane = lax.broadcasted_iota(jnp.int32, q_ref.shape, 1) // HEAD_DIM
     same_doc = column_ref[...] == row_ref[...]
@@ -454,132 +477,229 @@
                 inner_rows(probabilities.astype(jnp.bfloat16), d_context),
             )
         )
-    pairs = pl.num_programs(1)
-    first = pl.program_id(0) * 3 * pairs + pl.program_id(1)
+    half = pl.num_programs(1) // 2
+    at = pl.program_id(1)
+    own = at < half
+    first = pl.program_id(0) * 3 * half + jnp.where(own, at, at - half)
     for part, (left, right) in enumerate(zip(*results)):
-        place = pl.multiple_of((first + part * pairs) * 128, 128)
-        out_ref[:, pl.ds(place, 128)] = jnp.where(lane == 0, left, right).astype(jnp.bfloat16)
-
-
-def kernel_options():
+        place = pl.ds(pl.multiple_of((first + part * half) * 128, 128), 128)
+        gradient = jnp.where(lane == 0, left, right).astype(jnp.bfloat16)
+
+        total = jnp.sum(gradient.astype(jnp.float32), axis=0, keepdims=True)
+
+        @pl.when(own)
+        def _():
+            own_ref[:, place] = gradient
+            own_sum_ref[:, place] = total
+
+        @pl.when(jnp.logical_not(own))
+        def _():
+            send_ref[:, place] = gradient
+            send_sum_ref[:, place] = total
+
+
+def kernel_options(mebibytes):
     return dict(
         cost_estimate=pl.CostEstimate(flops=0, bytes_accessed=0, transcendentals=0),
-        compiler_params=pltpu.CompilerParams(vmem_limit_bytes=32 << 20),
-    )
+        compiler_params=pltpu.CompilerParams(vmem_limit_bytes=mebibytes << 20),
+    )
+
+
+def call_kernel(
+    kernel, core, mebibytes, grid, in_specs, out_specs, out_shape, operands, scratch_shapes=()
+):
+    return pl.pallas_call(
+        kernel,
+        grid_spec=pltpu.PrefetchScalarGridSpec(
+            num_scalar_prefetch=1,
+            grid=grid,
+            in_specs=in_specs,
+            out_specs=out_specs,
+            scratch_shapes=scratch_shapes,
+        ),
+        out_shape=out_shape,
+        **kernel_options(mebibytes),
+    )(core, *operands)
 
 
 def attention_inputs(rows, pairs, column, row):
     def place(part):
-        return lambda group, pair: (0, group * 3 * pairs + part * pairs + pair)
-
-    whole = lambda group, pair: (0, 0)
+        return lambda group, at, core: (
+            0,
+            group * 3 * pairs + part * pairs + (at ^ (core[0] * (pairs // 2))),
+        )
+
+    whole = lambda group, at, core: (0, 0)
     return [pl.BlockSpec((rows, 128), place(part)) for part in range(3)] + [
         pl.BlockSpec(column.shape, whole),
         pl.BlockSpec(row.shape, whole),
     ]
 
 
-def attend_rows_forward(qkv, column, row):
+def attend_rows_forward(core, qkv, column, row):
     rows, pairs = qkv.shape[0], qkv.shape[1] // 768
-    own = pl.BlockSpec((rows, 128), lambda group, pair: (0, group * pairs + pair))
-    return pl.pallas_call(
+    half = pairs // 2
+    own = pl.BlockSpec((rows, 128), lambda group, at, core: (0, group * half + jnp.minimum(at, half - 1)))
+    send = pl.BlockSpec((rows, 128), lambda group, at, core: (0, group * half + jnp.maximum(at - half, 0)))
+    flat = pl.BlockSpec((rows, 128), lambda group, at, core: (0, group * pairs + at))
+    pair_shape = jax.ShapeDtypeStruct((rows, pairs * 128), jnp.bfloat16)
+    own, send, logsum = call_kernel(
         attend_forward_kernel,
-        grid=(2, pairs),
-        in_specs=attention_inputs(rows, pairs, column, row),
-        out_specs=[own, own],
-        out_shape=[
-            jax.ShapeDtypeStruct((rows, pairs * 256), jnp.bfloat16),
-            jax.ShapeDtypeStruct((rows, pairs * 256), jnp.float32),
-        ],
-        **kernel_options(),
-    )(qkv, qkv, qkv, column, row)
-
-
-def attend_rows_backward(qkv, column, row, logsum, d_context):
+        core,
+        16,
+        (2, pairs),
+        attention_inputs(rows, pairs, column, row),
+        [own, send, flat],
+        [pair_shape, pair_shape, jax.ShapeDtypeStruct((rows, pairs * 256), jnp.float32)],
+        (qkv, qkv, qkv, column, row),
+    )
+    return (own, send), logsum
+
+
+def attend_rows_backward(core, qkv, column, row, logsum, d_context):
     rows, pairs = qkv.shape[0], qkv.shape[1] // 768
-    own = pl.BlockSpec((rows, 128), lambda group, pair: (0, group * pairs + pair))
-    return pl.pallas_call(
+    flat = pl.BlockSpec((rows, 128), lambda group, at, core: (0, group * pairs + at))
+    pair_spec = pl.BlockSpec((rows, qkv.shape[1] // 2), lambda group, at, core: (0, 0))
+    pair_shape = jax.ShapeDtypeStruct((rows, qkv.shape[1] // 2), jnp.bfloat16)
+    sum_spec = pl.BlockSpec((1, qkv.shape[1] // 2), lambda group, at, core: (0, 0))
+    sum_shape = jax.ShapeDtypeStruct((1, qkv.shape[1] // 2), jnp.float32)
+    own, send, own_sum, send_sum = call_kernel(
         attend_backward_kernel,
-        grid=(2, pairs),
-        in_specs=attention_inputs(rows, pairs, column, row) + [own, own],
-        out_specs=pl.BlockSpec(qkv.shape, lambda group, pair: (0, 0)),
-        out_shape=jax.ShapeDtypeStruct(qkv.shape, jnp.bfloat16),
-        **kernel_options(),
-    )(qkv, qkv, qkv, column, row, logsum, d_context)
-
-
-def weight_specs(weight, start, steps, step):
+        core,
+        20,
+        (2, pairs),
+        attention_inputs(rows, pairs, column, row) + [flat, flat],
+        [pair_spec, pair_spec, sum_spec, sum_spec],
+        [pair_shape, pair_shape, sum_shape, sum_shape],
+        (qkv, qkv, qkv, column, row, logsum, d_context),
+    )
+    return (own, send), (own_sum, send_sum)
+
+
+def weight_specs(weight, start, parts, step):
     rows = weight[0].shape[0]
-    first = start // step
-    left = pl.BlockSpec((rows, step), lambda group, at: (0, first + jnp.where(group == 0, at, steps - 1)))
-    other = pl.BlockSpec((rows, step), lambda group, at: (0, first + jnp.where(group == 1, at, 0)))
-    right = pl.BlockSpec((rows // 2, step), lambda group, at: (group, first + at))
+    first, last = start // step, 2 * parts - 1
+
+    def column(at, core):
+        return first + (at ^ core[0])
+
+    left = pl.BlockSpec(
+        (rows, step), lambda group, at, core: (0, column(jnp.where(group == 0, at, last), core))
+    )
+    other = pl.BlockSpec(
+        (rows, step), lambda group, at, core: (0, column(jnp.where(group == 1, at, 0), core))
+    )
+    right = pl.BlockSpec((rows // 2, step), lambda group, at, core: (group, column(at, core)))
     return [left, other, right, right] * 2
 
 
-def with_block(refs, use):
+def load_block(refs, block_ref):
     for group in (0, 1):
 
         @pl.when(pl.program_id(0) == group)
         def _():
-            parts = (refs[group], refs[2], refs[3], refs[4 + group], refs[6], refs[7])
-            use(jnp.concatenate([part[...] for part in parts], axis=0))
-
-
-def expand_rows(rows, weight, start, width, step, finish, extras, out_types):
-    count = len(weight)
-
-    def kernel(rows_ref, *refs):
-        def use(block):
-            total = matmul(rows_ref[...], block)
-            results = finish(total, *[ref[...] for ref in refs[count : count + len(extras)]])
-            for ref, result in zip(refs[count + len(extras) :], results):
-                ref[...] = result
-
-        with_block(refs[:count], use)
-
-    steps = width // step
-
-    def own(height):
-        return pl.BlockSpec((height, step), lambda group, at: (0, group * steps + at))
-
-    return pl.pallas_call(
+            start = 0
+            for part in (refs[group], refs[2], refs[3], refs[4 + group], refs[6], refs[7]):
+                block_ref[start : start + part.shape[0], :] = part[...]
+                start += part.shape[0]
+
+
+def pair_specs(height, parts, step):
+    return [pl.BlockSpec((height, step), lambda group, at, core: (0, group * parts + at // 2))] * 2
+
+
+def expand_rows(core, rows, weight, start, width, parts, finish, extras, out_types):
+    step = width // (2 * parts)
+    in_specs = [pl.BlockSpec(rows.shape, lambda group, at, core: (0, 0))]
+    in_specs += weight_specs(weight, start, parts, step)
+    operands = [rows, *weight]
+    for extra in extras:
+        if isinstance(extra, tuple):
+            in_specs += pair_specs(extra[0].shape[0], parts, step)
+            operands += extra
+        else:
+            in_specs.append(
+                pl.BlockSpec((1, step), lambda group, at, core: (0, group * 2 * parts + (at ^ core[0])))
+            )
+            operands.append(extra)
+    out_specs, out_shape = [], []
+    for height, kind, paired in out_types:
+        if paired:
+            out_specs += pair_specs(height, parts, step)
+            out_shape += [jax.ShapeDtypeStruct((height, width), kind)] * 2
+        else:
+            out_specs.append(
+                pl.BlockSpec((height, step), lambda group, at, core: (0, group * 2 * parts + at))
+            )
+            out_shape.append(jax.ShapeDtypeStruct((height, 2 * width), kind))
+
+    def kernel(core_ref, rows_ref, *refs):
+        block_ref = refs[-1]
+        load_block(refs[:8], block_ref)
+        total = matmul(rows_ref[...], block_ref[...])
+        side = pl.program_id(1) % 2
+        place = 8
+        values = []
+        for extra in extras:
+            if isinstance(extra, tuple):
+                values.append(jnp.where(side == 0, refs[place][...], refs[place + 1][...]))
+                place += 2
+            else:
+                values.append(refs[place][...])
+                place += 1
+        for (_, _, paired), result in zip(out_types, finish(total, *values)):
+            if paired:
+                for index in (0, 1):
+
+                    @pl.when(side == index)
+                    def _():
+                        refs[place + index][...] = result
+
+                place += 2
+            else:
+                refs[place][...] = result
+                place += 1
+
+    return call_kernel(
         kernel,
-        grid=(2, steps),
-        in_specs=[pl.BlockSpec(rows.shape, lambda group, at: (0, 0))]
-        + weight_specs(weight, start, steps, step)
-        + [own(extra.shape[0]) for extra in extras],
-        out_specs=[own(height) for height, _ in out_types],
-        out_shape=[jax.ShapeDtypeStruct((height, 2 * width), kind) for height, kind in out_types],
-        **kernel_options(),
-    )(rows, *weight, *extras)
-
-
-def contract_rows(rows, weight, start, width, step):
-    steps = width // step
-    shape = (rows.shape[0], 4 * weight[0].shape[0])
-
-    def kernel(rows_ref, *refs):
-        out_ref = refs[-1]
+        core,
+        24,
+        (2, 2 * parts),
+        in_specs,
+        out_specs,
+        out_shape,
+        operands,
+        [pltpu.VMEM((rows.shape[1], step), jnp.bfloat16)],
+    )
+
+
+def contract_rows(core, pair, weight, start, width, parts):
+    step = width // (2 * parts)
+    height = pair[0].shape[0]
+    shape = (height, 4 * weight[0].shape[0])
+
+    def kernel(core_ref, own_ref, send_ref, *refs):
+        out_ref, block_ref = refs[-2:]
 
         @pl.when((pl.program_id(0) == 0) & (pl.program_id(1) == 0))
         def _():
             out_ref[...] = jnp.zeros_like(out_ref)
 
-        def use(block):
-            out_ref[...] += outer_cols(rows_ref[...], block)
-
-        with_block(refs[:-1], use)
-
-    return pl.pallas_call(
+        load_block(refs[:8], block_ref)
+        rows = jnp.where(pl.program_id(1) % 2 == 0, own_ref[...], send_ref[...])
+        out_ref[...] += outer_cols(rows, block_ref[...])
+
+    return call_kernel(
         kernel,
-        grid=(2, steps),
-        in_specs=[pl.BlockSpec((rows.shape[0], step), lambda group, at: (0, group * steps + at))]
-        + weight_specs(weight, start, steps, step),
-        out_specs=pl.BlockSpec(shape, lambda group, at: (0, 0)),
-        out_shape=jax.ShapeDtypeStruct(shape, jnp.float32),
-        **kernel_options(),
-    )(rows, *weight)
+        core,
+        20,
+        (2, 2 * parts),
+        pair_specs(height, parts, step) + weight_specs(weight, start, parts, step),
+        pl.BlockSpec(shape, lambda group, at, core: (0, 0)),
+        jax.ShapeDtypeStruct(shape, jnp.float32),
+        (*pair, *weight),
+        [pltpu.VMEM((shape[1], step), jnp.bfloat16)],
+    )
 
 
 def grad_parts(terms):
@@ -628,7 +748,7 @@
         in_specs=in_specs,
         out_specs=[y_spec, y_spec, x_spec, x_spec],
         out_shape=[jax.ShapeDtypeStruct((half, total_width), jnp.bfloat16)] * 4,
-        **kernel_options(),
+        **kernel_options(24),
     )(*[array for term in terms for array in term])
 
 
@@ -706,37 +826,52 @@
     )[None]
     units_bias = jnp.concatenate([group_of(bias_up, group, unit_width) for group in groups])[None]
 
+    core_index = dp_index % 2
+    core = core_index.astype(jnp.int32).reshape(1)
+
+    def ordered(own, send):
+        return jnp.where(
+            core_index == 0,
+            jnp.concatenate([own, send], axis=-1),
+            jnp.concatenate([send, own], axis=-1),
+        )
+
     def attention_work(weight):
         (qkv,) = expand_rows(
+            jnp.zeros_like(core),
             own_rows,
             weight,
             0,
             3 * head_width,
-            3 * head_width // 2,
+            1,
             lambda total, bias: ((total + bias).astype(low),),
             [qkv_bias],
-            [(rows, low)],
+            [(rows, low, False)],
         )
-        context, logsum = attend_rows_forward(qkv, column, row)
+        context, logsum = attend_rows_forward(core, qkv, column, row)
         return dict(qkv=qkv, context=context, logsum=logsum)
 
     def units_work(weight, results):
-        attn_rows = contract_rows(results["context"], weight, unit_width, head_width, head_width)
+        attn_rows = contract_rows(core, results["context"], weight, unit_width, head_width, 1)
         z_one = own_rows.astype(wide) + attn_rows + bias_out
         h_one, scaled_one, spread_one = norm_forward(z_one, ln1_gain, ln1_bias)
         h_low = h_one.astype(low)
-        activation, slope = expand_rows(
+        act_own, act_send, slope_own, slope_send = expand_rows(
+            core,
             h_low,
             weight,
             0,
             unit_width,
-            unit_width // 4,
+            1,
             lambda total, bias: gelu_pair(total + bias),
             [units_bias],
-            [(rows, low), (rows, low)],
+            [(rows, low, True), (rows, low, True)],
         )
         return results | dict(
-            norm=(h_one, scaled_one, spread_one), h_low=h_low, activation=activation, slope=slope
+            norm=(h_one, scaled_one, spread_one),
+            h_low=h_low,
+            activation=(act_own, act_send),
+            slope=(slope_own, slope_send),
         )
 
     (qkv_w, up_out_w, down_w), made = gather_weights(
@@ -751,119 +886,120 @@
     qkv, context, logsum = made["qkv"], made["context"], made["logsum"]
     h_one, scaled_one, spread_one = made["norm"]
     h_low, activation, slope = made["h_low"], made["activation"], made["slope"]
-    mlp_rows = contract_rows(activation, down_w, 0, unit_width, unit_width // 2)
+    mlp_rows = contract_rows(core, activation, down_w, 0, unit_width, 1)
     z_two = h_one + mlp_rows + bias_down
     normed, scaled_two, spread_two = norm_forward(z_two, ln2_gain, ln2_bias)
-    output = outer_cols(normed.astype(low), order).astype(low)
+    output_low = normed.astype(low)
 
     grad_two, d_gain_two, d_offset_two = norm_backward(cotangent, scaled_two, spread_two, ln2_gain)
     d_bias_down = jnp.sum(grad_two, axis=0)
     grad_two_low = grad_two.astype(low)
 
     after = lax.optimization_barrier
-    core_index = dp_index % 2
-
-    def core_halves(units, parts):
-        size = units.shape[1] // (4 * parts)
-        return [
-            jnp.concatenate(
-                [
-                    lax.dynamic_slice_in_dim(units, 2 * size * at + core * size, size, axis=1)
-                    for at in range(2 * parts)
-                ],
-                axis=1,
-            )
-            for core in (core_index, 1 - core_index)
-        ]
-
-    act_own, act_send = core_halves(activation, 1)
-    grad_two_low, slope, act_own, act_send = after((grad_two_low, slope, act_own, act_send))
-    grad_two_other, act_other = over_core(grad_two_low), over_core(act_send)
+    grad_two_low, slope, activation = after((grad_two_low, slope, activation))
+    grad_two_other, act_other = over_core(grad_two_low), over_core(activation[1])
 
     def finish_units(total, slope):
         units = (total * slope.astype(wide)).astype(low)
         return units, jnp.sum(units.astype(wide), axis=0, keepdims=True)
 
-    d_up, d_bias_units = expand_rows(
+    *d_up, d_bias_units = expand_rows(
+        core,
         grad_two_low,
         down_w,
         0,
         unit_width,
-        unit_width // 2,
+        1,
         finish_units,
         [slope],
-        [(rows, low), (1, wide)],
-    )
-    up_own, up_send = core_halves(d_up, 1)
-    context_own, context_send = core_halves(context, 1)
-    (grad_two_other, act_other, d_up, up_own, up_send, h_low, own_rows, context_own, context_send) = after(
-        (grad_two_other, act_other, d_up, up_own, up_send, h_low, own_rows, context_own, context_send)
-    )
-    up_other, h_other = over_core(up_send), over_core(h_low)
-    rows_other, context_other = over_core(own_rows), over_core(context_send)
-    down_sum = grad_parts([(grad_two_low, grad_two_other, act_own, act_other)])
+        [(rows, low, True), (1, wide, False)],
+    )
+    (grad_two_other, act_other, d_up, h_low, own_rows, context) = after(
+        (grad_two_other, act_other, d_up, h_low, own_rows, context)
+    )
+    up_other, h_other = over_core(d_up[1]), over_core(h_low)
+    rows_other, context_other = over_core(own_rows), over_core(context[1])
+    down_sum = grad_parts([(grad_two_low, grad_two_other, activation[0], act_other)])
     down_sum, up_other, h_other, rows_other, context_other, d_up = after(
         (down_sum, up_other, h_other, rows_other, context_other, d_up)
     )
     down_sum = scatter_first(down_sum)
-    mlp_back = contract_rows(d_up, up_out_w, 0, unit_width, unit_width // 2)
+    mlp_back = contract_rows(core, d_up, up_out_w, 0, unit_width, 1)
     grad_one, d_gain_one, d_offset_one = norm_backward(
         mlp_back + grad_two, scaled_one, spread_one, ln1_gain
     )
     d_bias_out = jnp.sum(grad_one, axis=0)
     grad_one_low = grad_one.astype(low)
-    up_sum = grad_parts([(h_low, h_other, up_own, up_other)])
+    up_sum = grad_parts([(h_low, h_other, d_up[0], up_other)])
     (d_ctx,) = expand_rows(
+        core,
         grad_one_low,
         up_out_w,
         unit_width,
         head_width,
-        head_width,
+        1,
         lambda total: (total.astype(low),),
         [],
-        [(rows, low)],
+        [(rows, low, False)],
     )
     down_sum, up_sum, d_ctx, grad_one_low = after((down_sum, up_sum, d_ctx, grad_one_low))
     down_sum, up_sum = scatter_both(down_sum, up_sum)
     grad_one_other = over_core(grad_one_low)
-    d_qkv = attend_rows_backward(qkv, column, row, logsum, d_ctx)
-    qkv_own, qkv_send = core_halves(d_qkv, 3)
-    qkv_other = over_core(qkv_send)
+    d_qkv, qkv_sums = attend_rows_backward(core, qkv, column, row, logsum, d_ctx)
+    qkv_other = over_core(d_qkv[1])
     last_sum = grad_parts(
         [
-            (own_rows, rows_other, qkv_own, qkv_other),
-            (grad_one_low, grad_one_other, context_own, context_other),
+            (own_rows, rows_other, d_qkv[0], qkv_other),
+            (grad_one_low, grad_one_other, context[0], context_other),
         ]
     )
     down_sum, up_sum, last_sum, d_qkv = after((down_sum, up_sum, last_sum, d_qkv))
     up_sum, last_sum = scatter_both(up_sum, last_sum)
     down_sum = scatter_near(down_sum)
-    attn_back = contract_rows(d_qkv, qkv_w, 0, 3 * head_width, 3 * head_width // 2)
+    narrow = jnp.dot(
+        jnp.stack([d_bias_out, d_gain_one, d_offset_one, d_bias_down, d_gain_two, d_offset_two]),
+        order.astype(wide).T,
+        precision=lax.Precision.HIGHEST,
+    )
+    size = head_width // 2
+
+    def qkv_row(part):
+        return whole_of(
+            [
+                ordered(*[total[:, (3 * group + part) * size :][:, :size] for total in qkv_sums])
+                for group in groups
+            ]
+        )
+
+    def unit_rows():
+        half = unit_width // 2
+        pieces = [
+            [d_bias_units[:, (2 * group + side) * half :][:, :half] for side in (0, 1)] for group in groups
+        ]
+        pieces = [
+            [jnp.where(core_index == 0, own, send), jnp.where(core_index == 0, send, own)]
+            for own, send in pieces
+        ]
+        first, last = [jnp.concatenate(piece) for piece in pieces]
+        return [jnp.where(tensor_index == 0, first, last), jnp.where(tensor_index == 0, last, first)]
+
+    small = jnp.concatenate([narrow, qkv_row(0), qkv_row(2), *unit_rows()])
+    down_sum, up_sum, last_sum, d_qkv, output_low = after((down_sum, up_sum, last_sum, d_qkv, output_low))
+    up_sum = scatter_near(up_sum)
+    last_sum = scatter_second(last_sum)
+    attn_back = contract_rows(core, d_qkv, qkv_w, 0, 3 * head_width, 3)
     grad_rows = attn_back + grad_one
     upper = grad_rows.astype(low)
     lower = (grad_rows - upper.astype(wide)).astype(low)
     grad_tokens = outer_cols(upper, order) + outer_cols(lower, order)
-    d_bias_up = whole_of([d_bias_units[0, :unit_width], d_bias_units[0, unit_width:]])
-    sums = jnp.sum(d_qkv, axis=0, dtype=wide).reshape(2, 3, head_width)
-    d_bias_q = whole_of([sums[0, 0], sums[1, 0]])
-    d_bias_v = whole_of([sums[0, 2], sums[1, 2]])
-    narrow = jnp.dot(
-        jnp.stack([d_bias_out, d_gain_one, d_offset_one, d_bias_down, d_gain_two, d_offset_two]),
-        order.astype(wide).T,
-        precision=lax.Precision.HIGHEST,
-    )
-    small = jnp.concatenate(
-        [narrow, d_bias_q[None], d_bias_v[None], d_bias_up.reshape(-1, width)], axis=0
-    )
-    down_sum, up_sum, last_sum = after((down_sum, up_sum, last_sum))
-    up_sum = scatter_near(up_sum)
-    last_sum = scatter_second(last_sum)
-    up_sum, last_sum, small = after((up_sum, last_sum, small))
+    output = outer_cols(output_low, order).astype(low)
+    up_sum, last_sum, small, down_sum = after((up_sum, last_sum, small, down_sum))
     last_sum = scatter_near(last_sum)
     small = sum_chips(small)
-    last_sum, small = after((last_sum, small))
+    pairs = scatter_last([down_sum, up_sum], core_index)
+    last_sum, small, pairs = after((last_sum, small, pairs))
     small = sum_near(small)
-    pairs = scatter_last([down_sum, up_sum, last_sum], core_index)
+    pairs = pairs + scatter_last([last_sum], core_index)
     grad_w_down = jnp.concatenate(pairs[0], axis=1).T
     grad_w_up = jnp.concatenate(pairs[1], axis=1)
     size = head_width // 2

time: 432 us -> 392 us (0.907)
  local copies, waits for them, and re-layouts: 52.1 us -> 21.7 us
  other arithmetic: 49.8 us -> 34.5 us
  Pallas kernels: 107 us -> 114 us
    unnamed x246 -> x141, local copies, waits for them, and re-layouts: 40.1 us -> 15.1 us
    pallas_call x10, Pallas kernels: 82 us -> 93.8 us  [call_kernel(): pl.pallas_call(kernel, grid_spec=pltpu.PrefetchScalarGridSpec(num_scalar_...]
    concatenate x7 -> x1, other arithmetic: 7.7 us -> 0.02 us  [scatter_last(): jnp.concatenate([total[at:][:rows] for at in (core * rows, (core + 2) * r...]
    dynamic_slice x3 -> x0, local copies, waits for them, and re-layouts: 4.77 us -> none  [core_halves(): lax.dynamic_slice_in_dim(units, 2 * size * at + core * size, size, axis=1)]
    pallas_call x3, Pallas kernels: 24.8 us -> 20.3 us  [grad_parts(): pl.pallas_call(kernel, grid=(2,), in_specs=in_specs, out_specs=[y_spec, y...]
    ppermute x65 -> x66, waiting for transfers between devices: 140 us -> 136 us  [swap(): lax.ppermute(array, name, [(index, index ^ mask) for index in range(size)])]
    ppermute x65 -> x66, starting transfers between devices: 61 us -> 64.4 us  [swap(): lax.ppermute(array, name, [(index, index ^ mask) for index in range(size)])]
  transfers between devices with their start and end apart: 65 -> 66, of which waited for: 24 -> 28; matrix products, arithmetic and copies ran while one was open for 15% -> 10% of each run, Pallas kernels for 19% -> 25%
where the time goes in v3:
time: 392 us; the launch traced here: 387 us
  waiting for transfers between devices  136 us (35%)
  Pallas kernels  114 us (29%)
  starting transfers between devices  64.4 us (16%)
  other arithmetic  34.5 us (9%)
  local copies, waits for them, and re-layouts  21.7 us (6%)
  matrix products  13.7 us (3%)
    ppermute x66, waiting for transfers between devices, swap(): lax.ppermute(array, name, [(index, index ^ mask) for index in range(size)])  136 us
    pallas_call x10, Pallas kernels, call_kernel(): pl.pallas_call(kernel, grid_spec=pltpu.PrefetchScalarGridSpec(num_scalar_...  93.8 us
    ppermute x66, starting transfers between devices, swap(): lax.ppermute(array, name, [(index, index ^ mask) for index in range(size)])  64.4 us
    pallas_call x3, Pallas kernels, grad_parts(): pl.pallas_call(kernel, grid=(2,), in_specs=in_specs, out_specs=[y_spec, y...  20.3 us
    unnamed x141, local copies, waits for them, and re-layouts  15.1 us
    convert_element_type x10, other arithmetic, add_low(): (left.astype(jnp.float32) + right.astype(jnp.float32)).astype(jnp.bfloat16)  11.5 us
    concatenate x10, other arithmetic, beside(): return jnp.concatenate([left, right])  8.22 us
  transfers between devices with their start and end apart: 66, of which 28 were waited for; matrix products, arithmetic and copies ran while one was open for 10% of the time, Pallas kernels for 25%

profile of v3, /device:TPU:0, one launch (start us, length us, event | category | flops | bytes accessed | tf_op | source)
XLA Modules:
  0.0 387.3 jit_solution(17958219797186478893)
XLA Ops:
  1.8 3.1 collective-permute-start.3
  5.8 2.5 collective-permute-start.2
  8.5 1.7 collective-permute-start
  10.3 10.0 %collective-permute-done.2 = bf16[64,1536]{1,0:T(8,128)(2,1)S(1)} collective-permute-done((bf16[64,1536]{1,0:T(8,128)(2,1)S(1)}, bf16[64,1536]{1,0:T(8,128)(2,1)S(1)}, u32[]{:S(2)}, u32[]{:S(2)}) %collective-permute-start.2) | collective-permute-done | bytes 196640 | tf_op jit(solution)/shard_map/ppermute | solution.py:265
  20.2 5.5 %collective-permute-done.1 = bf16[64,1536]{1,0:T(8,128)(2,1)S(1)} collective-permute-done((bf16[64,1536]{1,0:T(8,128)(2,1)S(1)}, bf16[64,1536]{1,0:T(8,128)(2,1)S(1)}, u32[]{:S(2)}, u32[]{:S(2)}) %collective-permute-start.1) | collective-permute-done | bytes 196640 | tf_op jit(solution)/shard_map/ppermute | solution.py:265
  25.8 1.6 collective-permute-start.4
  27.4 1.6 collective-permute-start.5
  29.0 2.3 collective-permute-start.6
  31.3 1.5 collective-permute-start.7
  32.8 9.7 %collective-permute-done.7 = bf16[64,2048]{1,0:T(8,128)(2,1)} collective-permute-done((bf16[64,2048]{1,0:T(8,128)(2,1)S(1)}, bf16[64,2048]{1,0:T(8,128)(2,1)}, u32[]{:S(2)}, u32[]{:S(2)}) %collective-permute-start.7) | collective-permute-done | bytes 262176 | tf_op jit(solution)/shard_map/ppermute | solution.py:265
  42.5 2.5 collective-permute-done.6
  46.5 17.3 %collective-permute-done.12 = bf16[64,2560]{1,0:T(8,128)(2,1)S(1)} collective-permute-done((bf16[64,2560]{1,0:T(8,128)(2,1)S(1)}, bf16[64,2560]{1,0:T(8,128)(2,1)S(1)}, u32[]{:S(2)}, u32[]{:S(2)}) %collective-permute-start.12) | collective-permute-done | bytes 327712 | tf_op jit(solution)/shard_map/ppermute | solution.py:265
  70.8 13.4 %collective-permute-done.17 = bf16[64,2048]{1,0:T(8,128)(2,1)S(1)} collective-permute-done((bf16[64,2048]{1,0:T(8,128)(2,1)S(1)}, bf16[64,2048]{1,0:T(8,128)(2,1)S(1)}, u32[]{:S(2)}, u32[]{:S(2)}) %collective-permute-start.17) | collective-permute-done | bytes 262176 | tf_op jit(solution)/shard_map/ppermute | solution.py:265
  84.2 1.9 collective-permute-done.16
  93.6 6.6 %shard_map.254.q_ref.k_ref.v_ref = bf16[512,3072]{1,0:T(8,128)(2,1)S(1)} custom-call(s32[1]{0:T(128)} %constant.124.clone.1.core_ref, bf16[512,1024]{1,0:T(8,128)(2,1)S(1)} %fusion.19.rows_ref.refs_0_, bf16[256,1536]{1,0:T(8,128)(2,1)S(1)} %copy-done.7, bf16[256,1536]{1,0:T(8,128)(2,1)} %collective-permute-done.8.refs_1_, ...), custom_call_target="tpu_custom_call" | custom-call | tf_op jit(solution)/shard_map/pallas_call | solution.py:511
  100.2 13.4 %shard_map.255 = (bf16[512,512]{1,0:T(8,128)(2,1)S(1)}, bf16[512,512]{1,0:T(8,128)(2,1)S(1)}, f32[512,1024]{1,0:T(8,128)S(1)}) custom-call(s32[1]{0:T(128)} %bitcast.5.core_ref, bf16[512,3072]{1,0:T(8,128)(2,1)S(1)} %shard_map.254.q_ref.k_ref.v_ref, bf16[512,3072]{1,0:T(8,128)(2,1)S(1)} %shard_map.254.q_ref.k_ref.v_ref, ...), custom_call_target="tpu_custom_call" | custom-call | tf_op jit(solution)/shard_map/pallas_call | solution.py:511
  113.7 6.1 %collective-permute-done.19.refs_3_ = bf16[256,2560]{1,0:T(8,128)(2,1)S(1)} collective-permute-done((bf16[256,2560]{1,0:T(8,128)(2,1)S(1)}, bf16[256,2560]{1,0:T(8,128)(2,1)S(1)}, u32[]{:S(2)}, u32[]{:S(2)}) %collective-permute-start.19) | collective-permute-done | bytes 1310752 | tf_op jit(solution)/shard_map/ppermute | solution.py:265
  119.7 2.0 collective-permute-done.18.refs_1_
  127.6 9.8 %collective-permute-done.25 = bf16[128,2048]{1,0:T(8,128)(2,1)S(1)} collective-permute-done((bf16[128,2048]{1,0:T(8,128)(2,1)S(1)}, bf16[128,2048]{1,0:T(8,128)(2,1)S(1)}, u32[]{:S(2)}, u32[]{:S(2)}) %collective-permute-start.25) | collective-permute-done | bytes 524320 | tf_op jit(solution)/shard_map/ppermute | solution.py:265
  140.9 3.0 shard_map.256
  144.8 1.9 fusion.52
  146.7 12.0 %shard_map.257 = (bf16[512,2048]{1,0:T(8,128)(2,1)S(1)}, bf16[512,2048]{1,0:T(8,128)(2,1)}, bf16[512,2048]{1,0:T(8,128)(2,1)S(1)}, bf16[512,2048]{1,0:T(8,128)(2,1)S(1)}) custom-call(s32[1]{0:T(128)} %bitcast.5.core_ref, bf16[512,1024]{1,0:T(8,128)(2,1)S(1)} %get-tuple-element.305.rows_ref.refs_0_, ...), custom_call_target="tpu_custom_call" | custom-call | tf_op jit(solution)/shard_map/pallas_call | solution.py:511
  160.1 4.2 %collective-permute-done.28.refs_3_ = bf16[256,2048]{1,0:T(8,128)(2,1)S(1)} collective-permute-done((bf16[256,2048]{1,0:T(8,128)(2,1)S(1)}, bf16[256,2048]{1,0:T(8,128)(2,1)S(1)}, u32[]{:S(2)}, u32[]{:S(2)}) %collective-permute-start.28) | collective-permute-done | bytes 1048608 | tf_op jit(solution)/shard_map/ppermute | solution.py:265
  165.8 2.1 collective-permute-done.31.refs_5_
  167.9 1.5 collective-permute-done.32.refs_7_
  169.4 8.4 %shard_map.258 = f32[512,1024]{1,0:T(8,128)S(1)} custom-call(s32[1]{0:T(128)} %bitcast.5.core_ref, bf16[512,2048]{1,0:T(8,128)(2,1)S(1)} %get-tuple-element.298.own_ref.refs_2_, bf16[512,2048]{1,0:T(8,128)(2,1)} %get-tuple-element.289.send_ref, bf16[256,2048]{1,0:T(8,128)(2,1)S(1)} %constant_dynamic-update-slice_fusion.9.refs_0_, ...), custom_call_target="tpu_custom_call" | custom-call | tf_op jit(solution)/shard_map/pallas_call | solution.py:511
  178.5 2.8 fusion.7
  184.4 8.0 %shard_map.259 = (bf16[512,2048]{1,0:T(8,128)(2,1)S(1)}, bf16[512,2048]{1,0:T(8,128)(2,1)S(1)}, f32[1,4096]{1,0:T(1,128)S(1)}) custom-call(s32[1]{0:T(128)} %bitcast.5.core_ref, bf16[512,1024]{1,0:T(8,128)(2,1)S(1)} %convert_element_type.291.rows_ref.refs_0_, bf16[256,2048]{1,0:T(8,128)(2,1)S(1)} %constant_dynamic-update-slice_fusion.9.refs_0_, ...), custom_call_target="tpu_custom_call" | custom-call | tf_op jit(solution)/shard_map/pallas_call | solution.py:511
  194.7 1.6 copy-done.22
  196.3 5.8 %shard_map.260 = (bf16[512,1024]{1,0:T(8,128)(2,1)S(1)}, bf16[512,1024]{1,0:T(8,128)(2,1)S(1)}, bf16[512,1024]{1,0:T(8,128)(2,1)S(1)}, bf16[512,1024]{1,0:T(8,128)(2,1)S(1)}) custom-call(bf16[512,1024]{1,0:T(8,128)(2,1)S(1)} %convert_element_type.291.rows_ref.refs_0_, bf16[512,1024]{1,0:T(8,128)(2,1)S(1)} %collective-permute-done.33.refs_1_, ...), custom_call_target="tpu_custom_call" | custom-call | tf_op jit(solution)/shard_map/pallas_call | solution.py:745
  205.6 8.0 %shard_map.262 = f32[512,1024]{1,0:T(8,128)S(1)} custom-call(s32[1]{0:T(128)} %bitcast.5.core_ref, bf16[512,2048]{1,0:T(8,128)(2,1)S(1)} %get-tuple-element.314.refs_2_.own_ref, bf16[512,2048]{1,0:T(8,128)(2,1)S(1)} %get-tuple-element.321.send_ref, bf16[256,2560]{1,0:T(8,128)(2,1)S(1)} %constant_dynamic-update-slice_fusion.4.refs_0_, ...), custom_call_target="tpu_custom_call" | custom-call | tf_op jit(solution)/shard_map/pallas_call | solution.py:511
  216.6 2.7 shard_map.263.dctx_ref
  219.3 5.8 %shard_map.261 = (bf16[512,1024]{1,0:T(8,128)(2,1)S(1)}, bf16[512,1024]{1,0:T(8,128)(2,1)S(1)}, bf16[512,1024]{1,0:T(8,128)(2,1)S(1)}, bf16[512,1024]{1,0:T(8,128)(2,1)S(1)}) custom-call(bf16[512,1024]{1,0:T(8,128)(2,1)S(1)} %get-tuple-element.305.rows_ref.refs_0_, bf16[512,1024]{1,0:T(8,128)(2,1)S(1)} %collective-permute-done.36.refs_1_, ...), custom_call_target="tpu_custom_call" | custom-call | tf_op jit(solution)/shard_map/pallas_call | solution.py:745
  225.1 3.1 collective-permute-done.39
  233.9 1.7 reduce_sum.139
  235.8 1.6 pad_maximum_fusion
  237.4 1.6 collective-permute-start.41
  239.0 1.9 fusion
  242.2 1.6 copy-done.24
  243.8 21.1 %shard_map.264 = (bf16[512,1536]{1,0:T(8,128)(2,1)S(1)}, bf16[512,1536]{1,0:T(8,128)(2,1)S(1)}, f32[1,1536]{1,0:T(1,128)S(1)}, f32[1,1536]{1,0:T(1,128)S(1)}) custom-call(s32[1]{0:T(128)} %bitcast.5.core_ref, bf16[512,3072]{1,0:T(8,128)(2,1)S(1)} %copy-done.3, bf16[512,3072]{1,0:T(8,128)(2,1)S(1)} %copy-done.3, bf16[512,3072]{1,0:T(8,128)(2,1)S(1)} %copy-done.3, ...), custom_call_target="tpu_custom_call" | custom-call | tf_op jit(solution)/shard_map/pallas_call | solution.py:511
  265.5 3.2 collective-permute-done.42
  268.8 1.6 add_convert_fusion.21
  272.8 1.5 add_convert_fusion.7
  274.4 8.7 %shard_map.265 = (bf16[512,1024]{1,0:T(8,128)(2,1)S(1)}, bf16[512,1024]{1,0:T(8,128)(2,1)S(1)}, bf16[512,1024]{1,0:T(8,128)(2,1)S(1)}, bf16[512,1024]{1,0:T(8,128)(2,1)S(1)}) custom-call(bf16[512,1024]{1,0:T(8,128)(2,1)S(1)} %fusion.19.rows_ref.refs_0_, bf16[512,1024]{1,0:T(8,128)(2,1)S(1)} %copy-done.41, ...), custom_call_target="tpu_custom_call" | custom-call | tf_op jit(solution)/shard_map/pallas_call | solution.py:745
  288.4 2.9 collective-permute-start.46
  291.3 1.6 collective-permute-start.47
  293.0 1.6 collective-permute-done.45
  294.7 14.2 %collective-permute-done.46 = bf16[128,1024]{1,0:T(8,128)(2,1)S(1)} collective-permute-done((bf16[128,1024]{1,0:T(8,128)(2,1)S(1)}, bf16[128,1024]{1,0:T(8,128)(2,1)S(1)}, u32[]{:S(2)}, u32[]{:S(2)}) %collective-permute-start.46) | collective-permute-done | bytes 262176 | tf_op jit(solution)/shard_map/ppermute | solution.py:265
  310.0 9.2 %collective-permute-done.49 = bf16[768,1024]{1,0:T(8,128)(2,1)} collective-permute-done((bf16[768,1024]{1,0:T(8,128)(2,1)}, bf16[768,1024]{1,0:T(8,128)(2,1)}, u32[]{:S(2)}, u32[]{:S(2)}) %collective-permute-start.49) | collective-permute-done | bytes 1572896 | tf_op jit(solution)/shard_map/ppermute | solution.py:265
  319.3 1.6 add_convert_fusion.17
  322.4 2.2 add_convert_fusion.3
  325.8 2.0 collective-permute-start.51
  327.8 1.5 collective-permute-start.52
  332.0 10.7 %shard_map.266 = f32[512,1024]{1,0:T(8,128)S(1)} custom-call(s32[1]{0:T(128)} %bitcast.5.core_ref, bf16[512,1536]{1,0:T(8,128)(2,1)S(1)} %copy-done.5, bf16[512,1536]{1,0:T(8,128)(2,1)S(1)} %copy-done.30, bf16[256,1536]{1,0:T(8,128)(2,1)S(1)} %copy-done.8, bf16[256,1536]{1,0:T(8,128)(2,1)} %collective-permute-done.8.refs_1_, ...), custom_call_target="tpu_custom_call" | custom-call | tf_op jit(solution)/shard_map/pallas_call | solution.py:511
  344.1 2.7 fusion.16
  347.5 2.3 collective-permute-start.55
  350.8 1.6 collective-permute-start.57
  352.5 1.7 collective-permute-start.59
  354.3 2.6 collective-permute-done.59
  357.9 2.3 fusion.18
  361.9 9.4 %collective-permute-done.56 = bf16[128,1024]{1,0:T(8,128)(2,1)S(1)} collective-permute-done((bf16[128,1024]{1,0:T(8,128)(2,1)S(1)}, bf16[128,1024]{1,0:T(8,128)(2,1)S(1)}, u32[]{:S(2)}, u32[]{:S(2)}) %collective-permute-start.56) | collective-permute-done | bytes 262176 | tf_op jit(solution)/shard_map/ppermute | solution.py:265
  371.5 2.4 collective-permute-start.65
  373.9 5.3 %collective-permute-start.64 = (f32[12,1024]{1,0:T(8,128)S(1)}, f32[12,1024]{1,0:T(8,128)S(1)}, u32[]{:S(2)}, u32[]{:S(2)}) collective-permute-start(f32[12,1024]{1,0:T(8,128)S(1)} %add.364), channel_id=1, source_target_pairs={{0,16},{2,18},{4,20},{6,22},{8,24},{10,26},{12,28},{14,30},{16,0},... | collective-permute-start | bytes 147464 | tf_op jit(solution)/shard_map/ppermute | solution.py:265
  381.0 1.8 collective-permute-done.64
  (357 shorter events, 77.3 us)
Async XLA Ops:
  1.8 24.0 %collective-permute-start.3 = (bf16[64,2560]{1,0:T(8,128)(2,1)S(1)}, bf16[64,2560]{1,0:T(8,128)(2,1)S(1)}, u32[]{:S(2)}, u32[]{:S(2)}) collective-permute-start(bf16[64,2560]{1,0:T(8,128)(2,1)S(1)} %pad_maximum_fusion.18), channel_id=1, source_target_pairs={{0,8},{2,10},{4,12},{6,14},{8,0},{10,2},{12,4},{14,6},{16,24},{18,... | collective-permute-start | bytes 983048 | tf_op jit(solution)/shard_map/ppermute | solution.py:265
  5.8 14.4 %collective-permute-start.2 = (bf16[64,1536]{1,0:T(8,128)(2,1)S(1)}, bf16[64,1536]{1,0:T(8,128)(2,1)S(1)}, u32[]{:S(2)}, u32[]{:S(2)}) collective-permute-start(bf16[64,1536]{1,0:T(8,128)(2,1)S(1)} %pad_maximum_fusion.32), channel_id=1, source_target_pairs={{0,24},{2,26},{4,28},{6,30},{8,16},{10,18},{12,20},{14,22},{16,8},... | collective-permute-start | bytes 589832 | tf_op jit(solution)/shard_map/ppermute | solution.py:265
  8.3 17.4 %collective-permute-start.1 = (bf16[64,1536]{1,0:T(8,128)(2,1)S(1)}, bf16[64,1536]{1,0:T(8,128)(2,1)S(1)}, u32[]{:S(2)}, u32[]{:S(2)}) collective-permute-start(bf16[64,1536]{1,0:T(8,128)(2,1)S(1)} %pad_maximum_fusion.32), channel_id=1, source_target_pairs={{0,16},{2,18},{4,20},{6,22},{8,24},{10,26},{12,28},{14,30},{16,0},... | collective-permute-start | bytes 589832 | tf_op jit(solution)/shard_map/ppermute | solution.py:265
  8.5 17.2 %collective-permute-start = (bf16[64,1536]{1,0:T(8,128)(2,1)S(1)}, bf16[64,1536]{1,0:T(8,128)(2,1)S(1)}, u32[]{:S(2)}, u32[]{:S(2)}) collective-permute-start(bf16[64,1536]{1,0:T(8,128)(2,1)S(1)} %pad_maximum_fusion.32), channel_id=1, source_target_pairs={{0,8},{2,10},{4,12},{6,14},{8,0},{10,2},{12,4},{14,6},{16,24},{18,... | collective-permute-start | bytes 589832 | tf_op jit(solution)/shard_map/ppermute | solution.py:265
  25.8 19.1 %collective-permute-start.4 = (bf16[128,1536]{1,0:T(8,128)(2,1)S(1)}, bf16[128,1536]{1,0:T(8,128)(2,1)S(1)}, u32[]{:S(2)}, u32[]{:S(2)}) collective-permute-start(bf16[128,1536]{1,0:T(8,128)(2,1)S(1)} %pad_maximum_fusion.15), channel_id=1, source_target_pairs={{0,4},{2,6},{4,0},{6,2},{8,12},{10,14},{12,8},{14,10},{16,20},{18,... | collective-permute-start | bytes 1179656 | tf_op jit(solution)/shard_map/ppermute | solution.py:265
  27.4 17.5 %collective-permute-start.5 = (bf16[128,1536]{1,0:T(8,128)(2,1)S(1)}, bf16[128,1536]{1,0:T(8,128)(2,1)S(1)}, u32[]{:S(2)}, u32[]{:S(2)}) collective-permute-start(bf16[128,1536]{1,0:T(8,128)(2,1)S(1)} %pad_maximum_fusion.16), channel_id=1, source_target_pairs={{0,1},{1,0},{2,3},{3,2},{4,5},{5,4},{6,7},{7,6},{8,9},{9,8},{10,11... | collective-permute-start | bytes 1179656 | tf_op jit(solution)/shard_map/ppermute | solution.py:265
  29.0 15.9 %collective-permute-start.6 = (bf16[64,2560]{1,0:T(8,128)(2,1)S(1)}, bf16[64,2560]{1,0:T(8,128)(2,1)S(1)}, u32[]{:S(2)}, u32[]{:S(2)}) collective-permute-start(bf16[64,2560]{1,0:T(8,128)(2,1)S(1)} %pad_maximum_fusion.18), channel_id=1, source_target_pairs={{0,16},{2,18},{4,20},{6,22},{8,24},{10,26},{12,28},{14,30},{16,0},... | collective-permute-start | bytes 983048 | tf_op jit(solution)/shard_map/ppermute | solution.py:265
  31.3 11.2 %collective-permute-start.7 = (bf16[64,2048]{1,0:T(8,128)(2,1)S(1)}, bf16[64,2048]{1,0:T(8,128)(2,1)}, u32[]{:S(2)}, u32[]{:S(2)}) collective-permute-start(bf16[64,2048]{1,0:T(8,128)(2,1)S(1)} %bitcast.199), channel_id=1, source_target_pairs={{0,8},{2,10},{4,12},{6,14},{8,0},{10,2},{12,4},{14,6},{16,24},{18,... | collective-permute-start | bytes 786440 | tf_op jit(solution)/shard_map/ppermute | solution.py:265
  45.0 18.8 %collective-permute-start.11 = (bf16[256,1536]{1,0:T(8,128)(2,1)S(1)}, bf16[256,1536]{1,0:T(8,128)(2,1)S(1)}, u32[]{:S(2)}, u32[]{:S(2)}) collective-permute-start(bf16[256,1536]{1,0:T(8,128)(2,1)S(1)} %constant_dynamic-update-slice_fusion.2.refs_2_), channel_id=1, source_target_pairs={{0,2},{2,0},{4,6},{6,4},{8,10},{10,8},{12,14},{14,12},{16,18},{18,... | collective-permute-start | bytes 2359304 | tf_op jit(solution)/shard_map/ppermute | solution.py:265
  45.1 20.1 %collective-permute-start.9 = (bf16[256,1536]{1,0:T(8,128)(2,1)S(1)}, bf16[256,1536]{1,0:T(8,128)(2,1)}, u32[]{:S(2)}, u32[]{:S(2)}) collective-permute-start(bf16[256,1536]{1,0:T(8,128)(2,1)S(1)} %constant_dynamic-update-slice_fusion.2.refs_2_), channel_id=1, source_target_pairs={{0,4},{2,6},{4,0},{6,2},{8,12},{10,14},{12,8},{14,10},{16,20},{18,... | collective-permute-start | bytes 2359304 | tf_op jit(solution)/shard_map/ppermute | solution.py:265
  45.8 19.4 %collective-permute-start.10 = (bf16[256,1536]{1,0:T(8,128)(2,1)S(1)}, bf16[256,1536]{1,0:T(8,128)(2,1)S(1)}, u32[]{:S(2)}, u32[]{:S(2)}) collective-permute-start(bf16[256,1536]{1,0:T(8,128)(2,1)S(1)} %constant_dynamic-update-slice_fusion.refs_0_), channel_id=1, source_target_pairs={{0,2},{2,0},{4,6},{6,4},{8,10},{10,8},{12,14},{14,12},{16,18},{18,... | collective-permute-start | bytes 2359304 | tf_op jit(solution)/shard_map/ppermute | solution.py:265
  46.0 20.1 %collective-permute-start.8 = (bf16[256,1536]{1,0:T(8,128)(2,1)S(1)}, bf16[256,1536]{1,0:T(8,128)(2,1)}, u32[]{:S(2)}, u32[]{:S(2)}) collective-permute-start(bf16[256,1536]{1,0:T(8,128)(2,1)S(1)} %constant_dynamic-update-slice_fusion.refs_0_), channel_id=1, source_target_pairs={{0,1},{1,0},{2,3},{3,2},{4,5},{5,4},{6,7},{7,6},{8,9},{9,8},{10,11... | collective-permute-start | bytes 2359304 | tf_op jit(solution)/shard_map/ppermute | solution.py:265
  46.5 17.3 %collective-permute-start.12 = (bf16[64,2560]{1,0:T(8,128)(2,1)S(1)}, bf16[64,2560]{1,0:T(8,128)(2,1)S(1)}, u32[]{:S(2)}, u32[]{:S(2)}) collective-permute-start(bf16[64,2560]{1,0:T(8,128)(2,1)S(1)} %collective-permute-done.3), channel_id=1, source_target_pairs={{0,16},{2,18},{4,20},{6,22},{8,24},{10,26},{12,28},{14,30},{16,0},... | collective-permute-start | bytes 983048 | tf_op jit(solution)/shard_map/ppermute | solution.py:265
  66.3 17.8 %collective-permute-start.15 = (bf16[128,2560]{1,0:T(8,128)(2,1)S(1)}, bf16[128,2560]{1,0:T(8,128)(2,1)}, u32[]{:S(2)}, u32[]{:S(2)}) collective-permute-start(bf16[128,2560]{1,0:T(8,128)(2,1)S(1)} %pad_maximum_fusion.4), channel_id=1, source_target_pairs={{0,4},{2,6},{4,0},{6,2},{8,12},{10,14},{12,8},{14,10},{16,20},{18,... | collective-permute-start | bytes 1966088 | tf_op jit(solution)/shard_map/ppermute | solution.py:265
  67.7 18.4 %collective-permute-start.13 = (bf16[256,1536]{1,0:T(8,128)(2,1)}, bf16[256,1536]{1,0:T(8,128)(2,1)}, u32[]{:S(2)}, u32[]{:S(2)}) collective-permute-start(bf16[256,1536]{1,0:T(8,128)(2,1)} %collective-permute-done.8.refs_1_), channel_id=1, source_target_pairs={{0,2},{2,0},{4,6},{6,4},{8,10},{10,8},{12,14},{14,12},{16,18},{18,... | collective-permute-start | bytes 2359304 | tf_op jit(solution)/shard_map/ppermute | solution.py:265
  67.7 18.4 %collective-permute-start.14 = (bf16[256,1536]{1,0:T(8,128)(2,1)}, bf16[256,1536]{1,0:T(8,128)(2,1)}, u32[]{:S(2)}, u32[]{:S(2)}) collective-permute-start(bf16[256,1536]{1,0:T(8,128)(2,1)} %collective-permute-done.9.refs_3_), channel_id=1, source_target_pairs={{0,2},{2,0},{4,6},{6,4},{8,10},{10,8},{12,14},{14,12},{16,18},{18,... | collective-permute-start | bytes 2359304 | tf_op jit(solution)/shard_map/ppermute | solution.py:265
  69.1 17.0 %collective-permute-start.16 = (bf16[128,2560]{1,0:T(8,128)(2,1)}, bf16[128,2560]{1,0:T(8,128)(2,1)}, u32[]{:S(2)}, u32[]{:S(2)}) collective-permute-start(bf16[128,2560]{1,0:T(8,128)(2,1)} %pad_maximum_fusion.5), channel_id=1, source_target_pairs={{0,1},{1,0},{2,3},{3,2},{4,5},{5,4},{6,7},{7,6},{8,9},{9,8},{10,11... | collective-permute-start | bytes 1966088 | tf_op jit(solution)/shard_map/ppermute | solution.py:265
  70.7 13.5 %collective-permute-start.17 = (bf16[64,2048]{1,0:T(8,128)(2,1)S(1)}, bf16[64,2048]{1,0:T(8,128)(2,1)S(1)}, u32[]{:S(2)}, u32[]{:S(2)}) collective-permute-start(bf16[64,2048]{1,0:T(8,128)(2,1)S(1)} %bitcast.200), channel_id=1, source_target_pairs={{0,16},{2,18},{4,20},{6,22},{8,24},{10,26},{12,28},{14,30},{16,0},... | collective-permute-start | bytes 786440 | tf_op jit(solution)/shard_map/ppermute | solution.py:265
  88.5 25.2 %collective-permute-start.21 = (bf16[256,2560]{1,0:T(8,128)(2,1)S(1)}, bf16[256,2560]{1,0:T(8,128)(2,1)S(1)}, u32[]{:S(2)}, u32[]{:S(2)}) collective-permute-start(bf16[256,2560]{1,0:T(8,128)(2,1)S(1)} %constant_dynamic-update-slice_fusion.6.refs_2_), channel_id=1, source_target_pairs={{0,2},{2,0},{4,6},{6,4},{8,10},{10,8},{12,14},{14,12},{16,18},{18,... | collective-permute-start | bytes 3932168 | tf_op jit(solution)/shard_map/ppermute | solution.py:265
  88.5 31.2 %collective-permute-start.19 = (bf16[256,2560]{1,0:T(8,128)(2,1)S(1)}, bf16[256,2560]{1,0:T(8,128)(2,1)S(1)}, u32[]{:S(2)}, u32[]{:S(2)}) collective-permute-start(bf16[256,2560]{1,0:T(8,128)(2,1)S(1)} %constant_dynamic-update-slice_fusion.6.refs_2_), channel_id=1, source_target_pairs={{0,4},{2,6},{4,0},{6,2},{8,12},{10,14},{12,8},{14,10},{16,20},{18,... | collective-permute-start | bytes 3932168 | tf_op jit(solution)/shard_map/ppermute | solution.py:265
  90.5 29.2 %collective-permute-start.20 = (bf16[256,2560]{1,0:T(8,128)(2,1)S(1)}, bf16[256,2560]{1,0:T(8,128)(2,1)S(1)}, u32[]{:S(2)}, u32[]{:S(2)}) collective-permute-start(bf16[256,2560]{1,0:T(8,128)(2,1)S(1)} %constant_dynamic-update-slice_fusion.4.refs_0_), channel_id=1, source_target_pairs={{0,2},{2,0},{4,6},{6,4},{8,10},{10,8},{12,14},{14,12},{16,18},{18,... | collective-permute-start | bytes 3932168 | tf_op jit(solution)/shard_map/ppermute | solution.py:265
  90.7 31.0 %collective-permute-start.18 = (bf16[256,2560]{1,0:T(8,128)(2,1)S(1)}, bf16[256,2560]{1,0:T(8,128)(2,1)S(1)}, u32[]{:S(2)}, u32[]{:S(2)}) collective-permute-start(bf16[256,2560]{1,0:T(8,128)(2,1)S(1)} %constant_dynamic-update-slice_fusion.4.refs_0_), channel_id=1, source_target_pairs={{0,1},{1,0},{2,3},{3,2},{4,5},{5,4},{6,7},{7,6},{8,9},{9,8},{10,11... | collective-permute-start | bytes 3932168 | tf_op jit(solution)/shard_map/ppermute | solution.py:265
  92.0 21.7 %collective-permute-start.22 = (bf16[64,2048]{1,0:T(8,128)(2,1)}, bf16[64,2048]{1,0:T(8,128)(2,1)S(1)}, u32[]{:S(2)}, u32[]{:S(2)}) collective-permute-start(bf16[64,2048]{1,0:T(8,128)(2,1)} %collective-permute-done.7), channel_id=1, source_target_pairs={{0,16},{2,18},{4,20},{6,22},{8,24},{10,26},{12,28},{14,30},{16,0},... | collective-permute-start | bytes 786440 | tf_op jit(solution)/shard_map/ppermute | solution.py:265
  122.8 15.8 %collective-permute-start.23 = (bf16[256,2560]{1,0:T(8,128)(2,1)S(1)}, bf16[256,2560]{1,0:T(8,128)(2,1)S(1)}, u32[]{:S(2)}, u32[]{:S(2)}) collective-permute-start(bf16[256,2560]{1,0:T(8,128)(2,1)S(1)} %collective-permute-done.18.refs_1_), channel_id=1, source_target_pairs={{0,2},{2,0},{4,6},{6,4},{8,10},{10,8},{12,14},{14,12},{16,18},{18,... | collective-permute-start | bytes 3932168 | tf_op jit(solution)/shard_map/ppermute | solution.py:265
  122.9 15.7 %collective-permute-start.24 = (bf16[256,2560]{1,0:T(8,128)(2,1)S(1)}, bf16[256,2560]{1,0:T(8,128)(2,1)S(1)}, u32[]{:S(2)}, u32[]{:S(2)}) collective-permute-start(bf16[256,2560]{1,0:T(8,128)(2,1)S(1)} %collective-permute-done.19.refs_3_), channel_id=1, source_target_pairs={{0,2},{2,0},{4,6},{6,4},{8,10},{10,8},{12,14},{14,12},{16,18},{18,... | collective-permute-start | bytes 3932168 | tf_op jit(solution)/shard_map/ppermute | solution.py:265
  123.4 14.0 %collective-permute-start.25 = (bf16[128,2048]{1,0:T(8,128)(2,1)S(1)}, bf16[128,2048]{1,0:T(8,128)(2,1)S(1)}, u32[]{:S(2)}, u32[]{:S(2)}) collective-permute-start(bf16[128,2048]{1,0:T(8,128)(2,1)S(1)} %pad_maximum_fusion.6), channel_id=1, source_target_pairs={{0,4},{2,6},{4,0},{6,2},{8,12},{10,14},{12,8},{14,10},{16,20},{18,... | collective-permute-start | bytes 1572872 | tf_op jit(solution)/shard_map/ppermute | solution.py:265
  124.9 13.7 %collective-permute-start.26 = (bf16[128,2048]{1,0:T(8,128)(2,1)S(1)}, bf16[128,2048]{1,0:T(8,128)(2,1)S(1)}, u32[]{:S(2)}, u32[]{:S(2)}) collective-permute-start(bf16[128,2048]{1,0:T(8,128)(2,1)S(1)} %pad_maximum_fusion.7), channel_id=1, source_target_pairs={{0,1},{1,0},{2,3},{3,2},{4,5},{5,4},{6,7},{7,6},{8,9},{9,8},{10,11... | collective-permute-start | bytes 1572872 | tf_op jit(solution)/shard_map/ppermute | solution.py:265
  138.7 21.4 %collective-permute-start.30 = (bf16[256,2048]{1,0:T(8,128)(2,1)S(1)}, bf16[256,2048]{1,0:T(8,128)(2,1)S(1)}, u32[]{:S(2)}, u32[]{:S(2)}) collective-permute-start(bf16[256,2048]{1,0:T(8,128)(2,1)S(1)} %constant_dynamic-update-slice_fusion.11.refs_2_), channel_id=1, source_target_pairs={{0,2},{2,0},{4,6},{6,4},{8,10},{10,8},{12,14},{14,12},{16,18},{18,... | collective-permute-start | bytes 3145736 | tf_op jit(solution)/shard_map/ppermute | solution.py:265
  138.7 25.6 %collective-permute-start.28 = (bf16[256,2048]{1,0:T(8,128)(2,1)S(1)}, bf16[256,2048]{1,0:T(8,128)(2,1)S(1)}, u32[]{:S(2)}, u32[]{:S(2)}) collective-permute-start(bf16[256,2048]{1,0:T(8,128)(2,1)S(1)} %constant_dynamic-update-slice_fusion.11.refs_2_), channel_id=1, source_target_pairs={{0,4},{2,6},{4,0},{6,2},{8,12},{10,14},{12,8},{14,10},{16,20},{18,... | collective-permute-start | bytes 3145736 | tf_op jit(solution)/shard_map/ppermute | solution.py:265
  139.6 24.7 %collective-permute-start.29 = (bf16[256,2048]{1,0:T(8,128)(2,1)S(1)}, bf16[256,2048]{1,0:T(8,128)(2,1)S(1)}, u32[]{:S(2)}, u32[]{:S(2)}) collective-permute-start(bf16[256,2048]{1,0:T(8,128)(2,1)S(1)} %constant_dynamic-update-slice_fusion.9.refs_0_), channel_id=1, source_target_pairs={{0,2},{2,0},{4,6},{6,4},{8,10},{10,8},{12,14},{14,12},{16,18},{18,... | collective-permute-start | bytes 3145736 | tf_op jit(solution)/shard_map/ppermute | solution.py:265
  139.8 25.4 %collective-permute-start.27 = (bf16[256,2048]{1,0:T(8,128)(2,1)S(1)}, bf16[256,2048]{1,0:T(8,128)(2,1)S(1)}, u32[]{:S(2)}, u32[]{:S(2)}) collective-permute-start(bf16[256,2048]{1,0:T(8,128)(2,1)S(1)} %constant_dynamic-update-slice_fusion.9.refs_0_), channel_id=1, source_target_pairs={{0,1},{1,0},{2,3},{3,2},{4,5},{5,4},{6,7},{7,6},{8,9},{9,8},{10,11... | collective-permute-start | bytes 3145736 | tf_op jit(solution)/shard_map/ppermute | solution.py:265
  182.9 9.5 %collective-permute-start.34 = (bf16[512,2048]{1,0:T(8,128)(2,1)}, bf16[512,2048]{1,0:T(8,128)(2,1)S(1)}, u32[]{:S(2)}, u32[]{:S(2)}) collective-permute-start(bf16[512,2048]{1,0:T(8,128)(2,1)} %get-tuple-element.289.send_ref), channel_id=1, source_target_pairs={{0,2},{2,0},{4,6},{6,4},{8,10},{10,8},{12,14},{14,12},{16,18},{18,... | collective-permute-start | bytes 6291464 | tf_op jit(solution)/shard_map/ppermute | solution.py:265
  183.1 9.3 %collective-permute-start.33 = (bf16[512,1024]{1,0:T(8,128)(2,1)S(1)}, bf16[512,1024]{1,0:T(8,128)(2,1)S(1)}, u32[]{:S(2)}, u32[]{:S(2)}) collective-permute-start(bf16[512,1024]{1,0:T(8,128)(2,1)S(1)} %convert_element_type.291.rows_ref.refs_0_), channel_id=1, source_target_pairs={{0,2},{2,0},{4,6},{6,4},{8,10},{10,8},{12,14},{14,12},{16,18},{18,... | collective-permute-start | bytes 3145736 | tf_op jit(solution)/shard_map/ppermute | solution.py:265
  193.7 9.2 %collective-permute-start.35 = (bf16[512,2048]{1,0:T(8,128)(2,1)S(1)}, bf16[512,2048]{1,0:T(8,128)(2,1)S(1)}, u32[]{:S(2)}, u32[]{:S(2)}) collective-permute-start(bf16[512,2048]{1,0:T(8,128)(2,1)S(1)} %get-tuple-element.321.send_ref), channel_id=1, source_target_pairs={{0,2},{2,0},{4,6},{6,4},{8,10},{10,8},{12,14},{14,12},{16,18},{18,... | collective-permute-start | bytes 6291464 | tf_op jit(solution)/shard_map/ppermute | solution.py:265
  193.8 9.1 %collective-permute-start.36 = (bf16[512,1024]{1,0:T(8,128)(2,1)S(1)}, bf16[512,1024]{1,0:T(8,128)(2,1)S(1)}, u32[]{:S(2)}, u32[]{:S(2)}) collective-permute-start(bf16[512,1024]{1,0:T(8,128)(2,1)S(1)} %get-tuple-element.305.rows_ref.refs_0_), channel_id=1, source_target_pairs={{0,2},{2,0},{4,6},{6,4},{8,10},{10,8},{12,14},{14,12},{16,18},{18,... | collective-permute-start | bytes 3145736 | tf_op jit(solution)/shard_map/ppermute | solution.py:265
  194.2 8.7 %collective-permute-start.37 = (bf16[512,1024]{1,0:T(8,128)(2,1)S(1)}, bf16[512,1024]{1,0:T(8,128)(2,1)S(1)}, u32[]{:S(2)}, u32[]{:S(2)}) collective-permute-start(bf16[512,1024]{1,0:T(8,128)(2,1)S(1)} %fusion.19.rows_ref.refs_0_), channel_id=1, source_target_pairs={{0,2},{2,0},{4,6},{6,4},{8,10},{10,8},{12,14},{14,12},{16,18},{18,... | collective-permute-start | bytes 3145736 | tf_op jit(solution)/shard_map/ppermute | solution.py:265
  194.3 7.8 %collective-permute-start.38 = (bf16[512,512]{1,0:T(8,128)(2,1)S(1)}, bf16[512,512]{1,0:T(8,128)(2,1)S(1)}, u32[]{:S(2)}, u32[]{:S(2)}) collective-permute-start(bf16[512,512]{1,0:T(8,128)(2,1)S(1)} %get-tuple-element.307.send_ref), channel_id=1, source_target_pairs={{0,2},{2,0},{4,6},{6,4},{8,10},{10,8},{12,14},{14,12},{16,18},{18,... | collective-permute-start | bytes 1572872 | tf_op jit(solution)/shard_map/ppermute | solution.py:265
  203.0 25.3 %collective-permute-start.39 = (bf16[512,1024]{1,0:T(8,128)(2,1)S(1)}, bf16[512,1024]{1,0:T(8,128)(2,1)S(1)}, u32[]{:S(2)}, u32[]{:S(2)}) collective-permute-start(bf16[512,1024]{1,0:T(8,128)(2,1)S(1)} %get-tuple-element.310), channel_id=1, source_target_pairs={{0,1},{1,0},{2,3},{3,2},{4,5},{5,4},{6,7},{7,6},{8,9},{9,8},{10,11... | collective-permute-start | bytes 3145736 | tf_op jit(solution)/shard_map/ppermute | solution.py:265
  204.1 26.2 %collective-permute-start.40 = (bf16[512,1024]{1,0:T(8,128)(2,1)S(1)}, bf16[512,1024]{1,0:T(8,128)(2,1)S(1)}, u32[]{:S(2)}, u32[]{:S(2)}) collective-permute-start(bf16[512,1024]{1,0:T(8,128)(2,1)S(1)} %get-tuple-element.312), channel_id=1, source_target_pairs={{0,4},{2,6},{4,0},{6,2},{8,12},{10,14},{12,8},{14,10},{16,20},{18,... | collective-permute-start | bytes 3145736 | tf_op jit(solution)/shard_map/ppermute | solution.py:265
  232.8 35.9 %collective-permute-start.42 = (bf16[768,1024]{1,0:T(8,128)(2,1)}, bf16[768,1024]{1,0:T(8,128)(2,1)}, u32[]{:S(2)}, u32[]{:S(2)}) collective-permute-start(bf16[768,1024]{1,0:T(8,128)(2,1)} %pad_maximum_fusion.1), channel_id=1, source_target_pairs={{0,1},{1,0},{2,3},{3,2},{4,5},{5,4},{6,7},{7,6},{8,9},{9,8},{10,11... | collective-permute-start | bytes 4718600 | tf_op jit(solution)/shard_map/ppermute | solution.py:265
  237.4 35.4 %collective-permute-start.41 = (bf16[768,1024]{1,0:T(8,128)(2,1)S(1)}, bf16[768,1024]{1,0:T(8,128)(2,1)S(1)}, u32[]{:S(2)}, u32[]{:S(2)}) collective-permute-start(bf16[768,1024]{1,0:T(8,128)(2,1)S(1)} %pad_maximum_fusion), channel_id=1, source_target_pairs={{0,4},{2,6},{4,0},{6,2},{8,12},{10,14},{12,8},{14,10},{16,20},{18,... | collective-permute-start | bytes 4718600 | tf_op jit(solution)/shard_map/ppermute | solution.py:265
  240.9 33.4 %collective-permute-start.44 = (bf16[512,1024]{1,0:T(8,128)(2,1)S(1)}, bf16[512,1024]{1,0:T(8,128)(2,1)S(1)}, u32[]{:S(2)}, u32[]{:S(2)}) collective-permute-start(bf16[512,1024]{1,0:T(8,128)(2,1)S(1)} %convert_element_type.310.rows_ref.refs_4_), channel_id=1, source_target_pairs={{0,2},{2,0},{4,6},{6,4},{8,10},{10,8},{12,14},{14,12},{16,18},{18,... | collective-permute-start | bytes 3145736 | tf_op jit(solution)/shard_map/ppermute | solution.py:265
  264.9 9.4 %collective-permute-start.43 = (bf16[512,1536]{1,0:T(8,128)(2,1)S(1)}, bf16[512,1536]{1,0:T(8,128)(2,1)S(1)}, u32[]{:S(2)}, u32[]{:S(2)}) collective-permute-start(bf16[512,1536]{1,0:T(8,128)(2,1)S(1)} %get-tuple-element.358.send_ref), channel_id=1, source_target_pairs={{0,2},{2,0},{4,6},{6,4},{8,10},{10,8},{12,14},{14,12},{16,18},{18,... | collective-permute-start | bytes 4718600 | tf_op jit(solution)/shard_map/ppermute | solution.py:265
  284.5 34.7 %collective-permute-start.49 = (bf16[768,1024]{1,0:T(8,128)(2,1)}, bf16[768,1024]{1,0:T(8,128)(2,1)}, u32[]{:S(2)}, u32[]{:S(2)}) collective-permute-start(bf16[768,1024]{1,0:T(8,128)(2,1)} %pad_maximum_fusion.3), channel_id=1, source_target_pairs={{0,1},{1,0},{2,3},{3,2},{4,5},{5,4},{6,7},{7,6},{8,9},{9,8},{10,11... | collective-permute-start | bytes 4718600 | tf_op jit(solution)/shard_map/ppermute | solution.py:265
  285.6 9.1 %collective-permute-start.45 = (bf16[128,1024]{1,0:T(8,128)(2,1)S(1)}, bf16[128,1024]{1,0:T(8,128)(2,1)S(1)}, u32[]{:S(2)}, u32[]{:S(2)}) collective-permute-start(bf16[128,1024]{1,0:T(8,128)(2,1)S(1)} %pad_maximum_fusion.19), channel_id=1, source_target_pairs={{0,8},{2,10},{4,12},{6,14},{8,0},{10,2},{12,4},{14,6},{16,24},{18,... | collective-permute-start | bytes 786440 | tf_op jit(solution)/shard_map/ppermute | solution.py:265
  287.1 35.2 %collective-permute-start.48 = (bf16[768,1024]{1,0:T(8,128)(2,1)}, bf16[768,1024]{1,0:T(8,128)(2,1)}, u32[]{:S(2)}, u32[]{:S(2)}) collective-permute-start(bf16[768,1024]{1,0:T(8,128)(2,1)} %pad_maximum_fusion.2), channel_id=1, source_target_pairs={{0,4},{2,6},{4,0},{6,2},{8,12},{10,14},{12,8},{14,10},{16,20},{18,... | collective-permute-start | bytes 4718600 | tf_op jit(solution)/shard_map/ppermute | solution.py:265
  288.4 20.5 %collective-permute-start.46 = (bf16[128,1024]{1,0:T(8,128)(2,1)S(1)}, bf16[128,1024]{1,0:T(8,128)(2,1)S(1)}, u32[]{:S(2)}, u32[]{:S(2)}) collective-permute-start(bf16[128,1024]{1,0:T(8,128)(2,1)S(1)} %pad_maximum_fusion.20), channel_id=1, source_target_pairs={{0,16},{2,18},{4,20},{6,22},{8,24},{10,26},{12,28},{14,30},{16,0},... | collective-permute-start | bytes 786440 | tf_op jit(solution)/shard_map/ppermute | solution.py:265
  291.3 17.6 %collective-permute-start.47 = (bf16[128,1024]{1,0:T(8,128)(2,1)S(1)}, bf16[128,1024]{1,0:T(8,128)(2,1)}, u32[]{:S(2)}, u32[]{:S(2)}) collective-permute-start(bf16[128,1024]{1,0:T(8,128)(2,1)S(1)} %pad_maximum_fusion.21), channel_id=1, source_target_pairs={{0,24},{2,26},{4,28},{6,30},{8,16},{10,18},{12,20},{14,22},{16,8},... | collective-permute-start | bytes 786440 | tf_op jit(solution)/shard_map/ppermute | solution.py:265
  324.7 22.0 %collective-permute-start.50 = (bf16[128,1024]{1,0:T(8,128)(2,1)S(1)}, bf16[128,1024]{1,0:T(8,128)(2,1)S(1)}, u32[]{:S(2)}, u32[]{:S(2)}) collective-permute-start(bf16[128,1024]{1,0:T(8,128)(2,1)S(1)} %pad_maximum_fusion.22), channel_id=1, source_target_pairs={{0,8},{2,10},{4,12},{6,14},{8,0},{10,2},{12,4},{14,6},{16,24},{18,... | collective-permute-start | bytes 786440 | tf_op jit(solution)/shard_map/ppermute | solution.py:265
  325.8 20.9 %collective-permute-start.51 = (bf16[128,1024]{1,0:T(8,128)(2,1)S(1)}, bf16[128,1024]{1,0:T(8,128)(2,1)S(1)}, u32[]{:S(2)}, u32[]{:S(2)}) collective-permute-start(bf16[128,1024]{1,0:T(8,128)(2,1)S(1)} %pad_maximum_fusion.23), channel_id=1, source_target_pairs={{0,16},{2,18},{4,20},{6,22},{8,24},{10,26},{12,28},{14,30},{16,0},... | collective-permute-start | bytes 786440 | tf_op jit(solution)/shard_map/ppermute | solution.py:265
  327.8 18.9 %collective-permute-start.52 = (bf16[128,1024]{1,0:T(8,128)(2,1)S(1)}, bf16[128,1024]{1,0:T(8,128)(2,1)S(1)}, u32[]{:S(2)}, u32[]{:S(2)}) collective-permute-start(bf16[128,1024]{1,0:T(8,128)(2,1)S(1)} %pad_maximum_fusion.24), channel_id=1, source_target_pairs={{0,24},{2,26},{4,28},{6,30},{8,16},{10,18},{12,20},{14,22},{16,8},... | collective-permute-start | bytes 786440 | tf_op jit(solution)/shard_map/ppermute | solution.py:265
  329.3 17.6 %collective-permute-start.53 = (bf16[256,1024]{1,0:T(8,128)(2,1)S(1)}, bf16[256,1024]{1,0:T(8,128)(2,1)S(1)}, u32[]{:S(2)}, u32[]{:S(2)}) collective-permute-start(bf16[256,1024]{1,0:T(8,128)(2,1)S(1)} %pad_maximum_fusion.13), channel_id=1, source_target_pairs={{0,4},{2,6},{4,0},{6,2},{8,12},{10,14},{12,8},{14,10},{16,20},{18,... | collective-permute-start | bytes 1572872 | tf_op jit(solution)/shard_map/ppermute | solution.py:265
  330.8 16.3 %collective-permute-start.54 = (bf16[256,1024]{1,0:T(8,128)(2,1)S(1)}, bf16[256,1024]{1,0:T(8,128)(2,1)S(1)}, u32[]{:S(2)}, u32[]{:S(2)}) collective-permute-start(bf16[256,1024]{1,0:T(8,128)(2,1)S(1)} %get-tuple-element.364), channel_id=1, source_target_pairs={{0,1},{1,0},{2,3},{3,2},{4,5},{5,4},{6,7},{7,6},{8,9},{9,8},{10,11... | collective-permute-start | bytes 1572872 | tf_op jit(solution)/shard_map/ppermute | solution.py:265
  347.4 5.0 %collective-permute-start.58 = (f32[12,1024]{1,0:T(8,128)S(1)}, f32[12,1024]{1,0:T(8,128)S(1)}, u32[]{:S(2)}, u32[]{:S(2)}) collective-permute-start(f32[12,1024]{1,0:T(8,128)S(1)} %concatenate.418), channel_id=1, source_target_pairs={{0,2},{2,0},{4,6},{6,4},{8,10},{10,8},{12,14},{14,12},{16,18},{18,... | collective-permute-start | bytes 147464 | tf_op jit(solution)/shard_map/ppermute | solution.py:265
  347.5 14.3 %collective-permute-start.55 = (bf16[128,1024]{1,0:T(8,128)(2,1)S(1)}, bf16[128,1024]{1,0:T(8,128)(2,1)S(1)}, u32[]{:S(2)}, u32[]{:S(2)}) collective-permute-start(bf16[128,1024]{1,0:T(8,128)(2,1)S(1)} %pad_maximum_fusion.25), channel_id=1, source_target_pairs={{0,8},{2,10},{4,12},{6,14},{8,0},{10,2},{12,4},{14,6},{16,24},{18,... | collective-permute-start | bytes 786440 | tf_op jit(solution)/shard_map/ppermute | solution.py:265
  349.9 21.4 %collective-permute-start.56 = (bf16[128,1024]{1,0:T(8,128)(2,1)S(1)}, bf16[128,1024]{1,0:T(8,128)(2,1)S(1)}, u32[]{:S(2)}, u32[]{:S(2)}) collective-permute-start(bf16[128,1024]{1,0:T(8,128)(2,1)S(1)} %pad_maximum_fusion.26), channel_id=1, source_target_pairs={{0,16},{2,18},{4,20},{6,22},{8,24},{10,26},{12,28},{14,30},{16,0},... | collective-permute-start | bytes 786440 | tf_op jit(solution)/shard_map/ppermute | solution.py:265
  350.8 20.4 %collective-permute-start.57 = (bf16[128,1024]{1,0:T(8,128)(2,1)S(1)}, bf16[128,1024]{1,0:T(8,128)(2,1)S(1)}, u32[]{:S(2)}, u32[]{:S(2)}) collective-permute-start(bf16[128,1024]{1,0:T(8,128)(2,1)S(1)} %pad_maximum_fusion.27), channel_id=1, source_target_pairs={{0,24},{2,26},{4,28},{6,30},{8,16},{10,18},{12,20},{14,22},{16,8},... | collective-permute-start | bytes 786440 | tf_op jit(solution)/shard_map/ppermute | solution.py:265
  352.5 4.3 %collective-permute-start.59 = (f32[12,1024]{1,0:T(8,128)S(1)}, f32[12,1024]{1,0:T(8,128)S(1)}, u32[]{:S(2)}, u32[]{:S(2)}) collective-permute-start(f32[12,1024]{1,0:T(8,128)S(1)} %add.362), channel_id=1, source_target_pairs={{0,4},{2,6},{4,0},{6,2},{8,12},{10,14},{12,8},{14,10},{16,20},{18,... | collective-permute-start | bytes 147464 | tf_op jit(solution)/shard_map/ppermute | solution.py:265
  354.2 17.2 %collective-permute-start.61 = (f32[64,2048]{1,0:T(8,128)S(1)}, f32[64,2048]{1,0:T(8,128)S(1)}, u32[]{:S(2)}, u32[]{:S(2)}) collective-permute-start(f32[64,2048]{1,0:T(8,128)S(1)} %maximum_maximum_fusion), channel_id=1, source_target_pairs={{0,2},{2,0},{4,6},{6,4},{8,10},{10,8},{12,14},{14,12},{16,18},{18,... | collective-permute-start | bytes 1572872 | tf_op jit(solution)/shard_map/ppermute | solution.py:265
  356.9 4.3 %collective-permute-start.60 = (f32[12,1024]{1,0:T(8,128)S(1)}, f32[12,1024]{1,0:T(8,128)S(1)}, u32[]{:S(2)}, u32[]{:S(2)}) collective-permute-start(f32[12,1024]{1,0:T(8,128)S(1)} %add.363), channel_id=1, source_target_pairs={{0,1},{1,0},{2,3},{3,2},{4,5},{5,4},{6,7},{7,6},{8,9},{9,8},{10,11... | collective-permute-start | bytes 147464 | tf_op jit(solution)/shard_map/ppermute | solution.py:265
  371.5 9.5 %collective-permute-start.65 = (f32[12,1024]{1,0:T(8,128)S(1)}, f32[12,1024]{1,0:T(8,128)S(1)}, u32[]{:S(2)}, u32[]{:S(2)}) collective-permute-start(f32[12,1024]{1,0:T(8,128)S(1)} %add.364), channel_id=1, source_target_pairs={{0,24},{2,26},{4,28},{6,30},{8,16},{10,18},{12,20},{14,22},{16,8},... | collective-permute-start | bytes 147464 | tf_op jit(solution)/shard_map/ppermute | solution.py:265
  373.9 9.0 %collective-permute-start.64 = (f32[12,1024]{1,0:T(8,128)S(1)}, f32[12,1024]{1,0:T(8,128)S(1)}, u32[]{:S(2)}, u32[]{:S(2)}) collective-permute-start(f32[12,1024]{1,0:T(8,128)S(1)} %add.364), channel_id=1, source_target_pairs={{0,16},{2,18},{4,20},{6,22},{8,24},{10,26},{12,28},{14,30},{16,0},... | collective-permute-start | bytes 147464 | tf_op jit(solution)/shard_map/ppermute | solution.py:265
  379.2 4.3 %collective-permute-start.63 = (f32[12,1024]{1,0:T(8,128)S(1)}, f32[12,1024]{1,0:T(8,128)S(1)}, u32[]{:S(2)}, u32[]{:S(2)}) collective-permute-start(f32[12,1024]{1,0:T(8,128)S(1)} %add.364), channel_id=1, source_target_pairs={{0,8},{2,10},{4,12},{6,14},{8,0},{10,2},{12,4},{14,6},{16,24},{18,... | collective-permute-start | bytes 147464 | tf_op jit(solution)/shard_map/ppermute | solution.py:265
  379.3 6.1 %collective-permute-start.62 = (f32[64,1024]{1,0:T(8,128)S(1)}, f32[64,1024]{1,0:T(8,128)S(1)}, u32[]{:S(2)}, u32[]{:S(2)}) collective-permute-start(f32[64,1024]{1,0:T(8,128)S(1)} %pad_maximum_fusion.31), channel_id=1, source_target_pairs={{0,2},{2,0},{4,6},{6,4},{8,10},{10,8},{12,14},{14,12},{16,18},{18,... | collective-permute-start | bytes 786440 | tf_op jit(solution)/shard_map/ppermute | solution.py:265
  (66 other events, 607.8 us)

commit v4 on v3

--- a/solution.py
+++ b/solution.py
@@ -403,7 +403,8 @@
 
 
 def sum_near(array):
-    return (array + over_z(array, 1)) + (over_z(array, 2) + over_z(array, 3))
+    array = array + over_z(array, 1)
+    return array + over_z(array, 2)
 
 
 def head_scores(queries, key_rows, same_doc):
@@ -928,7 +929,6 @@
     grad_one, d_gain_one, d_offset_one = norm_backward(
         mlp_back + grad_two, scaled_one, spread_one, ln1_gain
     )
-    d_bias_out = jnp.sum(grad_one, axis=0)
     grad_one_low = grad_one.astype(low)
     up_sum = grad_parts([(h_low, h_other, d_up[0], up_other)])
     (d_ctx,) = expand_rows(
@@ -953,7 +953,10 @@
             (grad_one_low, grad_one_other, context[0], context_other),
         ]
     )
-    down_sum, up_sum, last_sum, d_qkv = after((down_sum, up_sum, last_sum, d_qkv))
+    down_sum, up_sum, last_sum, d_qkv, grad_one, d_gain_one = after(
+        (down_sum, up_sum, last_sum, d_qkv, grad_one, d_gain_one)
+    )
+    d_bias_out = jnp.sum(grad_one, axis=0)
     up_sum, last_sum = scatter_both(up_sum, last_sum)
     down_sum = scatter_near(down_sum)
     narrow = jnp.dot(
@@ -995,16 +998,15 @@
     output = outer_cols(output_low, order).astype(low)
     up_sum, last_sum, small, down_sum = after((up_sum, last_sum, small, down_sum))
     last_sum = scatter_near(last_sum)
-    small = sum_chips(small)
+    small = sum_near(sum_chips(small))
     pairs = scatter_last([down_sum, up_sum], core_index)
-    last_sum, small, pairs = after((last_sum, small, pairs))
-    small = sum_near(small)
-    pairs = pairs + scatter_last([last_sum], core_index)
     grad_w_down = jnp.concatenate(pairs[0], axis=1).T
     grad_w_up = jnp.concatenate(pairs[1], axis=1)
+    last_sum, small, grad_w_down, grad_w_up = after((last_sum, small, grad_w_down, grad_w_up))
+    last_pair = scatter_last([last_sum], core_index)[0]
     size = head_width // 2
     parts = [
-        jnp.concatenate([part[:, at * size :][:, :size] for part in pairs[2]], axis=1) for at in range(4)
+        jnp.concatenate([part[:, at * size :][:, :size] for part in last_pair], axis=1) for at in range(4)
     ]
     grad_w_qkv = jnp.stack(parts[:3])
     grad_w_out = parts[3].T

time: 392 us -> 389 us (level)
  starting transfers between devices: 64.4 us -> 58.8 us
    ppermute x66 -> x65, starting transfers between devices: 64.4 us -> 58.8 us  [swap(): lax.ppermute(array, name, [(index, index ^ mask) for index in range(size)])]
    unnamed x141 -> x139, local copies, waits for them, and re-layouts: 15.1 us -> 13.7 us
    ppermute x66 -> x65, waiting for transfers between devices: 136 us -> 137 us  [swap(): lax.ppermute(array, name, [(index, index ^ mask) for index in range(size)])]
  transfers between devices with their start and end apart: 66 -> 65, of which waited for: 28 -> 25; matrix products, arithmetic and copies ran while one was open for 10% -> 11% of each run, Pallas kernels for 25% -> 25%
where the time goes in v4:
time: 389 us; the launch traced here: 384 us
  waiting for transfers between devices  137 us (35%)
  Pallas kernels  114 us (29%)
  starting transfers between devices  58.8 us (15%)
  other arithmetic  37.4 us (10%)
  local copies, waits for them, and re-layouts  20.3 us (5%)
  matrix products  13.7 us (4%)
    ppermute x65, waiting for transfers between devices, swap(): lax.ppermute(array, name, [(index, index ^ mask) for index in range(size)])  137 us
    pallas_call x10, Pallas kernels, call_kernel(): pl.pallas_call(kernel, grid_spec=pltpu.PrefetchScalarGridSpec(num_scalar_...  93.8 us
    ppermute x65, starting transfers between devices, swap(): lax.ppermute(array, name, [(index, index ^ mask) for index in range(size)])  58.8 us
    pallas_call x3, Pallas kernels, grad_parts(): pl.pallas_call(kernel, grid=(2,), in_specs=in_specs, out_specs=[y_spec, y...  20.3 us
    unnamed x139, local copies, waits for them, and re-layouts  13.7 us
    convert_element_type x10, other arithmetic, add_low(): (left.astype(jnp.float32) + right.astype(jnp.float32)).astype(jnp.bfloat16)  11.5 us
    concatenate x10, other arithmetic, beside(): return jnp.concatenate([left, right])  8.2 us
  transfers between devices with their start and end apart: 65, of which 25 were waited for; matrix products, arithmetic and copies ran while one was open for 11% of the time, Pallas kernels for 25%

profile of v4, /device:TPU:0, one launch (start us, length us, event | category | flops | bytes accessed | tf_op | source)
XLA Modules:
  0.0 384.4 jit_solution(5107713950176345853)
XLA Ops:
  1.8 3.1 collective-permute-start.3
  5.8 2.5 collective-permute-start.2
  8.5 1.7 collective-permute-start
  10.3 10.0 %collective-permute-done.2 = bf16[64,1536]{1,0:T(8,128)(2,1)S(1)} collective-permute-done((bf16[64,1536]{1,0:T(8,128)(2,1)S(1)}, bf16[64,1536]{1,0:T(8,128)(2,1)S(1)}, u32[]{:S(2)}, u32[]{:S(2)}) %collective-permute-start.2) | collective-permute-done | bytes 196640 | tf_op jit(solution)/shard_map/ppermute | solution.py:265
  20.2 5.5 %collective-permute-done.1 = bf16[64,1536]{1,0:T(8,128)(2,1)S(1)} collective-permute-done((bf16[64,1536]{1,0:T(8,128)(2,1)S(1)}, bf16[64,1536]{1,0:T(8,128)(2,1)S(1)}, u32[]{:S(2)}, u32[]{:S(2)}) %collective-permute-start.1) | collective-permute-done | bytes 196640 | tf_op jit(solution)/shard_map/ppermute | solution.py:265
  25.8 1.6 collective-permute-start.4
  27.4 1.6 collective-permute-start.5
  29.0 2.3 collective-permute-start.6
  31.3 1.5 collective-permute-start.7
  32.8 9.7 %collective-permute-done.7 = bf16[64,2048]{1,0:T(8,128)(2,1)} collective-permute-done((bf16[64,2048]{1,0:T(8,128)(2,1)S(1)}, bf16[64,2048]{1,0:T(8,128)(2,1)}, u32[]{:S(2)}, u32[]{:S(2)}) %collective-permute-start.7) | collective-permute-done | bytes 262176 | tf_op jit(solution)/shard_map/ppermute | solution.py:265
  42.5 2.5 collective-permute-done.6
  46.5 17.3 %collective-permute-done.12 = bf16[64,2560]{1,0:T(8,128)(2,1)S(1)} collective-permute-done((bf16[64,2560]{1,0:T(8,128)(2,1)S(1)}, bf16[64,2560]{1,0:T(8,128)(2,1)S(1)}, u32[]{:S(2)}, u32[]{:S(2)}) %collective-permute-start.12) | collective-permute-done | bytes 327712 | tf_op jit(solution)/shard_map/ppermute | solution.py:265
  70.8 13.4 %collective-permute-done.17 = bf16[64,2048]{1,0:T(8,128)(2,1)S(1)} collective-permute-done((bf16[64,2048]{1,0:T(8,128)(2,1)S(1)}, bf16[64,2048]{1,0:T(8,128)(2,1)S(1)}, u32[]{:S(2)}, u32[]{:S(2)}) %collective-permute-start.17) | collective-permute-done | bytes 262176 | tf_op jit(solution)/shard_map/ppermute | solution.py:265
  84.2 1.9 collective-permute-done.16
  93.6 6.8 %shard_map.254.q_ref.k_ref.v_ref = bf16[512,3072]{1,0:T(8,128)(2,1)S(1)} custom-call(s32[1]{0:T(128)} %constant.124.clone.1.core_ref, bf16[512,1024]{1,0:T(8,128)(2,1)S(1)} %fusion.19.rows_ref.refs_0_, bf16[256,1536]{1,0:T(8,128)(2,1)S(1)} %copy-done.7, bf16[256,1536]{1,0:T(8,128)(2,1)} %collective-permute-done.8.refs_1_, ...), custom_call_target="tpu_custom_call" | custom-call | tf_op jit(solution)/shard_map/pallas_call | solution.py:512
  100.4 13.4 %shard_map.255 = (bf16[512,512]{1,0:T(8,128)(2,1)S(1)}, bf16[512,512]{1,0:T(8,128)(2,1)S(1)}, f32[512,1024]{1,0:T(8,128)S(1)}) custom-call(s32[1]{0:T(128)} %bitcast.5.core_ref, bf16[512,3072]{1,0:T(8,128)(2,1)S(1)} %shard_map.254.q_ref.k_ref.v_ref, bf16[512,3072]{1,0:T(8,128)(2,1)S(1)} %shard_map.254.q_ref.k_ref.v_ref, ...), custom_call_target="tpu_custom_call" | custom-call | tf_op jit(solution)/shard_map/pallas_call | solution.py:512
  113.9 5.9 %collective-permute-done.19.refs_3_ = bf16[256,2560]{1,0:T(8,128)(2,1)S(1)} collective-permute-done((bf16[256,2560]{1,0:T(8,128)(2,1)S(1)}, bf16[256,2560]{1,0:T(8,128)(2,1)S(1)}, u32[]{:S(2)}, u32[]{:S(2)}) %collective-permute-start.19) | collective-permute-done | bytes 1310752 | tf_op jit(solution)/shard_map/ppermute | solution.py:265
  119.7 2.0 collective-permute-done.18.refs_1_
  127.6 9.8 %collective-permute-done.25 = bf16[128,2048]{1,0:T(8,128)(2,1)S(1)} collective-permute-done((bf16[128,2048]{1,0:T(8,128)(2,1)S(1)}, bf16[128,2048]{1,0:T(8,128)(2,1)S(1)}, u32[]{:S(2)}, u32[]{:S(2)}) %collective-permute-start.25) | collective-permute-done | bytes 524320 | tf_op jit(solution)/shard_map/ppermute | solution.py:265
  140.9 3.0 shard_map.256
  144.8 1.9 fusion.52
  146.7 11.9 %shard_map.257 = (bf16[512,2048]{1,0:T(8,128)(2,1)S(1)}, bf16[512,2048]{1,0:T(8,128)(2,1)}, bf16[512,2048]{1,0:T(8,128)(2,1)S(1)}, bf16[512,2048]{1,0:T(8,128)(2,1)S(1)}) custom-call(s32[1]{0:T(128)} %bitcast.5.core_ref, bf16[512,1024]{1,0:T(8,128)(2,1)S(1)} %get-tuple-element.305.rows_ref.refs_0_, ...), custom_call_target="tpu_custom_call" | custom-call | tf_op jit(solution)/shard_map/pallas_call | solution.py:512
  160.1 4.2 %collective-permute-done.28.refs_3_ = bf16[256,2048]{1,0:T(8,128)(2,1)S(1)} collective-permute-done((bf16[256,2048]{1,0:T(8,128)(2,1)S(1)}, bf16[256,2048]{1,0:T(8,128)(2,1)S(1)}, u32[]{:S(2)}, u32[]{:S(2)}) %collective-permute-start.28) | collective-permute-done | bytes 1048608 | tf_op jit(solution)/shard_map/ppermute | solution.py:265
  165.8 2.1 collective-permute-done.31.refs_5_
  167.9 1.5 collective-permute-done.32.refs_7_
  169.4 8.0 %shard_map.258 = f32[512,1024]{1,0:T(8,128)S(1)} custom-call(s32[1]{0:T(128)} %bitcast.5.core_ref, bf16[512,2048]{1,0:T(8,128)(2,1)S(1)} %get-tuple-element.298.own_ref.refs_2_, bf16[512,2048]{1,0:T(8,128)(2,1)} %get-tuple-element.289.send_ref, bf16[256,2048]{1,0:T(8,128)(2,1)S(1)} %constant_dynamic-update-slice_fusion.9.refs_0_, ...), custom_call_target="tpu_custom_call" | custom-call | tf_op jit(solution)/shard_map/pallas_call | solution.py:512
  178.2 2.8 fusion.7
  184.0 8.0 %shard_map.259 = (bf16[512,2048]{1,0:T(8,128)(2,1)S(1)}, bf16[512,2048]{1,0:T(8,128)(2,1)S(1)}, f32[1,4096]{1,0:T(1,128)S(1)}) custom-call(s32[1]{0:T(128)} %bitcast.5.core_ref, bf16[512,1024]{1,0:T(8,128)(2,1)S(1)} %convert_element_type.291.rows_ref.refs_0_, bf16[256,2048]{1,0:T(8,128)(2,1)S(1)} %constant_dynamic-update-slice_fusion.9.refs_0_, ...), custom_call_target="tpu_custom_call" | custom-call | tf_op jit(solution)/shard_map/pallas_call | solution.py:512
  194.4 1.6 copy-done.22
  195.9 5.8 %shard_map.260 = (bf16[512,1024]{1,0:T(8,128)(2,1)S(1)}, bf16[512,1024]{1,0:T(8,128)(2,1)S(1)}, bf16[512,1024]{1,0:T(8,128)(2,1)S(1)}, bf16[512,1024]{1,0:T(8,128)(2,1)S(1)}) custom-call(bf16[512,1024]{1,0:T(8,128)(2,1)S(1)} %convert_element_type.291.rows_ref.refs_0_, bf16[512,1024]{1,0:T(8,128)(2,1)S(1)} %collective-permute-done.33.refs_1_, ...), custom_call_target="tpu_custom_call" | custom-call | tf_op jit(solution)/shard_map/pallas_call | solution.py:746
  205.2 8.1 %shard_map.262 = f32[512,1024]{1,0:T(8,128)S(1)} custom-call(s32[1]{0:T(128)} %bitcast.5.core_ref, bf16[512,2048]{1,0:T(8,128)(2,1)S(1)} %get-tuple-element.314.refs_2_.own_ref, bf16[512,2048]{1,0:T(8,128)(2,1)S(1)} %get-tuple-element.321.send_ref, bf16[256,2560]{1,0:T(8,128)(2,1)S(1)} %constant_dynamic-update-slice_fusion.4.refs_0_, ...), custom_call_target="tpu_custom_call" | custom-call | tf_op jit(solution)/shard_map/pallas_call | solution.py:512
  214.3 1.8 fusion.50
  216.1 2.6 shard_map.263.dctx_ref
  218.7 5.8 %shard_map.261 = (bf16[512,1024]{1,0:T(8,128)(2,1)S(1)}, bf16[512,1024]{1,0:T(8,128)(2,1)S(1)}, bf16[512,1024]{1,0:T(8,128)(2,1)S(1)}, bf16[512,1024]{1,0:T(8,128)(2,1)S(1)}) custom-call(bf16[512,1024]{1,0:T(8,128)(2,1)S(1)} %get-tuple-element.305.rows_ref.refs_0_, bf16[512,1024]{1,0:T(8,128)(2,1)S(1)} %collective-permute-done.36.refs_1_, ...), custom_call_target="tpu_custom_call" | custom-call | tf_op jit(solution)/shard_map/pallas_call | solution.py:746
  224.5 3.3 collective-permute-done.39
  233.5 1.7 reduce_sum.139
  235.3 1.6 pad_maximum_fusion
  237.0 1.6 collective-permute-start.41
  239.8 1.6 copy-done.24
  241.4 21.3 %shard_map.264 = (bf16[512,1536]{1,0:T(8,128)(2,1)S(1)}, bf16[512,1536]{1,0:T(8,128)(2,1)S(1)}, f32[1,1536]{1,0:T(1,128)S(1)}, f32[1,1536]{1,0:T(1,128)S(1)}) custom-call(s32[1]{0:T(128)} %bitcast.5.core_ref, bf16[512,3072]{1,0:T(8,128)(2,1)S(1)} %copy-done.3, bf16[512,3072]{1,0:T(8,128)(2,1)S(1)} %copy-done.3, bf16[512,3072]{1,0:T(8,128)(2,1)S(1)} %copy-done.3, ...), custom_call_target="tpu_custom_call" | custom-call | tf_op jit(solution)/shard_map/pallas_call | solution.py:512
  263.4 5.0 %collective-permute-done.42 = bf16[768,1024]{1,0:T(8,128)(2,1)} collective-permute-done((bf16[768,1024]{1,0:T(8,128)(2,1)}, bf16[768,1024]{1,0:T(8,128)(2,1)}, u32[]{:S(2)}, u32[]{:S(2)}) %collective-permute-start.42) | collective-permute-done | bytes 1572896 | tf_op jit(solution)/shard_map/ppermute | solution.py:265
  268.4 1.6 add_convert_fusion.21
  272.4 1.5 add_convert_fusion.7
  273.9 8.7 %shard_map.265 = (bf16[512,1024]{1,0:T(8,128)(2,1)S(1)}, bf16[512,1024]{1,0:T(8,128)(2,1)S(1)}, bf16[512,1024]{1,0:T(8,128)(2,1)S(1)}, bf16[512,1024]{1,0:T(8,128)(2,1)S(1)}) custom-call(bf16[512,1024]{1,0:T(8,128)(2,1)S(1)} %fusion.19.rows_ref.refs_0_, bf16[512,1024]{1,0:T(8,128)(2,1)S(1)} %copy-done.41, ...), custom_call_target="tpu_custom_call" | custom-call | tf_op jit(solution)/shard_map/pallas_call | solution.py:746
  288.0 2.8 collective-permute-start.46
  290.9 1.7 collective-permute-start.47
  292.6 1.8 reduce_sum.135
  294.4 1.9 fusion
  296.5 12.1 %collective-permute-done.46 = bf16[128,1024]{1,0:T(8,128)(2,1)S(1)} collective-permute-done((bf16[128,1024]{1,0:T(8,128)(2,1)S(1)}, bf16[128,1024]{1,0:T(8,128)(2,1)S(1)}, u32[]{:S(2)}, u32[]{:S(2)}) %collective-permute-start.46) | collective-permute-done | bytes 262176 | tf_op jit(solution)/shard_map/ppermute | solution.py:265
  309.6 9.3 %collective-permute-done.49 = bf16[768,1024]{1,0:T(8,128)(2,1)} collective-permute-done((bf16[768,1024]{1,0:T(8,128)(2,1)}, bf16[768,1024]{1,0:T(8,128)(2,1)}, u32[]{:S(2)}, u32[]{:S(2)}) %collective-permute-start.49) | collective-permute-done | bytes 1572896 | tf_op jit(solution)/shard_map/ppermute | solution.py:265
  318.9 1.6 add_convert_fusion.17
  322.0 2.2 add_convert_fusion.3
  325.4 2.0 collective-permute-start.51
  327.5 1.5 collective-permute-start.52
  331.6 10.6 %shard_map.266 = f32[512,1024]{1,0:T(8,128)S(1)} custom-call(s32[1]{0:T(128)} %bitcast.5.core_ref, bf16[512,1536]{1,0:T(8,128)(2,1)S(1)} %copy-done.5, bf16[512,1536]{1,0:T(8,128)(2,1)S(1)} %copy-done.30, bf16[256,1536]{1,0:T(8,128)(2,1)S(1)} %copy-done.8, bf16[256,1536]{1,0:T(8,128)(2,1)} %collective-permute-done.8.refs_1_, ...), custom_call_target="tpu_custom_call" | custom-call | tf_op jit(solution)/shard_map/pallas_call | solution.py:512
  343.6 2.7 fusion.16
  347.1 2.4 collective-permute-start.55
  350.5 1.6 collective-permute-start.57
  352.1 1.6 collective-permute-start.59
  353.7 2.7 collective-permute-done.59
  357.5 3.2 collective-permute-done.60
  362.0 8.9 %collective-permute-done.61 = f32[12,1024]{1,0:T(8,128)S(1)} collective-permute-done((f32[12,1024]{1,0:T(8,128)S(1)}, f32[12,1024]{1,0:T(8,128)S(1)}, u32[]{:S(2)}, u32[]{:S(2)}) %collective-permute-start.61) | collective-permute-done | bytes 49184 | tf_op jit(solution)/shard_map/ppermute | solution.py:265
  371.8 2.3 fusion.18
  374.1 4.5 %collective-permute-done.62 = f32[12,1024]{1,0:T(8,128)S(1)} collective-permute-done((f32[12,1024]{1,0:T(8,128)S(1)}, f32[12,1024]{1,0:T(8,128)S(1)}, u32[]{:S(2)}, u32[]{:S(2)}) %collective-permute-start.62) | collective-permute-done | bytes 49184 | tf_op jit(solution)/shard_map/ppermute | solution.py:265
  (354 shorter events, 75.0 us)
Async XLA Ops:
  1.8 24.0 %collective-permute-start.3 = (bf16[64,2560]{1,0:T(8,128)(2,1)S(1)}, bf16[64,2560]{1,0:T(8,128)(2,1)S(1)}, u32[]{:S(2)}, u32[]{:S(2)}) collective-permute-start(bf16[64,2560]{1,0:T(8,128)(2,1)S(1)} %pad_maximum_fusion.18), channel_id=1, source_target_pairs={{0,8},{2,10},{4,12},{6,14},{8,0},{10,2},{12,4},{14,6},{16,24},{18,... | collective-permute-start | bytes 983048 | tf_op jit(solution)/shard_map/ppermute | solution.py:265
  5.8 14.4 %collective-permute-start.2 = (bf16[64,1536]{1,0:T(8,128)(2,1)S(1)}, bf16[64,1536]{1,0:T(8,128)(2,1)S(1)}, u32[]{:S(2)}, u32[]{:S(2)}) collective-permute-start(bf16[64,1536]{1,0:T(8,128)(2,1)S(1)} %pad_maximum_fusion.32), channel_id=1, source_target_pairs={{0,24},{2,26},{4,28},{6,30},{8,16},{10,18},{12,20},{14,22},{16,8},... | collective-permute-start | bytes 589832 | tf_op jit(solution)/shard_map/ppermute | solution.py:265
  8.3 17.4 %collective-permute-start.1 = (bf16[64,1536]{1,0:T(8,128)(2,1)S(1)}, bf16[64,1536]{1,0:T(8,128)(2,1)S(1)}, u32[]{:S(2)}, u32[]{:S(2)}) collective-permute-start(bf16[64,1536]{1,0:T(8,128)(2,1)S(1)} %pad_maximum_fusion.32), channel_id=1, source_target_pairs={{0,16},{2,18},{4,20},{6,22},{8,24},{10,26},{12,28},{14,30},{16,0},... | collective-permute-start | bytes 589832 | tf_op jit(solution)/shard_map/ppermute | solution.py:265
  8.5 17.2 %collective-permute-start = (bf16[64,1536]{1,0:T(8,128)(2,1)S(1)}, bf16[64,1536]{1,0:T(8,128)(2,1)S(1)}, u32[]{:S(2)}, u32[]{:S(2)}) collective-permute-start(bf16[64,1536]{1,0:T(8,128)(2,1)S(1)} %pad_maximum_fusion.32), channel_id=1, source_target_pairs={{0,8},{2,10},{4,12},{6,14},{8,0},{10,2},{12,4},{14,6},{16,24},{18,... | collective-permute-start | bytes 589832 | tf_op jit(solution)/shard_map/ppermute | solution.py:265
  25.8 19.1 %collective-permute-start.4 = (bf16[128,1536]{1,0:T(8,128)(2,1)S(1)}, bf16[128,1536]{1,0:T(8,128)(2,1)S(1)}, u32[]{:S(2)}, u32[]{:S(2)}) collective-permute-start(bf16[128,1536]{1,0:T(8,128)(2,1)S(1)} %pad_maximum_fusion.15), channel_id=1, source_target_pairs={{0,4},{2,6},{4,0},{6,2},{8,12},{10,14},{12,8},{14,10},{16,20},{18,... | collective-permute-start | bytes 1179656 | tf_op jit(solution)/shard_map/ppermute | solution.py:265
  27.4 17.5 %collective-permute-start.5 = (bf16[128,1536]{1,0:T(8,128)(2,1)S(1)}, bf16[128,1536]{1,0:T(8,128)(2,1)S(1)}, u32[]{:S(2)}, u32[]{:S(2)}) collective-permute-start(bf16[128,1536]{1,0:T(8,128)(2,1)S(1)} %pad_maximum_fusion.16), channel_id=1, source_target_pairs={{0,1},{1,0},{2,3},{3,2},{4,5},{5,4},{6,7},{7,6},{8,9},{9,8},{10,11... | collective-permute-start | bytes 1179656 | tf_op jit(solution)/shard_map/ppermute | solution.py:265
  29.0 15.9 %collective-permute-start.6 = (bf16[64,2560]{1,0:T(8,128)(2,1)S(1)}, bf16[64,2560]{1,0:T(8,128)(2,1)S(1)}, u32[]{:S(2)}, u32[]{:S(2)}) collective-permute-start(bf16[64,2560]{1,0:T(8,128)(2,1)S(1)} %pad_maximum_fusion.18), channel_id=1, source_target_pairs={{0,16},{2,18},{4,20},{6,22},{8,24},{10,26},{12,28},{14,30},{16,0},... | collective-permute-start | bytes 983048 | tf_op jit(solution)/shard_map/ppermute | solution.py:265
  31.3 11.2 %collective-permute-start.7 = (bf16[64,2048]{1,0:T(8,128)(2,1)S(1)}, bf16[64,2048]{1,0:T(8,128)(2,1)}, u32[]{:S(2)}, u32[]{:S(2)}) collective-permute-start(bf16[64,2048]{1,0:T(8,128)(2,1)S(1)} %bitcast.199), channel_id=1, source_target_pairs={{0,8},{2,10},{4,12},{6,14},{8,0},{10,2},{12,4},{14,6},{16,24},{18,... | collective-permute-start | bytes 786440 | tf_op jit(solution)/shard_map/ppermute | solution.py:265
  45.0 18.8 %collective-permute-start.11 = (bf16[256,1536]{1,0:T(8,128)(2,1)S(1)}, bf16[256,1536]{1,0:T(8,128)(2,1)S(1)}, u32[]{:S(2)}, u32[]{:S(2)}) collective-permute-start(bf16[256,1536]{1,0:T(8,128)(2,1)S(1)} %constant_dynamic-update-slice_fusion.2.refs_2_), channel_id=1, source_target_pairs={{0,2},{2,0},{4,6},{6,4},{8,10},{10,8},{12,14},{14,12},{16,18},{18,... | collective-permute-start | bytes 2359304 | tf_op jit(solution)/shard_map/ppermute | solution.py:265
  45.1 20.1 %collective-permute-start.9 = (bf16[256,1536]{1,0:T(8,128)(2,1)S(1)}, bf16[256,1536]{1,0:T(8,128)(2,1)}, u32[]{:S(2)}, u32[]{:S(2)}) collective-permute-start(bf16[256,1536]{1,0:T(8,128)(2,1)S(1)} %constant_dynamic-update-slice_fusion.2.refs_2_), channel_id=1, source_target_pairs={{0,4},{2,6},{4,0},{6,2},{8,12},{10,14},{12,8},{14,10},{16,20},{18,... | collective-permute-start | bytes 2359304 | tf_op jit(solution)/shard_map/ppermute | solution.py:265
  45.8 19.4 %collective-permute-start.10 = (bf16[256,1536]{1,0:T(8,128)(2,1)S(1)}, bf16[256,1536]{1,0:T(8,128)(2,1)S(1)}, u32[]{:S(2)}, u32[]{:S(2)}) collective-permute-start(bf16[256,1536]{1,0:T(8,128)(2,1)S(1)} %constant_dynamic-update-slice_fusion.refs_0_), channel_id=1, source_target_pairs={{0,2},{2,0},{4,6},{6,4},{8,10},{10,8},{12,14},{14,12},{16,18},{18,... | collective-permute-start | bytes 2359304 | tf_op jit(solution)/shard_map/ppermute | solution.py:265
  46.0 20.1 %collective-permute-start.8 = (bf16[256,1536]{1,0:T(8,128)(2,1)S(1)}, bf16[256,1536]{1,0:T(8,128)(2,1)}, u32[]{:S(2)}, u32[]{:S(2)}) collective-permute-start(bf16[256,1536]{1,0:T(8,128)(2,1)S(1)} %constant_dynamic-update-slice_fusion.refs_0_), channel_id=1, source_target_pairs={{0,1},{1,0},{2,3},{3,2},{4,5},{5,4},{6,7},{7,6},{8,9},{9,8},{10,11... | collective-permute-start | bytes 2359304 | tf_op jit(solution)/shard_map/ppermute | solution.py:265
  46.5 17.3 %collective-permute-start.12 = (bf16[64,2560]{1,0:T(8,128)(2,1)S(1)}, bf16[64,2560]{1,0:T(8,128)(2,1)S(1)}, u32[]{:S(2)}, u32[]{:S(2)}) collective-permute-start(bf16[64,2560]{1,0:T(8,128)(2,1)S(1)} %collective-permute-done.3), channel_id=1, source_target_pairs={{0,16},{2,18},{4,20},{6,22},{8,24},{10,26},{12,28},{14,30},{16,0},... | collective-permute-start | bytes 983048 | tf_op jit(solution)/shard_map/ppermute | solution.py:265
  66.3 17.8 %collective-permute-start.15 = (bf16[128,2560]{1,0:T(8,128)(2,1)S(1)}, bf16[128,2560]{1,0:T(8,128)(2,1)}, u32[]{:S(2)}, u32[]{:S(2)}) collective-permute-start(bf16[128,2560]{1,0:T(8,128)(2,1)S(1)} %pad_maximum_fusion.4), channel_id=1, source_target_pairs={{0,4},{2,6},{4,0},{6,2},{8,12},{10,14},{12,8},{14,10},{16,20},{18,... | collective-permute-start | bytes 1966088 | tf_op jit(solution)/shard_map/ppermute | solution.py:265
  67.7 18.4 %collective-permute-start.13 = (bf16[256,1536]{1,0:T(8,128)(2,1)}, bf16[256,1536]{1,0:T(8,128)(2,1)}, u32[]{:S(2)}, u32[]{:S(2)}) collective-permute-start(bf16[256,1536]{1,0:T(8,128)(2,1)} %collective-permute-done.8.refs_1_), channel_id=1, source_target_pairs={{0,2},{2,0},{4,6},{6,4},{8,10},{10,8},{12,14},{14,12},{16,18},{18,... | collective-permute-start | bytes 2359304 | tf_op jit(solution)/shard_map/ppermute | solution.py:265
  67.7 18.4 %collective-permute-start.14 = (bf16[256,1536]{1,0:T(8,128)(2,1)}, bf16[256,1536]{1,0:T(8,128)(2,1)}, u32[]{:S(2)}, u32[]{:S(2)}) collective-permute-start(bf16[256,1536]{1,0:T(8,128)(2,1)} %collective-permute-done.9.refs_3_), channel_id=1, source_target_pairs={{0,2},{2,0},{4,6},{6,4},{8,10},{10,8},{12,14},{14,12},{16,18},{18,... | collective-permute-start | bytes 2359304 | tf_op jit(solution)/shard_map/ppermute | solution.py:265
  69.1 17.0 %collective-permute-start.16 = (bf16[128,2560]{1,0:T(8,128)(2,1)}, bf16[128,2560]{1,0:T(8,128)(2,1)}, u32[]{:S(2)}, u32[]{:S(2)}) collective-permute-start(bf16[128,2560]{1,0:T(8,128)(2,1)} %pad_maximum_fusion.5), channel_id=1, source_target_pairs={{0,1},{1,0},{2,3},{3,2},{4,5},{5,4},{6,7},{7,6},{8,9},{9,8},{10,11... | collective-permute-start | bytes 1966088 | tf_op jit(solution)/shard_map/ppermute | solution.py:265
  70.7 13.5 %collective-permute-start.17 = (bf16[64,2048]{1,0:T(8,128)(2,1)S(1)}, bf16[64,2048]{1,0:T(8,128)(2,1)S(1)}, u32[]{:S(2)}, u32[]{:S(2)}) collective-permute-start(bf16[64,2048]{1,0:T(8,128)(2,1)S(1)} %bitcast.200), channel_id=1, source_target_pairs={{0,16},{2,18},{4,20},{6,22},{8,24},{10,26},{12,28},{14,30},{16,0},... | collective-permute-start | bytes 786440 | tf_op jit(solution)/shard_map/ppermute | solution.py:265
  88.5 25.4 %collective-permute-start.21 = (bf16[256,2560]{1,0:T(8,128)(2,1)S(1)}, bf16[256,2560]{1,0:T(8,128)(2,1)S(1)}, u32[]{:S(2)}, u32[]{:S(2)}) collective-permute-start(bf16[256,2560]{1,0:T(8,128)(2,1)S(1)} %constant_dynamic-update-slice_fusion.6.refs_2_), channel_id=1, source_target_pairs={{0,2},{2,0},{4,6},{6,4},{8,10},{10,8},{12,14},{14,12},{16,18},{18,... | collective-permute-start | bytes 3932168 | tf_op jit(solution)/shard_map/ppermute | solution.py:265
  88.5 31.2 %collective-permute-start.19 = (bf16[256,2560]{1,0:T(8,128)(2,1)S(1)}, bf16[256,2560]{1,0:T(8,128)(2,1)S(1)}, u32[]{:S(2)}, u32[]{:S(2)}) collective-permute-start(bf16[256,2560]{1,0:T(8,128)(2,1)S(1)} %constant_dynamic-update-slice_fusion.6.refs_2_), channel_id=1, source_target_pairs={{0,4},{2,6},{4,0},{6,2},{8,12},{10,14},{12,8},{14,10},{16,20},{18,... | collective-permute-start | bytes 3932168 | tf_op jit(solution)/shard_map/ppermute | solution.py:265
  90.5 29.2 %collective-permute-start.20 = (bf16[256,2560]{1,0:T(8,128)(2,1)S(1)}, bf16[256,2560]{1,0:T(8,128)(2,1)S(1)}, u32[]{:S(2)}, u32[]{:S(2)}) collective-permute-start(bf16[256,2560]{1,0:T(8,128)(2,1)S(1)} %constant_dynamic-update-slice_fusion.4.refs_0_), channel_id=1, source_target_pairs={{0,2},{2,0},{4,6},{6,4},{8,10},{10,8},{12,14},{14,12},{16,18},{18,... | collective-permute-start | bytes 3932168 | tf_op jit(solution)/shard_map/ppermute | solution.py:265
  90.7 31.0 %collective-permute-start.18 = (bf16[256,2560]{1,0:T(8,128)(2,1)S(1)}, bf16[256,2560]{1,0:T(8,128)(2,1)S(1)}, u32[]{:S(2)}, u32[]{:S(2)}) collective-permute-start(bf16[256,2560]{1,0:T(8,128)(2,1)S(1)} %constant_dynamic-update-slice_fusion.4.refs_0_), channel_id=1, source_target_pairs={{0,1},{1,0},{2,3},{3,2},{4,5},{5,4},{6,7},{7,6},{8,9},{9,8},{10,11... | collective-permute-start | bytes 3932168 | tf_op jit(solution)/shard_map/ppermute | solution.py:265
  92.0 21.9 %collective-permute-start.22 = (bf16[64,2048]{1,0:T(8,128)(2,1)}, bf16[64,2048]{1,0:T(8,128)(2,1)S(1)}, u32[]{:S(2)}, u32[]{:S(2)}) collective-permute-start(bf16[64,2048]{1,0:T(8,128)(2,1)} %collective-permute-done.7), channel_id=1, source_target_pairs={{0,16},{2,18},{4,20},{6,22},{8,24},{10,26},{12,28},{14,30},{16,0},... | collective-permute-start | bytes 786440 | tf_op jit(solution)/shard_map/ppermute | solution.py:265
  122.8 15.8 %collective-permute-start.23 = (bf16[256,2560]{1,0:T(8,128)(2,1)S(1)}, bf16[256,2560]{1,0:T(8,128)(2,1)S(1)}, u32[]{:S(2)}, u32[]{:S(2)}) collective-permute-start(bf16[256,2560]{1,0:T(8,128)(2,1)S(1)} %collective-permute-done.18.refs_1_), channel_id=1, source_target_pairs={{0,2},{2,0},{4,6},{6,4},{8,10},{10,8},{12,14},{14,12},{16,18},{18,... | collective-permute-start | bytes 3932168 | tf_op jit(solution)/shard_map/ppermute | solution.py:265
  122.9 15.7 %collective-permute-start.24 = (bf16[256,2560]{1,0:T(8,128)(2,1)S(1)}, bf16[256,2560]{1,0:T(8,128)(2,1)S(1)}, u32[]{:S(2)}, u32[]{:S(2)}) collective-permute-start(bf16[256,2560]{1,0:T(8,128)(2,1)S(1)} %collective-permute-done.19.refs_3_), channel_id=1, source_target_pairs={{0,2},{2,0},{4,6},{6,4},{8,10},{10,8},{12,14},{14,12},{16,18},{18,... | collective-permute-start | bytes 3932168 | tf_op jit(solution)/shard_map/ppermute | solution.py:265
  123.4 14.0 %collective-permute-start.25 = (bf16[128,2048]{1,0:T(8,128)(2,1)S(1)}, bf16[128,2048]{1,0:T(8,128)(2,1)S(1)}, u32[]{:S(2)}, u32[]{:S(2)}) collective-permute-start(bf16[128,2048]{1,0:T(8,128)(2,1)S(1)} %pad_maximum_fusion.6), channel_id=1, source_target_pairs={{0,4},{2,6},{4,0},{6,2},{8,12},{10,14},{12,8},{14,10},{16,20},{18,... | collective-permute-start | bytes 1572872 | tf_op jit(solution)/shard_map/ppermute | solution.py:265
  124.9 13.7 %collective-permute-start.26 = (bf16[128,2048]{1,0:T(8,128)(2,1)S(1)}, bf16[128,2048]{1,0:T(8,128)(2,1)S(1)}, u32[]{:S(2)}, u32[]{:S(2)}) collective-permute-start(bf16[128,2048]{1,0:T(8,128)(2,1)S(1)} %pad_maximum_fusion.7), channel_id=1, source_target_pairs={{0,1},{1,0},{2,3},{3,2},{4,5},{5,4},{6,7},{7,6},{8,9},{9,8},{10,11... | collective-permute-start | bytes 1572872 | tf_op jit(solution)/shard_map/ppermute | solution.py:265
  138.7 21.4 %collective-permute-start.30 = (bf16[256,2048]{1,0:T(8,128)(2,1)S(1)}, bf16[256,2048]{1,0:T(8,128)(2,1)S(1)}, u32[]{:S(2)}, u32[]{:S(2)}) collective-permute-start(bf16[256,2048]{1,0:T(8,128)(2,1)S(1)} %constant_dynamic-update-slice_fusion.11.refs_2_), channel_id=1, source_target_pairs={{0,2},{2,0},{4,6},{6,4},{8,10},{10,8},{12,14},{14,12},{16,18},{18,... | collective-permute-start | bytes 3145736 | tf_op jit(solution)/shard_map/ppermute | solution.py:265
  138.7 25.6 %collective-permute-start.28 = (bf16[256,2048]{1,0:T(8,128)(2,1)S(1)}, bf16[256,2048]{1,0:T(8,128)(2,1)S(1)}, u32[]{:S(2)}, u32[]{:S(2)}) collective-permute-start(bf16[256,2048]{1,0:T(8,128)(2,1)S(1)} %constant_dynamic-update-slice_fusion.11.refs_2_), channel_id=1, source_target_pairs={{0,4},{2,6},{4,0},{6,2},{8,12},{10,14},{12,8},{14,10},{16,20},{18,... | collective-permute-start | bytes 3145736 | tf_op jit(solution)/shard_map/ppermute | solution.py:265
  139.6 24.7 %collective-permute-start.29 = (bf16[256,2048]{1,0:T(8,128)(2,1)S(1)}, bf16[256,2048]{1,0:T(8,128)(2,1)S(1)}, u32[]{:S(2)}, u32[]{:S(2)}) collective-permute-start(bf16[256,2048]{1,0:T(8,128)(2,1)S(1)} %constant_dynamic-update-slice_fusion.9.refs_0_), channel_id=1, source_target_pairs={{0,2},{2,0},{4,6},{6,4},{8,10},{10,8},{12,14},{14,12},{16,18},{18,... | collective-permute-start | bytes 3145736 | tf_op jit(solution)/shard_map/ppermute | solution.py:265
  139.8 25.4 %collective-permute-start.27 = (bf16[256,2048]{1,0:T(8,128)(2,1)S(1)}, bf16[256,2048]{1,0:T(8,128)(2,1)S(1)}, u32[]{:S(2)}, u32[]{:S(2)}) collective-permute-start(bf16[256,2048]{1,0:T(8,128)(2,1)S(1)} %constant_dynamic-update-slice_fusion.9.refs_0_), channel_id=1, source_target_pairs={{0,1},{1,0},{2,3},{3,2},{4,5},{5,4},{6,7},{7,6},{8,9},{9,8},{10,11... | collective-permute-start | bytes 3145736 | tf_op jit(solution)/shard_map/ppermute | solution.py:265
  165.3 2.7 collective-permute-start.31
  165.3 4.2 %collective-permute-start.32 = (bf16[256,2048]{1,0:T(8,128)(2,1)S(1)}, bf16[256,2048]{1,0:T(8,128)(2,1)S(1)}, u32[]{:S(2)}, u32[]{:S(2)}) collective-permute-start(bf16[256,2048]{1,0:T(8,128)(2,1)S(1)} %collective-permute-done.28.refs_3_), channel_id=1, source_target_pairs={{0,2},{2,0},{4,6},{6,4},{8,10},{10,8},{12,14},{14,12},{16,18},{18,... | collective-permute-start | bytes 3145736 | tf_op jit(solution)/shard_map/ppermute | solution.py:265
  182.5 9.5 %collective-permute-start.34 = (bf16[512,2048]{1,0:T(8,128)(2,1)}, bf16[512,2048]{1,0:T(8,128)(2,1)S(1)}, u32[]{:S(2)}, u32[]{:S(2)}) collective-permute-start(bf16[512,2048]{1,0:T(8,128)(2,1)} %get-tuple-element.289.send_ref), channel_id=1, source_target_pairs={{0,2},{2,0},{4,6},{6,4},{8,10},{10,8},{12,14},{14,12},{16,18},{18,... | collective-permute-start | bytes 6291464 | tf_op jit(solution)/shard_map/ppermute | solution.py:265
  182.7 9.3 %collective-permute-start.33 = (bf16[512,1024]{1,0:T(8,128)(2,1)S(1)}, bf16[512,1024]{1,0:T(8,128)(2,1)S(1)}, u32[]{:S(2)}, u32[]{:S(2)}) collective-permute-start(bf16[512,1024]{1,0:T(8,128)(2,1)S(1)} %convert_element_type.291.rows_ref.refs_0_), channel_id=1, source_target_pairs={{0,2},{2,0},{4,6},{6,4},{8,10},{10,8},{12,14},{14,12},{16,18},{18,... | collective-permute-start | bytes 3145736 | tf_op jit(solution)/shard_map/ppermute | solution.py:265
  193.3 9.2 %collective-permute-start.35 = (bf16[512,2048]{1,0:T(8,128)(2,1)S(1)}, bf16[512,2048]{1,0:T(8,128)(2,1)S(1)}, u32[]{:S(2)}, u32[]{:S(2)}) collective-permute-start(bf16[512,2048]{1,0:T(8,128)(2,1)S(1)} %get-tuple-element.321.send_ref), channel_id=1, source_target_pairs={{0,2},{2,0},{4,6},{6,4},{8,10},{10,8},{12,14},{14,12},{16,18},{18,... | collective-permute-start | bytes 6291464 | tf_op jit(solution)/shard_map/ppermute | solution.py:265
  193.5 9.1 %collective-permute-start.36 = (bf16[512,1024]{1,0:T(8,128)(2,1)S(1)}, bf16[512,1024]{1,0:T(8,128)(2,1)S(1)}, u32[]{:S(2)}, u32[]{:S(2)}) collective-permute-start(bf16[512,1024]{1,0:T(8,128)(2,1)S(1)} %get-tuple-element.305.rows_ref.refs_0_), channel_id=1, source_target_pairs={{0,2},{2,0},{4,6},{6,4},{8,10},{10,8},{12,14},{14,12},{16,18},{18,... | collective-permute-start | bytes 3145736 | tf_op jit(solution)/shard_map/ppermute | solution.py:265
  193.8 8.7 %collective-permute-start.37 = (bf16[512,1024]{1,0:T(8,128)(2,1)S(1)}, bf16[512,1024]{1,0:T(8,128)(2,1)S(1)}, u32[]{:S(2)}, u32[]{:S(2)}) collective-permute-start(bf16[512,1024]{1,0:T(8,128)(2,1)S(1)} %fusion.19.rows_ref.refs_0_), channel_id=1, source_target_pairs={{0,2},{2,0},{4,6},{6,4},{8,10},{10,8},{12,14},{14,12},{16,18},{18,... | collective-permute-start | bytes 3145736 | tf_op jit(solution)/shard_map/ppermute | solution.py:265
  194.0 7.8 %collective-permute-start.38 = (bf16[512,512]{1,0:T(8,128)(2,1)S(1)}, bf16[512,512]{1,0:T(8,128)(2,1)S(1)}, u32[]{:S(2)}, u32[]{:S(2)}) collective-permute-start(bf16[512,512]{1,0:T(8,128)(2,1)S(1)} %get-tuple-element.307.send_ref), channel_id=1, source_target_pairs={{0,2},{2,0},{4,6},{6,4},{8,10},{10,8},{12,14},{14,12},{16,18},{18,... | collective-permute-start | bytes 1572872 | tf_op jit(solution)/shard_map/ppermute | solution.py:265
  202.6 25.3 %collective-permute-start.39 = (bf16[512,1024]{1,0:T(8,128)(2,1)S(1)}, bf16[512,1024]{1,0:T(8,128)(2,1)S(1)}, u32[]{:S(2)}, u32[]{:S(2)}) collective-permute-start(bf16[512,1024]{1,0:T(8,128)(2,1)S(1)} %get-tuple-element.310), channel_id=1, source_target_pairs={{0,1},{1,0},{2,3},{3,2},{4,5},{5,4},{6,7},{7,6},{8,9},{9,8},{10,11... | collective-permute-start | bytes 3145736 | tf_op jit(solution)/shard_map/ppermute | solution.py:265
  203.7 26.2 %collective-permute-start.40 = (bf16[512,1024]{1,0:T(8,128)(2,1)S(1)}, bf16[512,1024]{1,0:T(8,128)(2,1)S(1)}, u32[]{:S(2)}, u32[]{:S(2)}) collective-permute-start(bf16[512,1024]{1,0:T(8,128)(2,1)S(1)} %get-tuple-element.312), channel_id=1, source_target_pairs={{0,4},{2,6},{4,0},{6,2},{8,12},{10,14},{12,8},{14,10},{16,20},{18,... | collective-permute-start | bytes 3145736 | tf_op jit(solution)/shard_map/ppermute | solution.py:265
  232.4 35.9 %collective-permute-start.42 = (bf16[768,1024]{1,0:T(8,128)(2,1)}, bf16[768,1024]{1,0:T(8,128)(2,1)}, u32[]{:S(2)}, u32[]{:S(2)}) collective-permute-start(bf16[768,1024]{1,0:T(8,128)(2,1)} %pad_maximum_fusion.1), channel_id=1, source_target_pairs={{0,1},{1,0},{2,3},{3,2},{4,5},{5,4},{6,7},{7,6},{8,9},{9,8},{10,11... | collective-permute-start | bytes 4718600 | tf_op jit(solution)/shard_map/ppermute | solution.py:265
  237.0 35.4 %collective-permute-start.41 = (bf16[768,1024]{1,0:T(8,128)(2,1)S(1)}, bf16[768,1024]{1,0:T(8,128)(2,1)S(1)}, u32[]{:S(2)}, u32[]{:S(2)}) collective-permute-start(bf16[768,1024]{1,0:T(8,128)(2,1)S(1)} %pad_maximum_fusion), channel_id=1, source_target_pairs={{0,4},{2,6},{4,0},{6,2},{8,12},{10,14},{12,8},{14,10},{16,20},{18,... | collective-permute-start | bytes 4718600 | tf_op jit(solution)/shard_map/ppermute | solution.py:265
  262.7 11.2 %collective-permute-start.44 = (bf16[512,1024]{1,0:T(8,128)(2,1)S(1)}, bf16[512,1024]{1,0:T(8,128)(2,1)S(1)}, u32[]{:S(2)}, u32[]{:S(2)}) collective-permute-start(bf16[512,1024]{1,0:T(8,128)(2,1)S(1)} %get-tuple-element.337.rows_ref.refs_4_), channel_id=1, source_target_pairs={{0,2},{2,0},{4,6},{6,4},{8,10},{10,8},{12,14},{14,12},{16,18},{18,... | collective-permute-start | bytes 3145736 | tf_op jit(solution)/shard_map/ppermute | solution.py:265
  262.8 11.1 %collective-permute-start.43 = (bf16[512,1536]{1,0:T(8,128)(2,1)S(1)}, bf16[512,1536]{1,0:T(8,128)(2,1)S(1)}, u32[]{:S(2)}, u32[]{:S(2)}) collective-permute-start(bf16[512,1536]{1,0:T(8,128)(2,1)S(1)} %get-tuple-element.358.send_ref), channel_id=1, source_target_pairs={{0,2},{2,0},{4,6},{6,4},{8,10},{10,8},{12,14},{14,12},{16,18},{18,... | collective-permute-start | bytes 4718600 | tf_op jit(solution)/shard_map/ppermute | solution.py:265
  284.1 34.8 %collective-permute-start.49 = (bf16[768,1024]{1,0:T(8,128)(2,1)}, bf16[768,1024]{1,0:T(8,128)(2,1)}, u32[]{:S(2)}, u32[]{:S(2)}) collective-permute-start(bf16[768,1024]{1,0:T(8,128)(2,1)} %pad_maximum_fusion.3), channel_id=1, source_target_pairs={{0,1},{1,0},{2,3},{3,2},{4,5},{5,4},{6,7},{7,6},{8,9},{9,8},{10,11... | collective-permute-start | bytes 4718600 | tf_op jit(solution)/shard_map/ppermute | solution.py:265
  285.2 11.3 %collective-permute-start.45 = (bf16[128,1024]{1,0:T(8,128)(2,1)S(1)}, bf16[128,1024]{1,0:T(8,128)(2,1)S(1)}, u32[]{:S(2)}, u32[]{:S(2)}) collective-permute-start(bf16[128,1024]{1,0:T(8,128)(2,1)S(1)} %pad_maximum_fusion.19), channel_id=1, source_target_pairs={{0,8},{2,10},{4,12},{6,14},{8,0},{10,2},{12,4},{14,6},{16,24},{18,... | collective-permute-start | bytes 786440 | tf_op jit(solution)/shard_map/ppermute | solution.py:265
  286.7 35.2 %collective-permute-start.48 = (bf16[768,1024]{1,0:T(8,128)(2,1)}, bf16[768,1024]{1,0:T(8,128)(2,1)}, u32[]{:S(2)}, u32[]{:S(2)}) collective-permute-start(bf16[768,1024]{1,0:T(8,128)(2,1)} %pad_maximum_fusion.2), channel_id=1, source_target_pairs={{0,4},{2,6},{4,0},{6,2},{8,12},{10,14},{12,8},{14,10},{16,20},{18,... | collective-permute-start | bytes 4718600 | tf_op jit(solution)/shard_map/ppermute | solution.py:265
  288.0 20.5 %collective-permute-start.46 = (bf16[128,1024]{1,0:T(8,128)(2,1)S(1)}, bf16[128,1024]{1,0:T(8,128)(2,1)S(1)}, u32[]{:S(2)}, u32[]{:S(2)}) collective-permute-start(bf16[128,1024]{1,0:T(8,128)(2,1)S(1)} %pad_maximum_fusion.20), channel_id=1, source_target_pairs={{0,16},{2,18},{4,20},{6,22},{8,24},{10,26},{12,28},{14,30},{16,0},... | collective-permute-start | bytes 786440 | tf_op jit(solution)/shard_map/ppermute | solution.py:265
  290.9 17.6 %collective-permute-start.47 = (bf16[128,1024]{1,0:T(8,128)(2,1)S(1)}, bf16[128,1024]{1,0:T(8,128)(2,1)}, u32[]{:S(2)}, u32[]{:S(2)}) collective-permute-start(bf16[128,1024]{1,0:T(8,128)(2,1)S(1)} %pad_maximum_fusion.21), channel_id=1, source_target_pairs={{0,24},{2,26},{4,28},{6,30},{8,16},{10,18},{12,20},{14,22},{16,8},... | collective-permute-start | bytes 786440 | tf_op jit(solution)/shard_map/ppermute | solution.py:265
  324.3 21.9 %collective-permute-start.50 = (bf16[128,1024]{1,0:T(8,128)(2,1)S(1)}, bf16[128,1024]{1,0:T(8,128)(2,1)S(1)}, u32[]{:S(2)}, u32[]{:S(2)}) collective-permute-start(bf16[128,1024]{1,0:T(8,128)(2,1)S(1)} %pad_maximum_fusion.22), channel_id=1, source_target_pairs={{0,8},{2,10},{4,12},{6,14},{8,0},{10,2},{12,4},{14,6},{16,24},{18,... | collective-permute-start | bytes 786440 | tf_op jit(solution)/shard_map/ppermute | solution.py:265
  325.4 20.9 %collective-permute-start.51 = (bf16[128,1024]{1,0:T(8,128)(2,1)S(1)}, bf16[128,1024]{1,0:T(8,128)(2,1)S(1)}, u32[]{:S(2)}, u32[]{:S(2)}) collective-permute-start(bf16[128,1024]{1,0:T(8,128)(2,1)S(1)} %pad_maximum_fusion.23), channel_id=1, source_target_pairs={{0,16},{2,18},{4,20},{6,22},{8,24},{10,26},{12,28},{14,30},{16,0},... | collective-permute-start | bytes 786440 | tf_op jit(solution)/shard_map/ppermute | solution.py:265
  327.5 18.8 %collective-permute-start.52 = (bf16[128,1024]{1,0:T(8,128)(2,1)S(1)}, bf16[128,1024]{1,0:T(8,128)(2,1)S(1)}, u32[]{:S(2)}, u32[]{:S(2)}) collective-permute-start(bf16[128,1024]{1,0:T(8,128)(2,1)S(1)} %pad_maximum_fusion.24), channel_id=1, source_target_pairs={{0,24},{2,26},{4,28},{6,30},{8,16},{10,18},{12,20},{14,22},{16,8},... | collective-permute-start | bytes 786440 | tf_op jit(solution)/shard_map/ppermute | solution.py:265
  329.0 17.5 %collective-permute-start.53 = (bf16[256,1024]{1,0:T(8,128)(2,1)S(1)}, bf16[256,1024]{1,0:T(8,128)(2,1)S(1)}, u32[]{:S(2)}, u32[]{:S(2)}) collective-permute-start(bf16[256,1024]{1,0:T(8,128)(2,1)S(1)} %pad_maximum_fusion.13), channel_id=1, source_target_pairs={{0,4},{2,6},{4,0},{6,2},{8,12},{10,14},{12,8},{14,10},{16,20},{18,... | collective-permute-start | bytes 1572872 | tf_op jit(solution)/shard_map/ppermute | solution.py:265
  330.4 16.3 %collective-permute-start.54 = (bf16[256,1024]{1,0:T(8,128)(2,1)S(1)}, bf16[256,1024]{1,0:T(8,128)(2,1)S(1)}, u32[]{:S(2)}, u32[]{:S(2)}) collective-permute-start(bf16[256,1024]{1,0:T(8,128)(2,1)S(1)} %get-tuple-element.365), channel_id=1, source_target_pairs={{0,1},{1,0},{2,3},{3,2},{4,5},{5,4},{6,7},{7,6},{8,9},{9,8},{10,11... | collective-permute-start | bytes 1572872 | tf_op jit(solution)/shard_map/ppermute | solution.py:265
  347.0 5.1 %collective-permute-start.58 = (f32[12,1024]{1,0:T(8,128)S(1)}, f32[12,1024]{1,0:T(8,128)S(1)}, u32[]{:S(2)}, u32[]{:S(2)}) collective-permute-start(f32[12,1024]{1,0:T(8,128)S(1)} %concatenate.418), channel_id=1, source_target_pairs={{0,2},{2,0},{4,6},{6,4},{8,10},{10,8},{12,14},{14,12},{16,18},{18,... | collective-permute-start | bytes 147464 | tf_op jit(solution)/shard_map/ppermute | solution.py:265
  347.1 31.6 %collective-permute-start.55 = (bf16[128,1024]{1,0:T(8,128)(2,1)S(1)}, bf16[128,1024]{1,0:T(8,128)(2,1)S(1)}, u32[]{:S(2)}, u32[]{:S(2)}) collective-permute-start(bf16[128,1024]{1,0:T(8,128)(2,1)S(1)} %pad_maximum_fusion.25), channel_id=1, source_target_pairs={{0,8},{2,10},{4,12},{6,14},{8,0},{10,2},{12,4},{14,6},{16,24},{18,... | collective-permute-start | bytes 786440 | tf_op jit(solution)/shard_map/ppermute | solution.py:265
  349.5 29.2 %collective-permute-start.56 = (bf16[128,1024]{1,0:T(8,128)(2,1)S(1)}, bf16[128,1024]{1,0:T(8,128)(2,1)S(1)}, u32[]{:S(2)}, u32[]{:S(2)}) collective-permute-start(bf16[128,1024]{1,0:T(8,128)(2,1)S(1)} %pad_maximum_fusion.26), channel_id=1, source_target_pairs={{0,16},{2,18},{4,20},{6,22},{8,24},{10,26},{12,28},{14,30},{16,0},... | collective-permute-start | bytes 786440 | tf_op jit(solution)/shard_map/ppermute | solution.py:265
  350.5 28.2 %collective-permute-start.57 = (bf16[128,1024]{1,0:T(8,128)(2,1)S(1)}, bf16[128,1024]{1,0:T(8,128)(2,1)S(1)}, u32[]{:S(2)}, u32[]{:S(2)}) collective-permute-start(bf16[128,1024]{1,0:T(8,128)(2,1)S(1)} %pad_maximum_fusion.27), channel_id=1, source_target_pairs={{0,24},{2,26},{4,28},{6,30},{8,16},{10,18},{12,20},{14,22},{16,8},... | collective-permute-start | bytes 786440 | tf_op jit(solution)/shard_map/ppermute | solution.py:265
  352.1 4.3 %collective-permute-start.59 = (f32[12,1024]{1,0:T(8,128)S(1)}, f32[12,1024]{1,0:T(8,128)S(1)}, u32[]{:S(2)}, u32[]{:S(2)}) collective-permute-start(f32[12,1024]{1,0:T(8,128)S(1)} %add.359), channel_id=1, source_target_pairs={{0,4},{2,6},{4,0},{6,2},{8,12},{10,14},{12,8},{14,10},{16,20},{18,... | collective-permute-start | bytes 147464 | tf_op jit(solution)/shard_map/ppermute | solution.py:265
  356.4 4.3 %collective-permute-start.60 = (f32[12,1024]{1,0:T(8,128)S(1)}, f32[12,1024]{1,0:T(8,128)S(1)}, u32[]{:S(2)}, u32[]{:S(2)}) collective-permute-start(f32[12,1024]{1,0:T(8,128)S(1)} %add.360), channel_id=1, source_target_pairs={{0,1},{1,0},{2,3},{3,2},{4,5},{5,4},{6,7},{7,6},{8,9},{9,8},{10,11... | collective-permute-start | bytes 147464 | tf_op jit(solution)/shard_map/ppermute | solution.py:265
  360.7 10.2 %collective-permute-start.61 = (f32[12,1024]{1,0:T(8,128)S(1)}, f32[12,1024]{1,0:T(8,128)S(1)}, u32[]{:S(2)}, u32[]{:S(2)}) collective-permute-start(f32[12,1024]{1,0:T(8,128)S(1)} %add.361), channel_id=1, source_target_pairs={{0,8},{2,10},{4,12},{6,14},{8,0},{10,2},{12,4},{14,6},{16,24},{18,... | collective-permute-start | bytes 147464 | tf_op jit(solution)/shard_map/ppermute | solution.py:265
  362.0 16.9 %collective-permute-start.63 = (f32[64,2048]{1,0:T(8,128)S(1)}, f32[64,2048]{1,0:T(8,128)S(1)}, u32[]{:S(2)}, u32[]{:S(2)}) collective-permute-start(f32[64,2048]{1,0:T(8,128)S(1)} %maximum_maximum_fusion), channel_id=1, source_target_pairs={{0,2},{2,0},{4,6},{6,4},{8,10},{10,8},{12,14},{14,12},{16,18},{18,... | collective-permute-start | bytes 1572872 | tf_op jit(solution)/shard_map/ppermute | solution.py:265
  370.9 7.7 %collective-permute-start.62 = (f32[12,1024]{1,0:T(8,128)S(1)}, f32[12,1024]{1,0:T(8,128)S(1)}, u32[]{:S(2)}, u32[]{:S(2)}) collective-permute-start(f32[12,1024]{1,0:T(8,128)S(1)} %add.362), channel_id=1, source_target_pairs={{0,16},{2,18},{4,20},{6,22},{8,24},{10,26},{12,28},{14,30},{16,0},... | collective-permute-start | bytes 147464 | tf_op jit(solution)/shard_map/ppermute | solution.py:265
  (64 other events, 613.1 us)

commit v5 on v4

--- a/solution.py
+++ b/solution.py
@@ -413,13 +413,12 @@
 
 
 def attend_forward_kernel(
-    core_ref, q_ref, k_ref, v_ref, column_ref, row_ref, own_ref, send_ref, logsum_ref
+    core_ref, q_ref, k_ref, v_ref, column_ref, row_ref, own_ref, send_ref, prob_ref
 ):
     lane = lax.broadcasted_iota(jnp.int32, q_ref.shape, 1) // HEAD_DIM
     same_doc = column_ref[...] == row_ref[...]
     value_rows = v_ref[...]
     contexts = []
-    logsums = []
     for head in (0, 1):
         queries = jnp.where(lane == head, q_ref[...], jnp.bfloat16(0))
         scores = head_scores(queries, k_ref[...], same_doc)
@@ -427,8 +426,8 @@
         exponent = jnp.exp(scores - row_max)
         row_total = jnp.sum(exponent, axis=-1, keepdims=True)
         probabilities = (exponent * (1.0 / row_total)).astype(jnp.bfloat16)
+        prob_ref[head] = probabilities
         contexts.append(matmul(probabilities, value_rows))
-        logsums.append(row_max + jnp.log(row_total))
     context = jnp.where(lane == 0, contexts[0], contexts[1]).astype(jnp.bfloat16)
     own = pl.program_id(1) < pl.num_programs(1) // 2
 
@@ -439,8 +438,6 @@
     @pl.when(jnp.logical_not(own))
     def _():
         send_ref[...] = context
-
-    logsum_ref[...] = jnp.where(lane == 0, logsums[0], logsums[1])
 
 
 def attend_backward_kernel(
@@ -448,9 +445,7 @@
     q_ref,
     k_ref,
     v_ref,
-    column_ref,
-    row_ref,
-    logsum_ref,
+    prob_ref,
     dctx_ref,
     own_ref,
     send_ref,
@@ -458,24 +453,22 @@
     send_sum_ref,
 ):
     lane = lax.broadcasted_iota(jnp.int32, q_ref.shape, 1) // HEAD_DIM
-    same_doc = column_ref[...] == row_ref[...]
+    scale = HEAD_DIM ** (-0.5)
     key_rows = k_ref[...]
     value_rows = v_ref[...]
     results = []
     for head in (0, 1):
-        queries = jnp.where(lane == head, q_ref[...], jnp.bfloat16(0))
+        queries = jnp.where(lane == head, q_ref[...], jnp.bfloat16(0)) * jnp.bfloat16(scale)
         d_context = jnp.where(lane == head, dctx_ref[...], jnp.bfloat16(0))
-        scores = head_scores(queries, key_rows, same_doc)
-        place = head * HEAD_DIM
-        probabilities = jnp.exp(scores - logsum_ref[:, place : place + 1])
+        probabilities = prob_ref[head].astype(jnp.float32)
         d_probs = outer_cols(d_context, value_rows)
         row_dot = jnp.sum(d_probs * probabilities, axis=-1, keepdims=True)
-        d_raw = (probabilities * (d_probs - row_dot) * HEAD_DIM ** (-0.5)).astype(jnp.bfloat16)
+        d_raw = (probabilities * (d_probs - row_dot)).astype(jnp.bfloat16)
         results.append(
             (
-                matmul(d_raw, key_rows),
+                matmul(d_raw, key_rows) * scale,
                 inner_rows(d_raw, queries),
-                inner_rows(probabilities.astype(jnp.bfloat16), d_context),
+                inner_rows(prob_ref[head], d_context),
             )
         )
     half = pl.num_programs(1) // 2
@@ -523,18 +516,18 @@
     )(core, *operands)
 
 
-def attention_inputs(rows, pairs, column, row):
+def attention_inputs(rows, pairs):
     def place(part):
         return lambda group, at, core: (
             0,
             group * 3 * pairs + part * pairs + (at ^ (core[0] * (pairs // 2))),
         )
 
-    whole = lambda group, at, core: (0, 0)
-    return [pl.BlockSpec((rows, 128), place(part)) for part in range(3)] + [
-        pl.BlockSpec(column.shape, whole),
-        pl.BlockSpec(row.shape, whole),
-    ]
+    return [pl.BlockSpec((rows, 128), place(part)) for part in range(3)]
+
+
+def probability_spec(rows, pairs):
+    return pl.BlockSpec((2, rows, rows), lambda group, at, core: (group * pairs + at, 0, 0))
 
 
 def attend_rows_forward(core, qkv, column, row):
@@ -542,22 +535,23 @@
     half = pairs // 2
     own = pl.BlockSpec((rows, 128), lambda group, at, core: (0, group * half + jnp.minimum(at, half - 1)))
     send = pl.BlockSpec((rows, 128), lambda group, at, core: (0, group * half + jnp.maximum(at - half, 0)))
-    flat = pl.BlockSpec((rows, 128), lambda group, at, core: (0, group * pairs + at))
+    whole = lambda group, at, core: (0, 0)
     pair_shape = jax.ShapeDtypeStruct((rows, pairs * 128), jnp.bfloat16)
-    own, send, logsum = call_kernel(
+    own, send, probabilities = call_kernel(
         attend_forward_kernel,
         core,
         16,
         (2, pairs),
-        attention_inputs(rows, pairs, column, row),
-        [own, send, flat],
-        [pair_shape, pair_shape, jax.ShapeDtypeStruct((rows, pairs * 256), jnp.float32)],
+        attention_inputs(rows, pairs)
+        + [pl.BlockSpec(column.shape, whole), pl.BlockSpec(row.shape, whole)],
+        [own, send, probability_spec(rows, pairs)],
+        [pair_shape, pair_shape, jax.ShapeDtypeStruct((4 * pairs, rows, rows), jnp.bfloat16)],
         (qkv, qkv, qkv, column, row),
     )
-    return (own, send), logsum
-
-
-def attend_rows_backward(core, qkv, column, row, logsum, d_context):
+    return (own, send), probabilities
+
+
+def attend_rows_backward(core, qkv, probabilities, d_context):
     rows, pairs = qkv.shape[0], qkv.shape[1] // 768
     flat = pl.BlockSpec((rows, 128), lambda group, at, core: (0, group * pairs + at))
     pair_spec = pl.BlockSpec((rows, qkv.shape[1] // 2), lambda group, at, core: (0, 0))
@@ -569,10 +563,10 @@
         core,
         20,
         (2, pairs),
-        attention_inputs(rows, pairs, column, row) + [flat, flat],
+        attention_inputs(rows, pairs) + [probability_spec(rows, pairs), flat],
         [pair_spec, pair_spec, sum_spec, sum_spec],
         [pair_shape, pair_shape, sum_shape, sum_shape],
-        (qkv, qkv, qkv, column, row, logsum, d_context),
+        (qkv, qkv, qkv, probabilities, d_context),
     )
     return (own, send), (own_sum, send_sum)
 
@@ -849,8 +843,8 @@
             [qkv_bias],
             [(rows, low, False)],
         )
-        context, logsum = attend_rows_forward(core, qkv, column, row)
-        return dict(qkv=qkv, context=context, logsum=logsum)
+        context, probabilities = attend_rows_forward(core, qkv, column, row)
+        return dict(qkv=qkv, context=context, probabilities=probabilities)
 
     def units_work(weight, results):
         attn_rows = contract_rows(core, results["context"], weight, unit_width, head_width, 1)
@@ -884,7 +878,7 @@
         attention_work,
         units_work,
     )
-    qkv, context, logsum = made["qkv"], made["context"], made["logsum"]
+    qkv, context, probabilities = made["qkv"], made["context"], made["probabilities"]
     h_one, scaled_one, spread_one = made["norm"]
     h_low, activation, slope = made["h_low"], made["activation"], made["slope"]
     mlp_rows = contract_rows(core, activation, down_w, 0, unit_width, 1)
@@ -945,7 +939,7 @@
     down_sum, up_sum, d_ctx, grad_one_low = after((down_sum, up_sum, d_ctx, grad_one_low))
     down_sum, up_sum = scatter_both(down_sum, up_sum)
     grad_one_other = over_core(grad_one_low)
-    d_qkv, qkv_sums = attend_rows_backward(core, qkv, column, row, logsum, d_ctx)
+    d_qkv, qkv_sums = attend_rows_backward(core, qkv, probabilities, d_ctx)
     qkv_other = over_core(d_qkv[1])
     last_sum = grad_parts(
         [

time: 389 us -> 386 us (level)
  Pallas kernels: 114 us -> 110 us
    unnamed x139 -> x143, local copies, waits for them, and re-layouts: 13.7 us -> 17.6 us
where the time goes in v5:
time: 386 us; the launch traced here: 381 us
  waiting for transfers between devices  136 us (35%)
  Pallas kernels  110 us (28%)
  starting transfers between devices  58.7 us (15%)
  other arithmetic  36.6 us (9%)
  local copies, waits for them, and re-layouts  24 us (6%)
  matrix products  13.7 us (4%)
    ppermute x65, waiting for transfers between devices, swap(): lax.ppermute(array, name, [(index, index ^ mask) for index in range(size)])  136 us
    pallas_call x10, Pallas kernels, call_kernel(): pl.pallas_call(kernel, grid_spec=pltpu.PrefetchScalarGridSpec(num_scalar_...  90.1 us
    ppermute x65, starting transfers between devices, swap(): lax.ppermute(array, name, [(index, index ^ mask) for index in range(size)])  58.7 us
    pallas_call x3, Pallas kernels, grad_parts(): pl.pallas_call(kernel, grid=(2,), in_specs=in_specs, out_specs=[y_spec, y...  20.3 us
    unnamed x143, local copies, waits for them, and re-layouts  17.6 us
    convert_element_type x10, other arithmetic, add_low(): (left.astype(jnp.float32) + right.astype(jnp.float32)).astype(jnp.bfloat16)  11.4 us
    concatenate x10, other arithmetic, beside(): return jnp.concatenate([left, right])  8.27 us
  transfers between devices with their start and end apart: 65, of which 25 were waited for; matrix products, arithmetic and copies ran while one was open for 11% of the time, Pallas kernels for 25%

profile of v5, /device:TPU:0, one launch (start us, length us, event | category | flops | bytes accessed | tf_op | source)
XLA Modules:
  0.0 381.5 jit_solution(12241174567355649906)
XLA Ops:
  1.8 3.1 collective-permute-start.3
  5.8 2.5 collective-permute-start.2
  8.5 1.7 collective-permute-start
  10.3 10.0 %collective-permute-done.2 = bf16[64,1536]{1,0:T(8,128)(2,1)S(1)} collective-permute-done((bf16[64,1536]{1,0:T(8,128)(2,1)S(1)}, bf16[64,1536]{1,0:T(8,128)(2,1)S(1)}, u32[]{:S(2)}, u32[]{:S(2)}) %collective-permute-start.2) | collective-permute-done | bytes 196640 | tf_op jit(solution)/shard_map/ppermute | solution.py:265
  20.2 5.5 %collective-permute-done.1 = bf16[64,1536]{1,0:T(8,128)(2,1)S(1)} collective-permute-done((bf16[64,1536]{1,0:T(8,128)(2,1)S(1)}, bf16[64,1536]{1,0:T(8,128)(2,1)S(1)}, u32[]{:S(2)}, u32[]{:S(2)}) %collective-permute-start.1) | collective-permute-done | bytes 196640 | tf_op jit(solution)/shard_map/ppermute | solution.py:265
  25.8 1.6 collective-permute-start.4
  27.4 1.6 collective-permute-start.5
  29.0 2.3 collective-permute-start.6
  31.3 1.5 collective-permute-start.7
  32.8 9.7 %collective-permute-done.7 = bf16[64,2048]{1,0:T(8,128)(2,1)S(1)} collective-permute-done((bf16[64,2048]{1,0:T(8,128)(2,1)S(1)}, bf16[64,2048]{1,0:T(8,128)(2,1)S(1)}, u32[]{:S(2)}, u32[]{:S(2)}) %collective-permute-start.7) | collective-permute-done | bytes 262176 | tf_op jit(solution)/shard_map/ppermute | solution.py:265
  42.5 2.5 collective-permute-done.6
  46.5 17.3 %collective-permute-done.12 = bf16[64,2560]{1,0:T(8,128)(2,1)S(1)} collective-permute-done((bf16[64,2560]{1,0:T(8,128)(2,1)S(1)}, bf16[64,2560]{1,0:T(8,128)(2,1)S(1)}, u32[]{:S(2)}, u32[]{:S(2)}) %collective-permute-start.12) | collective-permute-done | bytes 327712 | tf_op jit(solution)/shard_map/ppermute | solution.py:265
  70.7 13.4 %collective-permute-done.17 = bf16[64,2048]{1,0:T(8,128)(2,1)S(1)} collective-permute-done((bf16[64,2048]{1,0:T(8,128)(2,1)S(1)}, bf16[64,2048]{1,0:T(8,128)(2,1)S(1)}, u32[]{:S(2)}, u32[]{:S(2)}) %collective-permute-start.17) | collective-permute-done | bytes 262176 | tf_op jit(solution)/shard_map/ppermute | solution.py:265
  91.5 6.8 %shard_map.254.q_ref.k_ref.v_ref = bf16[512,3072]{1,0:T(8,128)(2,1)S(1)} custom-call(s32[1]{0:T(128)} %constant.124.clone.1.core_ref, bf16[512,1024]{1,0:T(8,128)(2,1)S(1)} %fusion.19.rows_ref.refs_0_, bf16[256,1536]{1,0:T(8,128)(2,1)S(1)} %copy-done.9, bf16[256,1536]{1,0:T(8,128)(2,1)} %collective-permute-done.8.refs_1_, ...), custom_call_target="tpu_custom_call" | custom-call | tf_op jit(solution)/shard_map/pallas_call | solution.py:505
  98.4 12.9 %shard_map.255 = (bf16[512,512]{1,0:T(8,128)(2,1)S(1)}, bf16[512,512]{1,0:T(8,128)(2,1)S(1)}, bf16[16,512,512]{2,1,0:T(8,128)(2,1)S(1)}) custom-call(s32[1]{0:T(128)} %bitcast.5.core_ref, bf16[512,3072]{1,0:T(8,128)(2,1)S(1)} %shard_map.254.q_ref.k_ref.v_ref, bf16[512,3072]{1,0:T(8,128)(2,1)S(1)} %shard_map.254.q_ref.k_ref.v_ref, ...), custom_call_target="tpu_custom_call" | custom-call | tf_op jit(solution)/shard_map/pallas_call | solution.py:505
  111.3 3.3 copy-done.4
  114.7 3.1 collective-permute-done.19.refs_3_
  117.7 2.0 collective-permute-done.18.refs_1_
  124.6 9.8 %collective-permute-done.25 = bf16[128,2048]{1,0:T(8,128)(2,1)S(1)} collective-permute-done((bf16[128,2048]{1,0:T(8,128)(2,1)S(1)}, bf16[128,2048]{1,0:T(8,128)(2,1)S(1)}, u32[]{:S(2)}, u32[]{:S(2)}) %collective-permute-start.25) | collective-permute-done | bytes 524320 | tf_op jit(solution)/shard_map/ppermute | solution.py:265
  138.0 3.0 shard_map.256
  141.8 1.9 fusion.52
  143.7 12.0 %shard_map.257 = (bf16[512,2048]{1,0:T(8,128)(2,1)S(1)}, bf16[512,2048]{1,0:T(8,128)(2,1)}, bf16[512,2048]{1,0:T(8,128)(2,1)S(1)}, bf16[512,2048]{1,0:T(8,128)(2,1)S(1)}) custom-call(s32[1]{0:T(128)} %bitcast.5.core_ref, bf16[512,1024]{1,0:T(8,128)(2,1)S(1)} %get-tuple-element.305.rows_ref.refs_0_, ...), custom_call_target="tpu_custom_call" | custom-call | tf_op jit(solution)/shard_map/pallas_call | solution.py:505
  157.0 4.3 %collective-permute-done.28.refs_3_ = bf16[256,2048]{1,0:T(8,128)(2,1)S(1)} collective-permute-done((bf16[256,2048]{1,0:T(8,128)(2,1)S(1)}, bf16[256,2048]{1,0:T(8,128)(2,1)S(1)}, u32[]{:S(2)}, u32[]{:S(2)}) %collective-permute-start.28) | collective-permute-done | bytes 1048608 | tf_op jit(solution)/shard_map/ppermute | solution.py:265
  162.8 2.1 collective-permute-done.31.refs_5_
  166.4 8.0 %shard_map.258 = f32[512,1024]{1,0:T(8,128)S(1)} custom-call(s32[1]{0:T(128)} %bitcast.5.core_ref, bf16[512,2048]{1,0:T(8,128)(2,1)S(1)} %get-tuple-element.298.own_ref.refs_2_, bf16[512,2048]{1,0:T(8,128)(2,1)} %get-tuple-element.289.send_ref, bf16[256,2048]{1,0:T(8,128)(2,1)S(1)} %constant_dynamic-update-slice_fusion.9.refs_0_, ...), custom_call_target="tpu_custom_call" | custom-call | tf_op jit(solution)/shard_map/pallas_call | solution.py:505
  175.2 2.8 fusion.7
  181.0 8.0 %shard_map.259 = (bf16[512,2048]{1,0:T(8,128)(2,1)S(1)}, bf16[512,2048]{1,0:T(8,128)(2,1)S(1)}, f32[1,4096]{1,0:T(1,128)S(1)}) custom-call(s32[1]{0:T(128)} %bitcast.5.core_ref, bf16[512,1024]{1,0:T(8,128)(2,1)S(1)} %convert_element_type.291.rows_ref.refs_0_, bf16[256,2048]{1,0:T(8,128)(2,1)S(1)} %constant_dynamic-update-slice_fusion.9.refs_0_, ...), custom_call_target="tpu_custom_call" | custom-call | tf_op jit(solution)/shard_map/pallas_call | solution.py:505
  191.3 1.6 copy-done.24
  192.9 5.8 %shard_map.260 = (bf16[512,1024]{1,0:T(8,128)(2,1)S(1)}, bf16[512,1024]{1,0:T(8,128)(2,1)S(1)}, bf16[512,1024]{1,0:T(8,128)(2,1)S(1)}, bf16[512,1024]{1,0:T(8,128)(2,1)S(1)}) custom-call(bf16[512,1024]{1,0:T(8,128)(2,1)S(1)} %convert_element_type.291.rows_ref.refs_0_, bf16[512,1024]{1,0:T(8,128)(2,1)S(1)} %collective-permute-done.33.refs_1_, ...), custom_call_target="tpu_custom_call" | custom-call | tf_op jit(solution)/shard_map/pallas_call | solution.py:740
  200.7 1.5 collective-permute-start.40
  202.2 8.1 %shard_map.262 = f32[512,1024]{1,0:T(8,128)S(1)} custom-call(s32[1]{0:T(128)} %bitcast.5.core_ref, bf16[512,2048]{1,0:T(8,128)(2,1)S(1)} %get-tuple-element.314.refs_2_.own_ref, bf16[512,2048]{1,0:T(8,128)(2,1)S(1)} %get-tuple-element.321.send_ref, bf16[256,2560]{1,0:T(8,128)(2,1)S(1)} %constant_dynamic-update-slice_fusion.4.refs_0_, ...), custom_call_target="tpu_custom_call" | custom-call | tf_op jit(solution)/shard_map/pallas_call | solution.py:505
  211.2 1.8 fusion.50
  213.0 2.6 shard_map.263.dctx_ref
  215.7 5.8 %shard_map.261 = (bf16[512,1024]{1,0:T(8,128)(2,1)S(1)}, bf16[512,1024]{1,0:T(8,128)(2,1)S(1)}, bf16[512,1024]{1,0:T(8,128)(2,1)S(1)}, bf16[512,1024]{1,0:T(8,128)(2,1)S(1)}) custom-call(bf16[512,1024]{1,0:T(8,128)(2,1)S(1)} %get-tuple-element.305.rows_ref.refs_0_, bf16[512,1024]{1,0:T(8,128)(2,1)S(1)} %collective-permute-done.36.refs_1_, ...), custom_call_target="tpu_custom_call" | custom-call | tf_op jit(solution)/shard_map/pallas_call | solution.py:740
  221.5 3.3 collective-permute-done.39
  230.6 1.7 reduce_sum.139
  232.4 1.6 pad_maximum_fusion
  234.0 1.6 collective-permute-start.41
  235.6 3.4 copy-done.5
  240.2 18.2 %shard_map.264 = (bf16[512,1536]{1,0:T(8,128)(2,1)S(1)}, bf16[512,1536]{1,0:T(8,128)(2,1)S(1)}, f32[1,1536]{1,0:T(1,128)S(1)}, f32[1,1536]{1,0:T(1,128)S(1)}) custom-call(s32[1]{0:T(128)} %bitcast.5.core_ref, bf16[512,3072]{1,0:T(8,128)(2,1)S(1)} %copy-done.3, bf16[512,3072]{1,0:T(8,128)(2,1)S(1)} %copy-done.3, bf16[512,3072]{1,0:T(8,128)(2,1)S(1)} %copy-done.3, ...), custom_call_target="tpu_custom_call" | custom-call | tf_op jit(solution)/shard_map/pallas_call | solution.py:505
  259.1 6.3 %collective-permute-done.42 = bf16[768,1024]{1,0:T(8,128)(2,1)} collective-permute-done((bf16[768,1024]{1,0:T(8,128)(2,1)}, bf16[768,1024]{1,0:T(8,128)(2,1)}, u32[]{:S(2)}, u32[]{:S(2)}) %collective-permute-start.42) | collective-permute-done | bytes 1572896 | tf_op jit(solution)/shard_map/ppermute | solution.py:265
  265.4 1.6 add_convert_fusion.21
  269.4 1.5 add_convert_fusion.7
  271.0 8.7 %shard_map.265 = (bf16[512,1024]{1,0:T(8,128)(2,1)S(1)}, bf16[512,1024]{1,0:T(8,128)(2,1)S(1)}, bf16[512,1024]{1,0:T(8,128)(2,1)S(1)}, bf16[512,1024]{1,0:T(8,128)(2,1)S(1)}) custom-call(bf16[512,1024]{1,0:T(8,128)(2,1)S(1)} %fusion.19.rows_ref.refs_0_, bf16[512,1024]{1,0:T(8,128)(2,1)S(1)} %copy-done.40, ...), custom_call_target="tpu_custom_call" | custom-call | tf_op jit(solution)/shard_map/pallas_call | solution.py:740
  285.0 2.8 collective-permute-start.46
  287.9 1.7 collective-permute-start.47
  289.6 1.8 reduce_sum.135
  291.5 1.9 fusion
  293.5 12.1 %collective-permute-done.46 = bf16[128,1024]{1,0:T(8,128)(2,1)S(1)} collective-permute-done((bf16[128,1024]{1,0:T(8,128)(2,1)S(1)}, bf16[128,1024]{1,0:T(8,128)(2,1)S(1)}, u32[]{:S(2)}, u32[]{:S(2)}) %collective-permute-start.46) | collective-permute-done | bytes 262176 | tf_op jit(solution)/shard_map/ppermute | solution.py:265
  306.7 9.2 %collective-permute-done.49 = bf16[768,1024]{1,0:T(8,128)(2,1)} collective-permute-done((bf16[768,1024]{1,0:T(8,128)(2,1)}, bf16[768,1024]{1,0:T(8,128)(2,1)}, u32[]{:S(2)}, u32[]{:S(2)}) %collective-permute-start.49) | collective-permute-done | bytes 1572896 | tf_op jit(solution)/shard_map/ppermute | solution.py:265
  315.9 1.6 add_convert_fusion.17
  319.0 2.2 add_convert_fusion.3
  322.5 1.9 collective-permute-start.51
  324.4 1.6 collective-permute-start.52
  328.6 10.6 %shard_map.266 = f32[512,1024]{1,0:T(8,128)S(1)} custom-call(s32[1]{0:T(128)} %bitcast.5.core_ref, bf16[512,1536]{1,0:T(8,128)(2,1)S(1)} %copy-done.7, bf16[512,1536]{1,0:T(8,128)(2,1)S(1)} %copy-done.28, bf16[256,1536]{1,0:T(8,128)(2,1)S(1)} %copy-done.10, bf16[256,1536]{1,0:T(8,128)(2,1)} %collective-permute-done.8.refs_1_, ...), custom_call_target="tpu_custom_call" | custom-call | tf_op jit(solution)/shard_map/pallas_call | solution.py:505
  340.6 2.7 fusion.16
  344.1 2.5 collective-permute-start.55
  347.4 1.7 collective-permute-start.57
  349.2 1.5 collective-permute-start.59
  350.7 2.7 collective-permute-done.59
  354.6 3.3 collective-permute-done.60
  359.1 8.9 %collective-permute-done.61 = f32[12,1024]{1,0:T(8,128)S(1)} collective-permute-done((f32[12,1024]{1,0:T(8,128)S(1)}, f32[12,1024]{1,0:T(8,128)S(1)}, u32[]{:S(2)}, u32[]{:S(2)}) %collective-permute-start.61) | collective-permute-done | bytes 49184 | tf_op jit(solution)/shard_map/ppermute | solution.py:265
  368.8 2.3 fusion.18
  371.1 4.7 %collective-permute-done.62 = f32[12,1024]{1,0:T(8,128)S(1)} collective-permute-done((f32[12,1024]{1,0:T(8,128)S(1)}, f32[12,1024]{1,0:T(8,128)S(1)}, u32[]{:S(2)}, u32[]{:S(2)}) %collective-permute-start.62) | collective-permute-done | bytes 49184 | tf_op jit(solution)/shard_map/ppermute | solution.py:265
  (358 shorter events, 73.5 us)
Async XLA Ops:
  1.8 24.0 %collective-permute-start.3 = (bf16[64,2560]{1,0:T(8,128)(2,1)S(1)}, bf16[64,2560]{1,0:T(8,128)(2,1)S(1)}, u32[]{:S(2)}, u32[]{:S(2)}) collective-permute-start(bf16[64,2560]{1,0:T(8,128)(2,1)S(1)} %pad_maximum_fusion.18), channel_id=1, source_target_pairs={{0,8},{2,10},{4,12},{6,14},{8,0},{10,2},{12,4},{14,6},{16,24},{18,... | collective-permute-start | bytes 983048 | tf_op jit(solution)/shard_map/ppermute | solution.py:265
  5.8 14.4 %collective-permute-start.2 = (bf16[64,1536]{1,0:T(8,128)(2,1)S(1)}, bf16[64,1536]{1,0:T(8,128)(2,1)S(1)}, u32[]{:S(2)}, u32[]{:S(2)}) collective-permute-start(bf16[64,1536]{1,0:T(8,128)(2,1)S(1)} %pad_maximum_fusion.32), channel_id=1, source_target_pairs={{0,24},{2,26},{4,28},{6,30},{8,16},{10,18},{12,20},{14,22},{16,8},... | collective-permute-start | bytes 589832 | tf_op jit(solution)/shard_map/ppermute | solution.py:265
  8.3 17.4 %collective-permute-start.1 = (bf16[64,1536]{1,0:T(8,128)(2,1)S(1)}, bf16[64,1536]{1,0:T(8,128)(2,1)S(1)}, u32[]{:S(2)}, u32[]{:S(2)}) collective-permute-start(bf16[64,1536]{1,0:T(8,128)(2,1)S(1)} %pad_maximum_fusion.32), channel_id=1, source_target_pairs={{0,16},{2,18},{4,20},{6,22},{8,24},{10,26},{12,28},{14,30},{16,0},... | collective-permute-start | bytes 589832 | tf_op jit(solution)/shard_map/ppermute | solution.py:265
  8.5 17.2 %collective-permute-start = (bf16[64,1536]{1,0:T(8,128)(2,1)S(1)}, bf16[64,1536]{1,0:T(8,128)(2,1)S(1)}, u32[]{:S(2)}, u32[]{:S(2)}) collective-permute-start(bf16[64,1536]{1,0:T(8,128)(2,1)S(1)} %pad_maximum_fusion.32), channel_id=1, source_target_pairs={{0,8},{2,10},{4,12},{6,14},{8,0},{10,2},{12,4},{14,6},{16,24},{18,... | collective-permute-start | bytes 589832 | tf_op jit(solution)/shard_map/ppermute | solution.py:265
  25.8 19.1 %collective-permute-start.4 = (bf16[128,1536]{1,0:T(8,128)(2,1)S(1)}, bf16[128,1536]{1,0:T(8,128)(2,1)S(1)}, u32[]{:S(2)}, u32[]{:S(2)}) collective-permute-start(bf16[128,1536]{1,0:T(8,128)(2,1)S(1)} %pad_maximum_fusion.15), channel_id=1, source_target_pairs={{0,4},{2,6},{4,0},{6,2},{8,12},{10,14},{12,8},{14,10},{16,20},{18,... | collective-permute-start | bytes 1179656 | tf_op jit(solution)/shard_map/ppermute | solution.py:265
  27.4 17.5 %collective-permute-start.5 = (bf16[128,1536]{1,0:T(8,128)(2,1)S(1)}, bf16[128,1536]{1,0:T(8,128)(2,1)S(1)}, u32[]{:S(2)}, u32[]{:S(2)}) collective-permute-start(bf16[128,1536]{1,0:T(8,128)(2,1)S(1)} %pad_maximum_fusion.16), channel_id=1, source_target_pairs={{0,1},{1,0},{2,3},{3,2},{4,5},{5,4},{6,7},{7,6},{8,9},{9,8},{10,11... | collective-permute-start | bytes 1179656 | tf_op jit(solution)/shard_map/ppermute | solution.py:265
  29.0 15.9 %collective-permute-start.6 = (bf16[64,2560]{1,0:T(8,128)(2,1)S(1)}, bf16[64,2560]{1,0:T(8,128)(2,1)S(1)}, u32[]{:S(2)}, u32[]{:S(2)}) collective-permute-start(bf16[64,2560]{1,0:T(8,128)(2,1)S(1)} %pad_maximum_fusion.18), channel_id=1, source_target_pairs={{0,16},{2,18},{4,20},{6,22},{8,24},{10,26},{12,28},{14,30},{16,0},... | collective-permute-start | bytes 983048 | tf_op jit(solution)/shard_map/ppermute | solution.py:265
  31.3 11.2 %collective-permute-start.7 = (bf16[64,2048]{1,0:T(8,128)(2,1)S(1)}, bf16[64,2048]{1,0:T(8,128)(2,1)S(1)}, u32[]{:S(2)}, u32[]{:S(2)}) collective-permute-start(bf16[64,2048]{1,0:T(8,128)(2,1)S(1)} %bitcast.199), channel_id=1, source_target_pairs={{0,8},{2,10},{4,12},{6,14},{8,0},{10,2},{12,4},{14,6},{16,24},{18,... | collective-permute-start | bytes 786440 | tf_op jit(solution)/shard_map/ppermute | solution.py:265
  45.0 18.8 %collective-permute-start.11 = (bf16[256,1536]{1,0:T(8,128)(2,1)S(1)}, bf16[256,1536]{1,0:T(8,128)(2,1)S(1)}, u32[]{:S(2)}, u32[]{:S(2)}) collective-permute-start(bf16[256,1536]{1,0:T(8,128)(2,1)S(1)} %constant_dynamic-update-slice_fusion.2.refs_2_), channel_id=1, source_target_pairs={{0,2},{2,0},{4,6},{6,4},{8,10},{10,8},{12,14},{14,12},{16,18},{18,... | collective-permute-start | bytes 2359304 | tf_op jit(solution)/shard_map/ppermute | solution.py:265
  45.1 20.1 %collective-permute-start.9 = (bf16[256,1536]{1,0:T(8,128)(2,1)S(1)}, bf16[256,1536]{1,0:T(8,128)(2,1)}, u32[]{:S(2)}, u32[]{:S(2)}) collective-permute-start(bf16[256,1536]{1,0:T(8,128)(2,1)S(1)} %constant_dynamic-update-slice_fusion.2.refs_2_), channel_id=1, source_target_pairs={{0,4},{2,6},{4,0},{6,2},{8,12},{10,14},{12,8},{14,10},{16,20},{18,... | collective-permute-start | bytes 2359304 | tf_op jit(solution)/shard_map/ppermute | solution.py:265
  45.8 19.4 %collective-permute-start.10 = (bf16[256,1536]{1,0:T(8,128)(2,1)S(1)}, bf16[256,1536]{1,0:T(8,128)(2,1)S(1)}, u32[]{:S(2)}, u32[]{:S(2)}) collective-permute-start(bf16[256,1536]{1,0:T(8,128)(2,1)S(1)} %constant_dynamic-update-slice_fusion.refs_0_), channel_id=1, source_target_pairs={{0,2},{2,0},{4,6},{6,4},{8,10},{10,8},{12,14},{14,12},{16,18},{18,... | collective-permute-start | bytes 2359304 | tf_op jit(solution)/shard_map/ppermute | solution.py:265
  46.0 20.1 %collective-permute-start.8 = (bf16[256,1536]{1,0:T(8,128)(2,1)S(1)}, bf16[256,1536]{1,0:T(8,128)(2,1)}, u32[]{:S(2)}, u32[]{:S(2)}) collective-permute-start(bf16[256,1536]{1,0:T(8,128)(2,1)S(1)} %constant_dynamic-update-slice_fusion.refs_0_), channel_id=1, source_target_pairs={{0,1},{1,0},{2,3},{3,2},{4,5},{5,4},{6,7},{7,6},{8,9},{9,8},{10,11... | collective-permute-start | bytes 2359304 | tf_op jit(solution)/shard_map/ppermute | solution.py:265
  46.5 17.3 %collective-permute-start.12 = (bf16[64,2560]{1,0:T(8,128)(2,1)S(1)}, bf16[64,2560]{1,0:T(8,128)(2,1)S(1)}, u32[]{:S(2)}, u32[]{:S(2)}) collective-permute-start(bf16[64,2560]{1,0:T(8,128)(2,1)S(1)} %collective-permute-done.3), channel_id=1, source_target_pairs={{0,16},{2,18},{4,20},{6,22},{8,24},{10,26},{12,28},{14,30},{16,0},... | collective-permute-start | bytes 983048 | tf_op jit(solution)/shard_map/ppermute | solution.py:265
  66.3 17.7 %collective-permute-start.15 = (bf16[128,2560]{1,0:T(8,128)(2,1)S(1)}, bf16[128,2560]{1,0:T(8,128)(2,1)}, u32[]{:S(2)}, u32[]{:S(2)}) collective-permute-start(bf16[128,2560]{1,0:T(8,128)(2,1)S(1)} %pad_maximum_fusion.4), channel_id=1, source_target_pairs={{0,4},{2,6},{4,0},{6,2},{8,12},{10,14},{12,8},{14,10},{16,20},{18,... | collective-permute-start | bytes 1966088 | tf_op jit(solution)/shard_map/ppermute | solution.py:265
  67.7 17.4 %collective-permute-start.13 = (bf16[256,1536]{1,0:T(8,128)(2,1)}, bf16[256,1536]{1,0:T(8,128)(2,1)}, u32[]{:S(2)}, u32[]{:S(2)}) collective-permute-start(bf16[256,1536]{1,0:T(8,128)(2,1)} %collective-permute-done.8.refs_1_), channel_id=1, source_target_pairs={{0,2},{2,0},{4,6},{6,4},{8,10},{10,8},{12,14},{14,12},{16,18},{18,... | collective-permute-start | bytes 2359304 | tf_op jit(solution)/shard_map/ppermute | solution.py:265
  67.7 17.4 %collective-permute-start.14 = (bf16[256,1536]{1,0:T(8,128)(2,1)}, bf16[256,1536]{1,0:T(8,128)(2,1)}, u32[]{:S(2)}, u32[]{:S(2)}) collective-permute-start(bf16[256,1536]{1,0:T(8,128)(2,1)} %collective-permute-done.9.refs_3_), channel_id=1, source_target_pairs={{0,2},{2,0},{4,6},{6,4},{8,10},{10,8},{12,14},{14,12},{16,18},{18,... | collective-permute-start | bytes 2359304 | tf_op jit(solution)/shard_map/ppermute | solution.py:265
  68.3 16.8 %collective-permute-start.16 = (bf16[128,2560]{1,0:T(8,128)(2,1)S(1)}, bf16[128,2560]{1,0:T(8,128)(2,1)}, u32[]{:S(2)}, u32[]{:S(2)}) collective-permute-start(bf16[128,2560]{1,0:T(8,128)(2,1)S(1)} %pad_maximum_fusion.5), channel_id=1, source_target_pairs={{0,1},{1,0},{2,3},{3,2},{4,5},{5,4},{6,7},{7,6},{8,9},{9,8},{10,11... | collective-permute-start | bytes 1966088 | tf_op jit(solution)/shard_map/ppermute | solution.py:265
  70.6 13.5 %collective-permute-start.17 = (bf16[64,2048]{1,0:T(8,128)(2,1)S(1)}, bf16[64,2048]{1,0:T(8,128)(2,1)S(1)}, u32[]{:S(2)}, u32[]{:S(2)}) collective-permute-start(bf16[64,2048]{1,0:T(8,128)(2,1)S(1)} %bitcast.200), channel_id=1, source_target_pairs={{0,16},{2,18},{4,20},{6,22},{8,24},{10,26},{12,28},{14,30},{16,0},... | collective-permute-start | bytes 786440 | tf_op jit(solution)/shard_map/ppermute | solution.py:265
  86.4 28.2 %collective-permute-start.21 = (bf16[256,2560]{1,0:T(8,128)(2,1)S(1)}, bf16[256,2560]{1,0:T(8,128)(2,1)S(1)}, u32[]{:S(2)}, u32[]{:S(2)}) collective-permute-start(bf16[256,2560]{1,0:T(8,128)(2,1)S(1)} %constant_dynamic-update-slice_fusion.6.refs_2_), channel_id=1, source_target_pairs={{0,2},{2,0},{4,6},{6,4},{8,10},{10,8},{12,14},{14,12},{16,18},{18,... | collective-permute-start | bytes 3932168 | tf_op jit(solution)/shard_map/ppermute | solution.py:265
  86.5 31.2 %collective-permute-start.19 = (bf16[256,2560]{1,0:T(8,128)(2,1)S(1)}, bf16[256,2560]{1,0:T(8,128)(2,1)S(1)}, u32[]{:S(2)}, u32[]{:S(2)}) collective-permute-start(bf16[256,2560]{1,0:T(8,128)(2,1)S(1)} %constant_dynamic-update-slice_fusion.6.refs_2_), channel_id=1, source_target_pairs={{0,4},{2,6},{4,0},{6,2},{8,12},{10,14},{12,8},{14,10},{16,20},{18,... | collective-permute-start | bytes 3932168 | tf_op jit(solution)/shard_map/ppermute | solution.py:265
  88.5 29.3 %collective-permute-start.20 = (bf16[256,2560]{1,0:T(8,128)(2,1)S(1)}, bf16[256,2560]{1,0:T(8,128)(2,1)S(1)}, u32[]{:S(2)}, u32[]{:S(2)}) collective-permute-start(bf16[256,2560]{1,0:T(8,128)(2,1)S(1)} %constant_dynamic-update-slice_fusion.4.refs_0_), channel_id=1, source_target_pairs={{0,2},{2,0},{4,6},{6,4},{8,10},{10,8},{12,14},{14,12},{16,18},{18,... | collective-permute-start | bytes 3932168 | tf_op jit(solution)/shard_map/ppermute | solution.py:265
  88.7 31.0 %collective-permute-start.18 = (bf16[256,2560]{1,0:T(8,128)(2,1)S(1)}, bf16[256,2560]{1,0:T(8,128)(2,1)S(1)}, u32[]{:S(2)}, u32[]{:S(2)}) collective-permute-start(bf16[256,2560]{1,0:T(8,128)(2,1)S(1)} %constant_dynamic-update-slice_fusion.4.refs_0_), channel_id=1, source_target_pairs={{0,1},{1,0},{2,3},{3,2},{4,5},{5,4},{6,7},{7,6},{8,9},{9,8},{10,11... | collective-permute-start | bytes 3932168 | tf_op jit(solution)/shard_map/ppermute | solution.py:265
  90.0 24.7 %collective-permute-start.22 = (bf16[64,2048]{1,0:T(8,128)(2,1)S(1)}, bf16[64,2048]{1,0:T(8,128)(2,1)S(1)}, u32[]{:S(2)}, u32[]{:S(2)}) collective-permute-start(bf16[64,2048]{1,0:T(8,128)(2,1)S(1)} %copy-done.53), channel_id=1, source_target_pairs={{0,16},{2,18},{4,20},{6,22},{8,24},{10,26},{12,28},{14,30},{16,0},... | collective-permute-start | bytes 786440 | tf_op jit(solution)/shard_map/ppermute | solution.py:265
  119.8 15.8 %collective-permute-start.23 = (bf16[256,2560]{1,0:T(8,128)(2,1)S(1)}, bf16[256,2560]{1,0:T(8,128)(2,1)S(1)}, u32[]{:S(2)}, u32[]{:S(2)}) collective-permute-start(bf16[256,2560]{1,0:T(8,128)(2,1)S(1)} %collective-permute-done.18.refs_1_), channel_id=1, source_target_pairs={{0,2},{2,0},{4,6},{6,4},{8,10},{10,8},{12,14},{14,12},{16,18},{18,... | collective-permute-start | bytes 3932168 | tf_op jit(solution)/shard_map/ppermute | solution.py:265
  119.9 15.7 %collective-permute-start.24 = (bf16[256,2560]{1,0:T(8,128)(2,1)S(1)}, bf16[256,2560]{1,0:T(8,128)(2,1)S(1)}, u32[]{:S(2)}, u32[]{:S(2)}) collective-permute-start(bf16[256,2560]{1,0:T(8,128)(2,1)S(1)} %collective-permute-done.19.refs_3_), channel_id=1, source_target_pairs={{0,2},{2,0},{4,6},{6,4},{8,10},{10,8},{12,14},{14,12},{16,18},{18,... | collective-permute-start | bytes 3932168 | tf_op jit(solution)/shard_map/ppermute | solution.py:265
  120.5 14.0 %collective-permute-start.25 = (bf16[128,2048]{1,0:T(8,128)(2,1)S(1)}, bf16[128,2048]{1,0:T(8,128)(2,1)S(1)}, u32[]{:S(2)}, u32[]{:S(2)}) collective-permute-start(bf16[128,2048]{1,0:T(8,128)(2,1)S(1)} %pad_maximum_fusion.6), channel_id=1, source_target_pairs={{0,4},{2,6},{4,0},{6,2},{8,12},{10,14},{12,8},{14,10},{16,20},{18,... | collective-permute-start | bytes 1572872 | tf_op jit(solution)/shard_map/ppermute | solution.py:265
  121.9 13.7 %collective-permute-start.26 = (bf16[128,2048]{1,0:T(8,128)(2,1)S(1)}, bf16[128,2048]{1,0:T(8,128)(2,1)S(1)}, u32[]{:S(2)}, u32[]{:S(2)}) collective-permute-start(bf16[128,2048]{1,0:T(8,128)(2,1)S(1)} %pad_maximum_fusion.7), channel_id=1, source_target_pairs={{0,1},{1,0},{2,3},{3,2},{4,5},{5,4},{6,7},{7,6},{8,9},{9,8},{10,11... | collective-permute-start | bytes 1572872 | tf_op jit(solution)/shard_map/ppermute | solution.py:265
  135.7 21.3 %collective-permute-start.30 = (bf16[256,2048]{1,0:T(8,128)(2,1)S(1)}, bf16[256,2048]{1,0:T(8,128)(2,1)S(1)}, u32[]{:S(2)}, u32[]{:S(2)}) collective-permute-start(bf16[256,2048]{1,0:T(8,128)(2,1)S(1)} %constant_dynamic-update-slice_fusion.11.refs_2_), channel_id=1, source_target_pairs={{0,2},{2,0},{4,6},{6,4},{8,10},{10,8},{12,14},{14,12},{16,18},{18,... | collective-permute-start | bytes 3145736 | tf_op jit(solution)/shard_map/ppermute | solution.py:265
  135.8 25.6 %collective-permute-start.28 = (bf16[256,2048]{1,0:T(8,128)(2,1)S(1)}, bf16[256,2048]{1,0:T(8,128)(2,1)S(1)}, u32[]{:S(2)}, u32[]{:S(2)}) collective-permute-start(bf16[256,2048]{1,0:T(8,128)(2,1)S(1)} %constant_dynamic-update-slice_fusion.11.refs_2_), channel_id=1, source_target_pairs={{0,4},{2,6},{4,0},{6,2},{8,12},{10,14},{12,8},{14,10},{16,20},{18,... | collective-permute-start | bytes 3145736 | tf_op jit(solution)/shard_map/ppermute | solution.py:265
  136.6 24.7 %collective-permute-start.29 = (bf16[256,2048]{1,0:T(8,128)(2,1)S(1)}, bf16[256,2048]{1,0:T(8,128)(2,1)S(1)}, u32[]{:S(2)}, u32[]{:S(2)}) collective-permute-start(bf16[256,2048]{1,0:T(8,128)(2,1)S(1)} %constant_dynamic-update-slice_fusion.9.refs_0_), channel_id=1, source_target_pairs={{0,2},{2,0},{4,6},{6,4},{8,10},{10,8},{12,14},{14,12},{16,18},{18,... | collective-permute-start | bytes 3145736 | tf_op jit(solution)/shard_map/ppermute | solution.py:265
  136.9 25.4 %collective-permute-start.27 = (bf16[256,2048]{1,0:T(8,128)(2,1)S(1)}, bf16[256,2048]{1,0:T(8,128)(2,1)S(1)}, u32[]{:S(2)}, u32[]{:S(2)}) collective-permute-start(bf16[256,2048]{1,0:T(8,128)(2,1)S(1)} %constant_dynamic-update-slice_fusion.9.refs_0_), channel_id=1, source_target_pairs={{0,1},{1,0},{2,3},{3,2},{4,5},{5,4},{6,7},{7,6},{8,9},{9,8},{10,11... | collective-permute-start | bytes 3145736 | tf_op jit(solution)/shard_map/ppermute | solution.py:265
  162.3 2.7 collective-permute-start.31
  162.3 4.2 %collective-permute-start.32 = (bf16[256,2048]{1,0:T(8,128)(2,1)S(1)}, bf16[256,2048]{1,0:T(8,128)(2,1)S(1)}, u32[]{:S(2)}, u32[]{:S(2)}) collective-permute-start(bf16[256,2048]{1,0:T(8,128)(2,1)S(1)} %collective-permute-done.28.refs_3_), channel_id=1, source_target_pairs={{0,2},{2,0},{4,6},{6,4},{8,10},{10,8},{12,14},{14,12},{16,18},{18,... | collective-permute-start | bytes 3145736 | tf_op jit(solution)/shard_map/ppermute | solution.py:265
  179.4 9.6 %collective-permute-start.34 = (bf16[512,2048]{1,0:T(8,128)(2,1)}, bf16[512,2048]{1,0:T(8,128)(2,1)S(1)}, u32[]{:S(2)}, u32[]{:S(2)}) collective-permute-start(bf16[512,2048]{1,0:T(8,128)(2,1)} %get-tuple-element.289.send_ref), channel_id=1, source_target_pairs={{0,2},{2,0},{4,6},{6,4},{8,10},{10,8},{12,14},{14,12},{16,18},{18,... | collective-permute-start | bytes 6291464 | tf_op jit(solution)/shard_map/ppermute | solution.py:265
  179.6 9.4 %collective-permute-start.33 = (bf16[512,1024]{1,0:T(8,128)(2,1)S(1)}, bf16[512,1024]{1,0:T(8,128)(2,1)S(1)}, u32[]{:S(2)}, u32[]{:S(2)}) collective-permute-start(bf16[512,1024]{1,0:T(8,128)(2,1)S(1)} %convert_element_type.291.rows_ref.refs_0_), channel_id=1, source_target_pairs={{0,2},{2,0},{4,6},{6,4},{8,10},{10,8},{12,14},{14,12},{16,18},{18,... | collective-permute-start | bytes 3145736 | tf_op jit(solution)/shard_map/ppermute | solution.py:265
  190.3 9.2 %collective-permute-start.35 = (bf16[512,2048]{1,0:T(8,128)(2,1)S(1)}, bf16[512,2048]{1,0:T(8,128)(2,1)S(1)}, u32[]{:S(2)}, u32[]{:S(2)}) collective-permute-start(bf16[512,2048]{1,0:T(8,128)(2,1)S(1)} %get-tuple-element.321.send_ref), channel_id=1, source_target_pairs={{0,2},{2,0},{4,6},{6,4},{8,10},{10,8},{12,14},{14,12},{16,18},{18,... | collective-permute-start | bytes 6291464 | tf_op jit(solution)/shard_map/ppermute | solution.py:265
  190.4 9.1 %collective-permute-start.36 = (bf16[512,1024]{1,0:T(8,128)(2,1)S(1)}, bf16[512,1024]{1,0:T(8,128)(2,1)S(1)}, u32[]{:S(2)}, u32[]{:S(2)}) collective-permute-start(bf16[512,1024]{1,0:T(8,128)(2,1)S(1)} %get-tuple-element.305.rows_ref.refs_0_), channel_id=1, source_target_pairs={{0,2},{2,0},{4,6},{6,4},{8,10},{10,8},{12,14},{14,12},{16,18},{18,... | collective-permute-start | bytes 3145736 | tf_op jit(solution)/shard_map/ppermute | solution.py:265
  190.8 8.7 %collective-permute-start.37 = (bf16[512,1024]{1,0:T(8,128)(2,1)S(1)}, bf16[512,1024]{1,0:T(8,128)(2,1)S(1)}, u32[]{:S(2)}, u32[]{:S(2)}) collective-permute-start(bf16[512,1024]{1,0:T(8,128)(2,1)S(1)} %fusion.19.rows_ref.refs_0_), channel_id=1, source_target_pairs={{0,2},{2,0},{4,6},{6,4},{8,10},{10,8},{12,14},{14,12},{16,18},{18,... | collective-permute-start | bytes 3145736 | tf_op jit(solution)/shard_map/ppermute | solution.py:265
  191.0 7.8 %collective-permute-start.38 = (bf16[512,512]{1,0:T(8,128)(2,1)S(1)}, bf16[512,512]{1,0:T(8,128)(2,1)S(1)}, u32[]{:S(2)}, u32[]{:S(2)}) collective-permute-start(bf16[512,512]{1,0:T(8,128)(2,1)S(1)} %get-tuple-element.307.send_ref), channel_id=1, source_target_pairs={{0,2},{2,0},{4,6},{6,4},{8,10},{10,8},{12,14},{14,12},{16,18},{18,... | collective-permute-start | bytes 1572872 | tf_op jit(solution)/shard_map/ppermute | solution.py:265
  199.6 25.3 %collective-permute-start.39 = (bf16[512,1024]{1,0:T(8,128)(2,1)S(1)}, bf16[512,1024]{1,0:T(8,128)(2,1)S(1)}, u32[]{:S(2)}, u32[]{:S(2)}) collective-permute-start(bf16[512,1024]{1,0:T(8,128)(2,1)S(1)} %get-tuple-element.310), channel_id=1, source_target_pairs={{0,1},{1,0},{2,3},{3,2},{4,5},{5,4},{6,7},{7,6},{8,9},{9,8},{10,11... | collective-permute-start | bytes 3145736 | tf_op jit(solution)/shard_map/ppermute | solution.py:265
  200.7 26.3 %collective-permute-start.40 = (bf16[512,1024]{1,0:T(8,128)(2,1)S(1)}, bf16[512,1024]{1,0:T(8,128)(2,1)S(1)}, u32[]{:S(2)}, u32[]{:S(2)}) collective-permute-start(bf16[512,1024]{1,0:T(8,128)(2,1)S(1)} %get-tuple-element.312), channel_id=1, source_target_pairs={{0,4},{2,6},{4,0},{6,2},{8,12},{10,14},{12,8},{14,10},{16,20},{18,... | collective-permute-start | bytes 3145736 | tf_op jit(solution)/shard_map/ppermute | solution.py:265
  229.5 35.9 %collective-permute-start.42 = (bf16[768,1024]{1,0:T(8,128)(2,1)}, bf16[768,1024]{1,0:T(8,128)(2,1)}, u32[]{:S(2)}, u32[]{:S(2)}) collective-permute-start(bf16[768,1024]{1,0:T(8,128)(2,1)} %pad_maximum_fusion.1), channel_id=1, source_target_pairs={{0,1},{1,0},{2,3},{3,2},{4,5},{5,4},{6,7},{7,6},{8,9},{9,8},{10,11... | collective-permute-start | bytes 4718600 | tf_op jit(solution)/shard_map/ppermute | solution.py:265
  234.0 35.4 %collective-permute-start.41 = (bf16[768,1024]{1,0:T(8,128)(2,1)S(1)}, bf16[768,1024]{1,0:T(8,128)(2,1)S(1)}, u32[]{:S(2)}, u32[]{:S(2)}) collective-permute-start(bf16[768,1024]{1,0:T(8,128)(2,1)S(1)} %pad_maximum_fusion), channel_id=1, source_target_pairs={{0,4},{2,6},{4,0},{6,2},{8,12},{10,14},{12,8},{14,10},{16,20},{18,... | collective-permute-start | bytes 4718600 | tf_op jit(solution)/shard_map/ppermute | solution.py:265
  258.4 12.6 %collective-permute-start.44 = (bf16[512,1024]{1,0:T(8,128)(2,1)S(1)}, bf16[512,1024]{1,0:T(8,128)(2,1)S(1)}, u32[]{:S(2)}, u32[]{:S(2)}) collective-permute-start(bf16[512,1024]{1,0:T(8,128)(2,1)S(1)} %get-tuple-element.337.rows_ref.refs_4_), channel_id=1, source_target_pairs={{0,2},{2,0},{4,6},{6,4},{8,10},{10,8},{12,14},{14,12},{16,18},{18,... | collective-permute-start | bytes 3145736 | tf_op jit(solution)/shard_map/ppermute | solution.py:265
  258.5 12.5 %collective-permute-start.43 = (bf16[512,1536]{1,0:T(8,128)(2,1)S(1)}, bf16[512,1536]{1,0:T(8,128)(2,1)S(1)}, u32[]{:S(2)}, u32[]{:S(2)}) collective-permute-start(bf16[512,1536]{1,0:T(8,128)(2,1)S(1)} %get-tuple-element.358.send_ref), channel_id=1, source_target_pairs={{0,2},{2,0},{4,6},{6,4},{8,10},{10,8},{12,14},{14,12},{16,18},{18,... | collective-permute-start | bytes 4718600 | tf_op jit(solution)/shard_map/ppermute | solution.py:265
  281.1 34.8 %collective-permute-start.49 = (bf16[768,1024]{1,0:T(8,128)(2,1)}, bf16[768,1024]{1,0:T(8,128)(2,1)}, u32[]{:S(2)}, u32[]{:S(2)}) collective-permute-start(bf16[768,1024]{1,0:T(8,128)(2,1)} %pad_maximum_fusion.3), channel_id=1, source_target_pairs={{0,1},{1,0},{2,3},{3,2},{4,5},{5,4},{6,7},{7,6},{8,9},{9,8},{10,11... | collective-permute-start | bytes 4718600 | tf_op jit(solution)/shard_map/ppermute | solution.py:265
  282.2 11.3 %collective-permute-start.45 = (bf16[128,1024]{1,0:T(8,128)(2,1)S(1)}, bf16[128,1024]{1,0:T(8,128)(2,1)S(1)}, u32[]{:S(2)}, u32[]{:S(2)}) collective-permute-start(bf16[128,1024]{1,0:T(8,128)(2,1)S(1)} %pad_maximum_fusion.19), channel_id=1, source_target_pairs={{0,8},{2,10},{4,12},{6,14},{8,0},{10,2},{12,4},{14,6},{16,24},{18,... | collective-permute-start | bytes 786440 | tf_op jit(solution)/shard_map/ppermute | solution.py:265
  283.6 35.4 %collective-permute-start.48 = (bf16[768,1024]{1,0:T(8,128)(2,1)}, bf16[768,1024]{1,0:T(8,128)(2,1)}, u32[]{:S(2)}, u32[]{:S(2)}) collective-permute-start(bf16[768,1024]{1,0:T(8,128)(2,1)} %pad_maximum_fusion.2), channel_id=1, source_target_pairs={{0,4},{2,6},{4,0},{6,2},{8,12},{10,14},{12,8},{14,10},{16,20},{18,... | collective-permute-start | bytes 4718600 | tf_op jit(solution)/shard_map/ppermute | solution.py:265
  285.0 20.5 %collective-permute-start.46 = (bf16[128,1024]{1,0:T(8,128)(2,1)S(1)}, bf16[128,1024]{1,0:T(8,128)(2,1)S(1)}, u32[]{:S(2)}, u32[]{:S(2)}) collective-permute-start(bf16[128,1024]{1,0:T(8,128)(2,1)S(1)} %pad_maximum_fusion.20), channel_id=1, source_target_pairs={{0,16},{2,18},{4,20},{6,22},{8,24},{10,26},{12,28},{14,30},{16,0},... | collective-permute-start | bytes 786440 | tf_op jit(solution)/shard_map/ppermute | solution.py:265
  287.9 17.7 %collective-permute-start.47 = (bf16[128,1024]{1,0:T(8,128)(2,1)S(1)}, bf16[128,1024]{1,0:T(8,128)(2,1)}, u32[]{:S(2)}, u32[]{:S(2)}) collective-permute-start(bf16[128,1024]{1,0:T(8,128)(2,1)S(1)} %pad_maximum_fusion.21), channel_id=1, source_target_pairs={{0,24},{2,26},{4,28},{6,30},{8,16},{10,18},{12,20},{14,22},{16,8},... | collective-permute-start | bytes 786440 | tf_op jit(solution)/shard_map/ppermute | solution.py:265
  321.3 21.9 %collective-permute-start.50 = (bf16[128,1024]{1,0:T(8,128)(2,1)S(1)}, bf16[128,1024]{1,0:T(8,128)(2,1)S(1)}, u32[]{:S(2)}, u32[]{:S(2)}) collective-permute-start(bf16[128,1024]{1,0:T(8,128)(2,1)S(1)} %pad_maximum_fusion.22), channel_id=1, source_target_pairs={{0,8},{2,10},{4,12},{6,14},{8,0},{10,2},{12,4},{14,6},{16,24},{18,... | collective-permute-start | bytes 786440 | tf_op jit(solution)/shard_map/ppermute | solution.py:265
  322.5 20.8 %collective-permute-start.51 = (bf16[128,1024]{1,0:T(8,128)(2,1)S(1)}, bf16[128,1024]{1,0:T(8,128)(2,1)S(1)}, u32[]{:S(2)}, u32[]{:S(2)}) collective-permute-start(bf16[128,1024]{1,0:T(8,128)(2,1)S(1)} %pad_maximum_fusion.23), channel_id=1, source_target_pairs={{0,16},{2,18},{4,20},{6,22},{8,24},{10,26},{12,28},{14,30},{16,0},... | collective-permute-start | bytes 786440 | tf_op jit(solution)/shard_map/ppermute | solution.py:265
  324.4 18.9 %collective-permute-start.52 = (bf16[128,1024]{1,0:T(8,128)(2,1)S(1)}, bf16[128,1024]{1,0:T(8,128)(2,1)S(1)}, u32[]{:S(2)}, u32[]{:S(2)}) collective-permute-start(bf16[128,1024]{1,0:T(8,128)(2,1)S(1)} %pad_maximum_fusion.24), channel_id=1, source_target_pairs={{0,24},{2,26},{4,28},{6,30},{8,16},{10,18},{12,20},{14,22},{16,8},... | collective-permute-start | bytes 786440 | tf_op jit(solution)/shard_map/ppermute | solution.py:265
  326.0 17.5 %collective-permute-start.53 = (bf16[256,1024]{1,0:T(8,128)(2,1)S(1)}, bf16[256,1024]{1,0:T(8,128)(2,1)S(1)}, u32[]{:S(2)}, u32[]{:S(2)}) collective-permute-start(bf16[256,1024]{1,0:T(8,128)(2,1)S(1)} %pad_maximum_fusion.13), channel_id=1, source_target_pairs={{0,4},{2,6},{4,0},{6,2},{8,12},{10,14},{12,8},{14,10},{16,20},{18,... | collective-permute-start | bytes 1572872 | tf_op jit(solution)/shard_map/ppermute | solution.py:265
  327.4 16.3 %collective-permute-start.54 = (bf16[256,1024]{1,0:T(8,128)(2,1)S(1)}, bf16[256,1024]{1,0:T(8,128)(2,1)S(1)}, u32[]{:S(2)}, u32[]{:S(2)}) collective-permute-start(bf16[256,1024]{1,0:T(8,128)(2,1)S(1)} %get-tuple-element.365), channel_id=1, source_target_pairs={{0,1},{1,0},{2,3},{3,2},{4,5},{5,4},{6,7},{7,6},{8,9},{9,8},{10,11... | collective-permute-start | bytes 1572872 | tf_op jit(solution)/shard_map/ppermute | solution.py:265
  344.0 5.2 %collective-permute-start.58 = (f32[12,1024]{1,0:T(8,128)S(1)}, f32[12,1024]{1,0:T(8,128)S(1)}, u32[]{:S(2)}, u32[]{:S(2)}) collective-permute-start(f32[12,1024]{1,0:T(8,128)S(1)} %concatenate.418), channel_id=1, source_target_pairs={{0,2},{2,0},{4,6},{6,4},{8,10},{10,8},{12,14},{14,12},{16,18},{18,... | collective-permute-start | bytes 147464 | tf_op jit(solution)/shard_map/ppermute | solution.py:265
  344.1 31.7 %collective-permute-start.55 = (bf16[128,1024]{1,0:T(8,128)(2,1)S(1)}, bf16[128,1024]{1,0:T(8,128)(2,1)S(1)}, u32[]{:S(2)}, u32[]{:S(2)}) collective-permute-start(bf16[128,1024]{1,0:T(8,128)(2,1)S(1)} %pad_maximum_fusion.25), channel_id=1, source_target_pairs={{0,8},{2,10},{4,12},{6,14},{8,0},{10,2},{12,4},{14,6},{16,24},{18,... | collective-permute-start | bytes 786440 | tf_op jit(solution)/shard_map/ppermute | solution.py:265
  346.6 29.2 %collective-permute-start.56 = (bf16[128,1024]{1,0:T(8,128)(2,1)S(1)}, bf16[128,1024]{1,0:T(8,128)(2,1)S(1)}, u32[]{:S(2)}, u32[]{:S(2)}) collective-permute-start(bf16[128,1024]{1,0:T(8,128)(2,1)S(1)} %pad_maximum_fusion.26), channel_id=1, source_target_pairs={{0,16},{2,18},{4,20},{6,22},{8,24},{10,26},{12,28},{14,30},{16,0},... | collective-permute-start | bytes 786440 | tf_op jit(solution)/shard_map/ppermute | solution.py:265
  347.4 28.4 %collective-permute-start.57 = (bf16[128,1024]{1,0:T(8,128)(2,1)S(1)}, bf16[128,1024]{1,0:T(8,128)(2,1)S(1)}, u32[]{:S(2)}, u32[]{:S(2)}) collective-permute-start(bf16[128,1024]{1,0:T(8,128)(2,1)S(1)} %pad_maximum_fusion.27), channel_id=1, source_target_pairs={{0,24},{2,26},{4,28},{6,30},{8,16},{10,18},{12,20},{14,22},{16,8},... | collective-permute-start | bytes 786440 | tf_op jit(solution)/shard_map/ppermute | solution.py:265
  349.2 4.3 %collective-permute-start.59 = (f32[12,1024]{1,0:T(8,128)S(1)}, f32[12,1024]{1,0:T(8,128)S(1)}, u32[]{:S(2)}, u32[]{:S(2)}) collective-permute-start(f32[12,1024]{1,0:T(8,128)S(1)} %add.359), channel_id=1, source_target_pairs={{0,4},{2,6},{4,0},{6,2},{8,12},{10,14},{12,8},{14,10},{16,20},{18,... | collective-permute-start | bytes 147464 | tf_op jit(solution)/shard_map/ppermute | solution.py:265
  353.5 4.3 %collective-permute-start.60 = (f32[12,1024]{1,0:T(8,128)S(1)}, f32[12,1024]{1,0:T(8,128)S(1)}, u32[]{:S(2)}, u32[]{:S(2)}) collective-permute-start(f32[12,1024]{1,0:T(8,128)S(1)} %add.360), channel_id=1, source_target_pairs={{0,1},{1,0},{2,3},{3,2},{4,5},{5,4},{6,7},{7,6},{8,9},{9,8},{10,11... | collective-permute-start | bytes 147464 | tf_op jit(solution)/shard_map/ppermute | solution.py:265
  357.8 10.2 %collective-permute-start.61 = (f32[12,1024]{1,0:T(8,128)S(1)}, f32[12,1024]{1,0:T(8,128)S(1)}, u32[]{:S(2)}, u32[]{:S(2)}) collective-permute-start(f32[12,1024]{1,0:T(8,128)S(1)} %add.361), channel_id=1, source_target_pairs={{0,8},{2,10},{4,12},{6,14},{8,0},{10,2},{12,4},{14,6},{16,24},{18,... | collective-permute-start | bytes 147464 | tf_op jit(solution)/shard_map/ppermute | solution.py:265
  359.1 16.9 %collective-permute-start.63 = (f32[64,2048]{1,0:T(8,128)S(1)}, f32[64,2048]{1,0:T(8,128)S(1)}, u32[]{:S(2)}, u32[]{:S(2)}) collective-permute-start(f32[64,2048]{1,0:T(8,128)S(1)} %maximum_maximum_fusion), channel_id=1, source_target_pairs={{0,2},{2,0},{4,6},{6,4},{8,10},{10,8},{12,14},{14,12},{16,18},{18,... | collective-permute-start | bytes 1572872 | tf_op jit(solution)/shard_map/ppermute | solution.py:265
  368.0 7.7 %collective-permute-start.62 = (f32[12,1024]{1,0:T(8,128)S(1)}, f32[12,1024]{1,0:T(8,128)S(1)}, u32[]{:S(2)}, u32[]{:S(2)}) collective-permute-start(f32[12,1024]{1,0:T(8,128)S(1)} %add.362), channel_id=1, source_target_pairs={{0,16},{2,18},{4,20},{6,22},{8,24},{10,26},{12,28},{14,30},{16,0},... | collective-permute-start | bytes 147464 | tf_op jit(solution)/shard_map/ppermute | solution.py:265
  (66 other events, 631.7 us)
